TPU v7x, 32 devices: a whole 2x2x4 slice. The times are simulated.
32 devices in a mesh: func: 4 (over z), box: 8 (over y, x, core).
Axes of the slice: x: 2, y: 2, z: 4, core: 2. Of those that a mesh axis runs over, the one named last changes fastest.
Arguments:
- coeffs: bfloat16 [768, 32, 1024], P(('func', 'box')), may hold values from -8 to 8
- centers: int32 [768], replicated, may hold values from 0 to 383, as said below
- kinetic: bfloat16 [1024, 1024], replicated, may hold values from -0.1875 to 0.1875
- potential: float32 [384, 1024], P(('func', 'box')), may hold values from -1 to 1
Outputs:
- filtered: bfloat16 [768, 32, 1024], P(('func', 'box'))
- gram_band: float32 [768, 256], P(('func', 'box'))
Inputs may be any that keep to these rules, and one draw needn't show every extreme that they name: `centers`: centers never fall. The boxes form aligned groups of 32, and the groups aligned blocks of four; every box of a group is the center of the same number of functions, 1, 2 or 4, and each block of four groups holds the numbers 1, 1, 2 and 4 in an order whose running total of (number - 2) stays between -1 and 1. So between 32 and 128 functions touch each box, and some box is touched by exactly 128.
All inputs are finite; a program needn't handle non-finite values.
Results may differ from a plain program's by a relative error of at most 0.0057.
Values may be sent and summed in bfloat16 or wider, within the bound.
No kernel may reach another device: no remote copies, remote signals or barrier semaphores. Data moves between devices by JAX's collectives and lax.ppermute only.
A program may use at most 64 MiB of HBM per device.

v0:
```python
import functools
import itertools

import jax
import jax.numpy as jnp
import numpy as np
from jax import lax
from jax.experimental import pallas as pl
from jax.experimental.pallas import tpu as pltpu
from jax.sharding import PartitionSpec as P

AXES = ("func", "box")
REACH = 3
SLOT = 32
STEP = 8


def passed_along(value, steps):
    count = lax.axis_size(AXES)
    pairs = [(source, (source + steps) % count) for source in range(count)]
    return lax.ppermute(value, AXES, pairs)


def sent_in_order(values, order, sign):
    there = {}
    for k in order:
        value = values[k]
        if k == order[-1]:
            value, there[order[0]] = lax.optimization_barrier((value, there[order[0]]))
        there[k] = passed_along(value, sign * k)
    return there


def rounded_up(value, multiple):
    return -(-int(value) // multiple) * multiple


@functools.lru_cache(maxsize=None)
def bounds(fun_dev, support):
    box_dev = fun_dev // 2
    orders = [
        order
        for order in sorted(set(itertools.permutations((1, 1, 2, 4))))
        if np.abs(np.cumsum(np.array(order) - 2)).max() <= 1
    ]
    box_all, fun_all = 12 * support, 24 * support
    assert fun_all % fun_dev == 0
    devices = fun_all // fun_dev
    rows = np.zeros(2 * REACH + 1, np.int64)
    low, high, boxes, end = 10**6, -(10**6), 0, 0
    for picks in itertools.product(orders, repeat=3):
        density = np.repeat(np.concatenate(picks), support)
        centers = np.repeat(np.arange(box_all), density)
        load = sum(np.roll(density, t) for t in range(support))
        below = np.concatenate([[0], np.cumsum(np.tile(load, 3))])
        over = np.clip(np.arange(box_all)[:, None] + support - box_all, 0, None)
        carried = int((over[:, 0] * density).sum())
        below = below - carried
        twice = below[:-1] + below[1:]
        cut = np.array([
            np.searchsorted(twice, 2 * support * fun_dev * (devices + d), side="right")
            for d in range(-REACH - 1, devices + REACH + 2)
        ]) - box_all
        first = REACH + 1
        width = np.diff(cut)
        place = cut - box_dev * (np.arange(len(cut)) - first)
        low, high = min(low, place.min()), max(high, place.max())
        boxes = max(boxes, width.max())
        end = max(end, (place[:-1] + width).max())
        box = centers[:, None] + np.arange(support)
        owner = np.searchsorted(cut, box, side="right") - 1 - first
        device = np.arange(fun_all)[:, None] // fun_dev
        offset = owner - device
        assert np.abs(offset).max() <= REACH
        count = np.bincount((device * (2 * REACH + 1) + offset + REACH).ravel(), minlength=devices * (2 * REACH + 1))
        rows = np.maximum(rows, count.reshape(devices, -1).max(0))
    return (
        tuple(int(r) for r in rows),
        int(low),
        int(high),
        rounded_up(boxes, STEP),
        -(-int(end) // box_dev),
    )


def iota(shape, dim):
    return lax.broadcasted_iota(jnp.int32, shape, dim).astype(jnp.float32)


def one_hot(mask):
    return jnp.where(mask, 1.0, 0.0).astype(jnp.bfloat16)


def spread_over(column, to):
    return jnp.sum(jnp.where(iota((column.shape[0], to.shape[1]), 0) == to, column, 0.0), axis=0, keepdims=True)


def times(a, b, dims=((1,), (0,)), precision=None):
    return lax.dot_general(
        a, b, (dims, ((), ())), precision=precision, preferred_element_type=jnp.float32
    )


def pack_kernel(plan, me_ref, centers_ref, flat_ref, potential_ref, *refs):
    fun_dev, support, devices, halo, rows, back, low_cut, high_cut = plan
    slots = 2 * REACH + 1
    outs = dict(zip([k for k in range(-REACH, REACH + 1) if k], refs[: slots - 1]))
    near_ref, cut_ref, home_ref, own_ref = refs[slots - 1 :]
    me = me_ref[0]
    box_dev = fun_dev // 2
    fun_all, box_all = fun_dev * devices, box_dev * devices
    count = near_ref.shape[0]

    start = me * fun_dev - halo * fun_dev
    start = jnp.where(start < 0, start + fun_all, start).astype(jnp.float32)
    at = start + iota((count, 1), 0)
    at = jnp.where(at >= fun_all, at - fun_all, at)
    near = jnp.sum(
        jnp.where(iota((count, fun_all), 1) == at, centers_ref[...].astype(jnp.float32), 0.0), axis=1, keepdims=True
    )
    near = near - (me * box_dev).astype(jnp.float32)
    near = jnp.where(near < -(box_all // 2), near + box_all, near)
    near = jnp.where(near >= box_all // 2, near - box_all, near)
    near_row = spread_over(near, iota((1, count), 1))
    near_ref[...] = jnp.broadcast_to(near, near_ref.shape)

    tries = high_cut - low_cut + 1
    trial = iota((rounded_up(tries, 8), 1), 0)
    cuts = []
    for k in range(-REACH, REACH + 2):
        gap = trial + float(low_cut + k * box_dev) - near_row
        twice = jnp.sum(
            jnp.clip(gap, 0.0, support) + jnp.clip(gap + 1.0, 0.0, support), axis=1, keepdims=True
        )
        goal = float(2 * support * fun_dev * (halo + k))
        passed = jnp.where((twice <= goal) & (trial < tries), 1.0, 0.0)
        cut = jnp.sum(passed) + float(low_cut + k * box_dev)
        cuts.append(cut)
        cut_ref[k + REACH] = cut.astype(jnp.int32)

    mine = near[halo * fun_dev : (halo + 1) * fun_dev]
    pieces = fun_dev * support
    piece = lax.broadcasted_iota(jnp.int32, (1, pieces), 1)
    of_fun = lax.shift_right_logical(piece, support.bit_length() - 1).astype(jnp.float32)
    step = piece.astype(jnp.float32) - of_fun * support
    mine_row = spread_over(mine, of_fun)
    earlier = iota((fun_dev, pieces), 0) < of_fun
    potential = potential_ref[...]
    high = potential.astype(jnp.bfloat16)
    own_ref[: potential.shape[0]] = high
    own_ref[potential.shape[0] :] = (potential - high.astype(jnp.float32)).astype(jnp.bfloat16)
    home, base = jnp.zeros((1, pieces), jnp.float32), 0
    for k in range(-REACH, REACH + 1):
        first, end = cuts[k + REACH], cuts[k + REACH + 1]
        leave = jnp.clip(end - mine, 0.0, support) - jnp.clip(first - mine, 0.0, support)
        leave_at = jnp.sum(jnp.where(earlier, leave, 0.0), axis=0, keepdims=True)
        low_edge = jnp.clip(first - mine_row, 0.0, support)
        goes = (step >= low_edge) & (step < jnp.clip(end - mine_row, 0.0, support))
        row = leave_at + step - low_edge
        home = home + jnp.where(goes, row + float(base), 0.0)
        base += back[k + REACH]
        if k:
            row = jnp.where(goes, row, -1.0)
            sent = outs[k].shape[0]
            value = times(one_hot(iota((sent, pieces), 0) == row), flat_ref[...])
            if k < 0:
                shape = (sent, own_ref.shape[0])
                part = iota(shape, 0) - float(rows[k + REACH])
                col = iota(shape, 1)
                half = float(own_ref.shape[0] // 2)
                from_col = jnp.where(part < box_dev, part, part - box_dev + half)
                inside = (part >= 0) & (part < 2 * box_dev)
                value = value + times(one_hot(inside & (col == from_col)), own_ref[...])
            outs[k][...] = value.astype(jnp.bfloat16)
    home_ref[...] = home


def table_kernel(plan, cut_ref, near_ref, column_ref, place_ref, active_ref):
    fun_dev, support, halo, boxes = plan
    slots = 2 * REACH + 1
    first = cut_ref[REACH].astype(jnp.float32)
    end = cut_ref[REACH + 1].astype(jnp.float32)
    lane = iota((SLOT, 128), 1)
    along = lax.broadcasted_iota(jnp.int32, (1, boxes * SLOT), 1)
    box = lax.shift_right_logical(along, SLOT.bit_length() - 1).astype(jnp.float32)
    of_fun = along.astype(jnp.float32) - box * SLOT
    for e in range(slots):
        at = (halo - REACH + e) * fun_dev
        others = near_ref[at : at + fun_dev, 0:1]
        edge_low = jnp.clip(first - others, 0.0, support)
        edge_high = jnp.clip(end - others, 0.0, support)
        come = edge_high - edge_low
        come_row = spread_over(come, lane[:1])
        come_at = jnp.sum(
            jnp.where(lane[:fun_dev] < iota((fun_dev, 128), 0), come_row, 0.0), axis=1, keepdims=True
        )
        box_low = edge_low + others - first
        box_high = edge_high + others - first
        packed = come_at - box_low
        unpacked = iota((fun_dev, 1), 0) * support + first - others if e == REACH else packed
        spare = jnp.zeros((SLOT - fun_dev, 1), jnp.float32)
        packed, unpacked, box_low, box_high = (
            jnp.concatenate([column, spare], axis=0) for column in (packed, unpacked, box_low, box_high)
        )
        column_ref[e * SLOT : (e + 1) * SLOT, :] = jnp.where(
            lane == 0.0, unpacked, jnp.where(lane == 1.0, box_low, box_high)
        )
        lies = (box >= spread_over(box_low, of_fun)) & (box < spread_over(box_high, of_fun))
        place_ref[e : e + 1, :] = jnp.where(lies, spread_over(packed, of_fun) + box, -1.0)
        for g in range(boxes // STEP):
            here = (box >= g * STEP) & (box < (g + 1) * STEP) & lies
            active_ref[e * (boxes // STEP) + g] = jnp.sum(jnp.where(here, 1.0, 0.0)).astype(jnp.int32)
    place_ref[slots:, :] = jnp.full((place_ref.shape[0] - slots, boxes * SLOT), -1.0, jnp.float32)


def function_of(shape, dim, fun_dev):
    row = lax.broadcasted_iota(jnp.int32, shape, dim)
    slot = lax.shift_right_logical(row, SLOT.bit_length() - 1)
    in_slot = row - slot * SLOT
    return jnp.where(in_slot < fun_dev, slot * fun_dev + in_slot, -1)


def moved(value, shift):
    return pltpu.roll(value, shift % value.shape[1], 1)


def skewed(value, sign):
    row = lax.broadcasted_iota(jnp.int32, value.shape, 0)
    bit = 1
    while bit < value.shape[0]:
        value = jnp.where((row & bit) != 0, moved(value, sign * bit), value)
        bit *= 2
    return value


def band_lanes(fun_dev, reading):
    window = (2 * REACH + 1) * fun_dev
    return rounded_up(window + reading + fun_dev + max(0, window - reading), 128)


def unpack_kernel(plan, cut_ref, active_ref, column_ref, own_ref, *refs):
    fun_dev, box_dev, reading, volume, rows, back, blocks = plan
    slots = 2 * REACH + 1
    sources = refs[:slots]
    window_ref, region_ref = refs[slots : slots + 2]
    gram_refs = refs[slots + 2 : -1]
    total = refs[-1]
    step, steps = pl.program_id(0), pl.num_programs(0)
    first = step * STEP
    width = cut_ref[REACH + 1] - cut_ref[REACH]

    @pl.when(step == 0)
    def _():
        total[...] = jnp.zeros_like(total)
        value = None
        for t in range(blocks):
            held = own_ref if t == 0 else sources[REACH + t]
            at = 0 if t == 0 else rows[REACH + t]
            from_row = at // 16 * 16
            held = held[from_row:]
            second = own_ref.shape[0] // 2 if t == 0 else box_dev
            shape = (region_ref.shape[0], held.shape[0])
            row, col = iota(shape, 0), iota(shape, 1)
            box = row - jnp.where(row >= SLOT, float(SLOT), 0.0) + cut_ref[REACH].astype(jnp.float32) - t * box_dev
            wanted = box + jnp.where(row >= SLOT, float(second), 0.0) + float(at - from_row)
            good = (box >= 0) & (box < box_dev) & (row < 2 * SLOT)
            term = times(one_hot(good & (col == wanted)), held)
            value = term if value is None else value + term
        region_ref[...] = value.astype(jnp.bfloat16)

    @pl.when(first < width)
    def _():
        for e in range(slots):
            used = active_ref[e * steps + step] > 0

            @pl.when(used)
            def _():
                start = column_ref[e * SLOT : (e + 1) * SLOT, 0:1]
                low = column_ref[e * SLOT : (e + 1) * SLOT, 1:2]
                high = column_ref[e * SLOT : (e + 1) * SLOT, 2:3]
                lane = iota((SLOT, back[e]), 1)
                picks = []
                for b in range(STEP):
                    box = (first + b).astype(jnp.float32)
                    row = jnp.where((box >= low) & (box < high), start + box, -1.0)
                    picks.append(one_hot(lane == row))
                found = times(jnp.concatenate(picks, axis=0), sources[e][: back[e]])
                window_ref[:, e * SLOT : (e + 1) * SLOT, :] = found.astype(jnp.bfloat16).reshape(
                    STEP, SLOT, found.shape[-1]
                )

            @pl.when(jnp.logical_not(used))
            def _():
                window_ref[:, e * SLOT : (e + 1) * SLOT, :] = jnp.zeros(
                    (STEP, SLOT, window_ref.shape[-1]), jnp.bfloat16
                )
        value = total[...]
        for b in range(STEP):
            here = window_ref[b]
            value = value + times(here, here, ((1,), (1,)))
        total[...] = value

    @pl.when(step == steps - 1)
    def _():
        wide, lanes = total.shape[0], band_lanes(fun_dev, reading)
        keep = jnp.where(
            function_of((wide, lanes), 0, fun_dev) == lax.broadcasted_iota(jnp.int32, (wide, lanes), 1), volume, 0.0
        )
        dense = times(total[...], keep, precision=lax.Precision.HIGHEST)
        for e in range(slots):
            rows_here = dense[e * SLOT : e * SLOT + fun_dev]
            gram_refs[e][...] = skewed(moved(rows_here, reading - 1 - e * fun_dev), -1)[:, : 2 * reading]


def sum_kernel(reading, *refs):
    gram_ref, mixing_ref = refs[-2:]
    value = refs[0][...]
    for ref in refs[1:-2]:
        value = value + ref[...]
    gram_ref[...] = value
    diagonal = jnp.where(lax.broadcasted_iota(jnp.int32, value.shape, 1) == reading - 1, 1.5, 0.0)
    row = diagonal - 0.5 * value
    spare = jnp.zeros((mixing_ref.shape[0] - row.shape[0], row.shape[1]), jnp.float32)
    mixing_ref[...] = jnp.concatenate([row, spare], axis=0).astype(jnp.bfloat16)


def mix_kernel(plan, cut_ref, active_ref, place_ref, window_ref, *refs):
    fun_dev, reading = plan
    slots = 2 * REACH + 1
    bands = refs[:slots]
    outs = refs[slots : 2 * slots]
    at_boxes = refs[2 * slots : 3 * slots]
    mixing, mixed = refs[3 * slots :]
    step, steps = pl.program_id(0), pl.num_programs(0)
    width = cut_ref[REACH + 1] - cut_ref[REACH]
    wide = slots * SLOT

    @pl.when(step == 0)
    def _():
        for out, at_box in zip(outs, at_boxes):
            out[...] = jnp.zeros_like(out)
            at_box[...] = jnp.zeros_like(at_box)
        lanes = band_lanes(fun_dev, reading)
        parts = []
        for e in range(slots):
            band = bands[e][...].astype(jnp.float32)
            band = jnp.concatenate([band, jnp.zeros((SLOT, lanes - 2 * reading), jnp.float32)], axis=1)
            parts.append(moved(skewed(band, 1), e * fun_dev - (reading - 1)))
        dense = jnp.concatenate(parts, axis=0).astype(jnp.bfloat16)
        keep = one_hot(
            function_of((lanes, wide), 1, fun_dev) == lax.broadcasted_iota(jnp.int32, (lanes, wide), 0)
        )
        mixing[...] = times(dense, keep).astype(jnp.bfloat16)

    @pl.when(step * STEP < width)
    def _():
        for b in range(STEP):
            mixed[b] = times(mixing[...], window_ref[b]).astype(jnp.bfloat16)
        shape = (STEP * SLOT, at_boxes[0].shape[1])
        along = lax.broadcasted_iota(jnp.int32, shape, 0)
        box = lax.shift_right_logical(along, SLOT.bit_length() - 1) + step * STEP
        col = lax.broadcasted_iota(jnp.int32, shape, 1)
        boxes_of = one_hot((col == box) | (col == box + SLOT))
        for e in range(slots):
            @pl.when(active_ref[e * steps + step] > 0)
            def _():
                pick = one_hot(iota((outs[e].shape[0], STEP * SLOT), 0) == place_ref[e : e + 1, :])
                part = mixed[:, e * SLOT : (e + 1) * SLOT, :].reshape(STEP * SLOT, mixed.shape[-1])
                outs[e][...] += times(pick, part).astype(jnp.bfloat16)
                at_boxes[e][...] += times(pick, boxes_of).astype(jnp.bfloat16)


def filter_kernel(region_ref, kinetic_ref, *refs):
    count = len(refs) // 3
    for here_ref, at_box_ref, out_ref in zip(refs[:count], refs[count : 2 * count], refs[2 * count :]):
        here = here_ref[...]
        local = times(at_box_ref[...], region_ref[...])
        applied = times(here, kinetic_ref[...])
        out_ref[...] = (applied + local * here.astype(jnp.float32)).astype(jnp.bfloat16)


def home_kernel(groups, home_ref, *refs):
    sources, out_ref = refs[:-1], refs[-1]
    count = out_ref.shape[0]
    shape = (count, home_ref.shape[1])
    at = iota(shape, 0) + (pl.program_id(0) * count).astype(jnp.float32)
    row = jnp.sum(jnp.where(iota(shape, 1) == at, home_ref[...], 0.0), axis=1, keepdims=True)
    value, base = None, 0
    for group in groups:
        parts = [sources[e][...] for e in group]
        held = parts[0] if len(parts) == 1 else jnp.concatenate(parts, axis=0)
        pick = one_hot(iota((count, held.shape[0]), 1) == row - float(base))
        base += held.shape[0]
        term = times(pick, held)
        value = term if value is None else value + term
    out_ref[...] = value.astype(jnp.bfloat16)


def whole(shape):
    return pl.BlockSpec(shape, lambda g: (0,) * len(shape))


def on_device(coeffs, centers, kinetic, potential):
    fun_dev, support, points = coeffs.shape
    devices = lax.axis_size(AXES)
    me = lax.axis_index(AXES).astype(jnp.int32).reshape(1)
    box_dev = fun_dev // 2
    volume = 1.0 / (support * points)
    reading = 4 * support
    slots = 2 * REACH + 1
    offsets = list(range(-REACH, REACH + 1))
    order = [REACH, -REACH] + [sign * k for k in range(REACH - 1, 0, -1) for sign in (1, -1)]
    rows, low_cut, high_cut, boxes, blocks = bounds(fun_dev, support)
    assert blocks <= REACH + 1 and support & (support - 1) == 0
    back = tuple(rounded_up(r, 16) for r in rows)
    rows_of = {k: back[k + REACH] for k in offsets}
    flat = coeffs.reshape(fun_dev * support, points)
    halo = REACH + -(-(reading + 8) // fun_dev)
    count = rounded_up((2 * halo + 2) * fun_dev, 128)
    half = rounded_up(box_dev, 16)
    bf16, f32 = jnp.bfloat16, jnp.float32
    smem = pl.BlockSpec(memory_space=pltpu.SMEM)
    vmem = pl.BlockSpec(memory_space=pltpu.VMEM)
    limit = pltpu.CompilerParams(vmem_limit_bytes=52 * 2**20)

    sent_rows = [rounded_up(rows[k + REACH] + (2 * box_dev if k < 0 else 0), 16) for k in offsets if k]
    *packed, near, cut, home_row, own_region = pl.pallas_call(
        functools.partial(pack_kernel, (fun_dev, support, devices, halo, rows, back, low_cut, high_cut)),
        out_shape=tuple(jax.ShapeDtypeStruct((r, points), bf16) for r in sent_rows)
        + (
            jax.ShapeDtypeStruct((count, 128), f32),
            jax.ShapeDtypeStruct((slots + 1,), jnp.int32),
            jax.ShapeDtypeStruct((1, fun_dev * support), f32),
            jax.ShapeDtypeStruct((2 * half, points), bf16),
        ),
        in_specs=[smem] + [vmem] * 3,
        out_specs=tuple(vmem for _ in range(slots)) + (smem,)
        + tuple(vmem for _ in range(2)),
        compiler_params=limit,
        name="pack",
    )(me, centers.reshape(1, -1), flat, jnp.pad(potential, ((0, half - box_dev), (0, 0))))
    packed = dict(zip([k for k in offsets if k], packed))
    arrived = sent_in_order(packed, order, 1)

    columns, places, active = pl.pallas_call(
        functools.partial(table_kernel, (fun_dev, support, halo, boxes)),
        out_shape=(
            jax.ShapeDtypeStruct((slots * SLOT, 128), f32),
            jax.ShapeDtypeStruct((8, boxes * SLOT), f32),
            jax.ShapeDtypeStruct((slots * (boxes // STEP),), jnp.int32),
        ),
        in_specs=[smem, vmem],
        out_specs=(vmem, vmem, smem),
        compiler_params=limit,
        name="tables",
    )(cut, near)

    wide = slots * SLOT
    sources = [flat if e == REACH else arrived[REACH - e] for e in range(slots)]
    read_rows = [flat.shape[0] if e == REACH else rows_of[REACH - e] for e in range(slots)]
    exact_rows = [rows[2 * REACH - e] for e in range(slots)]
    block = pl.BlockSpec((STEP, wide, points), lambda g: (g, 0, 0))
    band = (fun_dev, 2 * reading)
    pieces, region, *grams = pl.pallas_call(
        functools.partial(unpack_kernel, (fun_dev, box_dev, reading, volume, exact_rows, read_rows, blocks)),
        grid=(boxes // STEP,),
        out_shape=(
            jax.ShapeDtypeStruct((boxes, wide, points), bf16),
            jax.ShapeDtypeStruct((128, points), bf16),
        )
        + tuple(jax.ShapeDtypeStruct(band, f32) for _ in range(slots)),
        in_specs=[smem, smem, whole(columns.shape), whole(own_region.shape)] + [whole(s.shape) for s in sources],
        out_specs=(block, whole((128, points))) + tuple(whole(band) for _ in range(slots)),
        scratch_shapes=[pltpu.VMEM((wide, wide), f32)],
        compiler_params=limit,
        name="unpack",
    )(cut, active, columns, own_region, *sources)

    summed = sent_in_order({k: grams[REACH + k] for k in order}, order, 1)
    gram_band, mixing_rows = pl.pallas_call(
        functools.partial(sum_kernel, reading),
        out_shape=(jax.ShapeDtypeStruct(band, f32), jax.ShapeDtypeStruct((SLOT, 2 * reading), bf16)),
        in_specs=[vmem] * slots,
        out_specs=(vmem, vmem),
        compiler_params=limit,
        name="sum",
    )(grams[REACH], *[summed[k] for k in order])
    mixing_of = sent_in_order({k: mixing_rows for k in order}, order, 1)
    mixing_of[0] = mixing_rows

    out_rows = [rows_of[REACH - e] for e in range(slots)]
    shapes = [(r, points) for r in out_rows] + [(r, 128) for r in out_rows]
    mixed = pl.pallas_call(
        functools.partial(mix_kernel, (fun_dev, reading)),
        grid=(boxes // STEP,),
        out_shape=tuple(jax.ShapeDtypeStruct(shape, bf16) for shape in shapes),
        in_specs=[smem, smem, pl.BlockSpec((8, STEP * SLOT), lambda g: (0, g)), block]
        + [whole((SLOT, 2 * reading))] * slots,
        out_specs=tuple(whole(shape) for shape in shapes),
        scratch_shapes=[pltpu.VMEM((wide, wide), bf16), pltpu.VMEM((STEP, wide, points), bf16)],
        compiler_params=limit,
        name="mix",
    )(cut, active, places, pieces, *[mixing_of[REACH - e] for e in range(slots)])

    filtered_rows = {}
    for group in [order[:3]] + [order[3:5], order[5:], [0]]:
        at = [REACH - k for k in group]
        got = pl.pallas_call(
            filter_kernel,
            out_shape=tuple(jax.ShapeDtypeStruct((out_rows[e], points), bf16) for e in at),
            in_specs=[vmem] * (2 + 2 * len(at)),
            out_specs=tuple(vmem for _ in at),
            compiler_params=limit,
            name="filter",
        )(region, kinetic, *[mixed[e] for e in at], *[mixed[slots + e] for e in at])
        filtered_rows.update(zip(group, got))
    returned = sent_in_order({k: filtered_rows[k] for k in order}, order, -1)
    returned[0] = filtered_rows[0]

    groups, held = [], 257
    for e, k in enumerate(offsets):
        if held + rows_of[k] <= 256:
            groups[-1].append(e)
            held += rows_of[k]
        else:
            groups.append([e])
            held = rows_of[k]
    filtered = pl.pallas_call(
        functools.partial(home_kernel, groups),
        grid=(fun_dev * support // 256,),
        out_shape=jax.ShapeDtypeStruct((fun_dev * support, points), bf16),
        in_specs=[whole(home_row.shape)] + [whole((rows_of[k], points)) for k in offsets],
        out_specs=pl.BlockSpec((256, points), lambda g: (g, 0)),
        compiler_params=limit,
        name="home",
    )(home_row, *[returned[k] for k in offsets])
    return (filtered.reshape(coeffs.shape), gram_band)


def solution(mesh):
    placed = (P(AXES, None, None), P(), P(), P(AXES, None))
    return jax.shard_map(
        on_device,
        mesh=mesh,
        in_specs=placed,
        out_specs=(P(AXES, None, None), P(AXES, None)),
        check_vma=False,
    )
```

profile of v0, /device:TPU:31, one launch (start us, length us, event | category | flops | bytes accessed | tf_op | source)
XLA Modules:
  0.0 148.3 jit_solution(5613651480047361833)
XLA Ops:
  2.2 4.7 %pack.1 = (bf16[64,1024]{1,0:T(8,128)(2,1)S(1)}, bf16[192,1024]{1,0:T(8,128)(2,1)S(1)}, bf16[272,1024]{1,0:T(8,128)(2,1)}, bf16[240,1024]{1,0:T(8,128)(2,1)S(1)}...) custom-call(s32[1]{0:T(128)} %bitcast.me_ref, ...), custom_call_target="tpu_custom_call" | custom-call | tf_op jit(solution)/shard_map/pack/pallas_call | solution.py:427
  7.4 3.9 %collective-permute-done.refs_0_ = bf16[48,1024]{1,0:T(8,128)(2,1)S(1)} collective-permute-done((bf16[48,1024]{1,0:T(8,128)(2,1)S(1)}, bf16[48,1024]{1,0:T(8,128)(2,1)S(1)}, u32[]{:S(2)}, u32[]{:S(2)}) %collective-permute-start) | collective-permute-done | bytes 98336 | tf_op jit(solution)/shard_map/ppermute | solution.py:21
  11.7 4.9 %collective-permute-start.2 = (bf16[240,1024]{1,0:T(8,128)(2,1)S(1)}, bf16[240,1024]{1,0:T(8,128)(2,1)S(1)}, u32[]{:S(2)}, u32[]{:S(2)}) collective-permute-start(bf16[240,1024]{1,0:T(8,128)(2,1)S(1)} %get-tuple-element.63), channel_id=1, source_target_pairs={{0,1},{1,2},{2,3},{3,4},{4,5},{5,6},{6,7},{7,8},{8,9},{9,10},{10,1... | collective-permute-start | bytes 1474568 | tf_op jit(solution)/shard_map/ppermute | solution.py:21
  16.6 5.1 %collective-permute-start.1 = (bf16[160,1024]{1,0:T(8,128)(2,1)S(1)}, bf16[160,1024]{1,0:T(8,128)(2,1)S(1)}, u32[]{:S(2)}, u32[]{:S(2)}) collective-permute-start(bf16[160,1024]{1,0:T(8,128)(2,1)S(1)} %get-tuple-element.62), channel_id=1, source_target_pairs={{0,2},{1,3},{2,4},{3,5},{4,6},{5,7},{6,8},{7,9},{8,10},{9,11},{10,... | collective-permute-start | bytes 983048 | tf_op jit(solution)/shard_map/ppermute | solution.py:21
  21.7 2.3 %tables.1 = (f32[224,128]{1,0:T(8,128)S(1)}, f32[8,768]{1,0:T(8,128)S(1)}, s32[21]{0:T(128)S(1)}) custom-call(s32[8]{0:T(128)S(1)} %get-tuple-element.54.cut_ref, f32[512,128]{1,0:T(8,128)S(1)} %get-tuple-element.55.near_ref), custom_call_target="tpu_custom_call" | custom-call | tf_op jit(solution)/shard_map/tables/pallas_call | solution.py:445
  24.0 15.0 %collective-permute-done.5.refs_6_ = bf16[64,1024]{1,0:T(8,128)(2,1)S(1)} collective-permute-done((bf16[64,1024]{1,0:T(8,128)(2,1)S(1)}, bf16[64,1024]{1,0:T(8,128)(2,1)S(1)}, u32[]{:S(2)}, u32[]{:S(2)}) %collective-permute-start.5) | collective-permute-done | bytes 131104 | tf_op jit(solution)/shard_map/ppermute | solution.py:21
  42.1 13.2 %unpack.1 = (bf16[24,224,1024]{2,1,0:T(8,128)(2,1)}, bf16[128,1024]{1,0:T(8,128)(2,1)S(1)}, f32[24,256]{1,0:T(8,128)S(1)}, f32[24,256]{1,0:T(8,128)S(1)}, f32[24...) custom-call(s32[8]{0:T(128)S(1)} %get-tuple-element.54.cut_ref, ...), custom_call_target="tpu_custom_call" | custom-call | tf_op jit(solution)/shard_map/unpack/pallas_call | solution.py:464
  55.9 3.2 %collective-permute-start.7 = (f32[24,256]{1,0:T(8,128)S(1)}, f32[24,256]{1,0:T(8,128)S(1)}, u32[]{:S(2)}, u32[]{:S(2)}) collective-permute-start(f32[24,256]{1,0:T(8,128)S(1)} %get-tuple-element.74), channel_id=1, source_target_pairs={{0,29},{1,30},{2,31},{3,0},{4,1},{5,2},{6,3},{7,4},{8,5},{9,6},{10... | collective-permute-start | bytes 73736 | tf_op jit(solution)/shard_map/ppermute | solution.py:21
  59.0 3.3 %collective-permute-start.8 = (f32[24,256]{1,0:T(8,128)S(1)}, f32[24,256]{1,0:T(8,128)S(1)}, u32[]{:S(2)}, u32[]{:S(2)}) collective-permute-start(f32[24,256]{1,0:T(8,128)S(1)} %get-tuple-element.75), channel_id=1, source_target_pairs={{0,2},{1,3},{2,4},{3,5},{4,6},{5,7},{6,8},{7,9},{8,10},{9,11},{10,... | collective-permute-start | bytes 73736 | tf_op jit(solution)/shard_map/ppermute | solution.py:21
  62.4 7.1 %collective-permute-start.10 = (f32[24,256]{1,0:T(8,128)S(1)}, f32[24,256]{1,0:T(8,128)S(1)}, u32[]{:S(2)}, u32[]{:S(2)}) collective-permute-start(f32[24,256]{1,0:T(8,128)S(1)} %get-tuple-element.77), channel_id=1, source_target_pairs={{0,1},{1,2},{2,3},{3,4},{4,5},{5,6},{6,7},{7,8},{8,9},{9,10},{10,1... | collective-permute-start | bytes 73736 | tf_op jit(solution)/shard_map/ppermute | solution.py:21
  70.4 5.9 %collective-permute-done.11.refs_6_ = f32[24,256]{1,0:T(8,128)S(1)} collective-permute-done((f32[24,256]{1,0:T(8,128)S(1)}, f32[24,256]{1,0:T(8,128)S(1)}, u32[]{:S(2)}, u32[]{:S(2)}) %collective-permute-start.11) | collective-permute-done | bytes 24608 | tf_op jit(solution)/shard_map/ppermute | solution.py:21
  78.7 2.7 %collective-permute-start.14 = (bf16[32,256]{1,0:T(8,128)(2,1)S(1)}, bf16[32,256]{1,0:T(8,128)(2,1)S(1)}, u32[]{:S(2)}, u32[]{:S(2)}) collective-permute-start(bf16[32,256]{1,0:T(8,128)(2,1)S(1)} %get-tuple-element.81.refs_3_), channel_id=1, source_target_pairs={{0,1},{1,2},{2,3},{3,4},{4,5},{5,6},{6,7},{7,8},{8,9},{9,10},{10,1... | collective-permute-start | bytes 49160 | tf_op jit(solution)/shard_map/ppermute | solution.py:21
  81.4 2.3 %collective-permute-start.13 = (bf16[32,256]{1,0:T(8,128)(2,1)S(1)}, bf16[32,256]{1,0:T(8,128)(2,1)S(1)}, u32[]{:S(2)}, u32[]{:S(2)}) collective-permute-start(bf16[32,256]{1,0:T(8,128)(2,1)S(1)} %get-tuple-element.81.refs_3_), channel_id=1, source_target_pairs={{0,2},{1,3},{2,4},{3,5},{4,6},{5,7},{6,8},{7,9},{8,10},{9,11},{10,... | collective-permute-start | bytes 49160 | tf_op jit(solution)/shard_map/ppermute | solution.py:21
  84.8 5.6 %collective-permute-done.15.refs_4_ = bf16[32,256]{1,0:T(8,128)(2,1)S(1)} collective-permute-done((bf16[32,256]{1,0:T(8,128)(2,1)S(1)}, bf16[32,256]{1,0:T(8,128)(2,1)S(1)}, u32[]{:S(2)}, u32[]{:S(2)}) %collective-permute-start.15) | collective-permute-done | bytes 16416 | tf_op jit(solution)/shard_map/ppermute | solution.py:21
  90.5 10.9 %mix.1 = (bf16[48,1024]{1,0:T(8,128)(2,1)S(1)}, bf16[160,1024]{1,0:T(8,128)(2,1)S(1)}, bf16[240,1024]{1,0:T(8,128)(2,1)S(1)}, bf16[512,1024]{1,0:T(8,128)(2,1)},...) custom-call(s32[8]{0:T(128)S(1)} %get-tuple-element.54.cut_ref, ...), custom_call_target="tpu_custom_call" | custom-call | tf_op jit(solution)/shard_map/mix/pallas_call | solution.py:493
  101.4 3.0 %filter.4 = (bf16[48,1024]{1,0:T(8,128)(2,1)S(1)}, bf16[48,1024]{1,0:T(8,128)(2,1)S(1)}, bf16[160,1024]{1,0:T(8,128)(2,1)S(1)}) custom-call(bf16[128,1024]{1,0:T(8,128)(2,1)S(1)} %get-tuple-element.67.region_ref, bf16[1024,1024]{1,0:T(8,128)(2,1)} %kinetic_ref.7, bf16[48,1024]{1,0:T(8,128)(2,1)S(1)} %get-tuple-element.82.refs_0_, ...), custom_call_target="tpu_custom_call" | custom-call | tf_op jit(solution)/shard_map/filter/pallas_call | solution.py:508
  104.5 2.4 %filter.6 = bf16[256,1024]{1,0:T(8,128)(2,1)S(1)} custom-call(bf16[128,1024]{1,0:T(8,128)(2,1)S(1)} %get-tuple-element.67.region_ref, bf16[1024,1024]{1,0:T(8,128)(2,1)} %kinetic_ref.7, bf16[256,1024]{1,0:T(8,128)(2,1)S(1)} %copy-done.1, bf16[256,128]{1,0:T(8,128)(2,1)S(1)} %get-tuple-element.95.refs_1_), custom_call_target="tpu_custom_call" | custom-call | tf_op jit(solution)/shard_map/filter/pallas_call | solution.py:508
  106.9 5.8 %collective-permute-done.20.refs_6_ = bf16[48,1024]{1,0:T(8,128)(2,1)S(1)} collective-permute-done((bf16[48,1024]{1,0:T(8,128)(2,1)S(1)}, bf16[48,1024]{1,0:T(8,128)(2,1)S(1)}, u32[]{:S(2)}, u32[]{:S(2)}) %collective-permute-start.20) | collective-permute-done | bytes 98336 | tf_op jit(solution)/shard_map/ppermute | solution.py:21
  112.7 2.8 %filter.5 = (bf16[160,1024]{1,0:T(8,128)(2,1)S(1)}, bf16[240,1024]{1,0:T(8,128)(2,1)S(1)}) custom-call(bf16[128,1024]{1,0:T(8,128)(2,1)S(1)} %get-tuple-element.67.region_ref, bf16[1024,1024]{1,0:T(8,128)(2,1)} %kinetic_ref.7, bf16[160,1024]{1,0:T(8,128)(2,1)S(1)} %get-tuple-element.89.refs_0_, bf16[240,1024]{1,0:T(8,128)(2,1)S(1)} %get-tuple-element.90.refs_1_, ...), custom_call_target="tpu_custom_call" | custom-call | tf_op jit(solution)/shard_map/filter/pallas_call | solution.py:508
  116.2 2.2 %collective-permute-start.23 = (bf16[160,1024]{1,0:T(8,128)(2,1)S(1)}, bf16[160,1024]{1,0:T(8,128)(2,1)S(1)}, u32[]{:S(2)}, u32[]{:S(2)}) collective-permute-start(bf16[160,1024]{1,0:T(8,128)(2,1)S(1)} %get-tuple-element.101), channel_id=1, source_target_pairs={{0,30},{1,31},{2,0},{3,1},{4,2},{5,3},{6,4},{7,5},{8,6},{9,7},{10,... | collective-permute-start | bytes 983048 | tf_op jit(solution)/shard_map/ppermute | solution.py:21
  118.4 2.8 %collective-permute-start.19 = (bf16[160,1024]{1,0:T(8,128)(2,1)S(1)}, bf16[160,1024]{1,0:T(8,128)(2,1)S(1)}, u32[]{:S(2)}, u32[]{:S(2)}) collective-permute-start(bf16[160,1024]{1,0:T(8,128)(2,1)S(1)} %get-tuple-element.93), channel_id=1, source_target_pairs={{0,2},{1,3},{2,4},{3,5},{4,6},{5,7},{6,8},{7,9},{8,10},{9,11},{10,... | collective-permute-start | bytes 983048 | tf_op jit(solution)/shard_map/ppermute | solution.py:21
  121.6 3.4 %filter.7.refs_3_ = bf16[512,1024]{1,0:T(8,128)(2,1)S(1)} custom-call(bf16[128,1024]{1,0:T(8,128)(2,1)S(1)} %get-tuple-element.67.region_ref, bf16[1024,1024]{1,0:T(8,128)(2,1)} %kinetic_ref.7, bf16[512,1024]{1,0:T(8,128)(2,1)} %get-tuple-element.98.refs_0_, bf16[512,128]{1,0:T(8,128)(2,1)S(1)} %get-tuple-element.99.refs_1_), custom_call_target="tpu_custom_call" | custom-call | tf_op jit(solution)/shard_map/filter/pallas_call | solution.py:508
  125.9 17.1 %collective-permute-done.18.refs_0_ = bf16[48,1024]{1,0:T(8,128)(2,1)S(1)} collective-permute-done((bf16[48,1024]{1,0:T(8,128)(2,1)S(1)}, bf16[48,1024]{1,0:T(8,128)(2,1)S(1)}, u32[]{:S(2)}, u32[]{:S(2)}) %collective-permute-start.18) | collective-permute-done | bytes 98336 | tf_op jit(solution)/shard_map/ppermute | solution.py:21
  143.0 5.3 %home.1 = bf16[768,1024]{1,0:T(8,128)(2,1)} custom-call(f32[1,768]{1,0:T(1,128)S(1)} %get-tuple-element.53.home_ref, bf16[48,1024]{1,0:T(8,128)(2,1)S(1)} %collective-permute-done.18.refs_0_, bf16[160,1024]{1,0:T(8,128)(2,1)S(1)} %collective-permute-done.19.refs_1_, bf16[256,1024]{1,0:T(8,128)(2,1)S(1)} %collective-permute-done.21.refs_2_, ...), custom_call_target="tpu_custom_call" | custom-call | tf_op jit(solution)/shard_map/home/pallas_call | solution.py:528
  (44 shorter events, 12.5 us)
Async XLA Ops:
  6.9 4.4 %collective-permute-start = (bf16[48,1024]{1,0:T(8,128)(2,1)S(1)}, bf16[48,1024]{1,0:T(8,128)(2,1)S(1)}, u32[]{:S(2)}, u32[]{:S(2)}) collective-permute-start(bf16[48,1024]{1,0:T(8,128)(2,1)S(1)} %get-tuple-element.60), channel_id=1, source_target_pairs={{0,3},{1,4},{2,5},{3,6},{4,7},{5,8},{6,9},{7,10},{8,11},{9,12},{10... | collective-permute-start | bytes 294920 | tf_op jit(solution)/shard_map/ppermute | solution.py:21
  11.3 29.9 %collective-permute-start.3 = (bf16[272,1024]{1,0:T(8,128)(2,1)}, bf16[272,1024]{1,0:T(8,128)(2,1)S(1)}, u32[]{:S(2)}, u32[]{:S(2)}) collective-permute-start(bf16[272,1024]{1,0:T(8,128)(2,1)} %get-tuple-element.64), channel_id=1, source_target_pairs={{0,31},{1,0},{2,1},{3,2},{4,3},{5,4},{6,5},{7,6},{8,7},{9,8},{10,9... | collective-permute-start | bytes 1671176 | tf_op jit(solution)/shard_map/ppermute | solution.py:21
  11.7 29.5 %collective-permute-start.2 = (bf16[240,1024]{1,0:T(8,128)(2,1)S(1)}, bf16[240,1024]{1,0:T(8,128)(2,1)S(1)}, u32[]{:S(2)}, u32[]{:S(2)}) collective-permute-start(bf16[240,1024]{1,0:T(8,128)(2,1)S(1)} %get-tuple-element.63), channel_id=1, source_target_pairs={{0,1},{1,2},{2,3},{3,4},{4,5},{5,6},{6,7},{7,8},{8,9},{9,10},{10,1... | collective-permute-start | bytes 1474568 | tf_op jit(solution)/shard_map/ppermute | solution.py:21
  16.6 24.5 %collective-permute-start.4 = (bf16[192,1024]{1,0:T(8,128)(2,1)S(1)}, bf16[192,1024]{1,0:T(8,128)(2,1)S(1)}, u32[]{:S(2)}, u32[]{:S(2)}) collective-permute-start(bf16[192,1024]{1,0:T(8,128)(2,1)S(1)} %get-tuple-element.65), channel_id=1, source_target_pairs={{0,30},{1,31},{2,0},{3,1},{4,2},{5,3},{6,4},{7,5},{8,6},{9,7},{10,... | collective-permute-start | bytes 1179656 | tf_op jit(solution)/shard_map/ppermute | solution.py:21
  16.6 24.5 %collective-permute-start.1 = (bf16[160,1024]{1,0:T(8,128)(2,1)S(1)}, bf16[160,1024]{1,0:T(8,128)(2,1)S(1)}, u32[]{:S(2)}, u32[]{:S(2)}) collective-permute-start(bf16[160,1024]{1,0:T(8,128)(2,1)S(1)} %get-tuple-element.62), channel_id=1, source_target_pairs={{0,2},{1,3},{2,4},{3,5},{4,6},{5,7},{6,8},{7,9},{8,10},{9,11},{10,... | collective-permute-start | bytes 983048 | tf_op jit(solution)/shard_map/ppermute | solution.py:21
  21.7 17.3 %collective-permute-start.5 = (bf16[64,1024]{1,0:T(8,128)(2,1)S(1)}, bf16[64,1024]{1,0:T(8,128)(2,1)S(1)}, u32[]{:S(2)}, u32[]{:S(2)}) collective-permute-start(bf16[64,1024]{1,0:T(8,128)(2,1)S(1)} %get-tuple-element.66), channel_id=1, source_target_pairs={{0,29},{1,30},{2,31},{3,0},{4,1},{5,2},{6,3},{7,4},{8,5},{9,6},{10... | collective-permute-start | bytes 393224 | tf_op jit(solution)/shard_map/ppermute | solution.py:21
  55.3 14.1 %collective-permute-start.6 = (f32[24,256]{1,0:T(8,128)S(1)}, f32[24,256]{1,0:T(8,128)S(1)}, u32[]{:S(2)}, u32[]{:S(2)}) collective-permute-start(f32[24,256]{1,0:T(8,128)S(1)} %get-tuple-element.72), channel_id=1, source_target_pairs={{0,3},{1,4},{2,5},{3,6},{4,7},{5,8},{6,9},{7,10},{8,11},{9,12},{10... | collective-permute-start | bytes 73736 | tf_op jit(solution)/shard_map/ppermute | solution.py:21
  55.9 13.6 %collective-permute-start.7 = (f32[24,256]{1,0:T(8,128)S(1)}, f32[24,256]{1,0:T(8,128)S(1)}, u32[]{:S(2)}, u32[]{:S(2)}) collective-permute-start(f32[24,256]{1,0:T(8,128)S(1)} %get-tuple-element.74), channel_id=1, source_target_pairs={{0,29},{1,30},{2,31},{3,0},{4,1},{5,2},{6,3},{7,4},{8,5},{9,6},{10... | collective-permute-start | bytes 73736 | tf_op jit(solution)/shard_map/ppermute | solution.py:21
  59.0 10.4 %collective-permute-start.8 = (f32[24,256]{1,0:T(8,128)S(1)}, f32[24,256]{1,0:T(8,128)S(1)}, u32[]{:S(2)}, u32[]{:S(2)}) collective-permute-start(f32[24,256]{1,0:T(8,128)S(1)} %get-tuple-element.75), channel_id=1, source_target_pairs={{0,2},{1,3},{2,4},{3,5},{4,6},{5,7},{6,8},{7,9},{8,10},{9,11},{10,... | collective-permute-start | bytes 73736 | tf_op jit(solution)/shard_map/ppermute | solution.py:21
  62.4 7.1 %collective-permute-start.9 = (f32[24,256]{1,0:T(8,128)S(1)}, f32[24,256]{1,0:T(8,128)S(1)}, u32[]{:S(2)}, u32[]{:S(2)}) collective-permute-start(f32[24,256]{1,0:T(8,128)S(1)} %get-tuple-element.76), channel_id=1, source_target_pairs={{0,30},{1,31},{2,0},{3,1},{4,2},{5,3},{6,4},{7,5},{8,6},{9,7},{10,... | collective-permute-start | bytes 73736 | tf_op jit(solution)/shard_map/ppermute | solution.py:21
  62.4 8.0 %collective-permute-start.10 = (f32[24,256]{1,0:T(8,128)S(1)}, f32[24,256]{1,0:T(8,128)S(1)}, u32[]{:S(2)}, u32[]{:S(2)}) collective-permute-start(f32[24,256]{1,0:T(8,128)S(1)} %get-tuple-element.77), channel_id=1, source_target_pairs={{0,1},{1,2},{2,3},{3,4},{4,5},{5,6},{6,7},{7,8},{8,9},{9,10},{10,1... | collective-permute-start | bytes 73736 | tf_op jit(solution)/shard_map/ppermute | solution.py:21
  69.4 6.8 %collective-permute-start.11 = (f32[24,256]{1,0:T(8,128)S(1)}, f32[24,256]{1,0:T(8,128)S(1)}, u32[]{:S(2)}, u32[]{:S(2)}) collective-permute-start(f32[24,256]{1,0:T(8,128)S(1)} %get-tuple-element.78), channel_id=1, source_target_pairs={{0,31},{1,0},{2,1},{3,2},{4,3},{5,4},{6,5},{7,6},{8,7},{9,8},{10,9... | collective-permute-start | bytes 73736 | tf_op jit(solution)/shard_map/ppermute | solution.py:21
  76.9 6.8 %collective-permute-start.12 = (bf16[32,256]{1,0:T(8,128)(2,1)S(1)}, bf16[32,256]{1,0:T(8,128)(2,1)S(1)}, u32[]{:S(2)}, u32[]{:S(2)}) collective-permute-start(bf16[32,256]{1,0:T(8,128)(2,1)S(1)} %get-tuple-element.81.refs_3_), channel_id=1, source_target_pairs={{0,3},{1,4},{2,5},{3,6},{4,7},{5,8},{6,9},{7,10},{8,11},{9,12},{10... | collective-permute-start | bytes 49160 | tf_op jit(solution)/shard_map/ppermute | solution.py:21
  76.9 7.6 %collective-permute-start.17 = (bf16[32,256]{1,0:T(8,128)(2,1)S(1)}, bf16[32,256]{1,0:T(8,128)(2,1)S(1)}, u32[]{:S(2)}, u32[]{:S(2)}) collective-permute-start(bf16[32,256]{1,0:T(8,128)(2,1)S(1)} %get-tuple-element.81.refs_3_), channel_id=1, source_target_pairs={{0,29},{1,30},{2,31},{3,0},{4,1},{5,2},{6,3},{7,4},{8,5},{9,6},{10... | collective-permute-start | bytes 49160 | tf_op jit(solution)/shard_map/ppermute | solution.py:21
  78.7 6.2 %collective-permute-start.16 = (bf16[32,256]{1,0:T(8,128)(2,1)S(1)}, bf16[32,256]{1,0:T(8,128)(2,1)S(1)}, u32[]{:S(2)}, u32[]{:S(2)}) collective-permute-start(bf16[32,256]{1,0:T(8,128)(2,1)S(1)} %get-tuple-element.81.refs_3_), channel_id=1, source_target_pairs={{0,30},{1,31},{2,0},{3,1},{4,2},{5,3},{6,4},{7,5},{8,6},{9,7},{10,... | collective-permute-start | bytes 49160 | tf_op jit(solution)/shard_map/ppermute | solution.py:21
  78.7 6.2 %collective-permute-start.14 = (bf16[32,256]{1,0:T(8,128)(2,1)S(1)}, bf16[32,256]{1,0:T(8,128)(2,1)S(1)}, u32[]{:S(2)}, u32[]{:S(2)}) collective-permute-start(bf16[32,256]{1,0:T(8,128)(2,1)S(1)} %get-tuple-element.81.refs_3_), channel_id=1, source_target_pairs={{0,1},{1,2},{2,3},{3,4},{4,5},{5,6},{6,7},{7,8},{8,9},{9,10},{10,1... | collective-permute-start | bytes 49160 | tf_op jit(solution)/shard_map/ppermute | solution.py:21
  81.4 3.5 %collective-permute-start.13 = (bf16[32,256]{1,0:T(8,128)(2,1)S(1)}, bf16[32,256]{1,0:T(8,128)(2,1)S(1)}, u32[]{:S(2)}, u32[]{:S(2)}) collective-permute-start(bf16[32,256]{1,0:T(8,128)(2,1)S(1)} %get-tuple-element.81.refs_3_), channel_id=1, source_target_pairs={{0,2},{1,3},{2,4},{3,5},{4,6},{5,7},{6,8},{7,9},{8,10},{9,11},{10,... | collective-permute-start | bytes 49160 | tf_op jit(solution)/shard_map/ppermute | solution.py:21
  83.7 6.8 %collective-permute-start.15 = (bf16[32,256]{1,0:T(8,128)(2,1)S(1)}, bf16[32,256]{1,0:T(8,128)(2,1)S(1)}, u32[]{:S(2)}, u32[]{:S(2)}) collective-permute-start(bf16[32,256]{1,0:T(8,128)(2,1)S(1)} %get-tuple-element.81.refs_3_), channel_id=1, source_target_pairs={{0,31},{1,0},{2,1},{3,2},{4,3},{5,4},{6,5},{7,6},{8,7},{9,8},{10,9... | collective-permute-start | bytes 49160 | tf_op jit(solution)/shard_map/ppermute | solution.py:21
  104.4 8.3 %collective-permute-start.20 = (bf16[48,1024]{1,0:T(8,128)(2,1)S(1)}, bf16[48,1024]{1,0:T(8,128)(2,1)S(1)}, u32[]{:S(2)}, u32[]{:S(2)}) collective-permute-start(bf16[48,1024]{1,0:T(8,128)(2,1)S(1)} %get-tuple-element.96), channel_id=1, source_target_pairs={{0,29},{1,30},{2,31},{3,0},{4,1},{5,2},{6,3},{7,4},{8,5},{9,6},{10... | collective-permute-start | bytes 294920 | tf_op jit(solution)/shard_map/ppermute | solution.py:21
  112.7 30.3 %collective-permute-start.21 = (bf16[256,1024]{1,0:T(8,128)(2,1)S(1)}, bf16[256,1024]{1,0:T(8,128)(2,1)S(1)}, u32[]{:S(2)}, u32[]{:S(2)}) collective-permute-start(bf16[256,1024]{1,0:T(8,128)(2,1)S(1)} %filter.6), channel_id=1, source_target_pairs={{0,1},{1,2},{2,3},{3,4},{4,5},{5,6},{6,7},{7,8},{8,9},{9,10},{10,1... | collective-permute-start | bytes 1572872 | tf_op jit(solution)/shard_map/ppermute | solution.py:21
  115.6 27.4 %collective-permute-start.22 = (bf16[240,1024]{1,0:T(8,128)(2,1)S(1)}, bf16[240,1024]{1,0:T(8,128)(2,1)S(1)}, u32[]{:S(2)}, u32[]{:S(2)}) collective-permute-start(bf16[240,1024]{1,0:T(8,128)(2,1)S(1)} %get-tuple-element.100), channel_id=1, source_target_pairs={{0,31},{1,0},{2,1},{3,2},{4,3},{5,4},{6,5},{7,6},{8,7},{9,8},{10,9... | collective-permute-start | bytes 1474568 | tf_op jit(solution)/shard_map/ppermute | solution.py:21
  116.2 26.8 %collective-permute-start.23 = (bf16[160,1024]{1,0:T(8,128)(2,1)S(1)}, bf16[160,1024]{1,0:T(8,128)(2,1)S(1)}, u32[]{:S(2)}, u32[]{:S(2)}) collective-permute-start(bf16[160,1024]{1,0:T(8,128)(2,1)S(1)} %get-tuple-element.101), channel_id=1, source_target_pairs={{0,30},{1,31},{2,0},{3,1},{4,2},{5,3},{6,4},{7,5},{8,6},{9,7},{10,... | collective-permute-start | bytes 983048 | tf_op jit(solution)/shard_map/ppermute | solution.py:21
  118.4 24.6 %collective-permute-start.19 = (bf16[160,1024]{1,0:T(8,128)(2,1)S(1)}, bf16[160,1024]{1,0:T(8,128)(2,1)S(1)}, u32[]{:S(2)}, u32[]{:S(2)}) collective-permute-start(bf16[160,1024]{1,0:T(8,128)(2,1)S(1)} %get-tuple-element.93), channel_id=1, source_target_pairs={{0,2},{1,3},{2,4},{3,5},{4,6},{5,7},{6,8},{7,9},{8,10},{9,11},{10,... | collective-permute-start | bytes 983048 | tf_op jit(solution)/shard_map/ppermute | solution.py:21
  121.2 21.8 %collective-permute-start.18 = (bf16[48,1024]{1,0:T(8,128)(2,1)S(1)}, bf16[48,1024]{1,0:T(8,128)(2,1)S(1)}, u32[]{:S(2)}, u32[]{:S(2)}) collective-permute-start(bf16[48,1024]{1,0:T(8,128)(2,1)S(1)} %get-tuple-element.88), channel_id=1, source_target_pairs={{0,3},{1,4},{2,5},{3,6},{4,7},{5,8},{6,9},{7,10},{8,11},{9,12},{10... | collective-permute-start | bytes 294920 | tf_op jit(solution)/shard_map/ppermute | solution.py:21
  (4 other events, 5.8 us)
where the time goes:
time: 149 us; the launch traced here: 148 us
  waiting for transfers between devices  56.7 us (38%)
  Pallas kernels  48.7 us (33%)
  starting transfers between devices  38.6 us (26%)
  local copies, waits for them, and re-layouts  3.46 us (2%)
    ppermute x24, waiting for transfers between devices, passed_along(): return lax.ppermute(value, AXES, pairs)  56.7 us
    ppermute x24, starting transfers between devices, passed_along(): return lax.ppermute(value, AXES, pairs)  38.6 us
    pallas_call x1, Pallas kernels, on_device(): pl.pallas_call(functools.partial(unpack_kernel, (fun_dev, box_dev, readin...  13.2 us
    pallas_call x4, Pallas kernels, on_device(): pl.pallas_call(filter_kernel, out_shape=tuple((jax.ShapeDtypeStruct((out_...  11.7 us
    pallas_call x1, Pallas kernels, on_device(): pl.pallas_call(functools.partial(mix_kernel, (fun_dev, reading)), grid=(b...  10.9 us
    pallas_call x1, Pallas kernels, on_device(): pl.pallas_call(functools.partial(home_kernel, groups), grid=(fun_dev * su...  5.28 us
    pallas_call x1, Pallas kernels, on_device(): pl.pallas_call(functools.partial(pack_kernel, (fun_dev, support, devices,...  4.73 us
  transfers between devices with their start and end apart: 24, of which 9 were waited for; matrix products, arithmetic and copies ran while one was open for 0% of the time, Pallas kernels for 7%

commit v1 on v0

--- a/solution.py
+++ b/solution.py
@@ -21,14 +21,13 @@
     return lax.ppermute(value, AXES, pairs)
 
 
-def sent_in_order(values, order, sign):
-    there = {}
-    for k in order:
-        value = values[k]
-        if k == order[-1]:
-            value, there[order[0]] = lax.optimization_barrier((value, there[order[0]]))
-        there[k] = passed_along(value, sign * k)
-    return there
+def sent(values, keys, sign):
+    return {k: passed_along(values[k], sign * k) for k in keys}
+
+
+def after(values, keys, there):
+    held, there = lax.optimization_barrier(({k: values[k] for k in keys}, there))
+    return held, there
 
 
 def rounded_up(value, multiple):
@@ -102,10 +101,9 @@
 
 
 def pack_kernel(plan, me_ref, centers_ref, flat_ref, potential_ref, *refs):
-    fun_dev, support, devices, halo, rows, back, low_cut, high_cut = plan
-    slots = 2 * REACH + 1
-    outs = dict(zip([k for k in range(-REACH, REACH + 1) if k], refs[: slots - 1]))
-    near_ref, cut_ref, home_ref, own_ref = refs[slots - 1 :]
+    fun_dev, support, devices, halo, rows, back, low_cut, high_cut, now = plan
+    outs = dict(zip(now, refs[: len(now)]))
+    near_ref, cut_ref, row_ref, home_ref, own_ref = refs[len(now) :]
     me = me_ref[0]
     box_dev = fun_dev // 2
     fun_all, box_all = fun_dev * devices, box_dev * devices
@@ -138,6 +136,14 @@
         cuts.append(cut)
         cut_ref[k + REACH] = cut.astype(jnp.int32)
 
+    potential = potential_ref[...]
+    high = potential.astype(jnp.bfloat16)
+    low = (potential - high.astype(jnp.float32)).astype(jnp.bfloat16)
+    shape = (own_ref.shape[0], box_dev)
+    at_high = iota(shape, 0) == iota(shape, 1)
+    at_low = iota(shape, 0) - float(shape[0] // 2) == iota(shape, 1)
+    own_ref[...] = (times(one_hot(at_high), high) + times(one_hot(at_low), low)).astype(jnp.bfloat16)
+
     mine = near[halo * fun_dev : (halo + 1) * fun_dev]
     pieces = fun_dev * support
     piece = lax.broadcasted_iota(jnp.int32, (1, pieces), 1)
@@ -145,10 +151,6 @@
     step = piece.astype(jnp.float32) - of_fun * support
     mine_row = spread_over(mine, of_fun)
     earlier = iota((fun_dev, pieces), 0) < of_fun
-    potential = potential_ref[...]
-    high = potential.astype(jnp.bfloat16)
-    own_ref[: potential.shape[0]] = high
-    own_ref[potential.shape[0] :] = (potential - high.astype(jnp.float32)).astype(jnp.bfloat16)
     home, base = jnp.zeros((1, pieces), jnp.float32), 0
     for k in range(-REACH, REACH + 1):
         first, end = cuts[k + REACH], cuts[k + REACH + 1]
@@ -159,23 +161,42 @@
         row = leave_at + step - low_edge
         home = home + jnp.where(goes, row + float(base), 0.0)
         base += back[k + REACH]
-        if k:
-            row = jnp.where(goes, row, -1.0)
-            sent = outs[k].shape[0]
-            value = times(one_hot(iota((sent, pieces), 0) == row), flat_ref[...])
-            if k < 0:
-                shape = (sent, own_ref.shape[0])
-                part = iota(shape, 0) - float(rows[k + REACH])
-                col = iota(shape, 1)
-                half = float(own_ref.shape[0] // 2)
-                from_col = jnp.where(part < box_dev, part, part - box_dev + half)
-                inside = (part >= 0) & (part < 2 * box_dev)
-                value = value + times(one_hot(inside & (col == from_col)), own_ref[...])
-            outs[k][...] = value.astype(jnp.bfloat16)
+        row_ref[k + REACH : k + REACH + 1] = jnp.where(goes, row, -1.0)
+    row_ref[2 * REACH + 1 :] = jnp.full((row_ref.shape[0] - 2 * REACH - 1, pieces), -1.0, jnp.float32)
     home_ref[...] = home
-
-
-def table_kernel(plan, cut_ref, near_ref, column_ref, place_ref, active_ref):
+    packed_rows(rows, box_dev, row_ref, flat_ref, own_ref, outs)
+
+
+def packed_rows(rows, box_dev, row_ref, flat_ref, own_ref, outs):
+    for k, out_ref in outs.items():
+        sent = out_ref.shape[0]
+        row = row_ref[k + REACH : k + REACH + 1]
+        value = times(one_hot(iota((sent, row.shape[1]), 0) == row), flat_ref[...])
+        if k < 0:
+            shape = (sent, own_ref.shape[0])
+            part = iota(shape, 0) - float(rows[k + REACH])
+            from_col = jnp.where(part < box_dev, part, part - box_dev + float(shape[1] // 2))
+            inside = (part >= 0) & (part < 2 * box_dev)
+            value = value + times(one_hot(inside & (iota(shape, 1) == from_col)), own_ref[...])
+        out_ref[...] = value.astype(jnp.bfloat16)
+
+
+def pack_rest_kernel(plan, row_ref, flat_ref, own_ref, *refs):
+    rows, box_dev, now = plan
+    packed_rows(rows, box_dev, row_ref, flat_ref, own_ref, dict(zip(now, refs)))
+
+
+def picked(start, low, high, first, rows):
+    lane = iota((SLOT, rows), 1)
+    picks = []
+    for b in range(STEP):
+        box = first + float(b)
+        row = jnp.where((box >= low) & (box < high), start + box, -1.0)
+        picks.append(one_hot(lane == row))
+    return jnp.concatenate(picks, axis=0)
+
+
+def table_kernel(plan, cut_ref, near_ref, flat_ref, column_ref, place_ref, active_ref, local_ref):
     fun_dev, support, halo, boxes = plan
     slots = 2 * REACH + 1
     first = cut_ref[REACH].astype(jnp.float32)
@@ -184,6 +205,7 @@
     along = lax.broadcasted_iota(jnp.int32, (1, boxes * SLOT), 1)
     box = lax.shift_right_logical(along, SLOT.bit_length() - 1).astype(jnp.float32)
     of_fun = along.astype(jnp.float32) - box * SLOT
+    levels = [1] * (boxes // STEP)
     for e in range(slots):
         at = (halo - REACH + e) * fun_dev
         others = near_ref[at : at + fun_dev, 0:1]
@@ -197,19 +219,32 @@
         box_low = edge_low + others - first
         box_high = edge_high + others - first
         packed = come_at - box_low
-        unpacked = iota((fun_dev, 1), 0) * support + first - others if e == REACH else packed
         spare = jnp.zeros((SLOT - fun_dev, 1), jnp.float32)
-        packed, unpacked, box_low, box_high = (
-            jnp.concatenate([column, spare], axis=0) for column in (packed, unpacked, box_low, box_high)
+        if e == REACH:
+            own_start = iota((fun_dev, 1), 0) * support + first - others
+            own_start = jnp.concatenate([own_start, spare], axis=0)
+        packed, box_low, box_high = (
+            jnp.concatenate([column, spare], axis=0) for column in (packed, box_low, box_high)
         )
+        if e == REACH:
+            for g in range(boxes // STEP):
+                pick = picked(own_start, box_low, box_high, float(g * STEP), flat_ref.shape[0])
+                local_ref[g * STEP : (g + 1) * STEP] = times(pick, flat_ref[...]).astype(jnp.bfloat16).reshape(
+                    STEP, SLOT, flat_ref.shape[1]
+                )
         column_ref[e * SLOT : (e + 1) * SLOT, :] = jnp.where(
-            lane == 0.0, unpacked, jnp.where(lane == 1.0, box_low, box_high)
+            lane == 0.0, packed, jnp.where(lane == 1.0, box_low, box_high)
         )
         lies = (box >= spread_over(box_low, of_fun)) & (box < spread_over(box_high, of_fun))
         place_ref[e : e + 1, :] = jnp.where(lies, spread_over(packed, of_fun) + box, -1.0)
         for g in range(boxes // STEP):
             here = (box >= g * STEP) & (box < (g + 1) * STEP) & lies
-            active_ref[e * (boxes // STEP) + g] = jnp.sum(jnp.where(here, 1.0, 0.0)).astype(jnp.int32)
+            used = jnp.sum(jnp.where(here, 1.0, 0.0)).astype(jnp.int32)
+            active_ref[e * (boxes // STEP) + g] = used
+            level = jnp.where(used > 0, max(1, abs(e - REACH)), 1)
+            levels[g] = jnp.maximum(levels[g], level)
+    for g in range(boxes // STEP):
+        active_ref[slots * (boxes // STEP) + g] = levels[g]
     place_ref[slots:, :] = jnp.full((place_ref.shape[0] - slots, boxes * SLOT), -1.0, jnp.float32)
 
 
@@ -238,20 +273,26 @@
     return rounded_up(window + reading + fun_dev + max(0, window - reading), 128)
 
 
-def unpack_kernel(plan, cut_ref, active_ref, column_ref, own_ref, *refs):
+def level_rows(level):
+    return (REACH - level) * SLOT, (REACH + level + 1) * SLOT
+
+
+def unpack_kernel(plan, cut_ref, active_ref, column_ref, own_ref, local_ref, *refs):
     fun_dev, box_dev, reading, volume, rows, back, blocks = plan
     slots = 2 * REACH + 1
-    sources = refs[:slots]
-    window_ref, region_ref = refs[slots : slots + 2]
-    gram_refs = refs[slots + 2 : -1]
-    total = refs[-1]
+    sources = refs[:REACH] + (None,) + refs[REACH : slots - 1]
+    window_ref, region_ref = refs[slots - 1 : slots + 1]
+    gram_refs = refs[slots + 1 : 2 * slots + 1]
+    dense = refs[2 * slots + 1]
+    totals = refs[2 * slots + 2 :]
     step, steps = pl.program_id(0), pl.num_programs(0)
     first = step * STEP
     width = cut_ref[REACH + 1] - cut_ref[REACH]
 
     @pl.when(step == 0)
     def _():
-        total[...] = jnp.zeros_like(total)
+        for total in totals:
+            total[...] = jnp.zeros_like(total)
         value = None
         for t in range(blocks):
             held = own_ref if t == 0 else sources[REACH + t]
@@ -270,7 +311,11 @@
 
     @pl.when(first < width)
     def _():
+        level = active_ref[slots * steps + step]
+        window_ref[:, REACH * SLOT : (REACH + 1) * SLOT, :] = local_ref[...]
         for e in range(slots):
+            if e == REACH:
+                continue
             used = active_ref[e * steps + step] > 0
 
             @pl.when(used)
@@ -278,35 +323,37 @@
                 start = column_ref[e * SLOT : (e + 1) * SLOT, 0:1]
                 low = column_ref[e * SLOT : (e + 1) * SLOT, 1:2]
                 high = column_ref[e * SLOT : (e + 1) * SLOT, 2:3]
-                lane = iota((SLOT, back[e]), 1)
-                picks = []
-                for b in range(STEP):
-                    box = (first + b).astype(jnp.float32)
-                    row = jnp.where((box >= low) & (box < high), start + box, -1.0)
-                    picks.append(one_hot(lane == row))
-                found = times(jnp.concatenate(picks, axis=0), sources[e][: back[e]])
+                pick = picked(start, low, high, first.astype(jnp.float32), back[e])
+                found = times(pick, sources[e][: back[e]])
                 window_ref[:, e * SLOT : (e + 1) * SLOT, :] = found.astype(jnp.bfloat16).reshape(
                     STEP, SLOT, found.shape[-1]
                 )
 
-            @pl.when(jnp.logical_not(used))
+            @pl.when(jnp.logical_not(used) & (level >= abs(e - REACH)))
             def _():
                 window_ref[:, e * SLOT : (e + 1) * SLOT, :] = jnp.zeros(
                     (STEP, SLOT, window_ref.shape[-1]), jnp.bfloat16
                 )
-        value = total[...]
-        for b in range(STEP):
-            here = window_ref[b]
-            value = value + times(here, here, ((1,), (1,)))
-        total[...] = value
+        for part, total in enumerate(totals):
+            @pl.when(level == part + 1)
+            def _():
+                low, high = level_rows(part + 1)
+                value = total[...]
+                for b in range(STEP):
+                    here = window_ref[b, low:high]
+                    value = value + times(here, here, ((1,), (1,)))
+                total[...] = value
 
     @pl.when(step == steps - 1)
     def _():
-        wide, lanes = total.shape[0], band_lanes(fun_dev, reading)
+        wide, lanes = dense.shape
         keep = jnp.where(
             function_of((wide, lanes), 0, fun_dev) == lax.broadcasted_iota(jnp.int32, (wide, lanes), 1), volume, 0.0
         )
-        dense = times(total[...], keep, precision=lax.Precision.HIGHEST)
+        dense[...] = times(totals[-1][...], keep, precision=lax.Precision.HIGHEST)
+        for part, total in enumerate(totals[:-1]):
+            low, high = level_rows(part + 1)
+            dense[low:high] += times(total[...], keep[low:high], precision=lax.Precision.HIGHEST)
         for e in range(slots):
             rows_here = dense[e * SLOT : e * SLOT + fun_dev]
             gram_refs[e][...] = skewed(moved(rows_here, reading - 1 - e * fun_dev), -1)[:, : 2 * reading]
@@ -325,16 +372,15 @@
 
 
 def mix_kernel(plan, cut_ref, active_ref, place_ref, window_ref, *refs):
-    fun_dev, reading = plan
+    fun_dev, reading, band_order = plan
     slots = 2 * REACH + 1
-    bands = refs[:slots]
+    bands = dict(zip(band_order, refs[:slots]))
     outs = refs[slots : 2 * slots]
     at_boxes = refs[2 * slots : 3 * slots]
-    mixing, mixed = refs[3 * slots :]
+    mixed = refs[3 * slots]
+    mixings = refs[3 * slots + 1 :]
     step, steps = pl.program_id(0), pl.num_programs(0)
     width = cut_ref[REACH + 1] - cut_ref[REACH]
-    wide = slots * SLOT
-
     @pl.when(step == 0)
     def _():
         for out, at_box in zip(outs, at_boxes):
@@ -343,19 +389,27 @@
         lanes = band_lanes(fun_dev, reading)
         parts = []
         for e in range(slots):
-            band = bands[e][...].astype(jnp.float32)
+            band = bands[REACH - e][...].astype(jnp.float32)
             band = jnp.concatenate([band, jnp.zeros((SLOT, lanes - 2 * reading), jnp.float32)], axis=1)
             parts.append(moved(skewed(band, 1), e * fun_dev - (reading - 1)))
         dense = jnp.concatenate(parts, axis=0).astype(jnp.bfloat16)
-        keep = one_hot(
-            function_of((lanes, wide), 1, fun_dev) == lax.broadcasted_iota(jnp.int32, (lanes, wide), 0)
-        )
-        mixing[...] = times(dense, keep).astype(jnp.bfloat16)
+        for part, mixing in enumerate(mixings):
+            low, high = level_rows(part + 1)
+            shape = (lanes, mixing.shape[1])
+            column = function_of(shape, 1, fun_dev)
+            column = jnp.where(column >= 0, column + low // SLOT * fun_dev, -1)
+            keep = one_hot(column == lax.broadcasted_iota(jnp.int32, shape, 0))
+            mixing[...] = times(dense[low:high], keep).astype(jnp.bfloat16)
 
     @pl.when(step * STEP < width)
     def _():
-        for b in range(STEP):
-            mixed[b] = times(mixing[...], window_ref[b]).astype(jnp.bfloat16)
+        level = active_ref[slots * steps + step]
+        for part, mixing in enumerate(mixings):
+            @pl.when(level == part + 1)
+            def _():
+                low, high = level_rows(part + 1)
+                for b in range(STEP):
+                    mixed[b, low:high] = times(mixing[...], window_ref[b, low:high]).astype(jnp.bfloat16)
         shape = (STEP * SLOT, at_boxes[0].shape[1])
         along = lax.broadcasted_iota(jnp.int32, shape, 0)
         box = lax.shift_right_logical(along, SLOT.bit_length() - 1) + step * STEP
@@ -368,15 +422,6 @@
                 part = mixed[:, e * SLOT : (e + 1) * SLOT, :].reshape(STEP * SLOT, mixed.shape[-1])
                 outs[e][...] += times(pick, part).astype(jnp.bfloat16)
                 at_boxes[e][...] += times(pick, boxes_of).astype(jnp.bfloat16)
-
-
-def filter_kernel(region_ref, kinetic_ref, *refs):
-    count = len(refs) // 3
-    for here_ref, at_box_ref, out_ref in zip(refs[:count], refs[count : 2 * count], refs[2 * count :]):
-        here = here_ref[...]
-        local = times(at_box_ref[...], region_ref[...])
-        applied = times(here, kinetic_ref[...])
-        out_ref[...] = (applied + local * here.astype(jnp.float32)).astype(jnp.bfloat16)
 
 
 def home_kernel(groups, home_ref, *refs):
@@ -409,7 +454,9 @@
     reading = 4 * support
     slots = 2 * REACH + 1
     offsets = list(range(-REACH, REACH + 1))
-    order = [REACH, -REACH] + [sign * k for k in range(REACH - 1, 0, -1) for sign in (1, -1)]
+    far = [REACH, -REACH]
+    rest = [sign * k for k in range(1, REACH) for sign in (1, -1)]
+    one_way = list(range(REACH, 0, -1)) + list(range(-REACH, 0))
     rows, low_cut, high_cut, boxes, blocks = bounds(fun_dev, support)
     assert blocks <= REACH + 1 and support & (support - 1) == 0
     back = tuple(rounded_up(r, 16) for r in rows)
@@ -423,41 +470,53 @@
     vmem = pl.BlockSpec(memory_space=pltpu.VMEM)
     limit = pltpu.CompilerParams(vmem_limit_bytes=52 * 2**20)
 
-    sent_rows = [rounded_up(rows[k + REACH] + (2 * box_dev if k < 0 else 0), 16) for k in offsets if k]
-    *packed, near, cut, home_row, own_region = pl.pallas_call(
-        functools.partial(pack_kernel, (fun_dev, support, devices, halo, rows, back, low_cut, high_cut)),
-        out_shape=tuple(jax.ShapeDtypeStruct((r, points), bf16) for r in sent_rows)
+    sent_rows = {k: rounded_up(rows[k + REACH] + (2 * box_dev if k < 0 else 0), 16) for k in offsets if k}
+    *packed_far, near, cut, row_out, home_row, own_region = pl.pallas_call(
+        functools.partial(pack_kernel, (fun_dev, support, devices, halo, rows, back, low_cut, high_cut, far)),
+        out_shape=tuple(jax.ShapeDtypeStruct((sent_rows[k], points), bf16) for k in far)
         + (
             jax.ShapeDtypeStruct((count, 128), f32),
             jax.ShapeDtypeStruct((slots + 1,), jnp.int32),
+            jax.ShapeDtypeStruct((8, fun_dev * support), f32),
             jax.ShapeDtypeStruct((1, fun_dev * support), f32),
             jax.ShapeDtypeStruct((2 * half, points), bf16),
         ),
         in_specs=[smem] + [vmem] * 3,
-        out_specs=tuple(vmem for _ in range(slots)) + (smem,)
-        + tuple(vmem for _ in range(2)),
+        out_specs=(vmem,) * 3 + (smem,) + (vmem,) * 3,
         compiler_params=limit,
-        name="pack",
-    )(me, centers.reshape(1, -1), flat, jnp.pad(potential, ((0, half - box_dev), (0, 0))))
-    packed = dict(zip([k for k in offsets if k], packed))
-    arrived = sent_in_order(packed, order, 1)
-
-    columns, places, active = pl.pallas_call(
+        name="pack_far",
+    )(me, centers.reshape(1, -1), flat, potential)
+    arrived = sent(dict(zip(far, packed_far)), far, 1)
+    packed = dict(zip(rest, pl.pallas_call(
+        functools.partial(pack_rest_kernel, (rows, box_dev, rest)),
+        out_shape=tuple(jax.ShapeDtypeStruct((sent_rows[k], points), bf16) for k in rest),
+        in_specs=[vmem] * 3,
+        out_specs=(vmem,) * len(rest),
+        compiler_params=limit,
+        name="pack_rest",
+    )(row_out, flat, own_region)))
+    late, arrived = after(packed, rest[2:], arrived)
+    arrived.update(sent(packed, rest[:2], 1))
+    arrived.update(sent(late, rest[2:], 1))
+
+    columns, places, active, local = pl.pallas_call(
         functools.partial(table_kernel, (fun_dev, support, halo, boxes)),
         out_shape=(
             jax.ShapeDtypeStruct((slots * SLOT, 128), f32),
             jax.ShapeDtypeStruct((8, boxes * SLOT), f32),
-            jax.ShapeDtypeStruct((slots * (boxes // STEP),), jnp.int32),
+            jax.ShapeDtypeStruct(((slots + 1) * (boxes // STEP),), jnp.int32),
+            jax.ShapeDtypeStruct((boxes, SLOT, points), bf16),
         ),
-        in_specs=[smem, vmem],
-        out_specs=(vmem, vmem, smem),
+        in_specs=[smem, vmem, vmem],
+        out_specs=(vmem, vmem, smem, vmem),
         compiler_params=limit,
         name="tables",
-    )(cut, near)
+    )(cut, near, flat)
 
     wide = slots * SLOT
-    sources = [flat if e == REACH else arrived[REACH - e] for e in range(slots)]
-    read_rows = [flat.shape[0] if e == REACH else rows_of[REACH - e] for e in range(slots)]
+    sources = [arrived[REACH - e] for e in range(slots) if e != REACH]
+    read_rows = [rows_of[REACH - e] for e in range(slots)]
+    level_sizes = [level_rows(part + 1)[1] - level_rows(part + 1)[0] for part in range(REACH)]
     exact_rows = [rows[2 * REACH - e] for e in range(slots)]
     block = pl.BlockSpec((STEP, wide, points), lambda g: (g, 0, 0))
     band = (fun_dev, 2 * reading)
@@ -469,14 +528,16 @@
             jax.ShapeDtypeStruct((128, points), bf16),
         )
         + tuple(jax.ShapeDtypeStruct(band, f32) for _ in range(slots)),
-        in_specs=[smem, smem, whole(columns.shape), whole(own_region.shape)] + [whole(s.shape) for s in sources],
+        in_specs=[smem, smem, whole(columns.shape), whole(own_region.shape), pl.BlockSpec((STEP, SLOT, points), lambda g: (g, 0, 0))]
+        + [whole(s.shape) for s in sources],
         out_specs=(block, whole((128, points))) + tuple(whole(band) for _ in range(slots)),
-        scratch_shapes=[pltpu.VMEM((wide, wide), f32)],
+        scratch_shapes=[pltpu.VMEM((wide, band_lanes(fun_dev, reading)), f32)]
+        + [pltpu.VMEM((size, size), f32) for size in level_sizes],
         compiler_params=limit,
         name="unpack",
-    )(cut, active, columns, own_region, *sources)
-
-    summed = sent_in_order({k: grams[REACH + k] for k in order}, order, 1)
+    )(cut, active, columns, own_region, local, *sources)
+
+    summed = sent({k: grams[REACH + k] for k in one_way}, one_way, 1)
     gram_band, mixing_rows = pl.pallas_call(
         functools.partial(sum_kernel, reading),
         out_shape=(jax.ShapeDtypeStruct(band, f32), jax.ShapeDtypeStruct((SLOT, 2 * reading), bf16)),
@@ -484,38 +545,37 @@
         out_specs=(vmem, vmem),
         compiler_params=limit,
         name="sum",
-    )(grams[REACH], *[summed[k] for k in order])
-    mixing_of = sent_in_order({k: mixing_rows for k in order}, order, 1)
+    )(grams[REACH], *[summed[k] for k in one_way])
+    mixing_of = sent({k: mixing_rows for k in one_way}, one_way, 1)
     mixing_of[0] = mixing_rows
+    band_order = one_way + [0]
 
     out_rows = [rows_of[REACH - e] for e in range(slots)]
     shapes = [(r, points) for r in out_rows] + [(r, 128) for r in out_rows]
     mixed = pl.pallas_call(
-        functools.partial(mix_kernel, (fun_dev, reading)),
+        functools.partial(mix_kernel, (fun_dev, reading, band_order)),
         grid=(boxes // STEP,),
         out_shape=tuple(jax.ShapeDtypeStruct(shape, bf16) for shape in shapes),
         in_specs=[smem, smem, pl.BlockSpec((8, STEP * SLOT), lambda g: (0, g)), block]
         + [whole((SLOT, 2 * reading))] * slots,
         out_specs=tuple(whole(shape) for shape in shapes),
-        scratch_shapes=[pltpu.VMEM((wide, wide), bf16), pltpu.VMEM((STEP, wide, points), bf16)],
+        scratch_shapes=[pltpu.VMEM((STEP, wide, points), bf16)]
+        + [pltpu.VMEM((size, size), bf16) for size in level_sizes],
         compiler_params=limit,
         name="mix",
-    )(cut, active, places, pieces, *[mixing_of[REACH - e] for e in range(slots)])
-
-    filtered_rows = {}
-    for group in [order[:3]] + [order[3:5], order[5:], [0]]:
-        at = [REACH - k for k in group]
-        got = pl.pallas_call(
-            filter_kernel,
-            out_shape=tuple(jax.ShapeDtypeStruct((out_rows[e], points), bf16) for e in at),
-            in_specs=[vmem] * (2 + 2 * len(at)),
-            out_specs=tuple(vmem for _ in at),
-            compiler_params=limit,
-            name="filter",
-        )(region, kinetic, *[mixed[e] for e in at], *[mixed[slots + e] for e in at])
-        filtered_rows.update(zip(group, got))
-    returned = sent_in_order({k: filtered_rows[k] for k in order}, order, -1)
-    returned[0] = filtered_rows[0]
+    )(cut, active, places, pieces, *[mixing_of[k] for k in band_order])
+
+    ready = {}
+    for k in far + rest + [0]:
+        here, at_box = mixed[REACH - k], mixed[slots + REACH - k]
+        near_by = jnp.dot(at_box, region, preferred_element_type=f32)
+        applied = jnp.dot(here, kinetic, preferred_element_type=f32)
+        ready[k] = (applied + near_by * here.astype(f32)).astype(bf16)
+    returned = sent(ready, far, -1)
+    late, returned = after(ready, rest[2:], returned)
+    returned.update(sent(ready, rest[:2], -1))
+    returned.update(sent(late, rest[2:], -1))
+    returned[0] = ready[0]
 
     groups, held = [], 257
     for e, k in enumerate(offsets):

time: 149 us -> 134 us (0.90)
  the two profiles are of different devices: /device:TPU:31 before, /device:TPU:1 now
where the time goes in v1:
time: 134 us; the launch traced here: 133 us
  starting transfers between devices  45.5 us (34%)
  waiting for transfers between devices  42 us (31%)
  Pallas kernels  33.5 us (25%)
  matrix products  7.5 us (6%)
  local copies, waits for them, and re-layouts  4.04 us (3%)
    ppermute x24, starting transfers between devices, passed_along(): return lax.ppermute(value, AXES, pairs)  45.5 us
    ppermute x24, waiting for transfers between devices, passed_along(): return lax.ppermute(value, AXES, pairs)  42 us
    pallas_call x1, Pallas kernels, on_device(): pl.pallas_call(functools.partial(unpack_kernel, (fun_dev, box_dev, readin...  9.07 us
    pallas_call x1, Pallas kernels, on_device(): pl.pallas_call(functools.partial(mix_kernel, (fun_dev, reading, band_orde...  8.56 us
    dot_general x7, matrix products, on_device(): applied = jnp.dot(here, kinetic, preferred_element_type=f32)  5.72 us
    pallas_call x1, Pallas kernels, on_device(): pl.pallas_call(functools.partial(home_kernel, groups), grid=(fun_dev * su...  5.27 us
    pallas_call x1, Pallas kernels, on_device(): pl.pallas_call(functools.partial(table_kernel, (fun_dev, support, halo, b...  3.63 us
    pallas_call x1, Pallas kernels, on_device(): pl.pallas_call(functools.partial(pack_rest_kernel, (rows, box_dev, rest))...  3.2 us
  transfers between devices with their start and end apart: 24, of which 9 were waited for; matrix products, arithmetic and copies ran while one was open for 5% of the time, Pallas kernels for 3%

profile of v1, /device:TPU:1, one launch (start us, length us, event | category | flops | bytes accessed | tf_op | source)
XLA Modules:
  0.0 133.3 jit_solution(13742606846101293668)
XLA Ops:
  2.3 3.1 %pack_far.1 = (bf16[48,1024]{1,0:T(8,128)(2,1)S(1)}, bf16[64,1024]{1,0:T(8,128)(2,1)S(1)}, f32[512,128]{1,0:T(8,128)S(1)}, s32[8]{0:T(128)S(1)}, f32[8,768]{1,0:...) custom-call(s32[1]{0:T(128)} %bitcast.me_ref, s32[1,768]{1,0:T(1,128)S(1)} %reshape.17.centers_ref, ...), custom_call_target="tpu_custom_call" | custom-call | tf_op jit(solution)/shard_map/pack_far/pallas_call | solution.py:474
  5.4 3.2 %pack_rest.1 = (bf16[240,1024]{1,0:T(8,128)(2,1)S(1)}, bf16[272,1024]{1,0:T(8,128)(2,1)S(1)}, bf16[160,1024]{1,0:T(8,128)(2,1)S(1)}, bf16[192,1024]{1,0:T(8,128)(2,1)S(1)}) custom-call(f32[8,768]{1,0:T(8,128)S(1)} %get-tuple-element.58.row_ref, bf16[768,1024]{1,0:T(8,128)(2,1)} %bitcast.32, bf16[32,1024]{1,0:T(8,128)(2,1)S(1)} %get-tuple-element.56.own_ref), custom_call_target="tpu_custom_call" | custom-call | tf_op jit(solution)/shard_map/pack_rest/pallas_call | solution.py:490
  8.8 6.6 %collective-permute-start = (bf16[64,1024]{1,0:T(8,128)(2,1)S(1)}, bf16[64,1024]{1,0:T(8,128)(2,1)S(1)}, u32[]{:S(2)}, u32[]{:S(2)}) collective-permute-start(bf16[64,1024]{1,0:T(8,128)(2,1)S(1)} %get-tuple-element.61), channel_id=1, source_target_pairs={{0,29},{1,30},{2,31},{3,0},{4,1},{5,2},{6,3},{7,4},{8,5},{9,6},{10... | collective-permute-start | bytes 393224 | tf_op jit(solution)/shard_map/ppermute | solution.py:21
  16.0 7.6 %collective-permute-done.1.refs_0_ = bf16[48,1024]{1,0:T(8,128)(2,1)S(1)} collective-permute-done((bf16[48,1024]{1,0:T(8,128)(2,1)S(1)}, bf16[48,1024]{1,0:T(8,128)(2,1)S(1)}, u32[]{:S(2)}, u32[]{:S(2)}) %collective-permute-start.1) | collective-permute-done | bytes 98336 | tf_op jit(solution)/shard_map/ppermute | solution.py:21
  23.5 7.9 %collective-permute-start.5 = (bf16[192,1024]{1,0:T(8,128)(2,1)S(1)}, bf16[192,1024]{1,0:T(8,128)(2,1)S(1)}, u32[]{:S(2)}, u32[]{:S(2)}) collective-permute-start(bf16[192,1024]{1,0:T(8,128)(2,1)S(1)} %get-tuple-element.67), channel_id=1, source_target_pairs={{0,30},{1,31},{2,0},{3,1},{4,2},{5,3},{6,4},{7,5},{8,6},{9,7},{10,... | collective-permute-start | bytes 1179656 | tf_op jit(solution)/shard_map/ppermute | solution.py:21
  31.5 3.6 %tables.1 = (f32[224,128]{1,0:T(8,128)S(1)}, f32[8,768]{1,0:T(8,128)S(1)}, s32[24]{0:T(128)S(1)}, bf16[24,32,1024]{2,1,0:T(8,128)(2,1)S(1)}) custom-call(s32[8]{0:T(128)S(1)} %get-tuple-element.51.cut_ref, f32[512,128]{1,0:T(8,128)S(1)} %get-tuple-element.52.near_ref, bf16[768,1024]{1,0:T(8,128)(2,1)} %bitcast.33), custom_call_target="tpu_custom_call" | custom-call | tf_op jit(solution)/shard_map/tables/pallas_call | solution.py:502
  36.3 7.9 %collective-permute-done.2.refs_1_ = bf16[160,1024]{1,0:T(8,128)(2,1)S(1)} collective-permute-done((bf16[160,1024]{1,0:T(8,128)(2,1)S(1)}, bf16[160,1024]{1,0:T(8,128)(2,1)S(1)}, u32[]{:S(2)}, u32[]{:S(2)}) %collective-permute-start.2) | collective-permute-done | bytes 327712 | tf_op jit(solution)/shard_map/ppermute | solution.py:21
  45.2 9.1 %unpack.1 = (bf16[24,224,1024]{2,1,0:T(8,128)(2,1)}, bf16[128,1024]{1,0:T(8,128)(2,1)S(1)}, f32[24,256]{1,0:T(8,128)S(1)}, f32[24,256]{1,0:T(8,128)S(1)}, f32[24...) custom-call(s32[8]{0:T(128)S(1)} %get-tuple-element.51.cut_ref, ...), custom_call_target="tpu_custom_call" | custom-call | tf_op jit(solution)/shard_map/unpack/pallas_call | solution.py:523
  54.2 2.3 %collective-permute-start.6 = (f32[24,256]{1,0:T(8,128)S(1)}, f32[24,256]{1,0:T(8,128)S(1)}, u32[]{:S(2)}, u32[]{:S(2)}) collective-permute-start(f32[24,256]{1,0:T(8,128)S(1)} %get-tuple-element.71), channel_id=1, source_target_pairs={{0,3},{1,4},{2,5},{3,6},{4,7},{5,8},{6,9},{7,10},{8,11},{9,12},{10... | collective-permute-start | bytes 73736 | tf_op jit(solution)/shard_map/ppermute | solution.py:21
  56.6 1.7 %collective-permute-start.7 = (f32[24,256]{1,0:T(8,128)S(1)}, f32[24,256]{1,0:T(8,128)S(1)}, u32[]{:S(2)}, u32[]{:S(2)}) collective-permute-start(f32[24,256]{1,0:T(8,128)S(1)} %get-tuple-element.72), channel_id=1, source_target_pairs={{0,2},{1,3},{2,4},{3,5},{4,6},{5,7},{6,8},{7,9},{8,10},{9,11},{10,... | collective-permute-start | bytes 73736 | tf_op jit(solution)/shard_map/ppermute | solution.py:21
  58.2 5.6 %collective-permute-start.9 = (f32[24,256]{1,0:T(8,128)S(1)}, f32[24,256]{1,0:T(8,128)S(1)}, u32[]{:S(2)}, u32[]{:S(2)}) collective-permute-start(f32[24,256]{1,0:T(8,128)S(1)} %get-tuple-element.74), channel_id=1, source_target_pairs={{0,29},{1,30},{2,31},{3,0},{4,1},{5,2},{6,3},{7,4},{8,5},{9,6},{10... | collective-permute-start | bytes 73736 | tf_op jit(solution)/shard_map/ppermute | solution.py:21
  64.8 1.7 %collective-permute-done.10.refs_5_ = f32[24,256]{1,0:T(8,128)S(1)} collective-permute-done((f32[24,256]{1,0:T(8,128)S(1)}, f32[24,256]{1,0:T(8,128)S(1)}, u32[]{:S(2)}, u32[]{:S(2)}) %collective-permute-start.10) | collective-permute-done | bytes 24608 | tf_op jit(solution)/shard_map/ppermute | solution.py:21
  68.9 3.8 %collective-permute-start.16 = (bf16[32,256]{1,0:T(8,128)(2,1)S(1)}, bf16[32,256]{1,0:T(8,128)(2,1)S(1)}, u32[]{:S(2)}, u32[]{:S(2)}) collective-permute-start(bf16[32,256]{1,0:T(8,128)(2,1)S(1)} %get-tuple-element.77.refs_6_), channel_id=1, source_target_pairs={{0,30},{1,31},{2,0},{3,1},{4,2},{5,3},{6,4},{7,5},{8,6},{9,7},{10,... | collective-permute-start | bytes 49160 | tf_op jit(solution)/shard_map/ppermute | solution.py:21
  72.8 1.9 %collective-permute-start.14 = (bf16[32,256]{1,0:T(8,128)(2,1)S(1)}, bf16[32,256]{1,0:T(8,128)(2,1)S(1)}, u32[]{:S(2)}, u32[]{:S(2)}) collective-permute-start(bf16[32,256]{1,0:T(8,128)(2,1)S(1)} %get-tuple-element.77.refs_6_), channel_id=1, source_target_pairs={{0,1},{1,2},{2,3},{3,4},{4,5},{5,6},{6,7},{7,8},{8,9},{9,10},{10,1... | collective-permute-start | bytes 49160 | tf_op jit(solution)/shard_map/ppermute | solution.py:21
  76.4 4.6 %collective-permute-done.13.refs_1_ = bf16[32,256]{1,0:T(8,128)(2,1)S(1)} collective-permute-done((bf16[32,256]{1,0:T(8,128)(2,1)S(1)}, bf16[32,256]{1,0:T(8,128)(2,1)S(1)}, u32[]{:S(2)}, u32[]{:S(2)}) %collective-permute-start.13) | collective-permute-done | bytes 16416 | tf_op jit(solution)/shard_map/ppermute | solution.py:21
  81.0 1.5 %collective-permute-done.12.refs_0_ = bf16[32,256]{1,0:T(8,128)(2,1)S(1)} collective-permute-done((bf16[32,256]{1,0:T(8,128)(2,1)S(1)}, bf16[32,256]{1,0:T(8,128)(2,1)S(1)}, u32[]{:S(2)}, u32[]{:S(2)}) %collective-permute-start.12) | collective-permute-done | bytes 16416 | tf_op jit(solution)/shard_map/ppermute | solution.py:21
  82.5 8.6 %mix.1 = (bf16[48,1024]{1,0:T(8,128)(2,1)S(1)}, bf16[160,1024]{1,0:T(8,128)(2,1)S(1)}, bf16[240,1024]{1,0:T(8,128)(2,1)S(1)}, bf16[512,1024]{1,0:T(8,128)(2,1)},...) custom-call(s32[8]{0:T(128)S(1)} %get-tuple-element.51.cut_ref, ...), custom_call_target="tpu_custom_call" | custom-call | tf_op jit(solution)/shard_map/mix/pallas_call | solution.py:555
  92.4 5.4 %collective-permute-start.19 = (bf16[48,1024]{1,0:T(8,128)(2,1)S(1)}, bf16[48,1024]{1,0:T(8,128)(2,1)S(1)}, u32[]{:S(2)}, u32[]{:S(2)}) collective-permute-start(bf16[48,1024]{1,0:T(8,128)(2,1)S(1)} %fusion.5), channel_id=1, source_target_pairs={{0,29},{1,30},{2,31},{3,0},{4,1},{5,2},{6,3},{7,4},{8,5},{9,6},{10... | collective-permute-start | bytes 294920 | tf_op jit(solution)/shard_map/ppermute | solution.py:21
  101.8 1.5 %collective-permute-start.21 = (bf16[256,1024]{1,0:T(8,128)(2,1)S(1)}, bf16[256,1024]{1,0:T(8,128)(2,1)S(1)}, u32[]{:S(2)}, u32[]{:S(2)}) collective-permute-start(bf16[256,1024]{1,0:T(8,128)(2,1)S(1)} %fusion), channel_id=1, source_target_pairs={{0,1},{1,2},{2,3},{3,4},{4,5},{5,6},{6,7},{7,8},{8,9},{9,10},{10,1... | collective-permute-start | bytes 1572872 | tf_op jit(solution)/shard_map/ppermute | solution.py:21
  103.8 5.0 %collective-permute-start.23 = (bf16[160,1024]{1,0:T(8,128)(2,1)S(1)}, bf16[160,1024]{1,0:T(8,128)(2,1)S(1)}, u32[]{:S(2)}, u32[]{:S(2)}) collective-permute-start(bf16[160,1024]{1,0:T(8,128)(2,1)S(1)} %fusion.3), channel_id=1, source_target_pairs={{0,30},{1,31},{2,0},{3,1},{4,2},{5,3},{6,4},{7,5},{8,6},{9,7},{10,... | collective-permute-start | bytes 983048 | tf_op jit(solution)/shard_map/ppermute | solution.py:21
  108.8 2.3 %add_convert_fusion.refs_3_ = bf16[512,1024]{1,0:T(8,128)(2,1)} fusion(f32[512,1024]{1,0:T(8,128)S(1)} %fusion.6, bf16[512,1024]{1,0:T(8,128)(2,1)S(1)} %copy-done.6, bf16[1024,1024]{1,0:T(8,128)(2,1)S(1)} %copy-done), kind=kOutput, calls=%fused_computation | convolution fusion | flops 1075838976 | bytes 6291456 | tf_op jit(solution)/shard_map/dot_general | solution.py:572
  111.1 11.5 %collective-permute-done.20.refs_1_ = bf16[160,1024]{1,0:T(8,128)(2,1)S(1)} collective-permute-done((bf16[160,1024]{1,0:T(8,128)(2,1)S(1)}, bf16[160,1024]{1,0:T(8,128)(2,1)S(1)}, u32[]{:S(2)}, u32[]{:S(2)}) %collective-permute-start.20) | collective-permute-done | bytes 327712 | tf_op jit(solution)/shard_map/ppermute | solution.py:21
  122.6 5.4 %collective-permute-done.23.refs_5_ = bf16[160,1024]{1,0:T(8,128)(2,1)S(1)} collective-permute-done((bf16[160,1024]{1,0:T(8,128)(2,1)S(1)}, bf16[160,1024]{1,0:T(8,128)(2,1)S(1)}, u32[]{:S(2)}, u32[]{:S(2)}) %collective-permute-start.23) | collective-permute-done | bytes 327712 | tf_op jit(solution)/shard_map/ppermute | solution.py:21
  128.1 5.3 %home.1 = bf16[768,1024]{1,0:T(8,128)(2,1)} custom-call(f32[1,768]{1,0:T(1,128)S(1)} %get-tuple-element.50.home_ref, bf16[48,1024]{1,0:T(8,128)(2,1)S(1)} %collective-permute-done.18.refs_0_, bf16[160,1024]{1,0:T(8,128)(2,1)S(1)} %collective-permute-done.20.refs_1_, bf16[256,1024]{1,0:T(8,128)(2,1)S(1)} %collective-permute-done.21.refs_2_, ...), custom_call_target="tpu_custom_call" | custom-call | tf_op jit(solution)/shard_map/home/pallas_call | solution.py:588
  (60 shorter events, 15.2 us)
Async XLA Ops:
  8.7 35.5 %collective-permute-start.4 = (bf16[272,1024]{1,0:T(8,128)(2,1)S(1)}, bf16[272,1024]{1,0:T(8,128)(2,1)S(1)}, u32[]{:S(2)}, u32[]{:S(2)}) collective-permute-start(bf16[272,1024]{1,0:T(8,128)(2,1)S(1)} %get-tuple-element.66), channel_id=1, source_target_pairs={{0,31},{1,0},{2,1},{3,2},{4,3},{5,4},{6,5},{7,6},{8,7},{9,8},{10,9... | collective-permute-start | bytes 1671176 | tf_op jit(solution)/shard_map/ppermute | solution.py:21
  8.8 14.8 %collective-permute-start = (bf16[64,1024]{1,0:T(8,128)(2,1)S(1)}, bf16[64,1024]{1,0:T(8,128)(2,1)S(1)}, u32[]{:S(2)}, u32[]{:S(2)}) collective-permute-start(bf16[64,1024]{1,0:T(8,128)(2,1)S(1)} %get-tuple-element.61), channel_id=1, source_target_pairs={{0,29},{1,30},{2,31},{3,0},{4,1},{5,2},{6,3},{7,4},{8,5},{9,6},{10... | collective-permute-start | bytes 393224 | tf_op jit(solution)/shard_map/ppermute | solution.py:21
  15.4 8.2 %collective-permute-start.1 = (bf16[48,1024]{1,0:T(8,128)(2,1)S(1)}, bf16[48,1024]{1,0:T(8,128)(2,1)S(1)}, u32[]{:S(2)}, u32[]{:S(2)}) collective-permute-start(bf16[48,1024]{1,0:T(8,128)(2,1)S(1)} %get-tuple-element.62), channel_id=1, source_target_pairs={{0,3},{1,4},{2,5},{3,6},{4,7},{5,8},{6,9},{7,10},{8,11},{9,12},{10... | collective-permute-start | bytes 294920 | tf_op jit(solution)/shard_map/ppermute | solution.py:21
  15.4 28.8 %collective-permute-start.3 = (bf16[240,1024]{1,0:T(8,128)(2,1)S(1)}, bf16[240,1024]{1,0:T(8,128)(2,1)S(1)}, u32[]{:S(2)}, u32[]{:S(2)}) collective-permute-start(bf16[240,1024]{1,0:T(8,128)(2,1)S(1)} %get-tuple-element.65), channel_id=1, source_target_pairs={{0,1},{1,2},{2,3},{3,4},{4,5},{5,6},{6,7},{7,8},{8,9},{9,10},{10,1... | collective-permute-start | bytes 1474568 | tf_op jit(solution)/shard_map/ppermute | solution.py:21
  23.5 20.7 %collective-permute-start.5 = (bf16[192,1024]{1,0:T(8,128)(2,1)S(1)}, bf16[192,1024]{1,0:T(8,128)(2,1)S(1)}, u32[]{:S(2)}, u32[]{:S(2)}) collective-permute-start(bf16[192,1024]{1,0:T(8,128)(2,1)S(1)} %get-tuple-element.67), channel_id=1, source_target_pairs={{0,30},{1,31},{2,0},{3,1},{4,2},{5,3},{6,4},{7,5},{8,6},{9,7},{10,... | collective-permute-start | bytes 1179656 | tf_op jit(solution)/shard_map/ppermute | solution.py:21
  31.5 12.7 %collective-permute-start.2 = (bf16[160,1024]{1,0:T(8,128)(2,1)S(1)}, bf16[160,1024]{1,0:T(8,128)(2,1)S(1)}, u32[]{:S(2)}, u32[]{:S(2)}) collective-permute-start(bf16[160,1024]{1,0:T(8,128)(2,1)S(1)} %get-tuple-element.64), channel_id=1, source_target_pairs={{0,2},{1,3},{2,4},{3,5},{4,6},{5,7},{6,8},{7,9},{8,10},{9,11},{10,... | collective-permute-start | bytes 983048 | tf_op jit(solution)/shard_map/ppermute | solution.py:21
  54.2 9.6 %collective-permute-start.6 = (f32[24,256]{1,0:T(8,128)S(1)}, f32[24,256]{1,0:T(8,128)S(1)}, u32[]{:S(2)}, u32[]{:S(2)}) collective-permute-start(f32[24,256]{1,0:T(8,128)S(1)} %get-tuple-element.71), channel_id=1, source_target_pairs={{0,3},{1,4},{2,5},{3,6},{4,7},{5,8},{6,9},{7,10},{8,11},{9,12},{10... | collective-permute-start | bytes 73736 | tf_op jit(solution)/shard_map/ppermute | solution.py:21
  56.6 7.9 %collective-permute-start.7 = (f32[24,256]{1,0:T(8,128)S(1)}, f32[24,256]{1,0:T(8,128)S(1)}, u32[]{:S(2)}, u32[]{:S(2)}) collective-permute-start(f32[24,256]{1,0:T(8,128)S(1)} %get-tuple-element.72), channel_id=1, source_target_pairs={{0,2},{1,3},{2,4},{3,5},{4,6},{5,7},{6,8},{7,9},{8,10},{9,11},{10,... | collective-permute-start | bytes 73736 | tf_op jit(solution)/shard_map/ppermute | solution.py:21
  58.2 6.3 %collective-permute-start.8 = (f32[24,256]{1,0:T(8,128)S(1)}, f32[24,256]{1,0:T(8,128)S(1)}, u32[]{:S(2)}, u32[]{:S(2)}) collective-permute-start(f32[24,256]{1,0:T(8,128)S(1)} %get-tuple-element.73), channel_id=1, source_target_pairs={{0,1},{1,2},{2,3},{3,4},{4,5},{5,6},{6,7},{7,8},{8,9},{9,10},{10,1... | collective-permute-start | bytes 73736 | tf_op jit(solution)/shard_map/ppermute | solution.py:21
  58.2 6.5 %collective-permute-start.9 = (f32[24,256]{1,0:T(8,128)S(1)}, f32[24,256]{1,0:T(8,128)S(1)}, u32[]{:S(2)}, u32[]{:S(2)}) collective-permute-start(f32[24,256]{1,0:T(8,128)S(1)} %get-tuple-element.74), channel_id=1, source_target_pairs={{0,29},{1,30},{2,31},{3,0},{4,1},{5,2},{6,3},{7,4},{8,5},{9,6},{10... | collective-permute-start | bytes 73736 | tf_op jit(solution)/shard_map/ppermute | solution.py:21
  63.8 2.7 %collective-permute-start.10 = (f32[24,256]{1,0:T(8,128)S(1)}, f32[24,256]{1,0:T(8,128)S(1)}, u32[]{:S(2)}, u32[]{:S(2)}) collective-permute-start(f32[24,256]{1,0:T(8,128)S(1)} %get-tuple-element.75), channel_id=1, source_target_pairs={{0,30},{1,31},{2,0},{3,1},{4,2},{5,3},{6,4},{7,5},{8,6},{9,7},{10,... | collective-permute-start | bytes 73736 | tf_op jit(solution)/shard_map/ppermute | solution.py:21
  63.8 4.1 %collective-permute-start.11 = (f32[24,256]{1,0:T(8,128)S(1)}, f32[24,256]{1,0:T(8,128)S(1)}, u32[]{:S(2)}, u32[]{:S(2)}) collective-permute-start(f32[24,256]{1,0:T(8,128)S(1)} %get-tuple-element.76), channel_id=1, source_target_pairs={{0,31},{1,0},{2,1},{3,2},{4,3},{5,4},{6,5},{7,6},{8,7},{9,8},{10,9... | collective-permute-start | bytes 73736 | tf_op jit(solution)/shard_map/ppermute | solution.py:21
  68.5 7.2 %collective-permute-start.17 = (bf16[32,256]{1,0:T(8,128)(2,1)S(1)}, bf16[32,256]{1,0:T(8,128)(2,1)S(1)}, u32[]{:S(2)}, u32[]{:S(2)}) collective-permute-start(bf16[32,256]{1,0:T(8,128)(2,1)S(1)} %get-tuple-element.77.refs_6_), channel_id=1, source_target_pairs={{0,31},{1,0},{2,1},{3,2},{4,3},{5,4},{6,5},{7,6},{8,7},{9,8},{10,9... | collective-permute-start | bytes 49160 | tf_op jit(solution)/shard_map/ppermute | solution.py:21
  68.9 7.4 %collective-permute-start.16 = (bf16[32,256]{1,0:T(8,128)(2,1)S(1)}, bf16[32,256]{1,0:T(8,128)(2,1)S(1)}, u32[]{:S(2)}, u32[]{:S(2)}) collective-permute-start(bf16[32,256]{1,0:T(8,128)(2,1)S(1)} %get-tuple-element.77.refs_6_), channel_id=1, source_target_pairs={{0,30},{1,31},{2,0},{3,1},{4,2},{5,3},{6,4},{7,5},{8,6},{9,7},{10,... | collective-permute-start | bytes 49160 | tf_op jit(solution)/shard_map/ppermute | solution.py:21
  72.8 3.6 %collective-permute-start.15 = (bf16[32,256]{1,0:T(8,128)(2,1)S(1)}, bf16[32,256]{1,0:T(8,128)(2,1)S(1)}, u32[]{:S(2)}, u32[]{:S(2)}) collective-permute-start(bf16[32,256]{1,0:T(8,128)(2,1)S(1)} %get-tuple-element.77.refs_6_), channel_id=1, source_target_pairs={{0,29},{1,30},{2,31},{3,0},{4,1},{5,2},{6,3},{7,4},{8,5},{9,6},{10... | collective-permute-start | bytes 49160 | tf_op jit(solution)/shard_map/ppermute | solution.py:21
  72.8 3.5 %collective-permute-start.14 = (bf16[32,256]{1,0:T(8,128)(2,1)S(1)}, bf16[32,256]{1,0:T(8,128)(2,1)S(1)}, u32[]{:S(2)}, u32[]{:S(2)}) collective-permute-start(bf16[32,256]{1,0:T(8,128)(2,1)S(1)} %get-tuple-element.77.refs_6_), channel_id=1, source_target_pairs={{0,1},{1,2},{2,3},{3,4},{4,5},{5,6},{6,7},{7,8},{8,9},{9,10},{10,1... | collective-permute-start | bytes 49160 | tf_op jit(solution)/shard_map/ppermute | solution.py:21
  74.8 6.2 %collective-permute-start.13 = (bf16[32,256]{1,0:T(8,128)(2,1)S(1)}, bf16[32,256]{1,0:T(8,128)(2,1)S(1)}, u32[]{:S(2)}, u32[]{:S(2)}) collective-permute-start(bf16[32,256]{1,0:T(8,128)(2,1)S(1)} %get-tuple-element.77.refs_6_), channel_id=1, source_target_pairs={{0,2},{1,3},{2,4},{3,5},{4,6},{5,7},{6,8},{7,9},{8,10},{9,11},{10,... | collective-permute-start | bytes 49160 | tf_op jit(solution)/shard_map/ppermute | solution.py:21
  75.7 6.8 %collective-permute-start.12 = (bf16[32,256]{1,0:T(8,128)(2,1)S(1)}, bf16[32,256]{1,0:T(8,128)(2,1)S(1)}, u32[]{:S(2)}, u32[]{:S(2)}) collective-permute-start(bf16[32,256]{1,0:T(8,128)(2,1)S(1)} %get-tuple-element.77.refs_6_), channel_id=1, source_target_pairs={{0,3},{1,4},{2,5},{3,6},{4,7},{5,8},{6,9},{7,10},{8,11},{9,12},{10... | collective-permute-start | bytes 49160 | tf_op jit(solution)/shard_map/ppermute | solution.py:21
  91.7 12.0 %collective-permute-start.18 = (bf16[48,1024]{1,0:T(8,128)(2,1)S(1)}, bf16[48,1024]{1,0:T(8,128)(2,1)S(1)}, u32[]{:S(2)}, u32[]{:S(2)}) collective-permute-start(bf16[48,1024]{1,0:T(8,128)(2,1)S(1)} %fusion.4), channel_id=1, source_target_pairs={{0,3},{1,4},{2,5},{3,6},{4,7},{5,8},{6,9},{7,10},{8,11},{9,12},{10... | collective-permute-start | bytes 294920 | tf_op jit(solution)/shard_map/ppermute | solution.py:21
  92.4 11.3 %collective-permute-start.19 = (bf16[48,1024]{1,0:T(8,128)(2,1)S(1)}, bf16[48,1024]{1,0:T(8,128)(2,1)S(1)}, u32[]{:S(2)}, u32[]{:S(2)}) collective-permute-start(bf16[48,1024]{1,0:T(8,128)(2,1)S(1)} %fusion.5), channel_id=1, source_target_pairs={{0,29},{1,30},{2,31},{3,0},{4,1},{5,2},{6,3},{7,4},{8,5},{9,6},{10... | collective-permute-start | bytes 294920 | tf_op jit(solution)/shard_map/ppermute | solution.py:21
  100.4 27.7 %collective-permute-start.22 = (bf16[240,1024]{1,0:T(8,128)(2,1)S(1)}, bf16[240,1024]{1,0:T(8,128)(2,1)S(1)}, u32[]{:S(2)}, u32[]{:S(2)}) collective-permute-start(bf16[240,1024]{1,0:T(8,128)(2,1)S(1)} %fusion.1), channel_id=1, source_target_pairs={{0,31},{1,0},{2,1},{3,2},{4,3},{5,4},{6,5},{7,6},{8,7},{9,8},{10,9... | collective-permute-start | bytes 1474568 | tf_op jit(solution)/shard_map/ppermute | solution.py:21
  101.8 26.3 %collective-permute-start.21 = (bf16[256,1024]{1,0:T(8,128)(2,1)S(1)}, bf16[256,1024]{1,0:T(8,128)(2,1)S(1)}, u32[]{:S(2)}, u32[]{:S(2)}) collective-permute-start(bf16[256,1024]{1,0:T(8,128)(2,1)S(1)} %fusion), channel_id=1, source_target_pairs={{0,1},{1,2},{2,3},{3,4},{4,5},{5,6},{6,7},{7,8},{8,9},{9,10},{10,1... | collective-permute-start | bytes 1572872 | tf_op jit(solution)/shard_map/ppermute | solution.py:21
  103.7 18.9 %collective-permute-start.20 = (bf16[160,1024]{1,0:T(8,128)(2,1)S(1)}, bf16[160,1024]{1,0:T(8,128)(2,1)S(1)}, u32[]{:S(2)}, u32[]{:S(2)}) collective-permute-start(bf16[160,1024]{1,0:T(8,128)(2,1)S(1)} %fusion.2), channel_id=1, source_target_pairs={{0,2},{1,3},{2,4},{3,5},{4,6},{5,7},{6,8},{7,9},{8,10},{9,11},{10,... | collective-permute-start | bytes 983048 | tf_op jit(solution)/shard_map/ppermute | solution.py:21
  103.8 24.3 %collective-permute-start.23 = (bf16[160,1024]{1,0:T(8,128)(2,1)S(1)}, bf16[160,1024]{1,0:T(8,128)(2,1)S(1)}, u32[]{:S(2)}, u32[]{:S(2)}) collective-permute-start(bf16[160,1024]{1,0:T(8,128)(2,1)S(1)} %fusion.3), channel_id=1, source_target_pairs={{0,30},{1,31},{2,0},{3,1},{4,2},{5,3},{6,4},{7,5},{8,6},{9,7},{10,... | collective-permute-start | bytes 983048 | tf_op jit(solution)/shard_map/ppermute | solution.py:21
  (7 other events, 102.4 us)

commit v2 on v1

--- a/solution.py
+++ b/solution.py
@@ -25,9 +25,11 @@
     return {k: passed_along(values[k], sign * k) for k in keys}
 
 
-def after(values, keys, there):
-    held, there = lax.optimization_barrier(({k: values[k] for k in keys}, there))
-    return held, there
+def all_sent(values, now, last, sign):
+    there = sent(values, now, sign)
+    value, there[now[0]] = lax.optimization_barrier((values[last], there[now[0]]))
+    there[last] = passed_along(value, sign * last)
+    return there
 
 
 def rounded_up(value, multiple):
@@ -103,7 +105,7 @@
 def pack_kernel(plan, me_ref, centers_ref, flat_ref, potential_ref, *refs):
     fun_dev, support, devices, halo, rows, back, low_cut, high_cut, now = plan
     outs = dict(zip(now, refs[: len(now)]))
-    near_ref, cut_ref, row_ref, home_ref, own_ref = refs[len(now) :]
+    near_ref, cut_ref, home_ref, own_ref, row_ref = refs[len(now) :]
     me = me_ref[0]
     box_dev = fun_dev // 2
     fun_all, box_all = fun_dev * devices, box_dev * devices
@@ -179,11 +181,6 @@
             inside = (part >= 0) & (part < 2 * box_dev)
             value = value + times(one_hot(inside & (iota(shape, 1) == from_col)), own_ref[...])
         out_ref[...] = value.astype(jnp.bfloat16)
-
-
-def pack_rest_kernel(plan, row_ref, flat_ref, own_ref, *refs):
-    rows, box_dev, now = plan
-    packed_rows(rows, box_dev, row_ref, flat_ref, own_ref, dict(zip(now, refs)))
 
 
 def picked(start, low, high, first, rows):
@@ -236,8 +233,9 @@
             lane == 0.0, packed, jnp.where(lane == 1.0, box_low, box_high)
         )
         lies = (box >= spread_over(box_low, of_fun)) & (box < spread_over(box_high, of_fun))
-        place_ref[e : e + 1, :] = jnp.where(lies, spread_over(packed, of_fun) + box, -1.0)
+        place = jnp.where(lies, spread_over(packed, of_fun) + box, -1.0)
         for g in range(boxes // STEP):
+            place_ref[g, e : e + 1, :] = place[:, g * STEP * SLOT : (g + 1) * STEP * SLOT]
             here = (box >= g * STEP) & (box < (g + 1) * STEP) & lies
             used = jnp.sum(jnp.where(here, 1.0, 0.0)).astype(jnp.int32)
             active_ref[e * (boxes // STEP) + g] = used
@@ -245,7 +243,8 @@
             levels[g] = jnp.maximum(levels[g], level)
     for g in range(boxes // STEP):
         active_ref[slots * (boxes // STEP) + g] = levels[g]
-    place_ref[slots:, :] = jnp.full((place_ref.shape[0] - slots, boxes * SLOT), -1.0, jnp.float32)
+    spare = place_ref.shape[1] - slots
+    place_ref[:, slots:, :] = jnp.full((boxes // STEP, spare, STEP * SLOT), -1.0, jnp.float32)
 
 
 def function_of(shape, dim, fun_dev):
@@ -285,34 +284,32 @@
     gram_refs = refs[slots + 1 : 2 * slots + 1]
     dense = refs[2 * slots + 1]
     totals = refs[2 * slots + 2 :]
-    step, steps = pl.program_id(0), pl.num_programs(0)
-    first = step * STEP
+    steps = window_ref.shape[0] // STEP
     width = cut_ref[REACH + 1] - cut_ref[REACH]
 
-    @pl.when(step == 0)
-    def _():
-        for total in totals:
-            total[...] = jnp.zeros_like(total)
-        value = None
-        for t in range(blocks):
-            held = own_ref if t == 0 else sources[REACH + t]
-            at = 0 if t == 0 else rows[REACH + t]
-            from_row = at // 16 * 16
-            held = held[from_row:]
-            second = own_ref.shape[0] // 2 if t == 0 else box_dev
-            shape = (region_ref.shape[0], held.shape[0])
-            row, col = iota(shape, 0), iota(shape, 1)
-            box = row - jnp.where(row >= SLOT, float(SLOT), 0.0) + cut_ref[REACH].astype(jnp.float32) - t * box_dev
-            wanted = box + jnp.where(row >= SLOT, float(second), 0.0) + float(at - from_row)
-            good = (box >= 0) & (box < box_dev) & (row < 2 * SLOT)
-            term = times(one_hot(good & (col == wanted)), held)
-            value = term if value is None else value + term
-        region_ref[...] = value.astype(jnp.bfloat16)
-
-    @pl.when(first < width)
-    def _():
+    for total in totals:
+        total[...] = jnp.zeros_like(total)
+    value = None
+    for t in range(blocks):
+        held = own_ref if t == 0 else sources[REACH + t]
+        at = 0 if t == 0 else rows[REACH + t]
+        from_row = at // 16 * 16
+        held = held[from_row:]
+        second = own_ref.shape[0] // 2 if t == 0 else box_dev
+        shape = (region_ref.shape[0], held.shape[0])
+        row, col = iota(shape, 0), iota(shape, 1)
+        box = row - jnp.where(row >= SLOT, float(SLOT), 0.0) + cut_ref[REACH].astype(jnp.float32) - t * box_dev
+        wanted = box + jnp.where(row >= SLOT, float(second), 0.0) + float(at - from_row)
+        good = (box >= 0) & (box < box_dev) & (row < 2 * SLOT)
+        term = times(one_hot(good & (col == wanted)), held)
+        value = term if value is None else value + term
+    region_ref[...] = value.astype(jnp.bfloat16)
+
+    @pl.loop(0, lax.div(width + STEP - 1, STEP))
+    def _(step):
+        here_rows = pl.ds(step * STEP, STEP)
         level = active_ref[slots * steps + step]
-        window_ref[:, REACH * SLOT : (REACH + 1) * SLOT, :] = local_ref[...]
+        window_ref[here_rows, REACH * SLOT : (REACH + 1) * SLOT, :] = local_ref[here_rows]
         for e in range(slots):
             if e == REACH:
                 continue
@@ -323,15 +320,15 @@
                 start = column_ref[e * SLOT : (e + 1) * SLOT, 0:1]
                 low = column_ref[e * SLOT : (e + 1) * SLOT, 1:2]
                 high = column_ref[e * SLOT : (e + 1) * SLOT, 2:3]
-                pick = picked(start, low, high, first.astype(jnp.float32), back[e])
+                pick = picked(start, low, high, (step * STEP).astype(jnp.float32), back[e])
                 found = times(pick, sources[e][: back[e]])
-                window_ref[:, e * SLOT : (e + 1) * SLOT, :] = found.astype(jnp.bfloat16).reshape(
+                window_ref[here_rows, e * SLOT : (e + 1) * SLOT, :] = found.astype(jnp.bfloat16).reshape(
                     STEP, SLOT, found.shape[-1]
                 )
 
             @pl.when(jnp.logical_not(used) & (level >= abs(e - REACH)))
             def _():
-                window_ref[:, e * SLOT : (e + 1) * SLOT, :] = jnp.zeros(
+                window_ref[here_rows, e * SLOT : (e + 1) * SLOT, :] = jnp.zeros(
                     (STEP, SLOT, window_ref.shape[-1]), jnp.bfloat16
                 )
         for part, total in enumerate(totals):
@@ -340,23 +337,21 @@
                 low, high = level_rows(part + 1)
                 value = total[...]
                 for b in range(STEP):
-                    here = window_ref[b, low:high]
+                    here = window_ref[step * STEP + b, low:high]
                     value = value + times(here, here, ((1,), (1,)))
                 total[...] = value
 
-    @pl.when(step == steps - 1)
-    def _():
-        wide, lanes = dense.shape
-        keep = jnp.where(
-            function_of((wide, lanes), 0, fun_dev) == lax.broadcasted_iota(jnp.int32, (wide, lanes), 1), volume, 0.0
-        )
-        dense[...] = times(totals[-1][...], keep, precision=lax.Precision.HIGHEST)
-        for part, total in enumerate(totals[:-1]):
-            low, high = level_rows(part + 1)
-            dense[low:high] += times(total[...], keep[low:high], precision=lax.Precision.HIGHEST)
-        for e in range(slots):
-            rows_here = dense[e * SLOT : e * SLOT + fun_dev]
-            gram_refs[e][...] = skewed(moved(rows_here, reading - 1 - e * fun_dev), -1)[:, : 2 * reading]
+    wide, lanes = dense.shape
+    keep = jnp.where(
+        function_of((wide, lanes), 0, fun_dev) == lax.broadcasted_iota(jnp.int32, (wide, lanes), 1), volume, 0.0
+    )
+    dense[...] = times(totals[-1][...], keep, precision=lax.Precision.HIGHEST)
+    for part, total in enumerate(totals[:-1]):
+        low, high = level_rows(part + 1)
+        dense[low:high] += times(total[...], keep[low:high], precision=lax.Precision.HIGHEST)
+    for e in range(slots):
+        rows_here = dense[e * SLOT : e * SLOT + fun_dev]
+        gram_refs[e][...] = skewed(moved(rows_here, reading - 1 - e * fun_dev), -1)[:, : 2 * reading]
 
 
 def sum_kernel(reading, *refs):
@@ -379,37 +374,36 @@
     at_boxes = refs[2 * slots : 3 * slots]
     mixed = refs[3 * slots]
     mixings = refs[3 * slots + 1 :]
-    step, steps = pl.program_id(0), pl.num_programs(0)
+    steps = window_ref.shape[0] // STEP
     width = cut_ref[REACH + 1] - cut_ref[REACH]
-    @pl.when(step == 0)
-    def _():
-        for out, at_box in zip(outs, at_boxes):
-            out[...] = jnp.zeros_like(out)
-            at_box[...] = jnp.zeros_like(at_box)
-        lanes = band_lanes(fun_dev, reading)
-        parts = []
-        for e in range(slots):
-            band = bands[REACH - e][...].astype(jnp.float32)
-            band = jnp.concatenate([band, jnp.zeros((SLOT, lanes - 2 * reading), jnp.float32)], axis=1)
-            parts.append(moved(skewed(band, 1), e * fun_dev - (reading - 1)))
-        dense = jnp.concatenate(parts, axis=0).astype(jnp.bfloat16)
-        for part, mixing in enumerate(mixings):
-            low, high = level_rows(part + 1)
-            shape = (lanes, mixing.shape[1])
-            column = function_of(shape, 1, fun_dev)
-            column = jnp.where(column >= 0, column + low // SLOT * fun_dev, -1)
-            keep = one_hot(column == lax.broadcasted_iota(jnp.int32, shape, 0))
-            mixing[...] = times(dense[low:high], keep).astype(jnp.bfloat16)
-
-    @pl.when(step * STEP < width)
-    def _():
+    for out, at_box in zip(outs, at_boxes):
+        out[...] = jnp.zeros_like(out)
+        at_box[...] = jnp.zeros_like(at_box)
+    lanes = band_lanes(fun_dev, reading)
+    parts = []
+    for e in range(slots):
+        band = bands[REACH - e][...].astype(jnp.float32)
+        band = jnp.concatenate([band, jnp.zeros((SLOT, lanes - 2 * reading), jnp.float32)], axis=1)
+        parts.append(moved(skewed(band, 1), e * fun_dev - (reading - 1)))
+    dense = jnp.concatenate(parts, axis=0).astype(jnp.bfloat16)
+    for part, mixing in enumerate(mixings):
+        low, high = level_rows(part + 1)
+        shape = (lanes, mixing.shape[1])
+        column = function_of(shape, 1, fun_dev)
+        column = jnp.where(column >= 0, column + low // SLOT * fun_dev, -1)
+        keep = one_hot(column == lax.broadcasted_iota(jnp.int32, shape, 0))
+        mixing[...] = times(dense[low:high], keep).astype(jnp.bfloat16)
+
+    @pl.loop(0, lax.div(width + STEP - 1, STEP))
+    def _(step):
         level = active_ref[slots * steps + step]
         for part, mixing in enumerate(mixings):
             @pl.when(level == part + 1)
             def _():
                 low, high = level_rows(part + 1)
                 for b in range(STEP):
-                    mixed[b, low:high] = times(mixing[...], window_ref[b, low:high]).astype(jnp.bfloat16)
+                    here = window_ref[step * STEP + b, low:high]
+                    mixed[b, low:high] = times(mixing[...], here).astype(jnp.bfloat16)
         shape = (STEP * SLOT, at_boxes[0].shape[1])
         along = lax.broadcasted_iota(jnp.int32, shape, 0)
         box = lax.shift_right_logical(along, SLOT.bit_length() - 1) + step * STEP
@@ -418,31 +412,45 @@
         for e in range(slots):
             @pl.when(active_ref[e * steps + step] > 0)
             def _():
-                pick = one_hot(iota((outs[e].shape[0], STEP * SLOT), 0) == place_ref[e : e + 1, :])
+                place = place_ref[step, e : e + 1, :]
+                pick = one_hot(iota((outs[e].shape[0], STEP * SLOT), 0) == place)
                 part = mixed[:, e * SLOT : (e + 1) * SLOT, :].reshape(STEP * SLOT, mixed.shape[-1])
                 outs[e][...] += times(pick, part).astype(jnp.bfloat16)
                 at_boxes[e][...] += times(pick, boxes_of).astype(jnp.bfloat16)
 
 
-def home_kernel(groups, home_ref, *refs):
+def home_rows(bases, home_ref, sources, at, count):
+    shape = (count, home_ref.shape[1])
+    here = iota(shape, 1) == iota(shape, 0) + float(at)
+    row = jnp.sum(jnp.where(here, home_ref[...], 0.0), axis=1, keepdims=True)
+    value = None
+    for base, source in zip(bases, sources):
+        pick = one_hot(iota((count, source.shape[0]), 1) == row - float(base))
+        term = times(pick, source[...])
+        value = term if value is None else value + term
+    return value
+
+
+def early_kernel(bases, home_ref, *refs):
     sources, out_ref = refs[:-1], refs[-1]
-    count = out_ref.shape[0]
-    shape = (count, home_ref.shape[1])
-    at = iota(shape, 0) + (pl.program_id(0) * count).astype(jnp.float32)
-    row = jnp.sum(jnp.where(iota(shape, 1) == at, home_ref[...], 0.0), axis=1, keepdims=True)
-    value, base = None, 0
-    for group in groups:
-        parts = [sources[e][...] for e in group]
-        held = parts[0] if len(parts) == 1 else jnp.concatenate(parts, axis=0)
-        pick = one_hot(iota((count, held.shape[0]), 1) == row - float(base))
-        base += held.shape[0]
-        term = times(pick, held)
-        value = term if value is None else value + term
-    out_ref[...] = value.astype(jnp.bfloat16)
-
-
-def whole(shape):
-    return pl.BlockSpec(shape, lambda g: (0,) * len(shape))
+    count = 256
+    for at in range(0, out_ref.shape[0], count):
+        out_ref[at : at + count] = home_rows(bases, home_ref, sources, at, count).astype(jnp.bfloat16)
+
+
+def home_kernel(bases, home_ref, early_ref, *refs):
+    sources, out_ref, held, sems = refs[:-3], refs[-3], refs[-2], refs[-1]
+    copies = []
+    count = held.shape[1]
+    for part in range(held.shape[0]):
+        at = part * count
+        value = home_rows(bases, home_ref, sources, at, count) + early_ref[at : at + count].astype(jnp.float32)
+        held[part] = value.astype(jnp.bfloat16)
+        copy = pltpu.make_async_copy(held.at[part], out_ref.at[pl.ds(at, count)], sems.at[part])
+        copy.start()
+        copies.append(copy)
+    for copy in copies:
+        copy.wait()
 
 
 def on_device(coeffs, centers, kinetic, potential):
@@ -454,8 +462,8 @@
     reading = 4 * support
     slots = 2 * REACH + 1
     offsets = list(range(-REACH, REACH + 1))
-    far = [REACH, -REACH]
-    rest = [sign * k for k in range(1, REACH) for sign in (1, -1)]
+    first, last = REACH, -REACH
+    now = [first] + [sign * k for k in range(1, REACH) for sign in (1, -1)]
     one_way = list(range(REACH, 0, -1)) + list(range(-REACH, 0))
     rows, low_cut, high_cut, boxes, blocks = bounds(fun_dev, support)
     assert blocks <= REACH + 1 and support & (support - 1) == 0
@@ -468,42 +476,31 @@
     bf16, f32 = jnp.bfloat16, jnp.float32
     smem = pl.BlockSpec(memory_space=pltpu.SMEM)
     vmem = pl.BlockSpec(memory_space=pltpu.VMEM)
-    limit = pltpu.CompilerParams(vmem_limit_bytes=52 * 2**20)
+    limit = pltpu.CompilerParams(vmem_limit_bytes=26 * 2**20)
 
     sent_rows = {k: rounded_up(rows[k + REACH] + (2 * box_dev if k < 0 else 0), 16) for k in offsets if k}
-    *packed_far, near, cut, row_out, home_row, own_region = pl.pallas_call(
-        functools.partial(pack_kernel, (fun_dev, support, devices, halo, rows, back, low_cut, high_cut, far)),
-        out_shape=tuple(jax.ShapeDtypeStruct((sent_rows[k], points), bf16) for k in far)
+    *packed, near, cut, home_row, own_region = pl.pallas_call(
+        functools.partial(pack_kernel, (fun_dev, support, devices, halo, rows, back, low_cut, high_cut, now + [last])),
+        out_shape=tuple(jax.ShapeDtypeStruct((sent_rows[k], points), bf16) for k in now + [last])
         + (
             jax.ShapeDtypeStruct((count, 128), f32),
             jax.ShapeDtypeStruct((slots + 1,), jnp.int32),
-            jax.ShapeDtypeStruct((8, fun_dev * support), f32),
             jax.ShapeDtypeStruct((1, fun_dev * support), f32),
             jax.ShapeDtypeStruct((2 * half, points), bf16),
         ),
         in_specs=[smem] + [vmem] * 3,
-        out_specs=(vmem,) * 3 + (smem,) + (vmem,) * 3,
+        out_specs=(vmem,) * slots + (smem,) + (vmem,) * 2,
+        scratch_shapes=[pltpu.VMEM((8, fun_dev * support), f32)],
         compiler_params=limit,
-        name="pack_far",
+        name="pack",
     )(me, centers.reshape(1, -1), flat, potential)
-    arrived = sent(dict(zip(far, packed_far)), far, 1)
-    packed = dict(zip(rest, pl.pallas_call(
-        functools.partial(pack_rest_kernel, (rows, box_dev, rest)),
-        out_shape=tuple(jax.ShapeDtypeStruct((sent_rows[k], points), bf16) for k in rest),
-        in_specs=[vmem] * 3,
-        out_specs=(vmem,) * len(rest),
-        compiler_params=limit,
-        name="pack_rest",
-    )(row_out, flat, own_region)))
-    late, arrived = after(packed, rest[2:], arrived)
-    arrived.update(sent(packed, rest[:2], 1))
-    arrived.update(sent(late, rest[2:], 1))
+    arrived = all_sent(dict(zip(now + [last], packed)), now, last, 1)
 
     columns, places, active, local = pl.pallas_call(
         functools.partial(table_kernel, (fun_dev, support, halo, boxes)),
         out_shape=(
             jax.ShapeDtypeStruct((slots * SLOT, 128), f32),
-            jax.ShapeDtypeStruct((8, boxes * SLOT), f32),
+            jax.ShapeDtypeStruct((boxes // STEP, 8, STEP * SLOT), f32),
             jax.ShapeDtypeStruct(((slots + 1) * (boxes // STEP),), jnp.int32),
             jax.ShapeDtypeStruct((boxes, SLOT, points), bf16),
         ),
@@ -518,19 +515,16 @@
     read_rows = [rows_of[REACH - e] for e in range(slots)]
     level_sizes = [level_rows(part + 1)[1] - level_rows(part + 1)[0] for part in range(REACH)]
     exact_rows = [rows[2 * REACH - e] for e in range(slots)]
-    block = pl.BlockSpec((STEP, wide, points), lambda g: (g, 0, 0))
     band = (fun_dev, 2 * reading)
     pieces, region, *grams = pl.pallas_call(
         functools.partial(unpack_kernel, (fun_dev, box_dev, reading, volume, exact_rows, read_rows, blocks)),
-        grid=(boxes // STEP,),
         out_shape=(
             jax.ShapeDtypeStruct((boxes, wide, points), bf16),
             jax.ShapeDtypeStruct((128, points), bf16),
         )
         + tuple(jax.ShapeDtypeStruct(band, f32) for _ in range(slots)),
-        in_specs=[smem, smem, whole(columns.shape), whole(own_region.shape), pl.BlockSpec((STEP, SLOT, points), lambda g: (g, 0, 0))]
-        + [whole(s.shape) for s in sources],
-        out_specs=(block, whole((128, points))) + tuple(whole(band) for _ in range(slots)),
+        in_specs=[smem, smem] + [vmem] * (3 + len(sources)),
+        out_specs=(vmem,) * (2 + slots),
         scratch_shapes=[pltpu.VMEM((wide, band_lanes(fun_dev, reading)), f32)]
         + [pltpu.VMEM((size, size), f32) for size in level_sizes],
         compiler_params=limit,
@@ -554,11 +548,9 @@
     shapes = [(r, points) for r in out_rows] + [(r, 128) for r in out_rows]
     mixed = pl.pallas_call(
         functools.partial(mix_kernel, (fun_dev, reading, band_order)),
-        grid=(boxes // STEP,),
         out_shape=tuple(jax.ShapeDtypeStruct(shape, bf16) for shape in shapes),
-        in_specs=[smem, smem, pl.BlockSpec((8, STEP * SLOT), lambda g: (0, g)), block]
-        + [whole((SLOT, 2 * reading))] * slots,
-        out_specs=tuple(whole(shape) for shape in shapes),
+        in_specs=[smem, smem] + [vmem] * (2 + slots),
+        out_specs=(vmem,) * len(shapes),
         scratch_shapes=[pltpu.VMEM((STEP, wide, points), bf16)]
         + [pltpu.VMEM((size, size), bf16) for size in level_sizes],
         compiler_params=limit,
@@ -566,34 +558,36 @@
     )(cut, active, places, pieces, *[mixing_of[k] for k in band_order])
 
     ready = {}
-    for k in far + rest + [0]:
+    for k in now + [last, 0]:
         here, at_box = mixed[REACH - k], mixed[slots + REACH - k]
         near_by = jnp.dot(at_box, region, preferred_element_type=f32)
         applied = jnp.dot(here, kinetic, preferred_element_type=f32)
         ready[k] = (applied + near_by * here.astype(f32)).astype(bf16)
-    returned = sent(ready, far, -1)
-    late, returned = after(ready, rest[2:], returned)
-    returned.update(sent(ready, rest[:2], -1))
-    returned.update(sent(late, rest[2:], -1))
+    returned = all_sent(ready, now, last, -1)
     returned[0] = ready[0]
 
-    groups, held = [], 257
-    for e, k in enumerate(offsets):
-        if held + rows_of[k] <= 256:
-            groups[-1].append(e)
-            held += rows_of[k]
-        else:
-            groups.append([e])
-            held = rows_of[k]
+    bases = {k: sum(back[: k + REACH]) for k in offsets}
+    early, late = [0, first], now[1:] + [last]
+    begun = pl.pallas_call(
+        functools.partial(early_kernel, [bases[k] for k in early]),
+        out_shape=jax.ShapeDtypeStruct(flat.shape, bf16),
+        in_specs=[vmem] * (1 + len(early)),
+        out_specs=vmem,
+        compiler_params=limit,
+        name="early",
+    )(home_row, *[returned[k] for k in early])
     filtered = pl.pallas_call(
-        functools.partial(home_kernel, groups),
-        grid=(fun_dev * support // 256,),
-        out_shape=jax.ShapeDtypeStruct((fun_dev * support, points), bf16),
-        in_specs=[whole(home_row.shape)] + [whole((rows_of[k], points)) for k in offsets],
-        out_specs=pl.BlockSpec((256, points), lambda g: (g, 0)),
+        functools.partial(home_kernel, [bases[k] for k in late]),
+        out_shape=jax.ShapeDtypeStruct(flat.shape, bf16),
+        in_specs=[vmem] * (2 + len(late)),
+        out_specs=pl.BlockSpec(memory_space=pl.ANY),
+        scratch_shapes=[
+            pltpu.VMEM((flat.shape[0] // 256, 256, points), bf16),
+            pltpu.SemaphoreType.DMA((flat.shape[0] // 256,)),
+        ],
         compiler_params=limit,
         name="home",
-    )(home_row, *[returned[k] for k in offsets])
+    )(home_row, begun, *[returned[k] for k in late])
     return (filtered.reshape(coeffs.shape), gram_band)
 
 

time: 134 us -> 121 us (0.903)
  Pallas kernels: 33.5 us -> 26.1 us
  waiting for transfers between devices: 42 us -> 38.1 us
    ppermute x24, waiting for transfers between devices: 42 us -> 38.1 us  [passed_along(): return lax.ppermute(value, AXES, pairs)]
    pallas_call x2, Pallas kernels: 8.48 us -> 4.8 us  [the longest x1 3.31 us: on_device(): pl.pallas_call(functools.partial(home_kernel, [bases[k] for k in late]),...]
    pallas_call x1, Pallas kernels: 8.56 us -> 6.89 us  [on_device(): pl.pallas_call(functools.partial(mix_kernel, (fun_dev, reading, band_orde...]
    unnamed x14 -> x8, local copies, waits for them, and re-layouts: 3.2 us -> 2.26 us
  transfers between devices with their start and end apart: 24 -> 24, of which waited for: 9 -> 7; matrix products, arithmetic and copies ran while one was open for 5% -> 4% of each run, Pallas kernels for 3% -> 4%
where the time goes in v2:
time: 121 us; the launch traced here: 120 us
  starting transfers between devices  44.8 us (37%)
  waiting for transfers between devices  38.1 us (31%)
  Pallas kernels  26.1 us (22%)
  matrix products  6.51 us (5%)
  local copies, waits for them, and re-layouts  3.1 us (3%)
    ppermute x24, starting transfers between devices, passed_along(): return lax.ppermute(value, AXES, pairs)  44.8 us
    ppermute x24, waiting for transfers between devices, passed_along(): return lax.ppermute(value, AXES, pairs)  38.1 us
    pallas_call x1, Pallas kernels, on_device(): pl.pallas_call(functools.partial(unpack_kernel, (fun_dev, box_dev, readin...  7.74 us
    pallas_call x1, Pallas kernels, on_device(): pl.pallas_call(functools.partial(mix_kernel, (fun_dev, reading, band_orde...  6.89 us
    dot_general x7, matrix products, on_device(): applied = jnp.dot(here, kinetic, preferred_element_type=f32)  4.73 us
    pallas_call x1, Pallas kernels, on_device(): pl.pallas_call(functools.partial(home_kernel, [bases[k] for k in late]),...  3.31 us
    pallas_call x1, Pallas kernels, on_device(): pl.pallas_call(functools.partial(pack_kernel, (fun_dev, support, devices,...  3.22 us
    pallas_call x1, Pallas kernels, on_device(): pl.pallas_call(functools.partial(table_kernel, (fun_dev, support, halo, b...  2.79 us
  transfers between devices with their start and end apart: 24, of which 7 were waited for; matrix products, arithmetic and copies ran while one was open for 4% of the time, Pallas kernels for 4%

profile of v2, /device:TPU:1, one launch (start us, length us, event | category | flops | bytes accessed | tf_op | source)
XLA Modules:
  0.0 119.6 jit_solution(15867043866337314854)
XLA Ops:
  1.5 1.4 %copy-done.1 = bf16[24,32,1024]{2,1,0:T(8,128)(2,1)S(1)} copy-done((bf16[24,32,1024]{2,1,0:T(8,128)(2,1)S(1)}, bf16[24,32,1024]{2,1,0:T(8,128)(2,1)}, u32[]{:S(2)}) %copy-start.1) | copy-done | bytes 1572888
  3.7 3.2 %pack.1 = (bf16[48,1024]{1,0:T(8,128)(2,1)S(1)}, bf16[240,1024]{1,0:T(8,128)(2,1)S(1)}, bf16[272,1024]{1,0:T(8,128)(2,1)S(1)}, bf16[160,1024]{1,0:T(8,128)(2,1)S...) custom-call(s32[1]{0:T(128)} %bitcast.me_ref, ...), custom_call_target="tpu_custom_call" | custom-call | tf_op jit(solution)/shard_map/pack/pallas_call | solution.py:482
  7.1 2.6 %collective-permute-start.2 = (bf16[240,1024]{1,0:T(8,128)(2,1)S(1)}, bf16[240,1024]{1,0:T(8,128)(2,1)S(1)}, u32[]{:S(2)}, u32[]{:S(2)}) collective-permute-start(bf16[240,1024]{1,0:T(8,128)(2,1)S(1)} %get-tuple-element.57), channel_id=1, source_target_pairs={{0,1},{1,2},{2,3},{3,4},{4,5},{5,6},{6,7},{7,8},{8,9},{9,10},{10,1... | collective-permute-start | bytes 1474568 | tf_op jit(solution)/shard_map/ppermute | solution.py:21
  9.7 8.7 %collective-permute-start.4 = (bf16[192,1024]{1,0:T(8,128)(2,1)S(1)}, bf16[192,1024]{1,0:T(8,128)(2,1)S(1)}, u32[]{:S(2)}, u32[]{:S(2)}) collective-permute-start(bf16[192,1024]{1,0:T(8,128)(2,1)S(1)} %get-tuple-element.59), channel_id=1, source_target_pairs={{0,30},{1,31},{2,0},{3,1},{4,2},{5,3},{6,4},{7,5},{8,6},{9,7},{10,... | collective-permute-start | bytes 1179656 | tf_op jit(solution)/shard_map/ppermute | solution.py:21
  18.4 12.9 %collective-permute-done.refs_0_ = bf16[48,1024]{1,0:T(8,128)(2,1)S(1)} collective-permute-done((bf16[48,1024]{1,0:T(8,128)(2,1)S(1)}, bf16[48,1024]{1,0:T(8,128)(2,1)S(1)}, u32[]{:S(2)}, u32[]{:S(2)}) %collective-permute-start) | collective-permute-done | bytes 98336 | tf_op jit(solution)/shard_map/ppermute | solution.py:21
  31.3 4.4 %collective-permute-start.5 = (bf16[64,1024]{1,0:T(8,128)(2,1)S(1)}, bf16[64,1024]{1,0:T(8,128)(2,1)S(1)}, u32[]{:S(2)}, u32[]{:S(2)}) collective-permute-start(bf16[64,1024]{1,0:T(8,128)(2,1)S(1)} %get-tuple-element.60), channel_id=1, source_target_pairs={{0,29},{1,30},{2,31},{3,0},{4,1},{5,2},{6,3},{7,4},{8,5},{9,6},{10... | collective-permute-start | bytes 393224 | tf_op jit(solution)/shard_map/ppermute | solution.py:21
  35.8 2.8 %tables.1 = (f32[224,128]{1,0:T(8,128)S(1)}, f32[3,8,256]{2,1,0:T(8,128)S(1)}, s32[24]{0:T(128)S(1)}, bf16[24,32,1024]{2,1,0:T(8,128)(2,1)S(1)}) custom-call(s32[8]{0:T(128)S(1)} %get-tuple-element.46.cut_ref, f32[512,128]{1,0:T(8,128)S(1)} %get-tuple-element.47.near_ref, bf16[768,1024]{1,0:T(8,128)(2,1)S(1)} %bitcast.32), custom_call_target="tpu_custom_call" | custom-call | tf_op jit(solution)/shard_map/tables/pallas_call | solution.py:499
  38.6 3.4 %collective-permute-done.5.refs_5_ = bf16[64,1024]{1,0:T(8,128)(2,1)S(1)} collective-permute-done((bf16[64,1024]{1,0:T(8,128)(2,1)S(1)}, bf16[64,1024]{1,0:T(8,128)(2,1)S(1)}, u32[]{:S(2)}, u32[]{:S(2)}) %collective-permute-start.5) | collective-permute-done | bytes 131104 | tf_op jit(solution)/shard_map/ppermute | solution.py:21
  42.0 7.7 %unpack.1 = (bf16[24,224,1024]{2,1,0:T(8,128)(2,1)S(1)}, bf16[128,1024]{1,0:T(8,128)(2,1)S(1)}, f32[24,256]{1,0:T(8,128)S(1)}, f32[24,256]{1,0:T(8,128)S(1)}, f3...) custom-call(s32[8]{0:T(128)S(1)} %get-tuple-element.46.cut_ref, ...), custom_call_target="tpu_custom_call" | custom-call | tf_op jit(solution)/shard_map/unpack/pallas_call | solution.py:519
  50.6 4.9 %collective-permute-start.8 = (f32[24,256]{1,0:T(8,128)S(1)}, f32[24,256]{1,0:T(8,128)S(1)}, u32[]{:S(2)}, u32[]{:S(2)}) collective-permute-start(f32[24,256]{1,0:T(8,128)S(1)} %get-tuple-element.65), channel_id=1, source_target_pairs={{0,1},{1,2},{2,3},{3,4},{4,5},{5,6},{6,7},{7,8},{8,9},{9,10},{10,1... | collective-permute-start | bytes 73736 | tf_op jit(solution)/shard_map/ppermute | solution.py:21
  55.5 3.1 %collective-permute-start.9 = (f32[24,256]{1,0:T(8,128)S(1)}, f32[24,256]{1,0:T(8,128)S(1)}, u32[]{:S(2)}, u32[]{:S(2)}) collective-permute-start(f32[24,256]{1,0:T(8,128)S(1)} %get-tuple-element.66), channel_id=1, source_target_pairs={{0,29},{1,30},{2,31},{3,0},{4,1},{5,2},{6,3},{7,4},{8,5},{9,6},{10... | collective-permute-start | bytes 73736 | tf_op jit(solution)/shard_map/ppermute | solution.py:21
  60.0 1.7 %collective-permute-start.11 = (f32[24,256]{1,0:T(8,128)S(1)}, f32[24,256]{1,0:T(8,128)S(1)}, u32[]{:S(2)}, u32[]{:S(2)}) collective-permute-start(f32[24,256]{1,0:T(8,128)S(1)} %get-tuple-element.68), channel_id=1, source_target_pairs={{0,31},{1,0},{2,1},{3,2},{4,3},{5,4},{6,5},{7,6},{8,7},{9,8},{10,9... | collective-permute-start | bytes 73736 | tf_op jit(solution)/shard_map/ppermute | solution.py:21
  61.7 1.5 %collective-permute-done.11.refs_6_ = f32[24,256]{1,0:T(8,128)S(1)} collective-permute-done((f32[24,256]{1,0:T(8,128)S(1)}, f32[24,256]{1,0:T(8,128)S(1)}, u32[]{:S(2)}, u32[]{:S(2)}) %collective-permute-start.11) | collective-permute-done | bytes 24608 | tf_op jit(solution)/shard_map/ppermute | solution.py:21
  65.0 5.0 %collective-permute-start.16 = (bf16[32,256]{1,0:T(8,128)(2,1)S(1)}, bf16[32,256]{1,0:T(8,128)(2,1)S(1)}, u32[]{:S(2)}, u32[]{:S(2)}) collective-permute-start(bf16[32,256]{1,0:T(8,128)(2,1)S(1)} %get-tuple-element.69.refs_6_), channel_id=1, source_target_pairs={{0,30},{1,31},{2,0},{3,1},{4,2},{5,3},{6,4},{7,5},{8,6},{9,7},{10,... | collective-permute-start | bytes 49160 | tf_op jit(solution)/shard_map/ppermute | solution.py:21
  70.0 2.0 %collective-permute-start.14 = (bf16[32,256]{1,0:T(8,128)(2,1)S(1)}, bf16[32,256]{1,0:T(8,128)(2,1)S(1)}, u32[]{:S(2)}, u32[]{:S(2)}) collective-permute-start(bf16[32,256]{1,0:T(8,128)(2,1)S(1)} %get-tuple-element.69.refs_6_), channel_id=1, source_target_pairs={{0,1},{1,2},{2,3},{3,4},{4,5},{5,6},{6,7},{7,8},{8,9},{9,10},{10,1... | collective-permute-start | bytes 49160 | tf_op jit(solution)/shard_map/ppermute | solution.py:21
  73.6 4.6 %collective-permute-done.13.refs_1_ = bf16[32,256]{1,0:T(8,128)(2,1)S(1)} collective-permute-done((bf16[32,256]{1,0:T(8,128)(2,1)S(1)}, bf16[32,256]{1,0:T(8,128)(2,1)S(1)}, u32[]{:S(2)}, u32[]{:S(2)}) %collective-permute-start.13) | collective-permute-done | bytes 16416 | tf_op jit(solution)/shard_map/ppermute | solution.py:21
  78.2 1.5 %collective-permute-done.12.refs_0_ = bf16[32,256]{1,0:T(8,128)(2,1)S(1)} collective-permute-done((bf16[32,256]{1,0:T(8,128)(2,1)S(1)}, bf16[32,256]{1,0:T(8,128)(2,1)S(1)}, u32[]{:S(2)}, u32[]{:S(2)}) %collective-permute-start.12) | collective-permute-done | bytes 16416 | tf_op jit(solution)/shard_map/ppermute | solution.py:21
  79.7 6.9 %mix.1 = (bf16[48,1024]{1,0:T(8,128)(2,1)S(1)}, bf16[160,1024]{1,0:T(8,128)(2,1)S(1)}, bf16[240,1024]{1,0:T(8,128)(2,1)S(1)}, bf16[512,1024]{1,0:T(8,128)(2,1)S(...) custom-call(s32[8]{0:T(128)S(1)} %get-tuple-element.46.cut_ref, ...), custom_call_target="tpu_custom_call" | custom-call | tf_op jit(solution)/shard_map/mix/pallas_call | solution.py:549
  89.8 4.9 %collective-permute-start.21 = (bf16[160,1024]{1,0:T(8,128)(2,1)S(1)}, bf16[160,1024]{1,0:T(8,128)(2,1)S(1)}, u32[]{:S(2)}, u32[]{:S(2)}) collective-permute-start(bf16[160,1024]{1,0:T(8,128)(2,1)S(1)} %fusion.2), channel_id=1, source_target_pairs={{0,30},{1,31},{2,0},{3,1},{4,2},{5,3},{6,4},{7,5},{8,6},{9,7},{10,... | collective-permute-start | bytes 983048 | tf_op jit(solution)/shard_map/ppermute | solution.py:21
  96.8 1.8 %collective-permute-start.20 = (bf16[256,1024]{1,0:T(8,128)(2,1)S(1)}, bf16[256,1024]{1,0:T(8,128)(2,1)S(1)}, u32[]{:S(2)}, u32[]{:S(2)}) collective-permute-start(bf16[256,1024]{1,0:T(8,128)(2,1)S(1)} %fusion), channel_id=1, source_target_pairs={{0,1},{1,2},{2,3},{3,4},{4,5},{5,6},{6,7},{7,8},{8,9},{9,10},{10,1... | collective-permute-start | bytes 1572872 | tf_op jit(solution)/shard_map/ppermute | solution.py:21
  100.6 1.5 %early.1.early_ref = bf16[768,1024]{1,0:T(8,128)(2,1)S(1)} custom-call(f32[1,768]{1,0:T(1,128)S(1)} %get-tuple-element.45.home_ref, bf16[512,1024]{1,0:T(8,128)(2,1)S(1)} %add_convert_fusion.refs_0_, bf16[48,1024]{1,0:T(8,128)(2,1)S(1)} %collective-permute-done.18.refs_1_), custom_call_target="tpu_custom_call" | custom-call | tf_op jit(solution)/shard_map/early/pallas_call | solution.py:571
  102.1 7.0 %collective-permute-done.23.refs_4_ = bf16[48,1024]{1,0:T(8,128)(2,1)S(1)} collective-permute-done((bf16[48,1024]{1,0:T(8,128)(2,1)S(1)}, bf16[48,1024]{1,0:T(8,128)(2,1)S(1)}, u32[]{:S(2)}, u32[]{:S(2)}) %collective-permute-start.23) | collective-permute-done | bytes 98336 | tf_op jit(solution)/shard_map/ppermute | solution.py:21
  109.1 7.0 %collective-permute-done.19.refs_0_ = bf16[240,1024]{1,0:T(8,128)(2,1)S(1)} collective-permute-done((bf16[240,1024]{1,0:T(8,128)(2,1)S(1)}, bf16[240,1024]{1,0:T(8,128)(2,1)S(1)}, u32[]{:S(2)}, u32[]{:S(2)}) %collective-permute-start.19) | collective-permute-done | bytes 491552 | tf_op jit(solution)/shard_map/ppermute | solution.py:21
  116.1 3.3 %home.1 = bf16[768,1024]{1,0:T(8,128)(2,1)} custom-call(f32[1,768]{1,0:T(1,128)S(1)} %get-tuple-element.45.home_ref, bf16[768,1024]{1,0:T(8,128)(2,1)S(1)} %early.1.early_ref, bf16[240,1024]{1,0:T(8,128)(2,1)S(1)} %collective-permute-done.19.refs_0_, bf16[256,1024]{1,0:T(8,128)(2,1)S(1)} %collective-permute-done.20.refs_1_, ...), custom_call_target="tpu_custom_call" | custom-call | tf_op jit(solution)/shard_map/home/pallas_call | solution.py:579
  (54 shorter events, 14.6 us)
Async XLA Ops:
  7.0 35.0 %collective-permute-start.3 = (bf16[272,1024]{1,0:T(8,128)(2,1)S(1)}, bf16[272,1024]{1,0:T(8,128)(2,1)S(1)}, u32[]{:S(2)}, u32[]{:S(2)}) collective-permute-start(bf16[272,1024]{1,0:T(8,128)(2,1)S(1)} %get-tuple-element.58), channel_id=1, source_target_pairs={{0,31},{1,0},{2,1},{3,2},{4,3},{5,4},{6,5},{7,6},{8,7},{9,8},{10,9... | collective-permute-start | bytes 1671176 | tf_op jit(solution)/shard_map/ppermute | solution.py:21
  7.1 34.9 %collective-permute-start.2 = (bf16[240,1024]{1,0:T(8,128)(2,1)S(1)}, bf16[240,1024]{1,0:T(8,128)(2,1)S(1)}, u32[]{:S(2)}, u32[]{:S(2)}) collective-permute-start(bf16[240,1024]{1,0:T(8,128)(2,1)S(1)} %get-tuple-element.57), channel_id=1, source_target_pairs={{0,1},{1,2},{2,3},{3,4},{4,5},{5,6},{6,7},{7,8},{8,9},{9,10},{10,1... | collective-permute-start | bytes 1474568 | tf_op jit(solution)/shard_map/ppermute | solution.py:21
  9.7 32.3 %collective-permute-start.4 = (bf16[192,1024]{1,0:T(8,128)(2,1)S(1)}, bf16[192,1024]{1,0:T(8,128)(2,1)S(1)}, u32[]{:S(2)}, u32[]{:S(2)}) collective-permute-start(bf16[192,1024]{1,0:T(8,128)(2,1)S(1)} %get-tuple-element.59), channel_id=1, source_target_pairs={{0,30},{1,31},{2,0},{3,1},{4,2},{5,3},{6,4},{7,5},{8,6},{9,7},{10,... | collective-permute-start | bytes 1179656 | tf_op jit(solution)/shard_map/ppermute | solution.py:21
  18.4 23.6 %collective-permute-start.1 = (bf16[160,1024]{1,0:T(8,128)(2,1)S(1)}, bf16[160,1024]{1,0:T(8,128)(2,1)S(1)}, u32[]{:S(2)}, u32[]{:S(2)}) collective-permute-start(bf16[160,1024]{1,0:T(8,128)(2,1)S(1)} %get-tuple-element.56), channel_id=1, source_target_pairs={{0,2},{1,3},{2,4},{3,5},{4,6},{5,7},{6,8},{7,9},{8,10},{9,11},{10,... | collective-permute-start | bytes 983048 | tf_op jit(solution)/shard_map/ppermute | solution.py:21
  18.4 12.9 %collective-permute-start = (bf16[48,1024]{1,0:T(8,128)(2,1)S(1)}, bf16[48,1024]{1,0:T(8,128)(2,1)S(1)}, u32[]{:S(2)}, u32[]{:S(2)}) collective-permute-start(bf16[48,1024]{1,0:T(8,128)(2,1)S(1)} %get-tuple-element.54), channel_id=1, source_target_pairs={{0,3},{1,4},{2,5},{3,6},{4,7},{5,8},{6,9},{7,10},{8,11},{9,12},{10... | collective-permute-start | bytes 294920 | tf_op jit(solution)/shard_map/ppermute | solution.py:21
  31.3 10.7 %collective-permute-start.5 = (bf16[64,1024]{1,0:T(8,128)(2,1)S(1)}, bf16[64,1024]{1,0:T(8,128)(2,1)S(1)}, u32[]{:S(2)}, u32[]{:S(2)}) collective-permute-start(bf16[64,1024]{1,0:T(8,128)(2,1)S(1)} %get-tuple-element.60), channel_id=1, source_target_pairs={{0,29},{1,30},{2,31},{3,0},{4,1},{5,2},{6,3},{7,4},{8,5},{9,6},{10... | collective-permute-start | bytes 393224 | tf_op jit(solution)/shard_map/ppermute | solution.py:21
  49.8 10.2 %collective-permute-start.6 = (f32[24,256]{1,0:T(8,128)S(1)}, f32[24,256]{1,0:T(8,128)S(1)}, u32[]{:S(2)}, u32[]{:S(2)}) collective-permute-start(f32[24,256]{1,0:T(8,128)S(1)} %get-tuple-element.63), channel_id=1, source_target_pairs={{0,3},{1,4},{2,5},{3,6},{4,7},{5,8},{6,9},{7,10},{8,11},{9,12},{10... | collective-permute-start | bytes 73736 | tf_op jit(solution)/shard_map/ppermute | solution.py:21
  50.2 11.5 %collective-permute-start.7 = (f32[24,256]{1,0:T(8,128)S(1)}, f32[24,256]{1,0:T(8,128)S(1)}, u32[]{:S(2)}, u32[]{:S(2)}) collective-permute-start(f32[24,256]{1,0:T(8,128)S(1)} %get-tuple-element.64), channel_id=1, source_target_pairs={{0,2},{1,3},{2,4},{3,5},{4,6},{5,7},{6,8},{7,9},{8,10},{9,11},{10,... | collective-permute-start | bytes 73736 | tf_op jit(solution)/shard_map/ppermute | solution.py:21
  50.6 11.1 %collective-permute-start.8 = (f32[24,256]{1,0:T(8,128)S(1)}, f32[24,256]{1,0:T(8,128)S(1)}, u32[]{:S(2)}, u32[]{:S(2)}) collective-permute-start(f32[24,256]{1,0:T(8,128)S(1)} %get-tuple-element.65), channel_id=1, source_target_pairs={{0,1},{1,2},{2,3},{3,4},{4,5},{5,6},{6,7},{7,8},{8,9},{9,10},{10,1... | collective-permute-start | bytes 73736 | tf_op jit(solution)/shard_map/ppermute | solution.py:21
  55.5 6.3 %collective-permute-start.9 = (f32[24,256]{1,0:T(8,128)S(1)}, f32[24,256]{1,0:T(8,128)S(1)}, u32[]{:S(2)}, u32[]{:S(2)}) collective-permute-start(f32[24,256]{1,0:T(8,128)S(1)} %get-tuple-element.66), channel_id=1, source_target_pairs={{0,29},{1,30},{2,31},{3,0},{4,1},{5,2},{6,3},{7,4},{8,5},{9,6},{10... | collective-permute-start | bytes 73736 | tf_op jit(solution)/shard_map/ppermute | solution.py:21
  58.6 3.1 %collective-permute-start.10 = (f32[24,256]{1,0:T(8,128)S(1)}, f32[24,256]{1,0:T(8,128)S(1)}, u32[]{:S(2)}, u32[]{:S(2)}) collective-permute-start(f32[24,256]{1,0:T(8,128)S(1)} %get-tuple-element.67), channel_id=1, source_target_pairs={{0,30},{1,31},{2,0},{3,1},{4,2},{5,3},{6,4},{7,5},{8,6},{9,7},{10,... | collective-permute-start | bytes 73736 | tf_op jit(solution)/shard_map/ppermute | solution.py:21
  60.0 3.3 %collective-permute-start.11 = (f32[24,256]{1,0:T(8,128)S(1)}, f32[24,256]{1,0:T(8,128)S(1)}, u32[]{:S(2)}, u32[]{:S(2)}) collective-permute-start(f32[24,256]{1,0:T(8,128)S(1)} %get-tuple-element.68), channel_id=1, source_target_pairs={{0,31},{1,0},{2,1},{3,2},{4,3},{5,4},{6,5},{7,6},{8,7},{9,8},{10,9... | collective-permute-start | bytes 73736 | tf_op jit(solution)/shard_map/ppermute | solution.py:21
  63.9 9.0 %collective-permute-start.17 = (bf16[32,256]{1,0:T(8,128)(2,1)S(1)}, bf16[32,256]{1,0:T(8,128)(2,1)S(1)}, u32[]{:S(2)}, u32[]{:S(2)}) collective-permute-start(bf16[32,256]{1,0:T(8,128)(2,1)S(1)} %get-tuple-element.69.refs_6_), channel_id=1, source_target_pairs={{0,31},{1,0},{2,1},{3,2},{4,3},{5,4},{6,5},{7,6},{8,7},{9,8},{10,9... | collective-permute-start | bytes 49160 | tf_op jit(solution)/shard_map/ppermute | solution.py:21
  65.0 8.5 %collective-permute-start.16 = (bf16[32,256]{1,0:T(8,128)(2,1)S(1)}, bf16[32,256]{1,0:T(8,128)(2,1)S(1)}, u32[]{:S(2)}, u32[]{:S(2)}) collective-permute-start(bf16[32,256]{1,0:T(8,128)(2,1)S(1)} %get-tuple-element.69.refs_6_), channel_id=1, source_target_pairs={{0,30},{1,31},{2,0},{3,1},{4,2},{5,3},{6,4},{7,5},{8,6},{9,7},{10,... | collective-permute-start | bytes 49160 | tf_op jit(solution)/shard_map/ppermute | solution.py:21
  70.0 3.6 %collective-permute-start.15 = (bf16[32,256]{1,0:T(8,128)(2,1)S(1)}, bf16[32,256]{1,0:T(8,128)(2,1)S(1)}, u32[]{:S(2)}, u32[]{:S(2)}) collective-permute-start(bf16[32,256]{1,0:T(8,128)(2,1)S(1)} %get-tuple-element.69.refs_6_), channel_id=1, source_target_pairs={{0,29},{1,30},{2,31},{3,0},{4,1},{5,2},{6,3},{7,4},{8,5},{9,6},{10... | collective-permute-start | bytes 49160 | tf_op jit(solution)/shard_map/ppermute | solution.py:21
  70.0 3.6 %collective-permute-start.14 = (bf16[32,256]{1,0:T(8,128)(2,1)S(1)}, bf16[32,256]{1,0:T(8,128)(2,1)S(1)}, u32[]{:S(2)}, u32[]{:S(2)}) collective-permute-start(bf16[32,256]{1,0:T(8,128)(2,1)S(1)} %get-tuple-element.69.refs_6_), channel_id=1, source_target_pairs={{0,1},{1,2},{2,3},{3,4},{4,5},{5,6},{6,7},{7,8},{8,9},{9,10},{10,1... | collective-permute-start | bytes 49160 | tf_op jit(solution)/shard_map/ppermute | solution.py:21
  72.0 6.2 %collective-permute-start.13 = (bf16[32,256]{1,0:T(8,128)(2,1)S(1)}, bf16[32,256]{1,0:T(8,128)(2,1)S(1)}, u32[]{:S(2)}, u32[]{:S(2)}) collective-permute-start(bf16[32,256]{1,0:T(8,128)(2,1)S(1)} %get-tuple-element.69.refs_6_), channel_id=1, source_target_pairs={{0,2},{1,3},{2,4},{3,5},{4,6},{5,7},{6,8},{7,9},{8,10},{9,11},{10,... | collective-permute-start | bytes 49160 | tf_op jit(solution)/shard_map/ppermute | solution.py:21
  72.9 6.8 %collective-permute-start.12 = (bf16[32,256]{1,0:T(8,128)(2,1)S(1)}, bf16[32,256]{1,0:T(8,128)(2,1)S(1)}, u32[]{:S(2)}, u32[]{:S(2)}) collective-permute-start(bf16[32,256]{1,0:T(8,128)(2,1)S(1)} %get-tuple-element.69.refs_6_), channel_id=1, source_target_pairs={{0,3},{1,4},{2,5},{3,6},{4,7},{5,8},{6,9},{7,10},{8,11},{9,12},{10... | collective-permute-start | bytes 49160 | tf_op jit(solution)/shard_map/ppermute | solution.py:21
  87.9 11.1 %collective-permute-start.18 = (bf16[48,1024]{1,0:T(8,128)(2,1)S(1)}, bf16[48,1024]{1,0:T(8,128)(2,1)S(1)}, u32[]{:S(2)}, u32[]{:S(2)}) collective-permute-start(bf16[48,1024]{1,0:T(8,128)(2,1)S(1)} %fusion.5), channel_id=1, source_target_pairs={{0,29},{1,30},{2,31},{3,0},{4,1},{5,2},{6,3},{7,4},{8,5},{9,6},{10... | collective-permute-start | bytes 294920 | tf_op jit(solution)/shard_map/ppermute | solution.py:21
  88.8 20.3 %collective-permute-start.22 = (bf16[160,1024]{1,0:T(8,128)(2,1)S(1)}, bf16[160,1024]{1,0:T(8,128)(2,1)S(1)}, u32[]{:S(2)}, u32[]{:S(2)}) collective-permute-start(bf16[160,1024]{1,0:T(8,128)(2,1)S(1)} %fusion.3), channel_id=1, source_target_pairs={{0,2},{1,3},{2,4},{3,5},{4,6},{5,7},{6,8},{7,9},{8,10},{9,11},{10,... | collective-permute-start | bytes 983048 | tf_op jit(solution)/shard_map/ppermute | solution.py:21
  89.8 19.3 %collective-permute-start.21 = (bf16[160,1024]{1,0:T(8,128)(2,1)S(1)}, bf16[160,1024]{1,0:T(8,128)(2,1)S(1)}, u32[]{:S(2)}, u32[]{:S(2)}) collective-permute-start(bf16[160,1024]{1,0:T(8,128)(2,1)S(1)} %fusion.2), channel_id=1, source_target_pairs={{0,30},{1,31},{2,0},{3,1},{4,2},{5,3},{6,4},{7,5},{8,6},{9,7},{10,... | collective-permute-start | bytes 983048 | tf_op jit(solution)/shard_map/ppermute | solution.py:21
  95.7 20.4 %collective-permute-start.19 = (bf16[240,1024]{1,0:T(8,128)(2,1)S(1)}, bf16[240,1024]{1,0:T(8,128)(2,1)S(1)}, u32[]{:S(2)}, u32[]{:S(2)}) collective-permute-start(bf16[240,1024]{1,0:T(8,128)(2,1)S(1)} %fusion.1), channel_id=1, source_target_pairs={{0,31},{1,0},{2,1},{3,2},{4,3},{5,4},{6,5},{7,6},{8,7},{9,8},{10,9... | collective-permute-start | bytes 1474568 | tf_op jit(solution)/shard_map/ppermute | solution.py:21
  96.8 19.4 %collective-permute-start.20 = (bf16[256,1024]{1,0:T(8,128)(2,1)S(1)}, bf16[256,1024]{1,0:T(8,128)(2,1)S(1)}, u32[]{:S(2)}, u32[]{:S(2)}) collective-permute-start(bf16[256,1024]{1,0:T(8,128)(2,1)S(1)} %fusion), channel_id=1, source_target_pairs={{0,1},{1,2},{2,3},{3,4},{4,5},{5,6},{6,7},{7,8},{8,9},{9,10},{10,1... | collective-permute-start | bytes 1572872 | tf_op jit(solution)/shard_map/ppermute | solution.py:21
  99.0 10.1 %collective-permute-start.23 = (bf16[48,1024]{1,0:T(8,128)(2,1)S(1)}, bf16[48,1024]{1,0:T(8,128)(2,1)S(1)}, u32[]{:S(2)}, u32[]{:S(2)}) collective-permute-start(bf16[48,1024]{1,0:T(8,128)(2,1)S(1)} %fusion.4), channel_id=1, source_target_pairs={{0,3},{1,4},{2,5},{3,6},{4,7},{5,8},{6,9},{7,10},{8,11},{9,12},{10... | collective-permute-start | bytes 294920 | tf_op jit(solution)/shard_map/ppermute | solution.py:21
  (4 other events, 120.4 us)

commit v3 on v2

--- a/solution.py
+++ b/solution.py
@@ -102,10 +102,16 @@
     )
 
 
-def pack_kernel(plan, me_ref, centers_ref, flat_ref, potential_ref, *refs):
+def pack_kernel(plan, me_ref, centers_ref, flat_hbm, potential_hbm, *refs):
     fun_dev, support, devices, halo, rows, back, low_cut, high_cut, now = plan
     outs = dict(zip(now, refs[: len(now)]))
-    near_ref, cut_ref, home_ref, own_ref, row_ref = refs[len(now) :]
+    near_ref, cut_ref, home_ref, own_ref, row_ref, flat_ref, potential_ref, sems = refs[len(now) :]
+    copies = [
+        pltpu.make_async_copy(flat_hbm, flat_ref, sems.at[0]),
+        pltpu.make_async_copy(potential_hbm, potential_ref, sems.at[1]),
+    ]
+    for copy in copies:
+        copy.start()
     me = me_ref[0]
     box_dev = fun_dev // 2
     fun_all, box_all = fun_dev * devices, box_dev * devices
@@ -116,7 +122,7 @@
     at = start + iota((count, 1), 0)
     at = jnp.where(at >= fun_all, at - fun_all, at)
     near = jnp.sum(
-        jnp.where(iota((count, fun_all), 1) == at, centers_ref[...].astype(jnp.float32), 0.0), axis=1, keepdims=True
+        jnp.where(iota((count, fun_all), 1) == at, centers_ref[...].astype(jnp.float32)[None, :], 0.0), axis=1, keepdims=True
     )
     near = near - (me * box_dev).astype(jnp.float32)
     near = jnp.where(near < -(box_all // 2), near + box_all, near)
@@ -138,6 +144,7 @@
         cuts.append(cut)
         cut_ref[k + REACH] = cut.astype(jnp.int32)
 
+    copies[1].wait()
     potential = potential_ref[...]
     high = potential.astype(jnp.bfloat16)
     low = (potential - high.astype(jnp.float32)).astype(jnp.bfloat16)
@@ -166,6 +173,7 @@
         row_ref[k + REACH : k + REACH + 1] = jnp.where(goes, row, -1.0)
     row_ref[2 * REACH + 1 :] = jnp.full((row_ref.shape[0] - 2 * REACH - 1, pieces), -1.0, jnp.float32)
     home_ref[...] = home
+    copies[0].wait()
     packed_rows(rows, box_dev, row_ref, flat_ref, own_ref, outs)
 
 
@@ -366,7 +374,7 @@
     mixing_ref[...] = jnp.concatenate([row, spare], axis=0).astype(jnp.bfloat16)
 
 
-def mix_kernel(plan, cut_ref, active_ref, place_ref, window_ref, *refs):
+def mix_kernel(plan, cut_ref, active_ref, place_ref, window_ref, region_ref, kinetic_ref, *refs):
     fun_dev, reading, band_order = plan
     slots = 2 * REACH + 1
     bands = dict(zip(band_order, refs[:slots]))
@@ -418,6 +426,12 @@
                 outs[e][...] += times(pick, part).astype(jnp.bfloat16)
                 at_boxes[e][...] += times(pick, boxes_of).astype(jnp.bfloat16)
 
+    for e in (REACH - 1, REACH + 1):
+        here = outs[e][...]
+        applied = times(here, kinetic_ref[...])
+        near_by = times(at_boxes[e][...], region_ref[...])
+        outs[e][...] = (applied + near_by * here.astype(jnp.float32)).astype(jnp.bfloat16)
+
 
 def home_rows(bases, home_ref, sources, at, count):
     shape = (count, home_ref.shape[1])
@@ -462,8 +476,8 @@
     reading = 4 * support
     slots = 2 * REACH + 1
     offsets = list(range(-REACH, REACH + 1))
-    first, last = REACH, -REACH
-    now = [first] + [sign * k for k in range(1, REACH) for sign in (1, -1)]
+    last = -REACH
+    now = [sign * k for k in range(1, REACH) for sign in (-1, 1)] + [REACH]
     one_way = list(range(REACH, 0, -1)) + list(range(-REACH, 0))
     rows, low_cut, high_cut, boxes, blocks = bounds(fun_dev, support)
     assert blocks <= REACH + 1 and support & (support - 1) == 0
@@ -488,12 +502,17 @@
             jax.ShapeDtypeStruct((1, fun_dev * support), f32),
             jax.ShapeDtypeStruct((2 * half, points), bf16),
         ),
-        in_specs=[smem] + [vmem] * 3,
+        in_specs=[smem, vmem] + [pl.BlockSpec(memory_space=pltpu.HBM)] * 2,
         out_specs=(vmem,) * slots + (smem,) + (vmem,) * 2,
-        scratch_shapes=[pltpu.VMEM((8, fun_dev * support), f32)],
-        compiler_params=limit,
+        scratch_shapes=[
+            pltpu.VMEM((8, fun_dev * support), f32),
+            pltpu.VMEM(flat.shape, bf16),
+            pltpu.VMEM(potential.shape, f32),
+            pltpu.SemaphoreType.DMA((2,)),
+        ],
+        compiler_params=pltpu.CompilerParams(vmem_limit_bytes=52 * 2**20),
         name="pack",
-    )(me, centers.reshape(1, -1), flat, potential)
+    )(me, centers, flat, potential)
     arrived = all_sent(dict(zip(now + [last], packed)), now, last, 1)
 
     columns, places, active, local = pl.pallas_call(
@@ -549,17 +568,20 @@
     mixed = pl.pallas_call(
         functools.partial(mix_kernel, (fun_dev, reading, band_order)),
         out_shape=tuple(jax.ShapeDtypeStruct(shape, bf16) for shape in shapes),
-        in_specs=[smem, smem] + [vmem] * (2 + slots),
+        in_specs=[smem, smem] + [vmem] * (4 + slots),
         out_specs=(vmem,) * len(shapes),
         scratch_shapes=[pltpu.VMEM((STEP, wide, points), bf16)]
         + [pltpu.VMEM((size, size), bf16) for size in level_sizes],
         compiler_params=limit,
         name="mix",
-    )(cut, active, places, pieces, *[mixing_of[k] for k in band_order])
+    )(cut, active, places, pieces, region, kinetic, *[mixing_of[k] for k in band_order])
 
     ready = {}
     for k in now + [last, 0]:
         here, at_box = mixed[REACH - k], mixed[slots + REACH - k]
+        if abs(k) == 1:
+            ready[k] = here
+            continue
         near_by = jnp.dot(at_box, region, preferred_element_type=f32)
         applied = jnp.dot(here, kinetic, preferred_element_type=f32)
         ready[k] = (applied + near_by * here.astype(f32)).astype(bf16)
@@ -567,7 +589,7 @@
     returned[0] = ready[0]
 
     bases = {k: sum(back[: k + REACH]) for k in offsets}
-    early, late = [0, first], now[1:] + [last]
+    early, late = [0] + now[:2], now[2:] + [last]
     begun = pl.pallas_call(
         functools.partial(early_kernel, [bases[k] for k in early]),
         out_shape=jax.ShapeDtypeStruct(flat.shape, bf16),

time: 121 us -> 121 us (level); the launches traced: 120 us -> 122 us
  starting transfers between devices: 44.8 us -> 50.1 us
  waiting for transfers between devices: 38.1 us -> 35.6 us
  Pallas kernels: 26.1 us -> 28.5 us
  matrix products: 6.51 us -> 4.62 us
  local copies, waits for them, and re-layouts: 3.1 us -> 1.65 us
    ppermute x24, starting transfers between devices: 44.8 us -> 50.1 us  [passed_along(): return lax.ppermute(value, AXES, pairs)]
    ppermute x24, waiting for transfers between devices: 38.1 us -> 35.6 us  [passed_along(): return lax.ppermute(value, AXES, pairs)]
    pallas_call x1, Pallas kernels: 6.89 us -> 8.45 us  [on_device(): pl.pallas_call(functools.partial(mix_kernel, (fun_dev, reading, band_orde...]
    dot_general x7 -> x5, matrix products: 4.73 us -> 3.39 us  [on_device(): applied = jnp.dot(here, kinetic, preferred_element_type=f32)]
  transfers between devices with their start and end apart: 24 -> 24, of which waited for: 7 -> 10; matrix products, arithmetic and copies ran while one was open for 4% -> 3% of each run, Pallas kernels for 4% -> 4%
where the time goes in v3:
time: 121 us; the launch traced here: 122 us
  starting transfers between devices  50.1 us (41%)
  waiting for transfers between devices  35.6 us (29%)
  Pallas kernels  28.5 us (24%)
  matrix products  4.62 us (4%)
  local copies, waits for them, and re-layouts  1.65 us (1%)
    ppermute x24, starting transfers between devices, passed_along(): return lax.ppermute(value, AXES, pairs)  50.1 us
    ppermute x24, waiting for transfers between devices, passed_along(): return lax.ppermute(value, AXES, pairs)  35.6 us
    pallas_call x1, Pallas kernels, on_device(): pl.pallas_call(functools.partial(mix_kernel, (fun_dev, reading, band_orde...  8.45 us
    pallas_call x1, Pallas kernels, on_device(): pl.pallas_call(functools.partial(unpack_kernel, (fun_dev, box_dev, readin...  7.74 us
    pallas_call x1, Pallas kernels, on_device(): pl.pallas_call(functools.partial(pack_kernel, (fun_dev, support, devices,...  4.11 us
    dot_general x5, matrix products, on_device(): applied = jnp.dot(here, kinetic, preferred_element_type=f32)  3.39 us
    pallas_call x1, Pallas kernels, on_device(): pl.pallas_call(functools.partial(home_kernel, [bases[k] for k in late]),...  2.83 us
    pallas_call x1, Pallas kernels, on_device(): pl.pallas_call(functools.partial(table_kernel, (fun_dev, support, halo, b...  2.78 us
  transfers between devices with their start and end apart: 24, of which 10 were waited for; matrix products, arithmetic and copies ran while one was open for 3% of the time, Pallas kernels for 4%

profile of v3, /device:TPU:1, one launch (start us, length us, event | category | flops | bytes accessed | tf_op | source)
XLA Modules:
  0.0 121.5 jit_solution(6657703585565223012)
XLA Ops:
  2.3 4.1 %pack.1 = (bf16[272,1024]{1,0:T(8,128)(2,1)}, bf16[240,1024]{1,0:T(8,128)(2,1)S(1)}, bf16[192,1024]{1,0:T(8,128)(2,1)S(1)}, bf16[160,1024]{1,0:T(8,128)(2,1)S(1)...) custom-call(s32[1]{0:T(128)} %bitcast.me_ref, ...), custom_call_target="tpu_custom_call" | custom-call | tf_op jit(solution)/shard_map/pack/pallas_call | solution.py:496
  6.5 2.6 %collective-permute-start.2 = (bf16[240,1024]{1,0:T(8,128)(2,1)S(1)}, bf16[240,1024]{1,0:T(8,128)(2,1)S(1)}, u32[]{:S(2)}, u32[]{:S(2)}) collective-permute-start(bf16[240,1024]{1,0:T(8,128)(2,1)S(1)} %get-tuple-element.53), channel_id=1, source_target_pairs={{0,1},{1,2},{2,3},{3,4},{4,5},{5,6},{6,7},{7,8},{8,9},{9,10},{10,1... | collective-permute-start | bytes 1474568 | tf_op jit(solution)/shard_map/ppermute | solution.py:21
  9.1 8.7 %collective-permute-start.4 = (bf16[192,1024]{1,0:T(8,128)(2,1)S(1)}, bf16[192,1024]{1,0:T(8,128)(2,1)S(1)}, u32[]{:S(2)}, u32[]{:S(2)}) collective-permute-start(bf16[192,1024]{1,0:T(8,128)(2,1)S(1)} %get-tuple-element.57), channel_id=1, source_target_pairs={{0,30},{1,31},{2,0},{3,1},{4,2},{5,3},{6,4},{7,5},{8,6},{9,7},{10,... | collective-permute-start | bytes 1179656 | tf_op jit(solution)/shard_map/ppermute | solution.py:21
  17.8 3.3 %collective-permute-done.3.refs_3_ = bf16[272,1024]{1,0:T(8,128)(2,1)S(1)} collective-permute-done((bf16[272,1024]{1,0:T(8,128)(2,1)}, bf16[272,1024]{1,0:T(8,128)(2,1)S(1)}, u32[]{:S(2)}, u32[]{:S(2)}) %collective-permute-start.3) | collective-permute-done | bytes 557088 | tf_op jit(solution)/shard_map/ppermute | solution.py:21
  21.1 15.0 %collective-permute-start.5 = (bf16[64,1024]{1,0:T(8,128)(2,1)S(1)}, bf16[64,1024]{1,0:T(8,128)(2,1)S(1)}, u32[]{:S(2)}, u32[]{:S(2)}) collective-permute-start(bf16[64,1024]{1,0:T(8,128)(2,1)S(1)} %get-tuple-element.58), channel_id=1, source_target_pairs={{0,29},{1,30},{2,31},{3,0},{4,1},{5,2},{6,3},{7,4},{8,5},{9,6},{10... | collective-permute-start | bytes 393224 | tf_op jit(solution)/shard_map/ppermute | solution.py:21
  36.2 2.8 %tables.1 = (f32[224,128]{1,0:T(8,128)S(1)}, f32[3,8,256]{2,1,0:T(8,128)S(1)}, s32[24]{0:T(128)S(1)}, bf16[24,32,1024]{2,1,0:T(8,128)(2,1)S(1)}) custom-call(s32[8]{0:T(128)S(1)} %get-tuple-element.44.cut_ref, f32[512,128]{1,0:T(8,128)S(1)} %get-tuple-element.45.near_ref, bf16[768,1024]{1,0:T(8,128)(2,1)S(1)} %bitcast.24), custom_call_target="tpu_custom_call" | custom-call | tf_op jit(solution)/shard_map/tables/pallas_call | solution.py:518
  39.0 5.3 %collective-permute-done.refs_0_ = bf16[48,1024]{1,0:T(8,128)(2,1)S(1)} collective-permute-done((bf16[48,1024]{1,0:T(8,128)(2,1)S(1)}, bf16[48,1024]{1,0:T(8,128)(2,1)S(1)}, u32[]{:S(2)}, u32[]{:S(2)}) %collective-permute-start) | collective-permute-done | bytes 98336 | tf_op jit(solution)/shard_map/ppermute | solution.py:21
  44.3 7.7 %unpack.1 = (bf16[24,224,1024]{2,1,0:T(8,128)(2,1)S(1)}, bf16[128,1024]{1,0:T(8,128)(2,1)S(1)}, f32[24,256]{1,0:T(8,128)S(1)}, f32[24,256]{1,0:T(8,128)S(1)}, f3...) custom-call(s32[8]{0:T(128)S(1)} %get-tuple-element.44.cut_ref, ...), custom_call_target="tpu_custom_call" | custom-call | tf_op jit(solution)/shard_map/unpack/pallas_call | solution.py:538
  52.3 5.7 %collective-permute-start.9 = (f32[24,256]{1,0:T(8,128)S(1)}, f32[24,256]{1,0:T(8,128)S(1)}, u32[]{:S(2)}, u32[]{:S(2)}) collective-permute-start(f32[24,256]{1,0:T(8,128)S(1)} %get-tuple-element.65), channel_id=1, source_target_pairs={{0,29},{1,30},{2,31},{3,0},{4,1},{5,2},{6,3},{7,4},{8,5},{9,6},{10... | collective-permute-start | bytes 73736 | tf_op jit(solution)/shard_map/ppermute | solution.py:21
  59.4 1.6 %collective-permute-start.11 = (f32[24,256]{1,0:T(8,128)S(1)}, f32[24,256]{1,0:T(8,128)S(1)}, u32[]{:S(2)}, u32[]{:S(2)}) collective-permute-start(f32[24,256]{1,0:T(8,128)S(1)} %get-tuple-element.67), channel_id=1, source_target_pairs={{0,31},{1,0},{2,1},{3,2},{4,3},{5,4},{6,5},{7,6},{8,7},{9,8},{10,9... | collective-permute-start | bytes 73736 | tf_op jit(solution)/shard_map/ppermute | solution.py:21
  61.1 1.6 %collective-permute-done.11.refs_6_ = f32[24,256]{1,0:T(8,128)S(1)} collective-permute-done((f32[24,256]{1,0:T(8,128)S(1)}, f32[24,256]{1,0:T(8,128)S(1)}, u32[]{:S(2)}, u32[]{:S(2)}) %collective-permute-start.11) | collective-permute-done | bytes 24608 | tf_op jit(solution)/shard_map/ppermute | solution.py:21
  63.4 5.4 %collective-permute-start.16 = (bf16[32,256]{1,0:T(8,128)(2,1)S(1)}, bf16[32,256]{1,0:T(8,128)(2,1)S(1)}, u32[]{:S(2)}, u32[]{:S(2)}) collective-permute-start(bf16[32,256]{1,0:T(8,128)(2,1)S(1)} %get-tuple-element.68.refs_6_), channel_id=1, source_target_pairs={{0,30},{1,31},{2,0},{3,1},{4,2},{5,3},{6,4},{7,5},{8,6},{9,7},{10,... | collective-permute-start | bytes 49160 | tf_op jit(solution)/shard_map/ppermute | solution.py:21
  68.8 1.6 %collective-permute-start.14 = (bf16[32,256]{1,0:T(8,128)(2,1)S(1)}, bf16[32,256]{1,0:T(8,128)(2,1)S(1)}, u32[]{:S(2)}, u32[]{:S(2)}) collective-permute-start(bf16[32,256]{1,0:T(8,128)(2,1)S(1)} %get-tuple-element.68.refs_6_), channel_id=1, source_target_pairs={{0,1},{1,2},{2,3},{3,4},{4,5},{5,6},{6,7},{7,8},{8,9},{9,10},{10,1... | collective-permute-start | bytes 49160 | tf_op jit(solution)/shard_map/ppermute | solution.py:21
  70.5 1.3 %collective-permute-start.13 = (bf16[32,256]{1,0:T(8,128)(2,1)S(1)}, bf16[32,256]{1,0:T(8,128)(2,1)S(1)}, u32[]{:S(2)}, u32[]{:S(2)}) collective-permute-start(bf16[32,256]{1,0:T(8,128)(2,1)S(1)} %get-tuple-element.68.refs_6_), channel_id=1, source_target_pairs={{0,2},{1,3},{2,4},{3,5},{4,6},{5,7},{6,8},{7,9},{8,10},{9,11},{10,... | collective-permute-start | bytes 49160 | tf_op jit(solution)/shard_map/ppermute | solution.py:21
  72.2 4.5 %collective-permute-done.13.refs_1_ = bf16[32,256]{1,0:T(8,128)(2,1)S(1)} collective-permute-done((bf16[32,256]{1,0:T(8,128)(2,1)S(1)}, bf16[32,256]{1,0:T(8,128)(2,1)S(1)}, u32[]{:S(2)}, u32[]{:S(2)}) %collective-permute-start.13) | collective-permute-done | bytes 16416 | tf_op jit(solution)/shard_map/ppermute | solution.py:21
  76.7 2.0 %collective-permute-done.12.refs_0_ = bf16[32,256]{1,0:T(8,128)(2,1)S(1)} collective-permute-done((bf16[32,256]{1,0:T(8,128)(2,1)S(1)}, bf16[32,256]{1,0:T(8,128)(2,1)S(1)}, u32[]{:S(2)}, u32[]{:S(2)}) %collective-permute-start.12) | collective-permute-done | bytes 16416 | tf_op jit(solution)/shard_map/ppermute | solution.py:21
  78.7 8.5 %mix.1 = (bf16[48,1024]{1,0:T(8,128)(2,1)S(1)}, bf16[160,1024]{1,0:T(8,128)(2,1)S(1)}, bf16[240,1024]{1,0:T(8,128)(2,1)S(1)}, bf16[512,1024]{1,0:T(8,128)(2,1)S(...) custom-call(s32[8]{0:T(128)S(1)} %get-tuple-element.44.cut_ref, ...), custom_call_target="tpu_custom_call" | custom-call | tf_op jit(solution)/shard_map/mix/pallas_call | solution.py:568
  88.0 1.7 %collective-permute-start.18 = (bf16[256,1024]{1,0:T(8,128)(2,1)S(1)}, bf16[256,1024]{1,0:T(8,128)(2,1)S(1)}, u32[]{:S(2)}, u32[]{:S(2)}) collective-permute-start(bf16[256,1024]{1,0:T(8,128)(2,1)S(1)} %get-tuple-element.73), channel_id=1, source_target_pairs={{0,1},{1,2},{2,3},{3,4},{4,5},{5,6},{6,7},{7,8},{8,9},{9,10},{10,1... | collective-permute-start | bytes 1572872 | tf_op jit(solution)/shard_map/ppermute | solution.py:21
  90.5 4.2 %collective-permute-start.21 = (bf16[160,1024]{1,0:T(8,128)(2,1)S(1)}, bf16[160,1024]{1,0:T(8,128)(2,1)S(1)}, u32[]{:S(2)}, u32[]{:S(2)}) collective-permute-start(bf16[160,1024]{1,0:T(8,128)(2,1)S(1)} %fusion.1), channel_id=1, source_target_pairs={{0,30},{1,31},{2,0},{3,1},{4,2},{5,3},{6,4},{7,5},{8,6},{9,7},{10,... | collective-permute-start | bytes 983048 | tf_op jit(solution)/shard_map/ppermute | solution.py:21
  96.7 13.9 %collective-permute-done.18.refs_1_ = bf16[256,1024]{1,0:T(8,128)(2,1)S(1)} collective-permute-done((bf16[256,1024]{1,0:T(8,128)(2,1)S(1)}, bf16[256,1024]{1,0:T(8,128)(2,1)S(1)}, u32[]{:S(2)}, u32[]{:S(2)}) %collective-permute-start.18) | collective-permute-done | bytes 524320 | tf_op jit(solution)/shard_map/ppermute | solution.py:21
  110.5 1.3 %add_convert_fusion.refs_0_ = bf16[512,1024]{1,0:T(8,128)(2,1)S(1)} fusion(f32[512,1024]{1,0:T(8,128)S(1)} %fusion.4, bf16[512,1024]{1,0:T(8,128)(2,1)S(1)} %get-tuple-element.69, bf16[1024,1024]{1,0:T(8,128)(2,1)S(1)} %copy-done), kind=kOutput, calls=%fused_computation | convolution fusion | flops 1075838976 | bytes 6291456 | tf_op jit(solution)/shard_map/dot_general | solution.py:586
  111.9 2.0 %early.1.early_ref = bf16[768,1024]{1,0:T(8,128)(2,1)S(1)} custom-call(f32[1,768]{1,0:T(1,128)S(1)} %get-tuple-element.43.home_ref, bf16[512,1024]{1,0:T(8,128)(2,1)S(1)} %add_convert_fusion.refs_0_, bf16[256,1024]{1,0:T(8,128)(2,1)S(1)} %collective-permute-done.18.refs_1_, bf16[240,1024]{1,0:T(8,128)(2,1)S(1)} %collective-permute-done.19.refs_2_), custom_call_target="tpu_custom_call" | custom-call | tf_op jit(solution)/shard_map/early/pallas_call | solution.py:593
  114.0 4.5 %collective-permute-done.23.refs_3_ = bf16[48,1024]{1,0:T(8,128)(2,1)S(1)} collective-permute-done((bf16[48,1024]{1,0:T(8,128)(2,1)S(1)}, bf16[48,1024]{1,0:T(8,128)(2,1)S(1)}, u32[]{:S(2)}, u32[]{:S(2)}) %collective-permute-start.23) | collective-permute-done | bytes 98336 | tf_op jit(solution)/shard_map/ppermute | solution.py:21
  118.5 2.8 %home.1 = bf16[768,1024]{1,0:T(8,128)(2,1)} custom-call(f32[1,768]{1,0:T(1,128)S(1)} %get-tuple-element.43.home_ref, bf16[768,1024]{1,0:T(8,128)(2,1)S(1)} %early.1.early_ref, bf16[160,1024]{1,0:T(8,128)(2,1)S(1)} %collective-permute-done.20.refs_0_, bf16[160,1024]{1,0:T(8,128)(2,1)S(1)} %collective-permute-done.21.refs_1_, ...), custom_call_target="tpu_custom_call" | custom-call | tf_op jit(solution)/shard_map/home/pallas_call | solution.py:601
  (49 shorter events, 8.3 us)
Async XLA Ops:
  6.4 14.7 %collective-permute-start.3 = (bf16[272,1024]{1,0:T(8,128)(2,1)}, bf16[272,1024]{1,0:T(8,128)(2,1)S(1)}, u32[]{:S(2)}, u32[]{:S(2)}) collective-permute-start(bf16[272,1024]{1,0:T(8,128)(2,1)} %get-tuple-element.55), channel_id=1, source_target_pairs={{0,31},{1,0},{2,1},{3,2},{4,3},{5,4},{6,5},{7,6},{8,7},{9,8},{10,9... | collective-permute-start | bytes 1671176 | tf_op jit(solution)/shard_map/ppermute | solution.py:21
  6.5 37.8 %collective-permute-start.2 = (bf16[240,1024]{1,0:T(8,128)(2,1)S(1)}, bf16[240,1024]{1,0:T(8,128)(2,1)S(1)}, u32[]{:S(2)}, u32[]{:S(2)}) collective-permute-start(bf16[240,1024]{1,0:T(8,128)(2,1)S(1)} %get-tuple-element.53), channel_id=1, source_target_pairs={{0,1},{1,2},{2,3},{3,4},{4,5},{5,6},{6,7},{7,8},{8,9},{9,10},{10,1... | collective-permute-start | bytes 1474568 | tf_op jit(solution)/shard_map/ppermute | solution.py:21
  9.1 35.2 %collective-permute-start.4 = (bf16[192,1024]{1,0:T(8,128)(2,1)S(1)}, bf16[192,1024]{1,0:T(8,128)(2,1)S(1)}, u32[]{:S(2)}, u32[]{:S(2)}) collective-permute-start(bf16[192,1024]{1,0:T(8,128)(2,1)S(1)} %get-tuple-element.57), channel_id=1, source_target_pairs={{0,30},{1,31},{2,0},{3,1},{4,2},{5,3},{6,4},{7,5},{8,6},{9,7},{10,... | collective-permute-start | bytes 1179656 | tf_op jit(solution)/shard_map/ppermute | solution.py:21
  17.8 26.5 %collective-permute-start.1 = (bf16[160,1024]{1,0:T(8,128)(2,1)S(1)}, bf16[160,1024]{1,0:T(8,128)(2,1)S(1)}, u32[]{:S(2)}, u32[]{:S(2)}) collective-permute-start(bf16[160,1024]{1,0:T(8,128)(2,1)S(1)} %get-tuple-element.52), channel_id=1, source_target_pairs={{0,2},{1,3},{2,4},{3,5},{4,6},{5,7},{6,8},{7,9},{8,10},{9,11},{10,... | collective-permute-start | bytes 983048 | tf_op jit(solution)/shard_map/ppermute | solution.py:21
  21.1 23.2 %collective-permute-start.5 = (bf16[64,1024]{1,0:T(8,128)(2,1)S(1)}, bf16[64,1024]{1,0:T(8,128)(2,1)S(1)}, u32[]{:S(2)}, u32[]{:S(2)}) collective-permute-start(bf16[64,1024]{1,0:T(8,128)(2,1)S(1)} %get-tuple-element.58), channel_id=1, source_target_pairs={{0,29},{1,30},{2,31},{3,0},{4,1},{5,2},{6,3},{7,4},{8,5},{9,6},{10... | collective-permute-start | bytes 393224 | tf_op jit(solution)/shard_map/ppermute | solution.py:21
  36.2 8.1 %collective-permute-start = (bf16[48,1024]{1,0:T(8,128)(2,1)S(1)}, bf16[48,1024]{1,0:T(8,128)(2,1)S(1)}, u32[]{:S(2)}, u32[]{:S(2)}) collective-permute-start(bf16[48,1024]{1,0:T(8,128)(2,1)S(1)} %get-tuple-element.51), channel_id=1, source_target_pairs={{0,3},{1,4},{2,5},{3,6},{4,7},{5,8},{6,9},{7,10},{8,11},{9,12},{10... | collective-permute-start | bytes 294920 | tf_op jit(solution)/shard_map/ppermute | solution.py:21
  52.1 7.4 %collective-permute-start.6 = (f32[24,256]{1,0:T(8,128)S(1)}, f32[24,256]{1,0:T(8,128)S(1)}, u32[]{:S(2)}, u32[]{:S(2)}) collective-permute-start(f32[24,256]{1,0:T(8,128)S(1)} %get-tuple-element.62), channel_id=1, source_target_pairs={{0,3},{1,4},{2,5},{3,6},{4,7},{5,8},{6,9},{7,10},{8,11},{9,12},{10... | collective-permute-start | bytes 73736 | tf_op jit(solution)/shard_map/ppermute | solution.py:21
  52.1 9.0 %collective-permute-start.7 = (f32[24,256]{1,0:T(8,128)S(1)}, f32[24,256]{1,0:T(8,128)S(1)}, u32[]{:S(2)}, u32[]{:S(2)}) collective-permute-start(f32[24,256]{1,0:T(8,128)S(1)} %get-tuple-element.63), channel_id=1, source_target_pairs={{0,2},{1,3},{2,4},{3,5},{4,6},{5,7},{6,8},{7,9},{8,10},{9,11},{10,... | collective-permute-start | bytes 73736 | tf_op jit(solution)/shard_map/ppermute | solution.py:21
  52.2 8.9 %collective-permute-start.8 = (f32[24,256]{1,0:T(8,128)S(1)}, f32[24,256]{1,0:T(8,128)S(1)}, u32[]{:S(2)}, u32[]{:S(2)}) collective-permute-start(f32[24,256]{1,0:T(8,128)S(1)} %get-tuple-element.64), channel_id=1, source_target_pairs={{0,1},{1,2},{2,3},{3,4},{4,5},{5,6},{6,7},{7,8},{8,9},{9,10},{10,1... | collective-permute-start | bytes 73736 | tf_op jit(solution)/shard_map/ppermute | solution.py:21
  52.3 8.8 %collective-permute-start.9 = (f32[24,256]{1,0:T(8,128)S(1)}, f32[24,256]{1,0:T(8,128)S(1)}, u32[]{:S(2)}, u32[]{:S(2)}) collective-permute-start(f32[24,256]{1,0:T(8,128)S(1)} %get-tuple-element.65), channel_id=1, source_target_pairs={{0,29},{1,30},{2,31},{3,0},{4,1},{5,2},{6,3},{7,4},{8,5},{9,6},{10... | collective-permute-start | bytes 73736 | tf_op jit(solution)/shard_map/ppermute | solution.py:21
  57.9 3.2 %collective-permute-start.10 = (f32[24,256]{1,0:T(8,128)S(1)}, f32[24,256]{1,0:T(8,128)S(1)}, u32[]{:S(2)}, u32[]{:S(2)}) collective-permute-start(f32[24,256]{1,0:T(8,128)S(1)} %get-tuple-element.66), channel_id=1, source_target_pairs={{0,30},{1,31},{2,0},{3,1},{4,2},{5,3},{6,4},{7,5},{8,6},{9,7},{10,... | collective-permute-start | bytes 73736 | tf_op jit(solution)/shard_map/ppermute | solution.py:21
  59.4 3.3 %collective-permute-start.11 = (f32[24,256]{1,0:T(8,128)S(1)}, f32[24,256]{1,0:T(8,128)S(1)}, u32[]{:S(2)}, u32[]{:S(2)}) collective-permute-start(f32[24,256]{1,0:T(8,128)S(1)} %get-tuple-element.67), channel_id=1, source_target_pairs={{0,31},{1,0},{2,1},{3,2},{4,3},{5,4},{6,5},{7,6},{8,7},{9,8},{10,9... | collective-permute-start | bytes 73736 | tf_op jit(solution)/shard_map/ppermute | solution.py:21
  63.3 8.5 %collective-permute-start.17 = (bf16[32,256]{1,0:T(8,128)(2,1)S(1)}, bf16[32,256]{1,0:T(8,128)(2,1)S(1)}, u32[]{:S(2)}, u32[]{:S(2)}) collective-permute-start(bf16[32,256]{1,0:T(8,128)(2,1)S(1)} %get-tuple-element.68.refs_6_), channel_id=1, source_target_pairs={{0,31},{1,0},{2,1},{3,2},{4,3},{5,4},{6,5},{7,6},{8,7},{9,8},{10,9... | collective-permute-start | bytes 49160 | tf_op jit(solution)/shard_map/ppermute | solution.py:21
  63.4 8.6 %collective-permute-start.16 = (bf16[32,256]{1,0:T(8,128)(2,1)S(1)}, bf16[32,256]{1,0:T(8,128)(2,1)S(1)}, u32[]{:S(2)}, u32[]{:S(2)}) collective-permute-start(bf16[32,256]{1,0:T(8,128)(2,1)S(1)} %get-tuple-element.68.refs_6_), channel_id=1, source_target_pairs={{0,30},{1,31},{2,0},{3,1},{4,2},{5,3},{6,4},{7,5},{8,6},{9,7},{10,... | collective-permute-start | bytes 49160 | tf_op jit(solution)/shard_map/ppermute | solution.py:21
  68.8 3.3 %collective-permute-start.15 = (bf16[32,256]{1,0:T(8,128)(2,1)S(1)}, bf16[32,256]{1,0:T(8,128)(2,1)S(1)}, u32[]{:S(2)}, u32[]{:S(2)}) collective-permute-start(bf16[32,256]{1,0:T(8,128)(2,1)S(1)} %get-tuple-element.68.refs_6_), channel_id=1, source_target_pairs={{0,29},{1,30},{2,31},{3,0},{4,1},{5,2},{6,3},{7,4},{8,5},{9,6},{10... | collective-permute-start | bytes 49160 | tf_op jit(solution)/shard_map/ppermute | solution.py:21
  68.8 3.3 %collective-permute-start.14 = (bf16[32,256]{1,0:T(8,128)(2,1)S(1)}, bf16[32,256]{1,0:T(8,128)(2,1)S(1)}, u32[]{:S(2)}, u32[]{:S(2)}) collective-permute-start(bf16[32,256]{1,0:T(8,128)(2,1)S(1)} %get-tuple-element.68.refs_6_), channel_id=1, source_target_pairs={{0,1},{1,2},{2,3},{3,4},{4,5},{5,6},{6,7},{7,8},{8,9},{9,10},{10,1... | collective-permute-start | bytes 49160 | tf_op jit(solution)/shard_map/ppermute | solution.py:21
  70.5 6.2 %collective-permute-start.13 = (bf16[32,256]{1,0:T(8,128)(2,1)S(1)}, bf16[32,256]{1,0:T(8,128)(2,1)S(1)}, u32[]{:S(2)}, u32[]{:S(2)}) collective-permute-start(bf16[32,256]{1,0:T(8,128)(2,1)S(1)} %get-tuple-element.68.refs_6_), channel_id=1, source_target_pairs={{0,2},{1,3},{2,4},{3,5},{4,6},{5,7},{6,8},{7,9},{8,10},{9,11},{10,... | collective-permute-start | bytes 49160 | tf_op jit(solution)/shard_map/ppermute | solution.py:21
  71.8 6.9 %collective-permute-start.12 = (bf16[32,256]{1,0:T(8,128)(2,1)S(1)}, bf16[32,256]{1,0:T(8,128)(2,1)S(1)}, u32[]{:S(2)}, u32[]{:S(2)}) collective-permute-start(bf16[32,256]{1,0:T(8,128)(2,1)S(1)} %get-tuple-element.68.refs_6_), channel_id=1, source_target_pairs={{0,3},{1,4},{2,5},{3,6},{4,7},{5,8},{6,9},{7,10},{8,11},{9,12},{10... | collective-permute-start | bytes 49160 | tf_op jit(solution)/shard_map/ppermute | solution.py:21
  87.8 26.0 %collective-permute-start.22 = (bf16[48,1024]{1,0:T(8,128)(2,1)S(1)}, bf16[48,1024]{1,0:T(8,128)(2,1)S(1)}, u32[]{:S(2)}, u32[]{:S(2)}) collective-permute-start(bf16[48,1024]{1,0:T(8,128)(2,1)S(1)} %fusion.3), channel_id=1, source_target_pairs={{0,29},{1,30},{2,31},{3,0},{4,1},{5,2},{6,3},{7,4},{8,5},{9,6},{10... | collective-permute-start | bytes 294920 | tf_op jit(solution)/shard_map/ppermute | solution.py:21
  87.9 24.0 %collective-permute-start.19 = (bf16[240,1024]{1,0:T(8,128)(2,1)S(1)}, bf16[240,1024]{1,0:T(8,128)(2,1)S(1)}, u32[]{:S(2)}, u32[]{:S(2)}) collective-permute-start(bf16[240,1024]{1,0:T(8,128)(2,1)S(1)} %get-tuple-element.75), channel_id=1, source_target_pairs={{0,31},{1,0},{2,1},{3,2},{4,3},{5,4},{6,5},{7,6},{8,7},{9,8},{10,9... | collective-permute-start | bytes 1474568 | tf_op jit(solution)/shard_map/ppermute | solution.py:21
  88.0 22.6 %collective-permute-start.18 = (bf16[256,1024]{1,0:T(8,128)(2,1)S(1)}, bf16[256,1024]{1,0:T(8,128)(2,1)S(1)}, u32[]{:S(2)}, u32[]{:S(2)}) collective-permute-start(bf16[256,1024]{1,0:T(8,128)(2,1)S(1)} %get-tuple-element.73), channel_id=1, source_target_pairs={{0,1},{1,2},{2,3},{3,4},{4,5},{5,6},{6,7},{7,8},{8,9},{9,10},{10,1... | collective-permute-start | bytes 1572872 | tf_op jit(solution)/shard_map/ppermute | solution.py:21
  90.5 23.4 %collective-permute-start.21 = (bf16[160,1024]{1,0:T(8,128)(2,1)S(1)}, bf16[160,1024]{1,0:T(8,128)(2,1)S(1)}, u32[]{:S(2)}, u32[]{:S(2)}) collective-permute-start(bf16[160,1024]{1,0:T(8,128)(2,1)S(1)} %fusion.1), channel_id=1, source_target_pairs={{0,30},{1,31},{2,0},{3,1},{4,2},{5,3},{6,4},{7,5},{8,6},{9,7},{10,... | collective-permute-start | bytes 983048 | tf_op jit(solution)/shard_map/ppermute | solution.py:21
  95.5 18.5 %collective-permute-start.20 = (bf16[160,1024]{1,0:T(8,128)(2,1)S(1)}, bf16[160,1024]{1,0:T(8,128)(2,1)S(1)}, u32[]{:S(2)}, u32[]{:S(2)}) collective-permute-start(bf16[160,1024]{1,0:T(8,128)(2,1)S(1)} %fusion), channel_id=1, source_target_pairs={{0,2},{1,3},{2,4},{3,5},{4,6},{5,7},{6,8},{7,9},{8,10},{9,11},{10,... | collective-permute-start | bytes 983048 | tf_op jit(solution)/shard_map/ppermute | solution.py:21
  110.5 8.0 %collective-permute-start.23 = (bf16[48,1024]{1,0:T(8,128)(2,1)S(1)}, bf16[48,1024]{1,0:T(8,128)(2,1)S(1)}, u32[]{:S(2)}, u32[]{:S(2)}) collective-permute-start(bf16[48,1024]{1,0:T(8,128)(2,1)S(1)} %fusion.2), channel_id=1, source_target_pairs={{0,3},{1,4},{2,5},{3,6},{4,7},{5,8},{6,9},{7,10},{8,11},{9,12},{10... | collective-permute-start | bytes 294920 | tf_op jit(solution)/shard_map/ppermute | solution.py:21
  (4 other events, 76.9 us)

commit v4 on v3

--- a/solution.py
+++ b/solution.py
@@ -102,16 +102,12 @@
     )
 
 
-def pack_kernel(plan, me_ref, centers_ref, flat_hbm, potential_hbm, *refs):
-    fun_dev, support, devices, halo, rows, back, low_cut, high_cut, now = plan
+def pack_kernel(plan, me_ref, centers_ref, flat_hbm, *refs):
+    fun_dev, support, devices, halo, back, low_cut, high_cut, now = plan
     outs = dict(zip(now, refs[: len(now)]))
-    near_ref, cut_ref, home_ref, own_ref, row_ref, flat_ref, potential_ref, sems = refs[len(now) :]
-    copies = [
-        pltpu.make_async_copy(flat_hbm, flat_ref, sems.at[0]),
-        pltpu.make_async_copy(potential_hbm, potential_ref, sems.at[1]),
-    ]
-    for copy in copies:
-        copy.start()
+    near_ref, cut_ref, home_ref, row_ref, flat_ref, sem = refs[len(now) :]
+    copy = pltpu.make_async_copy(flat_hbm, flat_ref, sem)
+    copy.start()
     me = me_ref[0]
     box_dev = fun_dev // 2
     fun_all, box_all = fun_dev * devices, box_dev * devices
@@ -143,15 +139,6 @@
         cut = jnp.sum(passed) + float(low_cut + k * box_dev)
         cuts.append(cut)
         cut_ref[k + REACH] = cut.astype(jnp.int32)
-
-    copies[1].wait()
-    potential = potential_ref[...]
-    high = potential.astype(jnp.bfloat16)
-    low = (potential - high.astype(jnp.float32)).astype(jnp.bfloat16)
-    shape = (own_ref.shape[0], box_dev)
-    at_high = iota(shape, 0) == iota(shape, 1)
-    at_low = iota(shape, 0) - float(shape[0] // 2) == iota(shape, 1)
-    own_ref[...] = (times(one_hot(at_high), high) + times(one_hot(at_low), low)).astype(jnp.bfloat16)
 
     mine = near[halo * fun_dev : (halo + 1) * fun_dev]
     pieces = fun_dev * support
@@ -173,22 +160,11 @@
         row_ref[k + REACH : k + REACH + 1] = jnp.where(goes, row, -1.0)
     row_ref[2 * REACH + 1 :] = jnp.full((row_ref.shape[0] - 2 * REACH - 1, pieces), -1.0, jnp.float32)
     home_ref[...] = home
-    copies[0].wait()
-    packed_rows(rows, box_dev, row_ref, flat_ref, own_ref, outs)
-
-
-def packed_rows(rows, box_dev, row_ref, flat_ref, own_ref, outs):
+    copy.wait()
     for k, out_ref in outs.items():
-        sent = out_ref.shape[0]
         row = row_ref[k + REACH : k + REACH + 1]
-        value = times(one_hot(iota((sent, row.shape[1]), 0) == row), flat_ref[...])
-        if k < 0:
-            shape = (sent, own_ref.shape[0])
-            part = iota(shape, 0) - float(rows[k + REACH])
-            from_col = jnp.where(part < box_dev, part, part - box_dev + float(shape[1] // 2))
-            inside = (part >= 0) & (part < 2 * box_dev)
-            value = value + times(one_hot(inside & (iota(shape, 1) == from_col)), own_ref[...])
-        out_ref[...] = value.astype(jnp.bfloat16)
+        pick = one_hot(iota((out_ref.shape[0], pieces), 0) == row)
+        out_ref[...] = times(pick, flat_ref[...]).astype(jnp.bfloat16)
 
 
 def picked(start, low, high, first, rows):
@@ -284,35 +260,19 @@
     return (REACH - level) * SLOT, (REACH + level + 1) * SLOT
 
 
-def unpack_kernel(plan, cut_ref, active_ref, column_ref, own_ref, local_ref, *refs):
-    fun_dev, box_dev, reading, volume, rows, back, blocks = plan
+def unpack_kernel(plan, cut_ref, active_ref, column_ref, potential_ref, local_ref, *refs):
+    fun_dev, reading, volume, back = plan
     slots = 2 * REACH + 1
     sources = refs[:REACH] + (None,) + refs[REACH : slots - 1]
-    window_ref, region_ref = refs[slots - 1 : slots + 1]
-    gram_refs = refs[slots + 1 : 2 * slots + 1]
-    dense = refs[2 * slots + 1]
-    totals = refs[2 * slots + 2 :]
+    window_ref = refs[slots - 1]
+    gram_refs = refs[slots : 2 * slots]
+    dense = refs[2 * slots]
+    totals = refs[2 * slots + 1 :]
     steps = window_ref.shape[0] // STEP
     width = cut_ref[REACH + 1] - cut_ref[REACH]
 
     for total in totals:
         total[...] = jnp.zeros_like(total)
-    value = None
-    for t in range(blocks):
-        held = own_ref if t == 0 else sources[REACH + t]
-        at = 0 if t == 0 else rows[REACH + t]
-        from_row = at // 16 * 16
-        held = held[from_row:]
-        second = own_ref.shape[0] // 2 if t == 0 else box_dev
-        shape = (region_ref.shape[0], held.shape[0])
-        row, col = iota(shape, 0), iota(shape, 1)
-        box = row - jnp.where(row >= SLOT, float(SLOT), 0.0) + cut_ref[REACH].astype(jnp.float32) - t * box_dev
-        wanted = box + jnp.where(row >= SLOT, float(second), 0.0) + float(at - from_row)
-        good = (box >= 0) & (box < box_dev) & (row < 2 * SLOT)
-        term = times(one_hot(good & (col == wanted)), held)
-        value = term if value is None else value + term
-    region_ref[...] = value.astype(jnp.bfloat16)
-
     @pl.loop(0, lax.div(width + STEP - 1, STEP))
     def _(step):
         here_rows = pl.ds(step * STEP, STEP)
@@ -359,14 +319,44 @@
         dense[low:high] += times(total[...], keep[low:high], precision=lax.Precision.HIGHEST)
     for e in range(slots):
         rows_here = dense[e * SLOT : e * SLOT + fun_dev]
-        gram_refs[e][...] = skewed(moved(rows_here, reading - 1 - e * fun_dev), -1)[:, : 2 * reading]
+        gram_refs[e][:fun_dev] = skewed(moved(rows_here, reading - 1 - e * fun_dev), -1)[:, : 2 * reading]
+        if e < REACH:
+            box_dev, points = potential_ref.shape
+            gram_refs[e][fun_dev:] = jnp.zeros((gram_refs[e].shape[0] - fun_dev, 2 * reading), jnp.float32)
+            for q in range(points // (2 * reading)):
+                at = fun_dev + q * 16
+                gram_refs[e][at : at + box_dev] = potential_ref[:, q * 2 * reading : (q + 1) * 2 * reading]
+
+
+def region_kernel(fun_dev, cut_ref, potential_ref, *refs):
+    blocks, region_ref = refs[:-1], refs[-1]
+    box_dev = potential_ref.shape[0]
+    first = cut_ref[REACH].astype(jnp.float32)
+    shape = (region_ref.shape[0], box_dev)
+    row, col = iota(shape, 0), iota(shape, 1)
+    lanes = blocks[0].shape[1]
+    for q in range(potential_ref.shape[1] // lanes):
+        value = None
+        for t in range(1 + len(blocks)):
+            if t == 0:
+                held = potential_ref[:, q * lanes : (q + 1) * lanes]
+            else:
+                held = blocks[t - 1][fun_dev + q * 16 : fun_dev + q * 16 + box_dev]
+            high = held.astype(jnp.bfloat16)
+            low = (held - high.astype(jnp.float32)).astype(jnp.bfloat16)
+            at_high = (row < SLOT) & (col == first + row - t * box_dev)
+            at_low = (row >= SLOT) & (row < 2 * SLOT) & (col == first + row - SLOT - t * box_dev)
+            term = times(one_hot(at_high), high) + times(one_hot(at_low), low)
+            value = term if value is None else value + term
+        region_ref[:, q * lanes : (q + 1) * lanes] = value.astype(jnp.bfloat16)
 
 
 def sum_kernel(reading, *refs):
     gram_ref, mixing_ref = refs[-2:]
+    count = gram_ref.shape[0]
     value = refs[0][...]
     for ref in refs[1:-2]:
-        value = value + ref[...]
+        value = value + ref[:count]
     gram_ref[...] = value
     diagonal = jnp.where(lax.broadcasted_iota(jnp.int32, value.shape, 1) == reading - 1, 1.5, 0.0)
     row = diagonal - 0.5 * value
@@ -426,7 +416,9 @@
                 outs[e][...] += times(pick, part).astype(jnp.bfloat16)
                 at_boxes[e][...] += times(pick, boxes_of).astype(jnp.bfloat16)
 
-    for e in (REACH - 1, REACH + 1):
+    for e in range(slots):
+        if e == REACH:
+            continue
         here = outs[e][...]
         applied = times(here, kinetic_ref[...])
         near_by = times(at_boxes[e][...], region_ref[...])
@@ -438,9 +430,11 @@
     here = iota(shape, 1) == iota(shape, 0) + float(at)
     row = jnp.sum(jnp.where(here, home_ref[...], 0.0), axis=1, keepdims=True)
     value = None
-    for base, source in zip(bases, sources):
-        pick = one_hot(iota((count, source.shape[0]), 1) == row - float(base))
-        term = times(pick, source[...])
+    for base, group in bases:
+        parts = [sources[at][...] for at in group]
+        held = parts[0] if len(parts) == 1 else jnp.concatenate(parts, axis=0)
+        pick = one_hot(iota((count, held.shape[0]), 1) == row - float(base))
+        term = times(pick, held)
         value = term if value is None else value + term
     return value
 
@@ -486,33 +480,29 @@
     flat = coeffs.reshape(fun_dev * support, points)
     halo = REACH + -(-(reading + 8) // fun_dev)
     count = rounded_up((2 * halo + 2) * fun_dev, 128)
-    half = rounded_up(box_dev, 16)
     bf16, f32 = jnp.bfloat16, jnp.float32
     smem = pl.BlockSpec(memory_space=pltpu.SMEM)
     vmem = pl.BlockSpec(memory_space=pltpu.VMEM)
     limit = pltpu.CompilerParams(vmem_limit_bytes=26 * 2**20)
 
-    sent_rows = {k: rounded_up(rows[k + REACH] + (2 * box_dev if k < 0 else 0), 16) for k in offsets if k}
-    *packed, near, cut, home_row, own_region = pl.pallas_call(
-        functools.partial(pack_kernel, (fun_dev, support, devices, halo, rows, back, low_cut, high_cut, now + [last])),
-        out_shape=tuple(jax.ShapeDtypeStruct((sent_rows[k], points), bf16) for k in now + [last])
+    *packed, near, cut, home_row = pl.pallas_call(
+        functools.partial(pack_kernel, (fun_dev, support, devices, halo, back, low_cut, high_cut, now + [last])),
+        out_shape=tuple(jax.ShapeDtypeStruct((rows_of[k], points), bf16) for k in now + [last])
         + (
             jax.ShapeDtypeStruct((count, 128), f32),
             jax.ShapeDtypeStruct((slots + 1,), jnp.int32),
             jax.ShapeDtypeStruct((1, fun_dev * support), f32),
-            jax.ShapeDtypeStruct((2 * half, points), bf16),
         ),
-        in_specs=[smem, vmem] + [pl.BlockSpec(memory_space=pltpu.HBM)] * 2,
-        out_specs=(vmem,) * slots + (smem,) + (vmem,) * 2,
+        in_specs=[smem, vmem, pl.BlockSpec(memory_space=pltpu.HBM)],
+        out_specs=(vmem,) * slots + (smem, vmem),
         scratch_shapes=[
             pltpu.VMEM((8, fun_dev * support), f32),
             pltpu.VMEM(flat.shape, bf16),
-            pltpu.VMEM(potential.shape, f32),
-            pltpu.SemaphoreType.DMA((2,)),
+            pltpu.SemaphoreType.DMA,
         ],
         compiler_params=pltpu.CompilerParams(vmem_limit_bytes=52 * 2**20),
         name="pack",
-    )(me, centers, flat, potential)
+    )(me, centers, flat)
     arrived = all_sent(dict(zip(now + [last], packed)), now, last, 1)
 
     columns, places, active, local = pl.pallas_call(
@@ -533,22 +523,22 @@
     sources = [arrived[REACH - e] for e in range(slots) if e != REACH]
     read_rows = [rows_of[REACH - e] for e in range(slots)]
     level_sizes = [level_rows(part + 1)[1] - level_rows(part + 1)[0] for part in range(REACH)]
+    level_sizes = [level_rows(part + 1)[1] - level_rows(part + 1)[0] for part in range(REACH)]
     exact_rows = [rows[2 * REACH - e] for e in range(slots)]
     band = (fun_dev, 2 * reading)
-    pieces, region, *grams = pl.pallas_call(
-        functools.partial(unpack_kernel, (fun_dev, box_dev, reading, volume, exact_rows, read_rows, blocks)),
-        out_shape=(
-            jax.ShapeDtypeStruct((boxes, wide, points), bf16),
-            jax.ShapeDtypeStruct((128, points), bf16),
-        )
-        + tuple(jax.ShapeDtypeStruct(band, f32) for _ in range(slots)),
+    with_potential = (fun_dev + 16 * (points // (2 * reading)), 2 * reading)
+    assert box_dev <= 16
+    pieces, *grams = pl.pallas_call(
+        functools.partial(unpack_kernel, (fun_dev, reading, volume, read_rows)),
+        out_shape=(jax.ShapeDtypeStruct((boxes, wide, points), bf16),)
+        + tuple(jax.ShapeDtypeStruct(with_potential if e < REACH else band, f32) for e in range(slots)),
         in_specs=[smem, smem] + [vmem] * (3 + len(sources)),
-        out_specs=(vmem,) * (2 + slots),
+        out_specs=(vmem,) * (1 + slots),
         scratch_shapes=[pltpu.VMEM((wide, band_lanes(fun_dev, reading)), f32)]
         + [pltpu.VMEM((size, size), f32) for size in level_sizes],
         compiler_params=limit,
         name="unpack",
-    )(cut, active, columns, own_region, local, *sources)
+    )(cut, active, columns, potential, local, *sources)
 
     summed = sent({k: grams[REACH + k] for k in one_way}, one_way, 1)
     gram_band, mixing_rows = pl.pallas_call(
@@ -559,6 +549,14 @@
         compiler_params=limit,
         name="sum",
     )(grams[REACH], *[summed[k] for k in one_way])
+    region = pl.pallas_call(
+        functools.partial(region_kernel, fun_dev),
+        out_shape=jax.ShapeDtypeStruct((128, points), bf16),
+        in_specs=[smem] + [vmem] * blocks,
+        out_specs=vmem,
+        compiler_params=limit,
+        name="region",
+    )(cut, potential, *[summed[-t] for t in range(1, blocks)])
     mixing_of = sent({k: mixing_rows for k in one_way}, one_way, 1)
     mixing_of[0] = mixing_rows
     band_order = one_way + [0]
@@ -576,22 +574,19 @@
         name="mix",
     )(cut, active, places, pieces, region, kinetic, *[mixing_of[k] for k in band_order])
 
-    ready = {}
-    for k in now + [last, 0]:
-        here, at_box = mixed[REACH - k], mixed[slots + REACH - k]
-        if abs(k) == 1:
-            ready[k] = here
-            continue
-        near_by = jnp.dot(at_box, region, preferred_element_type=f32)
-        applied = jnp.dot(here, kinetic, preferred_element_type=f32)
-        ready[k] = (applied + near_by * here.astype(f32)).astype(bf16)
+    ready = {k: mixed[REACH - k] for k in now + [last]}
+    here, at_box = mixed[REACH], mixed[slots + REACH]
+    near_by = jnp.dot(at_box, region, preferred_element_type=f32)
+    applied = jnp.dot(here, kinetic, preferred_element_type=f32)
     returned = all_sent(ready, now, last, -1)
-    returned[0] = ready[0]
+    returned[0] = (applied + near_by * here.astype(f32)).astype(bf16)
 
     bases = {k: sum(back[: k + REACH]) for k in offsets}
-    early, late = [0] + now[:2], now[2:] + [last]
+    early, late = [0, -1, 1], [k for k in offsets if abs(k) > 1]
+    early_groups = [(bases[k], [at]) for at, k in enumerate(early)]
+    late_groups = [(bases[-REACH], list(range(REACH - 1))), (bases[2], list(range(REACH - 1, 2 * REACH - 2)))]
     begun = pl.pallas_call(
-        functools.partial(early_kernel, [bases[k] for k in early]),
+        functools.partial(early_kernel, early_groups),
         out_shape=jax.ShapeDtypeStruct(flat.shape, bf16),
         in_specs=[vmem] * (1 + len(early)),
         out_specs=vmem,
@@ -599,7 +594,7 @@
         name="early",
     )(home_row, *[returned[k] for k in early])
     filtered = pl.pallas_call(
-        functools.partial(home_kernel, [bases[k] for k in late]),
+        functools.partial(home_kernel, late_groups),
         out_shape=jax.ShapeDtypeStruct(flat.shape, bf16),
         in_specs=[vmem] * (2 + len(late)),
         out_specs=pl.BlockSpec(memory_space=pl.ANY),

time: 121 us -> 118 us (0.975)
  matrix products: 4.62 us -> 1.7 us
  waiting for transfers between devices: 35.6 us -> 36.9 us
    dot_general x5 -> x1, matrix products: 3.39 us -> 1.28 us  [on_device(): applied = jnp.dot(here, kinetic, preferred_element_type=f32)]
    pallas_call x3 -> x4, Pallas kernels: 12.6 us -> 11 us  [the longest x1 5.82 us: on_device(): pl.pallas_call(functools.partial(unpack_kernel, (fun_dev, reading, volume...]
    ppermute x24, waiting for transfers between devices: 35.6 us -> 36.9 us  [passed_along(): return lax.ppermute(value, AXES, pairs)]
    pallas_call x1, Pallas kernels: 8.45 us -> 9.7 us  [on_device(): pl.pallas_call(functools.partial(mix_kernel, (fun_dev, reading, band_orde...]
  transfers between devices with their start and end apart: 24 -> 24, of which waited for: 10 -> 8; matrix products, arithmetic and copies ran while one was open for 3% -> 1% of each run, Pallas kernels for 4% -> 5%
where the time goes in v4:
time: 118 us
  starting transfers between devices  48.9 us (41%)
  waiting for transfers between devices  36.9 us (31%)
  Pallas kernels  28.5 us (24%)
  matrix products  1.7 us (1%)
    ppermute x24, starting transfers between devices, passed_along(): return lax.ppermute(value, AXES, pairs)  48.9 us
    ppermute x24, waiting for transfers between devices, passed_along(): return lax.ppermute(value, AXES, pairs)  36.9 us
    pallas_call x1, Pallas kernels, on_device(): pl.pallas_call(functools.partial(mix_kernel, (fun_dev, reading, band_orde...  9.7 us
    pallas_call x1, Pallas kernels, on_device(): pl.pallas_call(functools.partial(unpack_kernel, (fun_dev, reading, volume...  5.82 us
    pallas_call x1, Pallas kernels, on_device(): pl.pallas_call(functools.partial(pack_kernel, (fun_dev, support, devices,...  4.45 us
    pallas_call x1, Pallas kernels, on_device(): pl.pallas_call(functools.partial(table_kernel, (fun_dev, support, halo, b...  2.79 us
  transfers between devices with their start and end apart: 24, of which 8 were waited for; matrix products, arithmetic and copies ran while one was open for 1% of the time, Pallas kernels for 5%

profile of v4, /device:TPU:1, one launch (start us, length us, event | category | flops | bytes accessed | tf_op | source)
XLA Modules:
  0.0 117.9 jit_solution(4959536898730334842)
XLA Ops:
  1.5 4.5 %pack.1 = (bf16[256,1024]{1,0:T(8,128)(2,1)}, bf16[240,1024]{1,0:T(8,128)(2,1)S(1)}, bf16[160,1024]{1,0:T(8,128)(2,1)S(1)}, bf16[160,1024]{1,0:T(8,128)(2,1)S(1)...) custom-call(s32[1]{0:T(128)} %bitcast.me_ref, ...), custom_call_target="tpu_custom_call" | custom-call | tf_op jit(solution)/shard_map/pack/pallas_call | solution.py:488
  6.0 2.6 %collective-permute-start.2 = (bf16[240,1024]{1,0:T(8,128)(2,1)S(1)}, bf16[240,1024]{1,0:T(8,128)(2,1)S(1)}, u32[]{:S(2)}, u32[]{:S(2)}) collective-permute-start(bf16[240,1024]{1,0:T(8,128)(2,1)S(1)} %get-tuple-element.46), channel_id=1, source_target_pairs={{0,1},{1,2},{2,3},{3,4},{4,5},{5,6},{6,7},{7,8},{8,9},{9,10},{10,1... | collective-permute-start | bytes 1474568 | tf_op jit(solution)/shard_map/ppermute | solution.py:21
  8.6 2.0 %collective-permute-start.1 = (bf16[160,1024]{1,0:T(8,128)(2,1)S(1)}, bf16[160,1024]{1,0:T(8,128)(2,1)S(1)}, u32[]{:S(2)}, u32[]{:S(2)}) collective-permute-start(bf16[160,1024]{1,0:T(8,128)(2,1)S(1)} %get-tuple-element.45), channel_id=1, source_target_pairs={{0,2},{1,3},{2,4},{3,5},{4,6},{5,7},{6,8},{7,9},{8,10},{9,11},{10,... | collective-permute-start | bytes 983048 | tf_op jit(solution)/shard_map/ppermute | solution.py:21
  10.7 6.7 %collective-permute-start.4 = (bf16[160,1024]{1,0:T(8,128)(2,1)S(1)}, bf16[160,1024]{1,0:T(8,128)(2,1)S(1)}, u32[]{:S(2)}, u32[]{:S(2)}) collective-permute-start(bf16[160,1024]{1,0:T(8,128)(2,1)S(1)} %get-tuple-element.50), channel_id=1, source_target_pairs={{0,30},{1,31},{2,0},{3,1},{4,2},{5,3},{6,4},{7,5},{8,6},{9,7},{10,... | collective-permute-start | bytes 983048 | tf_op jit(solution)/shard_map/ppermute | solution.py:21
  17.4 2.6 %collective-permute-done.3.refs_3_ = bf16[256,1024]{1,0:T(8,128)(2,1)S(1)} collective-permute-done((bf16[256,1024]{1,0:T(8,128)(2,1)}, bf16[256,1024]{1,0:T(8,128)(2,1)S(1)}, u32[]{:S(2)}, u32[]{:S(2)}) %collective-permute-start.3) | collective-permute-done | bytes 524320 | tf_op jit(solution)/shard_map/ppermute | solution.py:21
  19.9 16.1 %collective-permute-start.5 = (bf16[48,1024]{1,0:T(8,128)(2,1)S(1)}, bf16[48,1024]{1,0:T(8,128)(2,1)S(1)}, u32[]{:S(2)}, u32[]{:S(2)}) collective-permute-start(bf16[48,1024]{1,0:T(8,128)(2,1)S(1)} %get-tuple-element.51), channel_id=1, source_target_pairs={{0,29},{1,30},{2,31},{3,0},{4,1},{5,2},{6,3},{7,4},{8,5},{9,6},{10... | collective-permute-start | bytes 294920 | tf_op jit(solution)/shard_map/ppermute | solution.py:21
  36.0 2.8 %tables.1 = (f32[224,128]{1,0:T(8,128)S(1)}, f32[3,8,256]{2,1,0:T(8,128)S(1)}, s32[24]{0:T(128)S(1)}, bf16[24,32,1024]{2,1,0:T(8,128)(2,1)S(1)}) custom-call(s32[8]{0:T(128)S(1)} %get-tuple-element.38.cut_ref, f32[512,128]{1,0:T(8,128)S(1)} %get-tuple-element.39.near_ref, bf16[768,1024]{1,0:T(8,128)(2,1)S(1)} %bitcast.8), custom_call_target="tpu_custom_call" | custom-call | tf_op jit(solution)/shard_map/tables/pallas_call | solution.py:508
  38.9 5.8 %unpack.1 = (bf16[24,224,1024]{2,1,0:T(8,128)(2,1)S(1)}, f32[88,256]{1,0:T(8,128)S(1)}, f32[88,256]{1,0:T(8,128)S(1)}, f32[88,256]{1,0:T(8,128)S(1)}, f32[24,256...) custom-call(s32[8]{0:T(128)S(1)} %get-tuple-element.38.cut_ref, ...), custom_call_target="tpu_custom_call" | custom-call | tf_op jit(solution)/shard_map/unpack/pallas_call | solution.py:531
  44.7 1.9 %collective-permute-start.6 = (f32[88,256]{1,0:T(8,128)S(1)}, f32[88,256]{1,0:T(8,128)S(1)}, u32[]{:S(2)}, u32[]{:S(2)}) collective-permute-start(f32[88,256]{1,0:T(8,128)S(1)} %get-tuple-element.53), channel_id=1, source_target_pairs={{0,31},{1,0},{2,1},{3,2},{4,3},{5,4},{6,5},{7,6},{8,7},{9,8},{10,9... | collective-permute-start | bytes 270344 | tf_op jit(solution)/shard_map/ppermute | solution.py:21
  46.7 3.1 %collective-permute-start.7 = (f32[88,256]{1,0:T(8,128)S(1)}, f32[88,256]{1,0:T(8,128)S(1)}, u32[]{:S(2)}, u32[]{:S(2)}) collective-permute-start(f32[88,256]{1,0:T(8,128)S(1)} %get-tuple-element.54), channel_id=1, source_target_pairs={{0,30},{1,31},{2,0},{3,1},{4,2},{5,3},{6,4},{7,5},{8,6},{9,7},{10,... | collective-permute-start | bytes 270344 | tf_op jit(solution)/shard_map/ppermute | solution.py:21
  49.8 1.8 %collective-permute-start.8 = (f32[88,256]{1,0:T(8,128)S(1)}, f32[88,256]{1,0:T(8,128)S(1)}, u32[]{:S(2)}, u32[]{:S(2)}) collective-permute-start(f32[88,256]{1,0:T(8,128)S(1)} %get-tuple-element.55), channel_id=1, source_target_pairs={{0,29},{1,30},{2,31},{3,0},{4,1},{5,2},{6,3},{7,4},{8,5},{9,6},{10... | collective-permute-start | bytes 270344 | tf_op jit(solution)/shard_map/ppermute | solution.py:21
  52.3 6.1 %collective-permute-done.9.refs_1_ = f32[24,256]{1,0:T(8,128)S(1)} collective-permute-done((f32[24,256]{1,0:T(8,128)S(1)}, f32[24,256]{1,0:T(8,128)S(1)}, u32[]{:S(2)}, u32[]{:S(2)}) %collective-permute-start.9) | collective-permute-done | bytes 24608 | tf_op jit(solution)/shard_map/ppermute | solution.py:21
  60.3 4.1 %collective-permute-start.17 = (bf16[32,256]{1,0:T(8,128)(2,1)S(1)}, bf16[32,256]{1,0:T(8,128)(2,1)S(1)}, u32[]{:S(2)}, u32[]{:S(2)}) collective-permute-start(bf16[32,256]{1,0:T(8,128)(2,1)S(1)} %get-tuple-element.60.refs_6_), channel_id=1, source_target_pairs={{0,31},{1,0},{2,1},{3,2},{4,3},{5,4},{6,5},{7,6},{8,7},{9,8},{10,9... | collective-permute-start | bytes 49160 | tf_op jit(solution)/shard_map/ppermute | solution.py:21
  64.4 1.6 %collective-permute-start.14 = (bf16[32,256]{1,0:T(8,128)(2,1)S(1)}, bf16[32,256]{1,0:T(8,128)(2,1)S(1)}, u32[]{:S(2)}, u32[]{:S(2)}) collective-permute-start(bf16[32,256]{1,0:T(8,128)(2,1)S(1)} %get-tuple-element.60.refs_6_), channel_id=1, source_target_pairs={{0,1},{1,2},{2,3},{3,4},{4,5},{5,6},{6,7},{7,8},{8,9},{9,10},{10,1... | collective-permute-start | bytes 49160 | tf_op jit(solution)/shard_map/ppermute | solution.py:21
  66.0 1.3 %collective-permute-start.13 = (bf16[32,256]{1,0:T(8,128)(2,1)S(1)}, bf16[32,256]{1,0:T(8,128)(2,1)S(1)}, u32[]{:S(2)}, u32[]{:S(2)}) collective-permute-start(bf16[32,256]{1,0:T(8,128)(2,1)S(1)} %get-tuple-element.60.refs_6_), channel_id=1, source_target_pairs={{0,2},{1,3},{2,4},{3,5},{4,6},{5,7},{6,8},{7,9},{8,10},{9,11},{10,... | collective-permute-start | bytes 49160 | tf_op jit(solution)/shard_map/ppermute | solution.py:21
  69.2 3.0 %collective-permute-done.13.refs_1_ = bf16[32,256]{1,0:T(8,128)(2,1)S(1)} collective-permute-done((bf16[32,256]{1,0:T(8,128)(2,1)S(1)}, bf16[32,256]{1,0:T(8,128)(2,1)S(1)}, u32[]{:S(2)}, u32[]{:S(2)}) %collective-permute-start.13) | collective-permute-done | bytes 16416 | tf_op jit(solution)/shard_map/ppermute | solution.py:21
  72.2 2.0 %collective-permute-done.12.refs_0_ = bf16[32,256]{1,0:T(8,128)(2,1)S(1)} collective-permute-done((bf16[32,256]{1,0:T(8,128)(2,1)S(1)}, bf16[32,256]{1,0:T(8,128)(2,1)S(1)}, u32[]{:S(2)}, u32[]{:S(2)}) %collective-permute-start.12) | collective-permute-done | bytes 16416 | tf_op jit(solution)/shard_map/ppermute | solution.py:21
  74.3 9.7 %mix.1 = (bf16[48,1024]{1,0:T(8,128)(2,1)S(1)}, bf16[160,1024]{1,0:T(8,128)(2,1)S(1)}, bf16[240,1024]{1,0:T(8,128)(2,1)S(1)}, bf16[512,1024]{1,0:T(8,128)(2,1)S(...) custom-call(s32[8]{0:T(128)S(1)} %get-tuple-element.38.cut_ref, ...), custom_call_target="tpu_custom_call" | custom-call | tf_op jit(solution)/shard_map/mix/pallas_call | solution.py:566
  85.8 4.0 %collective-permute-start.22 = (bf16[160,1024]{1,0:T(8,128)(2,1)S(1)}, bf16[160,1024]{1,0:T(8,128)(2,1)S(1)}, u32[]{:S(2)}, u32[]{:S(2)}) collective-permute-start(bf16[160,1024]{1,0:T(8,128)(2,1)S(1)} %get-tuple-element.69), channel_id=1, source_target_pairs={{0,30},{1,31},{2,0},{3,1},{4,2},{5,3},{6,4},{7,5},{8,6},{9,7},{10,... | collective-permute-start | bytes 983048 | tf_op jit(solution)/shard_map/ppermute | solution.py:21
  90.6 17.2 %collective-permute-done.18.refs_1_ = bf16[256,1024]{1,0:T(8,128)(2,1)S(1)} collective-permute-done((bf16[256,1024]{1,0:T(8,128)(2,1)S(1)}, bf16[256,1024]{1,0:T(8,128)(2,1)S(1)}, u32[]{:S(2)}, u32[]{:S(2)}) %collective-permute-start.18) | collective-permute-done | bytes 524320 | tf_op jit(solution)/shard_map/ppermute | solution.py:21
  109.1 1.7 %collective-permute-done.19.refs_2_ = bf16[240,1024]{1,0:T(8,128)(2,1)S(1)} collective-permute-done((bf16[240,1024]{1,0:T(8,128)(2,1)S(1)}, bf16[240,1024]{1,0:T(8,128)(2,1)S(1)}, u32[]{:S(2)}, u32[]{:S(2)}) %collective-permute-start.19) | collective-permute-done | bytes 491552 | tf_op jit(solution)/shard_map/ppermute | solution.py:21
  110.7 2.0 %early.1.early_ref = bf16[768,1024]{1,0:T(8,128)(2,1)S(1)} custom-call(f32[1,768]{1,0:T(1,128)S(1)} %get-tuple-element.37.home_ref, bf16[512,1024]{1,0:T(8,128)(2,1)S(1)} %add_convert_fusion.refs_0_, bf16[256,1024]{1,0:T(8,128)(2,1)S(1)} %collective-permute-done.18.refs_1_, bf16[240,1024]{1,0:T(8,128)(2,1)S(1)} %collective-permute-done.19.refs_2_), custom_call_target="tpu_custom_call" | custom-call | tf_op jit(solution)/shard_map/early/pallas_call | solution.py:588
  112.8 3.0 %collective-permute-done.20.refs_0_ = bf16[48,1024]{1,0:T(8,128)(2,1)S(1)} collective-permute-done((bf16[48,1024]{1,0:T(8,128)(2,1)S(1)}, bf16[48,1024]{1,0:T(8,128)(2,1)S(1)}, u32[]{:S(2)}, u32[]{:S(2)}) %collective-permute-start.20) | collective-permute-done | bytes 98336 | tf_op jit(solution)/shard_map/ppermute | solution.py:21
  115.8 1.9 %home.1 = bf16[768,1024]{1,0:T(8,128)(2,1)} custom-call(f32[1,768]{1,0:T(1,128)S(1)} %get-tuple-element.37.home_ref, bf16[768,1024]{1,0:T(8,128)(2,1)S(1)} %early.1.early_ref, bf16[48,1024]{1,0:T(8,128)(2,1)S(1)} %collective-permute-done.20.refs_0_, bf16[160,1024]{1,0:T(8,128)(2,1)S(1)} %collective-permute-done.21.refs_1_, ...), custom_call_target="tpu_custom_call" | custom-call | tf_op jit(solution)/shard_map/home/pallas_call | solution.py:596
  (42 shorter events, 9.1 us)
Async XLA Ops:
  5.9 14.0 %collective-permute-start.3 = (bf16[256,1024]{1,0:T(8,128)(2,1)}, bf16[256,1024]{1,0:T(8,128)(2,1)S(1)}, u32[]{:S(2)}, u32[]{:S(2)}) collective-permute-start(bf16[256,1024]{1,0:T(8,128)(2,1)} %get-tuple-element.48), channel_id=1, source_target_pairs={{0,31},{1,0},{2,1},{3,2},{4,3},{5,4},{6,5},{7,6},{8,7},{9,8},{10,9... | collective-permute-start | bytes 1572872 | tf_op jit(solution)/shard_map/ppermute | solution.py:21
  6.0 32.8 %collective-permute-start.2 = (bf16[240,1024]{1,0:T(8,128)(2,1)S(1)}, bf16[240,1024]{1,0:T(8,128)(2,1)S(1)}, u32[]{:S(2)}, u32[]{:S(2)}) collective-permute-start(bf16[240,1024]{1,0:T(8,128)(2,1)S(1)} %get-tuple-element.46), channel_id=1, source_target_pairs={{0,1},{1,2},{2,3},{3,4},{4,5},{5,6},{6,7},{7,8},{8,9},{9,10},{10,1... | collective-permute-start | bytes 1474568 | tf_op jit(solution)/shard_map/ppermute | solution.py:21
  8.6 30.2 %collective-permute-start.1 = (bf16[160,1024]{1,0:T(8,128)(2,1)S(1)}, bf16[160,1024]{1,0:T(8,128)(2,1)S(1)}, u32[]{:S(2)}, u32[]{:S(2)}) collective-permute-start(bf16[160,1024]{1,0:T(8,128)(2,1)S(1)} %get-tuple-element.45), channel_id=1, source_target_pairs={{0,2},{1,3},{2,4},{3,5},{4,6},{5,7},{6,8},{7,9},{8,10},{9,11},{10,... | collective-permute-start | bytes 983048 | tf_op jit(solution)/shard_map/ppermute | solution.py:21
  10.7 28.2 %collective-permute-start.4 = (bf16[160,1024]{1,0:T(8,128)(2,1)S(1)}, bf16[160,1024]{1,0:T(8,128)(2,1)S(1)}, u32[]{:S(2)}, u32[]{:S(2)}) collective-permute-start(bf16[160,1024]{1,0:T(8,128)(2,1)S(1)} %get-tuple-element.50), channel_id=1, source_target_pairs={{0,30},{1,31},{2,0},{3,1},{4,2},{5,3},{6,4},{7,5},{8,6},{9,7},{10,... | collective-permute-start | bytes 983048 | tf_op jit(solution)/shard_map/ppermute | solution.py:21
  17.3 21.5 %collective-permute-start = (bf16[48,1024]{1,0:T(8,128)(2,1)S(1)}, bf16[48,1024]{1,0:T(8,128)(2,1)S(1)}, u32[]{:S(2)}, u32[]{:S(2)}) collective-permute-start(bf16[48,1024]{1,0:T(8,128)(2,1)S(1)} %get-tuple-element.44), channel_id=1, source_target_pairs={{0,3},{1,4},{2,5},{3,6},{4,7},{5,8},{6,9},{7,10},{8,11},{9,12},{10... | collective-permute-start | bytes 294920 | tf_op jit(solution)/shard_map/ppermute | solution.py:21
  19.9 18.9 %collective-permute-start.5 = (bf16[48,1024]{1,0:T(8,128)(2,1)S(1)}, bf16[48,1024]{1,0:T(8,128)(2,1)S(1)}, u32[]{:S(2)}, u32[]{:S(2)}) collective-permute-start(bf16[48,1024]{1,0:T(8,128)(2,1)S(1)} %get-tuple-element.51), channel_id=1, source_target_pairs={{0,29},{1,30},{2,31},{3,0},{4,1},{5,2},{6,3},{7,4},{8,5},{9,6},{10... | collective-permute-start | bytes 294920 | tf_op jit(solution)/shard_map/ppermute | solution.py:21
  44.7 15.0 %collective-permute-start.6 = (f32[88,256]{1,0:T(8,128)S(1)}, f32[88,256]{1,0:T(8,128)S(1)}, u32[]{:S(2)}, u32[]{:S(2)}) collective-permute-start(f32[88,256]{1,0:T(8,128)S(1)} %get-tuple-element.53), channel_id=1, source_target_pairs={{0,31},{1,0},{2,1},{3,2},{4,3},{5,4},{6,5},{7,6},{8,7},{9,8},{10,9... | collective-permute-start | bytes 270344 | tf_op jit(solution)/shard_map/ppermute | solution.py:21
  46.7 13.0 %collective-permute-start.7 = (f32[88,256]{1,0:T(8,128)S(1)}, f32[88,256]{1,0:T(8,128)S(1)}, u32[]{:S(2)}, u32[]{:S(2)}) collective-permute-start(f32[88,256]{1,0:T(8,128)S(1)} %get-tuple-element.54), channel_id=1, source_target_pairs={{0,30},{1,31},{2,0},{3,1},{4,2},{5,3},{6,4},{7,5},{8,6},{9,7},{10,... | collective-permute-start | bytes 270344 | tf_op jit(solution)/shard_map/ppermute | solution.py:21
  49.8 9.9 %collective-permute-start.8 = (f32[88,256]{1,0:T(8,128)S(1)}, f32[88,256]{1,0:T(8,128)S(1)}, u32[]{:S(2)}, u32[]{:S(2)}) collective-permute-start(f32[88,256]{1,0:T(8,128)S(1)} %get-tuple-element.55), channel_id=1, source_target_pairs={{0,29},{1,30},{2,31},{3,0},{4,1},{5,2},{6,3},{7,4},{8,5},{9,6},{10... | collective-permute-start | bytes 270344 | tf_op jit(solution)/shard_map/ppermute | solution.py:21
  51.6 6.8 %collective-permute-start.9 = (f32[24,256]{1,0:T(8,128)S(1)}, f32[24,256]{1,0:T(8,128)S(1)}, u32[]{:S(2)}, u32[]{:S(2)}) collective-permute-start(f32[24,256]{1,0:T(8,128)S(1)} %get-tuple-element.57), channel_id=1, source_target_pairs={{0,3},{1,4},{2,5},{3,6},{4,7},{5,8},{6,9},{7,10},{8,11},{9,12},{10... | collective-permute-start | bytes 73736 | tf_op jit(solution)/shard_map/ppermute | solution.py:21
  51.6 6.9 %collective-permute-start.10 = (f32[24,256]{1,0:T(8,128)S(1)}, f32[24,256]{1,0:T(8,128)S(1)}, u32[]{:S(2)}, u32[]{:S(2)}) collective-permute-start(f32[24,256]{1,0:T(8,128)S(1)} %get-tuple-element.58), channel_id=1, source_target_pairs={{0,2},{1,3},{2,4},{3,5},{4,6},{5,7},{6,8},{7,9},{8,10},{9,11},{10,... | collective-permute-start | bytes 73736 | tf_op jit(solution)/shard_map/ppermute | solution.py:21
  58.5 1.2 %collective-permute-start.11 = (f32[24,256]{1,0:T(8,128)S(1)}, f32[24,256]{1,0:T(8,128)S(1)}, u32[]{:S(2)}, u32[]{:S(2)}) collective-permute-start(f32[24,256]{1,0:T(8,128)S(1)} %get-tuple-element.59), channel_id=1, source_target_pairs={{0,1},{1,2},{2,3},{3,4},{4,5},{5,6},{6,7},{7,8},{8,9},{9,10},{10,1... | collective-permute-start | bytes 73736 | tf_op jit(solution)/shard_map/ppermute | solution.py:21
  60.3 7.0 %collective-permute-start.17 = (bf16[32,256]{1,0:T(8,128)(2,1)S(1)}, bf16[32,256]{1,0:T(8,128)(2,1)S(1)}, u32[]{:S(2)}, u32[]{:S(2)}) collective-permute-start(bf16[32,256]{1,0:T(8,128)(2,1)S(1)} %get-tuple-element.60.refs_6_), channel_id=1, source_target_pairs={{0,31},{1,0},{2,1},{3,2},{4,3},{5,4},{6,5},{7,6},{8,7},{9,8},{10,9... | collective-permute-start | bytes 49160 | tf_op jit(solution)/shard_map/ppermute | solution.py:21
  64.4 4.8 %collective-permute-start.16 = (bf16[32,256]{1,0:T(8,128)(2,1)S(1)}, bf16[32,256]{1,0:T(8,128)(2,1)S(1)}, u32[]{:S(2)}, u32[]{:S(2)}) collective-permute-start(bf16[32,256]{1,0:T(8,128)(2,1)S(1)} %get-tuple-element.60.refs_6_), channel_id=1, source_target_pairs={{0,30},{1,31},{2,0},{3,1},{4,2},{5,3},{6,4},{7,5},{8,6},{9,7},{10,... | collective-permute-start | bytes 49160 | tf_op jit(solution)/shard_map/ppermute | solution.py:21
  64.4 4.8 %collective-permute-start.15 = (bf16[32,256]{1,0:T(8,128)(2,1)S(1)}, bf16[32,256]{1,0:T(8,128)(2,1)S(1)}, u32[]{:S(2)}, u32[]{:S(2)}) collective-permute-start(bf16[32,256]{1,0:T(8,128)(2,1)S(1)} %get-tuple-element.60.refs_6_), channel_id=1, source_target_pairs={{0,29},{1,30},{2,31},{3,0},{4,1},{5,2},{6,3},{7,4},{8,5},{9,6},{10... | collective-permute-start | bytes 49160 | tf_op jit(solution)/shard_map/ppermute | solution.py:21
  64.4 4.8 %collective-permute-start.14 = (bf16[32,256]{1,0:T(8,128)(2,1)S(1)}, bf16[32,256]{1,0:T(8,128)(2,1)S(1)}, u32[]{:S(2)}, u32[]{:S(2)}) collective-permute-start(bf16[32,256]{1,0:T(8,128)(2,1)S(1)} %get-tuple-element.60.refs_6_), channel_id=1, source_target_pairs={{0,1},{1,2},{2,3},{3,4},{4,5},{5,6},{6,7},{7,8},{8,9},{9,10},{10,1... | collective-permute-start | bytes 49160 | tf_op jit(solution)/shard_map/ppermute | solution.py:21
  66.0 6.2 %collective-permute-start.13 = (bf16[32,256]{1,0:T(8,128)(2,1)S(1)}, bf16[32,256]{1,0:T(8,128)(2,1)S(1)}, u32[]{:S(2)}, u32[]{:S(2)}) collective-permute-start(bf16[32,256]{1,0:T(8,128)(2,1)S(1)} %get-tuple-element.60.refs_6_), channel_id=1, source_target_pairs={{0,2},{1,3},{2,4},{3,5},{4,6},{5,7},{6,8},{7,9},{8,10},{9,11},{10,... | collective-permute-start | bytes 49160 | tf_op jit(solution)/shard_map/ppermute | solution.py:21
  67.3 6.9 %collective-permute-start.12 = (bf16[32,256]{1,0:T(8,128)(2,1)S(1)}, bf16[32,256]{1,0:T(8,128)(2,1)S(1)}, u32[]{:S(2)}, u32[]{:S(2)}) collective-permute-start(bf16[32,256]{1,0:T(8,128)(2,1)S(1)} %get-tuple-element.60.refs_6_), channel_id=1, source_target_pairs={{0,3},{1,4},{2,5},{3,6},{4,7},{5,8},{6,9},{7,10},{8,11},{9,12},{10... | collective-permute-start | bytes 49160 | tf_op jit(solution)/shard_map/ppermute | solution.py:21
  84.0 23.8 %collective-permute-start.18 = (bf16[256,1024]{1,0:T(8,128)(2,1)S(1)}, bf16[256,1024]{1,0:T(8,128)(2,1)S(1)}, u32[]{:S(2)}, u32[]{:S(2)}) collective-permute-start(bf16[256,1024]{1,0:T(8,128)(2,1)S(1)} %get-tuple-element.64), channel_id=1, source_target_pairs={{0,1},{1,2},{2,3},{3,4},{4,5},{5,6},{6,7},{7,8},{8,9},{9,10},{10,1... | collective-permute-start | bytes 1572872 | tf_op jit(solution)/shard_map/ppermute | solution.py:21
  84.8 28.0 %collective-permute-start.23 = (bf16[48,1024]{1,0:T(8,128)(2,1)S(1)}, bf16[48,1024]{1,0:T(8,128)(2,1)S(1)}, u32[]{:S(2)}, u32[]{:S(2)}) collective-permute-start(bf16[48,1024]{1,0:T(8,128)(2,1)S(1)} %get-tuple-element.70), channel_id=1, source_target_pairs={{0,29},{1,30},{2,31},{3,0},{4,1},{5,2},{6,3},{7,4},{8,5},{9,6},{10... | collective-permute-start | bytes 294920 | tf_op jit(solution)/shard_map/ppermute | solution.py:21
  84.8 28.0 %collective-permute-start.21 = (bf16[160,1024]{1,0:T(8,128)(2,1)S(1)}, bf16[160,1024]{1,0:T(8,128)(2,1)S(1)}, u32[]{:S(2)}, u32[]{:S(2)}) collective-permute-start(bf16[160,1024]{1,0:T(8,128)(2,1)S(1)} %get-tuple-element.68), channel_id=1, source_target_pairs={{0,2},{1,3},{2,4},{3,5},{4,6},{5,7},{6,8},{7,9},{8,10},{9,11},{10,... | collective-permute-start | bytes 983048 | tf_op jit(solution)/shard_map/ppermute | solution.py:21
  85.8 27.0 %collective-permute-start.22 = (bf16[160,1024]{1,0:T(8,128)(2,1)S(1)}, bf16[160,1024]{1,0:T(8,128)(2,1)S(1)}, u32[]{:S(2)}, u32[]{:S(2)}) collective-permute-start(bf16[160,1024]{1,0:T(8,128)(2,1)S(1)} %get-tuple-element.69), channel_id=1, source_target_pairs={{0,30},{1,31},{2,0},{3,1},{4,2},{5,3},{6,4},{7,5},{8,6},{9,7},{10,... | collective-permute-start | bytes 983048 | tf_op jit(solution)/shard_map/ppermute | solution.py:21
  89.9 20.9 %collective-permute-start.19 = (bf16[240,1024]{1,0:T(8,128)(2,1)S(1)}, bf16[240,1024]{1,0:T(8,128)(2,1)S(1)}, u32[]{:S(2)}, u32[]{:S(2)}) collective-permute-start(bf16[240,1024]{1,0:T(8,128)(2,1)S(1)} %get-tuple-element.66), channel_id=1, source_target_pairs={{0,31},{1,0},{2,1},{3,2},{4,3},{5,4},{6,5},{7,6},{8,7},{9,8},{10,9... | collective-permute-start | bytes 1474568 | tf_op jit(solution)/shard_map/ppermute | solution.py:21
  107.8 8.0 %collective-permute-start.20 = (bf16[48,1024]{1,0:T(8,128)(2,1)S(1)}, bf16[48,1024]{1,0:T(8,128)(2,1)S(1)}, u32[]{:S(2)}, u32[]{:S(2)}) collective-permute-start(bf16[48,1024]{1,0:T(8,128)(2,1)S(1)} %get-tuple-element.67), channel_id=1, source_target_pairs={{0,3},{1,4},{2,5},{3,6},{4,7},{5,8},{6,9},{7,10},{8,11},{9,12},{10... | collective-permute-start | bytes 294920 | tf_op jit(solution)/shard_map/ppermute | solution.py:21
  (4 other events, 109.8 us)

commit v5 on v4

--- a/solution.py
+++ b/solution.py
@@ -364,14 +364,21 @@
     mixing_ref[...] = jnp.concatenate([row, spare], axis=0).astype(jnp.bfloat16)
 
 
+def in_level(group, level):
+    at = [place for place, e in enumerate(group) if abs(e - REACH) <= level]
+    assert not at or at == list(range(at[0], at[-1] + 1))
+    return (at[0], at[-1] + 1) if at else (0, 0)
+
+
 def mix_kernel(plan, cut_ref, active_ref, place_ref, window_ref, region_ref, kinetic_ref, *refs):
-    fun_dev, reading, band_order = plan
+    fun_dev, reading, group, whole = plan
+    count = len(group)
+    bands = refs[:count]
+    outs = refs[count : 2 * count]
+    at_boxes = refs[2 * count : 3 * count]
+    mixed = refs[3 * count]
+    mixings = dict(zip([v for v in range(1, REACH + 1) if in_level(group, v)[1]], refs[3 * count + 1 :]))
     slots = 2 * REACH + 1
-    bands = dict(zip(band_order, refs[:slots]))
-    outs = refs[slots : 2 * slots]
-    at_boxes = refs[2 * slots : 3 * slots]
-    mixed = refs[3 * slots]
-    mixings = refs[3 * slots + 1 :]
     steps = window_ref.shape[0] // STEP
     width = cut_ref[REACH + 1] - cut_ref[REACH]
     for out, at_box in zip(outs, at_boxes):
@@ -379,50 +386,48 @@
         at_box[...] = jnp.zeros_like(at_box)
     lanes = band_lanes(fun_dev, reading)
     parts = []
-    for e in range(slots):
-        band = bands[REACH - e][...].astype(jnp.float32)
+    for e, band_ref in zip(group, bands):
+        band = band_ref[...].astype(jnp.float32)
         band = jnp.concatenate([band, jnp.zeros((SLOT, lanes - 2 * reading), jnp.float32)], axis=1)
-        parts.append(moved(skewed(band, 1), e * fun_dev - (reading - 1)))
-    dense = jnp.concatenate(parts, axis=0).astype(jnp.bfloat16)
-    for part, mixing in enumerate(mixings):
-        low, high = level_rows(part + 1)
+        parts.append(moved(skewed(band, 1), e * fun_dev - (reading - 1)).astype(jnp.bfloat16))
+    for level, mixing in mixings.items():
+        start, end = in_level(group, level)
         shape = (lanes, mixing.shape[1])
         column = function_of(shape, 1, fun_dev)
-        column = jnp.where(column >= 0, column + low // SLOT * fun_dev, -1)
+        column = jnp.where(column >= 0, column + level_rows(level)[0] // SLOT * fun_dev, -1)
         keep = one_hot(column == lax.broadcasted_iota(jnp.int32, shape, 0))
-        mixing[...] = times(dense[low:high], keep).astype(jnp.bfloat16)
+        mixing[...] = times(jnp.concatenate(parts[start:end], axis=0), keep).astype(jnp.bfloat16)
 
     @pl.loop(0, lax.div(width + STEP - 1, STEP))
     def _(step):
-        level = active_ref[slots * steps + step]
-        for part, mixing in enumerate(mixings):
-            @pl.when(level == part + 1)
+        for level, mixing in mixings.items():
+            @pl.when(active_ref[slots * steps + step] == level)
             def _():
-                low, high = level_rows(part + 1)
+                low, high = level_rows(level)
+                start, end = in_level(group, level)
                 for b in range(STEP):
                     here = window_ref[step * STEP + b, low:high]
-                    mixed[b, low:high] = times(mixing[...], here).astype(jnp.bfloat16)
+                    mixed[b, start * SLOT : end * SLOT] = times(mixing[...], here).astype(jnp.bfloat16)
         shape = (STEP * SLOT, at_boxes[0].shape[1])
         along = lax.broadcasted_iota(jnp.int32, shape, 0)
         box = lax.shift_right_logical(along, SLOT.bit_length() - 1) + step * STEP
         col = lax.broadcasted_iota(jnp.int32, shape, 1)
         boxes_of = one_hot((col == box) | (col == box + SLOT))
-        for e in range(slots):
+        for at, e in enumerate(group):
             @pl.when(active_ref[e * steps + step] > 0)
             def _():
                 place = place_ref[step, e : e + 1, :]
-                pick = one_hot(iota((outs[e].shape[0], STEP * SLOT), 0) == place)
-                part = mixed[:, e * SLOT : (e + 1) * SLOT, :].reshape(STEP * SLOT, mixed.shape[-1])
-                outs[e][...] += times(pick, part).astype(jnp.bfloat16)
-                at_boxes[e][...] += times(pick, boxes_of).astype(jnp.bfloat16)
-
-    for e in range(slots):
-        if e == REACH:
-            continue
-        here = outs[e][...]
-        applied = times(here, kinetic_ref[...])
-        near_by = times(at_boxes[e][...], region_ref[...])
-        outs[e][...] = (applied + near_by * here.astype(jnp.float32)).astype(jnp.bfloat16)
+                pick = one_hot(iota((outs[at].shape[0], STEP * SLOT), 0) == place)
+                part = mixed[:, at * SLOT : (at + 1) * SLOT, :].reshape(STEP * SLOT, mixed.shape[-1])
+                outs[at][...] += times(pick, part).astype(jnp.bfloat16)
+                at_boxes[at][...] += times(pick, boxes_of).astype(jnp.bfloat16)
+
+    for at, e in enumerate(group):
+        if e in whole:
+            here = outs[at][...]
+            applied = times(here, kinetic_ref[...])
+            near_by = times(at_boxes[at][...], region_ref[...])
+            outs[at][...] = (applied + near_by * here.astype(jnp.float32)).astype(jnp.bfloat16)
 
 
 def home_rows(bases, home_ref, sources, at, count):
@@ -559,27 +564,40 @@
     )(cut, potential, *[summed[-t] for t in range(1, blocks)])
     mixing_of = sent({k: mixing_rows for k in one_way}, one_way, 1)
     mixing_of[0] = mixing_rows
-    band_order = one_way + [0]
-
-    out_rows = [rows_of[REACH - e] for e in range(slots)]
-    shapes = [(r, points) for r in out_rows] + [(r, 128) for r in out_rows]
-    mixed = pl.pallas_call(
-        functools.partial(mix_kernel, (fun_dev, reading, band_order)),
-        out_shape=tuple(jax.ShapeDtypeStruct(shape, bf16) for shape in shapes),
-        in_specs=[smem, smem] + [vmem] * (4 + slots),
-        out_specs=(vmem,) * len(shapes),
-        scratch_shapes=[pltpu.VMEM((STEP, wide, points), bf16)]
-        + [pltpu.VMEM((size, size), bf16) for size in level_sizes],
-        compiler_params=limit,
-        name="mix",
-    )(cut, active, places, pieces, region, kinetic, *[mixing_of[k] for k in band_order])
-
-    ready = {k: mixed[REACH - k] for k in now + [last]}
-    here, at_box = mixed[REACH], mixed[slots + REACH]
-    near_by = jnp.dot(at_box, region, preferred_element_type=f32)
-    applied = jnp.dot(here, kinetic, preferred_element_type=f32)
-    returned = all_sent(ready, now, last, -1)
-    returned[0] = (applied + near_by * here.astype(f32)).astype(bf16)
+
+    ready, at_boxes = {}, {}
+    for group, whole in [([2, -2, REACH, -REACH], [2, -2, REACH, -REACH]), ([0, 1, -1], [1, -1])]:
+        group, whole = sorted(REACH - k for k in group), [REACH - k for k in whole]
+        shapes = [(rows_of[REACH - e], points) for e in group] + [(rows_of[REACH - e], 128) for e in group]
+        sizes = [
+            ((in_level(group, v)[1] - in_level(group, v)[0]) * SLOT, level_sizes[v - 1])
+            for v in range(1, REACH + 1)
+            if in_level(group, v)[1]
+        ]
+        if ready:
+            cut, *held = lax.optimization_barrier((cut, *[ready[k] for k in ready]))
+            ready = dict(zip(ready, held))
+        mixed = pl.pallas_call(
+            functools.partial(mix_kernel, (fun_dev, reading, group, whole)),
+            out_shape=tuple(jax.ShapeDtypeStruct(shape, bf16) for shape in shapes),
+            in_specs=[smem, smem] + [vmem] * (4 + len(group)),
+            out_specs=(vmem,) * len(shapes),
+            scratch_shapes=[pltpu.VMEM((STEP, len(group) * SLOT, points), bf16)]
+            + [pltpu.VMEM(size, bf16) for size in sizes],
+            compiler_params=limit,
+            cost_estimate=pl.CostEstimate(
+                flops=8 * wide * len(group) * SLOT * boxes * points, bytes_accessed=40 * 2**20, transcendentals=0
+            ),
+            name="mix",
+        )(cut, active, places, pieces, region, kinetic, *[mixing_of[REACH - e] for e in group])
+        for at, e in enumerate(group):
+            ready[REACH - e], at_boxes[REACH - e] = mixed[at], mixed[len(group) + at]
+            if e not in whole:
+                near_by = jnp.dot(at_boxes[REACH - e], region, preferred_element_type=f32)
+                applied = jnp.dot(mixed[at], kinetic, preferred_element_type=f32)
+                ready[REACH - e] = (applied + near_by * mixed[at].astype(f32)).astype(bf16)
+    returned = all_sent(ready, [2, -2, 1, -1, REACH], -REACH, -1)
+    returned[0] = ready[0]
 
     bases = {k: sum(back[: k + REACH]) for k in offsets}
     early, late = [0, -1, 1], [k for k in offsets if abs(k) > 1]

time: 118 us -> 113 us (0.958)
  the two profiles are of different devices: /device:TPU:1 before, /device:TPU:0 now
where the time goes in v5:
time: 113 us
  starting transfers between devices  55.9 us (49%)
  Pallas kernels  32.1 us (28%)
  waiting for transfers between devices  21.7 us (19%)
  matrix products  1.71 us (2%)
    ppermute x24, starting transfers between devices, passed_along(): return lax.ppermute(value, AXES, pairs)  55.9 us
    ppermute x24, waiting for transfers between devices, passed_along(): return lax.ppermute(value, AXES, pairs)  21.7 us
    pallas_call x2, Pallas kernels, on_device(): pl.pallas_call(functools.partial(mix_kernel, (fun_dev, reading, group, wh...  12.5 us
    pallas_call x1, Pallas kernels, on_device(): pl.pallas_call(functools.partial(unpack_kernel, (fun_dev, reading, volume...  6.57 us
    pallas_call x1, Pallas kernels, on_device(): pl.pallas_call(functools.partial(pack_kernel, (fun_dev, support, devices,...  4.45 us
    pallas_call x1, Pallas kernels, on_device(): pl.pallas_call(functools.partial(table_kernel, (fun_dev, support, halo, b...  2.79 us
  transfers between devices with their start and end apart: 24, of which 6 were waited for; matrix products, arithmetic and copies ran while one was open for 2% of the time, Pallas kernels for 16%

profile of v5, /device:TPU:0, one launch (start us, length us, event | category | flops | bytes accessed | tf_op | source)
XLA Modules:
  0.0 113.3 jit_solution(5757774316163531849)
XLA Ops:
  1.5 4.4 %pack.1 = (bf16[256,1024]{1,0:T(8,128)(2,1)}, bf16[240,1024]{1,0:T(8,128)(2,1)S(1)}, bf16[160,1024]{1,0:T(8,128)(2,1)S(1)}, bf16[160,1024]{1,0:T(8,128)(2,1)S(1)...) custom-call(s32[1]{0:T(128)} %bitcast.me_ref, ...), custom_call_target="tpu_custom_call" | custom-call | tf_op jit(solution)/shard_map/pack/pallas_call | solution.py:493
  5.9 6.4 %collective-permute-start.3 = (bf16[256,1024]{1,0:T(8,128)(2,1)}, bf16[256,1024]{1,0:T(8,128)(2,1)S(1)}, u32[]{:S(2)}, u32[]{:S(2)}) collective-permute-start(bf16[256,1024]{1,0:T(8,128)(2,1)} %get-tuple-element.53), channel_id=1, source_target_pairs={{0,31},{1,0},{2,1},{3,2},{4,3},{5,4},{6,5},{7,6},{8,7},{9,8},{10,9... | collective-permute-start | bytes 1572872 | tf_op jit(solution)/shard_map/ppermute | solution.py:21
  12.3 5.6 %collective-permute-start.4 = (bf16[160,1024]{1,0:T(8,128)(2,1)S(1)}, bf16[160,1024]{1,0:T(8,128)(2,1)S(1)}, u32[]{:S(2)}, u32[]{:S(2)}) collective-permute-start(bf16[160,1024]{1,0:T(8,128)(2,1)S(1)} %get-tuple-element.55), channel_id=1, source_target_pairs={{0,30},{1,31},{2,0},{3,1},{4,2},{5,3},{6,4},{7,5},{8,6},{9,7},{10,... | collective-permute-start | bytes 983048 | tf_op jit(solution)/shard_map/ppermute | solution.py:21
  18.0 2.3 %collective-permute-done.3.refs_3_ = bf16[256,1024]{1,0:T(8,128)(2,1)S(1)} collective-permute-done((bf16[256,1024]{1,0:T(8,128)(2,1)}, bf16[256,1024]{1,0:T(8,128)(2,1)S(1)}, u32[]{:S(2)}, u32[]{:S(2)}) %collective-permute-start.3) | collective-permute-done | bytes 524320 | tf_op jit(solution)/shard_map/ppermute | solution.py:21
  20.3 16.4 %collective-permute-start.5 = (bf16[48,1024]{1,0:T(8,128)(2,1)S(1)}, bf16[48,1024]{1,0:T(8,128)(2,1)S(1)}, u32[]{:S(2)}, u32[]{:S(2)}) collective-permute-start(bf16[48,1024]{1,0:T(8,128)(2,1)S(1)} %get-tuple-element.56), channel_id=1, source_target_pairs={{0,29},{1,30},{2,31},{3,0},{4,1},{5,2},{6,3},{7,4},{8,5},{9,6},{10... | collective-permute-start | bytes 294920 | tf_op jit(solution)/shard_map/ppermute | solution.py:21
  36.7 2.8 %tables.1 = (f32[224,128]{1,0:T(8,128)S(1)}, f32[3,8,256]{2,1,0:T(8,128)S(1)}, s32[24]{0:T(128)S(1)}, bf16[24,32,1024]{2,1,0:T(8,128)(2,1)S(1)}) custom-call(s32[8]{0:T(128)S(1)} %get-tuple-element.70.cut_ref, f32[512,128]{1,0:T(8,128)S(1)} %get-tuple-element.44.near_ref, bf16[768,1024]{1,0:T(8,128)(2,1)S(1)} %bitcast.8), custom_call_target="tpu_custom_call" | custom-call | tf_op jit(solution)/shard_map/tables/pallas_call | solution.py:513
  39.6 6.6 %unpack.1 = (bf16[24,224,1024]{2,1,0:T(8,128)(2,1)S(1)}, f32[88,256]{1,0:T(8,128)S(1)}, f32[88,256]{1,0:T(8,128)S(1)}, f32[88,256]{1,0:T(8,128)S(1)}, f32[24,256...) custom-call(s32[8]{0:T(128)S(1)} %get-tuple-element.70.cut_ref, ...), custom_call_target="tpu_custom_call" | custom-call | tf_op jit(solution)/shard_map/unpack/pallas_call | solution.py:536
  46.1 3.7 %collective-permute-start.6 = (f32[88,256]{1,0:T(8,128)S(1)}, f32[88,256]{1,0:T(8,128)S(1)}, u32[]{:S(2)}, u32[]{:S(2)}) collective-permute-start(f32[88,256]{1,0:T(8,128)S(1)} %get-tuple-element.58), channel_id=1, source_target_pairs={{0,31},{1,0},{2,1},{3,2},{4,3},{5,4},{6,5},{7,6},{8,7},{9,8},{10,9... | collective-permute-start | bytes 270344 | tf_op jit(solution)/shard_map/ppermute | solution.py:21
  52.6 1.9 %collective-permute-start.10 = (f32[24,256]{1,0:T(8,128)S(1)}, f32[24,256]{1,0:T(8,128)S(1)}, u32[]{:S(2)}, u32[]{:S(2)}) collective-permute-start(f32[24,256]{1,0:T(8,128)S(1)} %get-tuple-element.63), channel_id=1, source_target_pairs={{0,2},{1,3},{2,4},{3,5},{4,6},{5,7},{6,8},{7,9},{8,10},{9,11},{10,... | collective-permute-start | bytes 73736 | tf_op jit(solution)/shard_map/ppermute | solution.py:21
  54.5 2.3 %collective-permute-done.9.refs_1_ = f32[24,256]{1,0:T(8,128)S(1)} collective-permute-done((f32[24,256]{1,0:T(8,128)S(1)}, f32[24,256]{1,0:T(8,128)S(1)}, u32[]{:S(2)}, u32[]{:S(2)}) %collective-permute-start.9) | collective-permute-done | bytes 24608 | tf_op jit(solution)/shard_map/ppermute | solution.py:21
  60.0 3.6 %collective-permute-done.11.refs_3_ = f32[24,256]{1,0:T(8,128)S(1)} collective-permute-done((f32[24,256]{1,0:T(8,128)S(1)}, f32[24,256]{1,0:T(8,128)S(1)}, u32[]{:S(2)}, u32[]{:S(2)}) %collective-permute-start.11) | collective-permute-done | bytes 24608 | tf_op jit(solution)/shard_map/ppermute | solution.py:21
  64.3 2.1 %collective-permute-start.13 = (bf16[32,256]{1,0:T(8,128)(2,1)S(1)}, bf16[32,256]{1,0:T(8,128)(2,1)S(1)}, u32[]{:S(2)}, u32[]{:S(2)}) collective-permute-start(bf16[32,256]{1,0:T(8,128)(2,1)S(1)} %get-tuple-element.65.refs_1_), channel_id=1, source_target_pairs={{0,2},{1,3},{2,4},{3,5},{4,6},{5,7},{6,8},{7,9},{8,10},{9,11},{10,... | collective-permute-start | bytes 49160 | tf_op jit(solution)/shard_map/ppermute | solution.py:21
  66.4 2.1 %collective-permute-start.12 = (bf16[32,256]{1,0:T(8,128)(2,1)S(1)}, bf16[32,256]{1,0:T(8,128)(2,1)S(1)}, u32[]{:S(2)}, u32[]{:S(2)}) collective-permute-start(bf16[32,256]{1,0:T(8,128)(2,1)S(1)} %get-tuple-element.65.refs_1_), channel_id=1, source_target_pairs={{0,3},{1,4},{2,5},{3,6},{4,7},{5,8},{6,9},{7,10},{8,11},{9,12},{10... | collective-permute-start | bytes 49160 | tf_op jit(solution)/shard_map/ppermute | solution.py:21
  68.4 2.7 %collective-permute-start.17 = (bf16[32,256]{1,0:T(8,128)(2,1)S(1)}, bf16[32,256]{1,0:T(8,128)(2,1)S(1)}, u32[]{:S(2)}, u32[]{:S(2)}) collective-permute-start(bf16[32,256]{1,0:T(8,128)(2,1)S(1)} %get-tuple-element.65.refs_1_), channel_id=1, source_target_pairs={{0,31},{1,0},{2,1},{3,2},{4,3},{5,4},{6,5},{7,6},{8,7},{9,8},{10,9... | collective-permute-start | bytes 49160 | tf_op jit(solution)/shard_map/ppermute | solution.py:21
  72.4 4.8 %mix.2 = (bf16[48,1024]{1,0:T(8,128)(2,1)S(1)}, bf16[160,1024]{1,0:T(8,128)(2,1)S(1)}, bf16[160,1024]{1,0:T(8,128)(2,1)S(1)}, bf16[48,1024]{1,0:T(8,128)(2,1)S(1...) custom-call(s32[8]{0:T(128)S(1)} %get-tuple-element.70.cut_ref, ...), custom_call_target="tpu_custom_call" | custom-call | flops 5637144576 | bytes 41943040 | tf_op jit(solution)/shard_map/mix/pallas_call | solution.py:580
  77.3 1.9 %collective-permute-start.23 = (bf16[48,1024]{1,0:T(8,128)(2,1)S(1)}, bf16[48,1024]{1,0:T(8,128)(2,1)S(1)}, u32[]{:S(2)}, u32[]{:S(2)}) collective-permute-start(bf16[48,1024]{1,0:T(8,128)(2,1)S(1)} %get-tuple-element.80), channel_id=1, source_target_pairs={{0,29},{1,30},{2,31},{3,0},{4,1},{5,2},{6,3},{7,4},{8,5},{9,6},{10... | collective-permute-start | bytes 294920 | tf_op jit(solution)/shard_map/ppermute | solution.py:21
  79.2 2.0 %collective-permute-start.20 = (bf16[160,1024]{1,0:T(8,128)(2,1)S(1)}, bf16[160,1024]{1,0:T(8,128)(2,1)S(1)}, u32[]{:S(2)}, u32[]{:S(2)}) collective-permute-start(bf16[160,1024]{1,0:T(8,128)(2,1)S(1)} %get-tuple-element.76), channel_id=1, source_target_pairs={{0,30},{1,31},{2,0},{3,1},{4,2},{5,3},{6,4},{7,5},{8,6},{9,7},{10,... | collective-permute-start | bytes 983048 | tf_op jit(solution)/shard_map/ppermute | solution.py:21
  81.2 1.9 %collective-permute-start.22 = (bf16[160,1024]{1,0:T(8,128)(2,1)S(1)}, bf16[160,1024]{1,0:T(8,128)(2,1)S(1)}, u32[]{:S(2)}, u32[]{:S(2)}) collective-permute-start(bf16[160,1024]{1,0:T(8,128)(2,1)S(1)} %get-tuple-element.78), channel_id=1, source_target_pairs={{0,2},{1,3},{2,4},{3,5},{4,6},{5,7},{6,8},{7,9},{8,10},{9,11},{10,... | collective-permute-start | bytes 983048 | tf_op jit(solution)/shard_map/ppermute | solution.py:21
  83.2 7.7 %mix.3 = (bf16[240,1024]{1,0:T(8,128)(2,1)S(1)}, bf16[512,1024]{1,0:T(8,128)(2,1)S(1)}, bf16[256,1024]{1,0:T(8,128)(2,1)S(1)}, bf16[240,128]{1,0:T(8,128)(2,1)},...) custom-call(s32[8]{0:T(128)S(1)} %get-tuple-element.70.cut_ref, s32[24]{0:T(128)S(1)} %get-tuple-element.45.active_ref, ...), custom_call_target="tpu_custom_call" | custom-call | flops 4227858432 | bytes 41943040 | tf_op jit(solution)/shard_map/mix/pallas_call | solution.py:580
  90.9 4.9 %collective-permute-start.19 = (bf16[240,1024]{1,0:T(8,128)(2,1)S(1)}, bf16[240,1024]{1,0:T(8,128)(2,1)S(1)}, u32[]{:S(2)}, u32[]{:S(2)}) collective-permute-start(bf16[240,1024]{1,0:T(8,128)(2,1)S(1)} %get-tuple-element.74), channel_id=1, source_target_pairs={{0,31},{1,0},{2,1},{3,2},{4,3},{5,4},{6,5},{7,6},{8,7},{9,8},{10,9... | collective-permute-start | bytes 1474568 | tf_op jit(solution)/shard_map/ppermute | solution.py:21
  97.5 4.5 %collective-permute-done.19.refs_2_ = bf16[240,1024]{1,0:T(8,128)(2,1)S(1)} collective-permute-done((bf16[240,1024]{1,0:T(8,128)(2,1)S(1)}, bf16[240,1024]{1,0:T(8,128)(2,1)S(1)}, u32[]{:S(2)}, u32[]{:S(2)}) %collective-permute-start.19) | collective-permute-done | bytes 491552 | tf_op jit(solution)/shard_map/ppermute | solution.py:21
  102.1 7.0 %collective-permute-done.18.refs_1_ = bf16[256,1024]{1,0:T(8,128)(2,1)S(1)} collective-permute-done((bf16[256,1024]{1,0:T(8,128)(2,1)S(1)}, bf16[256,1024]{1,0:T(8,128)(2,1)S(1)}, u32[]{:S(2)}, u32[]{:S(2)}) %collective-permute-start.18) | collective-permute-done | bytes 524320 | tf_op jit(solution)/shard_map/ppermute | solution.py:21
  109.1 2.0 %early.1.early_ref = bf16[768,1024]{1,0:T(8,128)(2,1)S(1)} custom-call(f32[1,768]{1,0:T(1,128)S(1)} %get-tuple-element.42.home_ref, bf16[512,1024]{1,0:T(8,128)(2,1)S(1)} %add_convert_fusion.refs_0_, bf16[256,1024]{1,0:T(8,128)(2,1)S(1)} %collective-permute-done.18.refs_1_, bf16[240,1024]{1,0:T(8,128)(2,1)S(1)} %collective-permute-done.19.refs_2_), custom_call_target="tpu_custom_call" | custom-call | tf_op jit(solution)/shard_map/early/pallas_call | solution.py:606
  111.2 1.9 %home.1 = bf16[768,1024]{1,0:T(8,128)(2,1)} custom-call(f32[1,768]{1,0:T(1,128)S(1)} %get-tuple-element.42.home_ref, bf16[768,1024]{1,0:T(8,128)(2,1)S(1)} %early.1.early_ref, bf16[48,1024]{1,0:T(8,128)(2,1)S(1)} %collective-permute-done.21.refs_0_, bf16[160,1024]{1,0:T(8,128)(2,1)S(1)} %collective-permute-done.22.refs_1_, ...), custom_call_target="tpu_custom_call" | custom-call | tf_op jit(solution)/shard_map/home/pallas_call | solution.py:614
  (43 shorter events, 10.5 us)
Async XLA Ops:
  5.9 14.4 %collective-permute-start.3 = (bf16[256,1024]{1,0:T(8,128)(2,1)}, bf16[256,1024]{1,0:T(8,128)(2,1)S(1)}, u32[]{:S(2)}, u32[]{:S(2)}) collective-permute-start(bf16[256,1024]{1,0:T(8,128)(2,1)} %get-tuple-element.53), channel_id=1, source_target_pairs={{0,31},{1,0},{2,1},{3,2},{4,3},{5,4},{6,5},{7,6},{8,7},{9,8},{10,9... | collective-permute-start | bytes 1572872 | tf_op jit(solution)/shard_map/ppermute | solution.py:21
  12.3 27.2 %collective-permute-start.2 = (bf16[240,1024]{1,0:T(8,128)(2,1)S(1)}, bf16[240,1024]{1,0:T(8,128)(2,1)S(1)}, u32[]{:S(2)}, u32[]{:S(2)}) collective-permute-start(bf16[240,1024]{1,0:T(8,128)(2,1)S(1)} %get-tuple-element.51), channel_id=1, source_target_pairs={{0,1},{1,2},{2,3},{3,4},{4,5},{5,6},{6,7},{7,8},{8,9},{9,10},{10,1... | collective-permute-start | bytes 1474568 | tf_op jit(solution)/shard_map/ppermute | solution.py:21
  12.3 27.2 %collective-permute-start.1 = (bf16[160,1024]{1,0:T(8,128)(2,1)S(1)}, bf16[160,1024]{1,0:T(8,128)(2,1)S(1)}, u32[]{:S(2)}, u32[]{:S(2)}) collective-permute-start(bf16[160,1024]{1,0:T(8,128)(2,1)S(1)} %get-tuple-element.50), channel_id=1, source_target_pairs={{0,2},{1,3},{2,4},{3,5},{4,6},{5,7},{6,8},{7,9},{8,10},{9,11},{10,... | collective-permute-start | bytes 983048 | tf_op jit(solution)/shard_map/ppermute | solution.py:21
  12.3 27.2 %collective-permute-start.4 = (bf16[160,1024]{1,0:T(8,128)(2,1)S(1)}, bf16[160,1024]{1,0:T(8,128)(2,1)S(1)}, u32[]{:S(2)}, u32[]{:S(2)}) collective-permute-start(bf16[160,1024]{1,0:T(8,128)(2,1)S(1)} %get-tuple-element.55), channel_id=1, source_target_pairs={{0,30},{1,31},{2,0},{3,1},{4,2},{5,3},{6,4},{7,5},{8,6},{9,7},{10,... | collective-permute-start | bytes 983048 | tf_op jit(solution)/shard_map/ppermute | solution.py:21
  18.0 21.5 %collective-permute-start = (bf16[48,1024]{1,0:T(8,128)(2,1)S(1)}, bf16[48,1024]{1,0:T(8,128)(2,1)S(1)}, u32[]{:S(2)}, u32[]{:S(2)}) collective-permute-start(bf16[48,1024]{1,0:T(8,128)(2,1)S(1)} %get-tuple-element.49), channel_id=1, source_target_pairs={{0,3},{1,4},{2,5},{3,6},{4,7},{5,8},{6,9},{7,10},{8,11},{9,12},{10... | collective-permute-start | bytes 294920 | tf_op jit(solution)/shard_map/ppermute | solution.py:21
  20.3 19.2 %collective-permute-start.5 = (bf16[48,1024]{1,0:T(8,128)(2,1)S(1)}, bf16[48,1024]{1,0:T(8,128)(2,1)S(1)}, u32[]{:S(2)}, u32[]{:S(2)}) collective-permute-start(bf16[48,1024]{1,0:T(8,128)(2,1)S(1)} %get-tuple-element.56), channel_id=1, source_target_pairs={{0,29},{1,30},{2,31},{3,0},{4,1},{5,2},{6,3},{7,4},{8,5},{9,6},{10... | collective-permute-start | bytes 294920 | tf_op jit(solution)/shard_map/ppermute | solution.py:21
  46.1 17.5 %collective-permute-start.6 = (f32[88,256]{1,0:T(8,128)S(1)}, f32[88,256]{1,0:T(8,128)S(1)}, u32[]{:S(2)}, u32[]{:S(2)}) collective-permute-start(f32[88,256]{1,0:T(8,128)S(1)} %get-tuple-element.58), channel_id=1, source_target_pairs={{0,31},{1,0},{2,1},{3,2},{4,3},{5,4},{6,5},{7,6},{8,7},{9,8},{10,9... | collective-permute-start | bytes 270344 | tf_op jit(solution)/shard_map/ppermute | solution.py:21
  49.8 13.8 %collective-permute-start.7 = (f32[88,256]{1,0:T(8,128)S(1)}, f32[88,256]{1,0:T(8,128)S(1)}, u32[]{:S(2)}, u32[]{:S(2)}) collective-permute-start(f32[88,256]{1,0:T(8,128)S(1)} %get-tuple-element.59), channel_id=1, source_target_pairs={{0,30},{1,31},{2,0},{3,1},{4,2},{5,3},{6,4},{7,5},{8,6},{9,7},{10,... | collective-permute-start | bytes 270344 | tf_op jit(solution)/shard_map/ppermute | solution.py:21
  50.9 12.8 %collective-permute-start.8 = (f32[88,256]{1,0:T(8,128)S(1)}, f32[88,256]{1,0:T(8,128)S(1)}, u32[]{:S(2)}, u32[]{:S(2)}) collective-permute-start(f32[88,256]{1,0:T(8,128)S(1)} %get-tuple-element.60), channel_id=1, source_target_pairs={{0,29},{1,30},{2,31},{3,0},{4,1},{5,2},{6,3},{7,4},{8,5},{9,6},{10... | collective-permute-start | bytes 270344 | tf_op jit(solution)/shard_map/ppermute | solution.py:21
  50.9 5.9 %collective-permute-start.9 = (f32[24,256]{1,0:T(8,128)S(1)}, f32[24,256]{1,0:T(8,128)S(1)}, u32[]{:S(2)}, u32[]{:S(2)}) collective-permute-start(f32[24,256]{1,0:T(8,128)S(1)} %get-tuple-element.62), channel_id=1, source_target_pairs={{0,3},{1,4},{2,5},{3,6},{4,7},{5,8},{6,9},{7,10},{8,11},{9,12},{10... | collective-permute-start | bytes 73736 | tf_op jit(solution)/shard_map/ppermute | solution.py:21
  52.6 7.4 %collective-permute-start.10 = (f32[24,256]{1,0:T(8,128)S(1)}, f32[24,256]{1,0:T(8,128)S(1)}, u32[]{:S(2)}, u32[]{:S(2)}) collective-permute-start(f32[24,256]{1,0:T(8,128)S(1)} %get-tuple-element.63), channel_id=1, source_target_pairs={{0,2},{1,3},{2,4},{3,5},{4,6},{5,7},{6,8},{7,9},{8,10},{9,11},{10,... | collective-permute-start | bytes 73736 | tf_op jit(solution)/shard_map/ppermute | solution.py:21
  56.8 6.8 %collective-permute-start.11 = (f32[24,256]{1,0:T(8,128)S(1)}, f32[24,256]{1,0:T(8,128)S(1)}, u32[]{:S(2)}, u32[]{:S(2)}) collective-permute-start(f32[24,256]{1,0:T(8,128)S(1)} %get-tuple-element.64), channel_id=1, source_target_pairs={{0,1},{1,2},{2,3},{3,4},{4,5},{5,6},{6,7},{7,8},{8,9},{9,10},{10,1... | collective-permute-start | bytes 73736 | tf_op jit(solution)/shard_map/ppermute | solution.py:21
  64.3 8.0 %collective-permute-start.15 = (bf16[32,256]{1,0:T(8,128)(2,1)S(1)}, bf16[32,256]{1,0:T(8,128)(2,1)S(1)}, u32[]{:S(2)}, u32[]{:S(2)}) collective-permute-start(bf16[32,256]{1,0:T(8,128)(2,1)S(1)} %get-tuple-element.65.refs_1_), channel_id=1, source_target_pairs={{0,29},{1,30},{2,31},{3,0},{4,1},{5,2},{6,3},{7,4},{8,5},{9,6},{10... | collective-permute-start | bytes 49160 | tf_op jit(solution)/shard_map/ppermute | solution.py:21
  64.3 8.1 %collective-permute-start.14 = (bf16[32,256]{1,0:T(8,128)(2,1)S(1)}, bf16[32,256]{1,0:T(8,128)(2,1)S(1)}, u32[]{:S(2)}, u32[]{:S(2)}) collective-permute-start(bf16[32,256]{1,0:T(8,128)(2,1)S(1)} %get-tuple-element.65.refs_1_), channel_id=1, source_target_pairs={{0,30},{1,31},{2,0},{3,1},{4,2},{5,3},{6,4},{7,5},{8,6},{9,7},{10,... | collective-permute-start | bytes 49160 | tf_op jit(solution)/shard_map/ppermute | solution.py:21
  64.3 8.1 %collective-permute-start.13 = (bf16[32,256]{1,0:T(8,128)(2,1)S(1)}, bf16[32,256]{1,0:T(8,128)(2,1)S(1)}, u32[]{:S(2)}, u32[]{:S(2)}) collective-permute-start(bf16[32,256]{1,0:T(8,128)(2,1)S(1)} %get-tuple-element.65.refs_1_), channel_id=1, source_target_pairs={{0,2},{1,3},{2,4},{3,5},{4,6},{5,7},{6,8},{7,9},{8,10},{9,11},{10,... | collective-permute-start | bytes 49160 | tf_op jit(solution)/shard_map/ppermute | solution.py:21
  66.4 6.1 %collective-permute-start.12 = (bf16[32,256]{1,0:T(8,128)(2,1)S(1)}, bf16[32,256]{1,0:T(8,128)(2,1)S(1)}, u32[]{:S(2)}, u32[]{:S(2)}) collective-permute-start(bf16[32,256]{1,0:T(8,128)(2,1)S(1)} %get-tuple-element.65.refs_1_), channel_id=1, source_target_pairs={{0,3},{1,4},{2,5},{3,6},{4,7},{5,8},{6,9},{7,10},{8,11},{9,12},{10... | collective-permute-start | bytes 49160 | tf_op jit(solution)/shard_map/ppermute | solution.py:21
  68.4 14.8 %collective-permute-start.17 = (bf16[32,256]{1,0:T(8,128)(2,1)S(1)}, bf16[32,256]{1,0:T(8,128)(2,1)S(1)}, u32[]{:S(2)}, u32[]{:S(2)}) collective-permute-start(bf16[32,256]{1,0:T(8,128)(2,1)S(1)} %get-tuple-element.65.refs_1_), channel_id=1, source_target_pairs={{0,31},{1,0},{2,1},{3,2},{4,3},{5,4},{6,5},{7,6},{8,7},{9,8},{10,9... | collective-permute-start | bytes 49160 | tf_op jit(solution)/shard_map/ppermute | solution.py:21
  72.3 10.8 %collective-permute-start.16 = (bf16[32,256]{1,0:T(8,128)(2,1)S(1)}, bf16[32,256]{1,0:T(8,128)(2,1)S(1)}, u32[]{:S(2)}, u32[]{:S(2)}) collective-permute-start(bf16[32,256]{1,0:T(8,128)(2,1)S(1)} %get-tuple-element.65.refs_1_), channel_id=1, source_target_pairs={{0,1},{1,2},{2,3},{3,4},{4,5},{5,6},{6,7},{7,8},{8,9},{9,10},{10,1... | collective-permute-start | bytes 49160 | tf_op jit(solution)/shard_map/ppermute | solution.py:21
  77.3 33.8 %collective-permute-start.23 = (bf16[48,1024]{1,0:T(8,128)(2,1)S(1)}, bf16[48,1024]{1,0:T(8,128)(2,1)S(1)}, u32[]{:S(2)}, u32[]{:S(2)}) collective-permute-start(bf16[48,1024]{1,0:T(8,128)(2,1)S(1)} %get-tuple-element.80), channel_id=1, source_target_pairs={{0,29},{1,30},{2,31},{3,0},{4,1},{5,2},{6,3},{7,4},{8,5},{9,6},{10... | collective-permute-start | bytes 294920 | tf_op jit(solution)/shard_map/ppermute | solution.py:21
  79.2 17.0 %collective-permute-start.20 = (bf16[160,1024]{1,0:T(8,128)(2,1)S(1)}, bf16[160,1024]{1,0:T(8,128)(2,1)S(1)}, u32[]{:S(2)}, u32[]{:S(2)}) collective-permute-start(bf16[160,1024]{1,0:T(8,128)(2,1)S(1)} %get-tuple-element.76), channel_id=1, source_target_pairs={{0,30},{1,31},{2,0},{3,1},{4,2},{5,3},{6,4},{7,5},{8,6},{9,7},{10,... | collective-permute-start | bytes 983048 | tf_op jit(solution)/shard_map/ppermute | solution.py:21
  81.2 29.9 %collective-permute-start.22 = (bf16[160,1024]{1,0:T(8,128)(2,1)S(1)}, bf16[160,1024]{1,0:T(8,128)(2,1)S(1)}, u32[]{:S(2)}, u32[]{:S(2)}) collective-permute-start(bf16[160,1024]{1,0:T(8,128)(2,1)S(1)} %get-tuple-element.78), channel_id=1, source_target_pairs={{0,2},{1,3},{2,4},{3,5},{4,6},{5,7},{6,8},{7,9},{8,10},{9,11},{10,... | collective-permute-start | bytes 983048 | tf_op jit(solution)/shard_map/ppermute | solution.py:21
  90.9 11.2 %collective-permute-start.19 = (bf16[240,1024]{1,0:T(8,128)(2,1)S(1)}, bf16[240,1024]{1,0:T(8,128)(2,1)S(1)}, u32[]{:S(2)}, u32[]{:S(2)}) collective-permute-start(bf16[240,1024]{1,0:T(8,128)(2,1)S(1)} %get-tuple-element.74), channel_id=1, source_target_pairs={{0,31},{1,0},{2,1},{3,2},{4,3},{5,4},{6,5},{7,6},{8,7},{9,8},{10,9... | collective-permute-start | bytes 1474568 | tf_op jit(solution)/shard_map/ppermute | solution.py:21
  95.7 13.4 %collective-permute-start.18 = (bf16[256,1024]{1,0:T(8,128)(2,1)S(1)}, bf16[256,1024]{1,0:T(8,128)(2,1)S(1)}, u32[]{:S(2)}, u32[]{:S(2)}) collective-permute-start(bf16[256,1024]{1,0:T(8,128)(2,1)S(1)} %get-tuple-element.73), channel_id=1, source_target_pairs={{0,1},{1,2},{2,3},{3,4},{4,5},{5,6},{6,7},{7,8},{8,9},{9,10},{10,1... | collective-permute-start | bytes 1572872 | tf_op jit(solution)/shard_map/ppermute | solution.py:21
  96.2 15.0 %collective-permute-start.21 = (bf16[48,1024]{1,0:T(8,128)(2,1)S(1)}, bf16[48,1024]{1,0:T(8,128)(2,1)S(1)}, u32[]{:S(2)}, u32[]{:S(2)}) collective-permute-start(bf16[48,1024]{1,0:T(8,128)(2,1)S(1)} %get-tuple-element.77), channel_id=1, source_target_pairs={{0,3},{1,4},{2,5},{3,6},{4,7},{5,8},{6,9},{7,10},{8,11},{9,12},{10... | collective-permute-start | bytes 294920 | tf_op jit(solution)/shard_map/ppermute | solution.py:21
  (4 other events, 108.7 us)

commit v6 on v3

--- a/solution.py
+++ b/solution.py
@@ -374,14 +374,21 @@
     mixing_ref[...] = jnp.concatenate([row, spare], axis=0).astype(jnp.bfloat16)
 
 
+def in_level(group, level):
+    at = [place for place, e in enumerate(group) if abs(e - REACH) <= level]
+    assert not at or at == list(range(at[0], at[-1] + 1))
+    return (at[0], at[-1] + 1) if at else (0, 0)
+
+
 def mix_kernel(plan, cut_ref, active_ref, place_ref, window_ref, region_ref, kinetic_ref, *refs):
-    fun_dev, reading, band_order = plan
+    fun_dev, reading, group, whole = plan
+    count = len(group)
+    bands = refs[:count]
+    outs = refs[count : 2 * count]
+    at_boxes = refs[2 * count : 3 * count]
+    mixed = refs[3 * count]
+    mixings = dict(zip([v for v in range(1, REACH + 1) if in_level(group, v)[1]], refs[3 * count + 1 :]))
     slots = 2 * REACH + 1
-    bands = dict(zip(band_order, refs[:slots]))
-    outs = refs[slots : 2 * slots]
-    at_boxes = refs[2 * slots : 3 * slots]
-    mixed = refs[3 * slots]
-    mixings = refs[3 * slots + 1 :]
     steps = window_ref.shape[0] // STEP
     width = cut_ref[REACH + 1] - cut_ref[REACH]
     for out, at_box in zip(outs, at_boxes):
@@ -389,48 +396,48 @@
         at_box[...] = jnp.zeros_like(at_box)
     lanes = band_lanes(fun_dev, reading)
     parts = []
-    for e in range(slots):
-        band = bands[REACH - e][...].astype(jnp.float32)
+    for e, band_ref in zip(group, bands):
+        band = band_ref[...].astype(jnp.float32)
         band = jnp.concatenate([band, jnp.zeros((SLOT, lanes - 2 * reading), jnp.float32)], axis=1)
-        parts.append(moved(skewed(band, 1), e * fun_dev - (reading - 1)))
-    dense = jnp.concatenate(parts, axis=0).astype(jnp.bfloat16)
-    for part, mixing in enumerate(mixings):
-        low, high = level_rows(part + 1)
+        parts.append(moved(skewed(band, 1), e * fun_dev - (reading - 1)).astype(jnp.bfloat16))
+    for level, mixing in mixings.items():
+        start, end = in_level(group, level)
         shape = (lanes, mixing.shape[1])
         column = function_of(shape, 1, fun_dev)
-        column = jnp.where(column >= 0, column + low // SLOT * fun_dev, -1)
+        column = jnp.where(column >= 0, column + level_rows(level)[0] // SLOT * fun_dev, -1)
         keep = one_hot(column == lax.broadcasted_iota(jnp.int32, shape, 0))
-        mixing[...] = times(dense[low:high], keep).astype(jnp.bfloat16)
+        mixing[...] = times(jnp.concatenate(parts[start:end], axis=0), keep).astype(jnp.bfloat16)
 
     @pl.loop(0, lax.div(width + STEP - 1, STEP))
     def _(step):
-        level = active_ref[slots * steps + step]
-        for part, mixing in enumerate(mixings):
-            @pl.when(level == part + 1)
+        for level, mixing in mixings.items():
+            @pl.when(active_ref[slots * steps + step] == level)
             def _():
-                low, high = level_rows(part + 1)
+                low, high = level_rows(level)
+                start, end = in_level(group, level)
                 for b in range(STEP):
                     here = window_ref[step * STEP + b, low:high]
-                    mixed[b, low:high] = times(mixing[...], here).astype(jnp.bfloat16)
+                    mixed[b, start * SLOT : end * SLOT] = times(mixing[...], here).astype(jnp.bfloat16)
         shape = (STEP * SLOT, at_boxes[0].shape[1])
         along = lax.broadcasted_iota(jnp.int32, shape, 0)
         box = lax.shift_right_logical(along, SLOT.bit_length() - 1) + step * STEP
         col = lax.broadcasted_iota(jnp.int32, shape, 1)
         boxes_of = one_hot((col == box) | (col == box + SLOT))
-        for e in range(slots):
+        for at, e in enumerate(group):
             @pl.when(active_ref[e * steps + step] > 0)
             def _():
                 place = place_ref[step, e : e + 1, :]
-                pick = one_hot(iota((outs[e].shape[0], STEP * SLOT), 0) == place)
-                part = mixed[:, e * SLOT : (e + 1) * SLOT, :].reshape(STEP * SLOT, mixed.shape[-1])
-                outs[e][...] += times(pick, part).astype(jnp.bfloat16)
-                at_boxes[e][...] += times(pick, boxes_of).astype(jnp.bfloat16)
-
-    for e in (REACH - 1, REACH + 1):
-        here = outs[e][...]
-        applied = times(here, kinetic_ref[...])
-        near_by = times(at_boxes[e][...], region_ref[...])
-        outs[e][...] = (applied + near_by * here.astype(jnp.float32)).astype(jnp.bfloat16)
+                pick = one_hot(iota((outs[at].shape[0], STEP * SLOT), 0) == place)
+                part = mixed[:, at * SLOT : (at + 1) * SLOT, :].reshape(STEP * SLOT, mixed.shape[-1])
+                outs[at][...] += times(pick, part).astype(jnp.bfloat16)
+                at_boxes[at][...] += times(pick, boxes_of).astype(jnp.bfloat16)
+
+    for at, e in enumerate(group):
+        if e in whole:
+            here = outs[at][...]
+            applied = times(here, kinetic_ref[...])
+            near_by = times(at_boxes[at][...], region_ref[...])
+            outs[at][...] = (applied + near_by * here.astype(jnp.float32)).astype(jnp.bfloat16)
 
 
 def home_rows(bases, home_ref, sources, at, count):
@@ -438,9 +445,11 @@
     here = iota(shape, 1) == iota(shape, 0) + float(at)
     row = jnp.sum(jnp.where(here, home_ref[...], 0.0), axis=1, keepdims=True)
     value = None
-    for base, source in zip(bases, sources):
-        pick = one_hot(iota((count, source.shape[0]), 1) == row - float(base))
-        term = times(pick, source[...])
+    for base, group in bases:
+        parts = [sources[at][...] for at in group]
+        held = parts[0] if len(parts) == 1 else jnp.concatenate(parts, axis=0)
+        pick = one_hot(iota((count, held.shape[0]), 1) == row - float(base))
+        term = times(pick, held)
         value = term if value is None else value + term
     return value
 
@@ -486,12 +495,12 @@
     flat = coeffs.reshape(fun_dev * support, points)
     halo = REACH + -(-(reading + 8) // fun_dev)
     count = rounded_up((2 * halo + 2) * fun_dev, 128)
-    half = rounded_up(box_dev, 16)
     bf16, f32 = jnp.bfloat16, jnp.float32
     smem = pl.BlockSpec(memory_space=pltpu.SMEM)
     vmem = pl.BlockSpec(memory_space=pltpu.VMEM)
     limit = pltpu.CompilerParams(vmem_limit_bytes=26 * 2**20)
 
+    half = rounded_up(box_dev, 16)
     sent_rows = {k: rounded_up(rows[k + REACH] + (2 * box_dev if k < 0 else 0), 16) for k in offsets if k}
     *packed, near, cut, home_row, own_region = pl.pallas_call(
         functools.partial(pack_kernel, (fun_dev, support, devices, halo, rows, back, low_cut, high_cut, now + [last])),
@@ -533,8 +542,10 @@
     sources = [arrived[REACH - e] for e in range(slots) if e != REACH]
     read_rows = [rows_of[REACH - e] for e in range(slots)]
     level_sizes = [level_rows(part + 1)[1] - level_rows(part + 1)[0] for part in range(REACH)]
+    level_sizes = [level_rows(part + 1)[1] - level_rows(part + 1)[0] for part in range(REACH)]
     exact_rows = [rows[2 * REACH - e] for e in range(slots)]
     band = (fun_dev, 2 * reading)
+    exact_rows = [rows[2 * REACH - e] for e in range(slots)]
     pieces, region, *grams = pl.pallas_call(
         functools.partial(unpack_kernel, (fun_dev, box_dev, reading, volume, exact_rows, read_rows, blocks)),
         out_shape=(
@@ -561,37 +572,48 @@
     )(grams[REACH], *[summed[k] for k in one_way])
     mixing_of = sent({k: mixing_rows for k in one_way}, one_way, 1)
     mixing_of[0] = mixing_rows
-    band_order = one_way + [0]
-
-    out_rows = [rows_of[REACH - e] for e in range(slots)]
-    shapes = [(r, points) for r in out_rows] + [(r, 128) for r in out_rows]
-    mixed = pl.pallas_call(
-        functools.partial(mix_kernel, (fun_dev, reading, band_order)),
-        out_shape=tuple(jax.ShapeDtypeStruct(shape, bf16) for shape in shapes),
-        in_specs=[smem, smem] + [vmem] * (4 + slots),
-        out_specs=(vmem,) * len(shapes),
-        scratch_shapes=[pltpu.VMEM((STEP, wide, points), bf16)]
-        + [pltpu.VMEM((size, size), bf16) for size in level_sizes],
-        compiler_params=limit,
-        name="mix",
-    )(cut, active, places, pieces, region, kinetic, *[mixing_of[k] for k in band_order])
-
-    ready = {}
-    for k in now + [last, 0]:
-        here, at_box = mixed[REACH - k], mixed[slots + REACH - k]
-        if abs(k) == 1:
-            ready[k] = here
-            continue
-        near_by = jnp.dot(at_box, region, preferred_element_type=f32)
-        applied = jnp.dot(here, kinetic, preferred_element_type=f32)
-        ready[k] = (applied + near_by * here.astype(f32)).astype(bf16)
-    returned = all_sent(ready, now, last, -1)
+
+    ready, at_boxes = {}, {}
+    for group, whole in [([2, -2, REACH, -REACH], [2, -2, REACH, -REACH]), ([0, 1, -1], [1, -1])]:
+        group, whole = sorted(REACH - k for k in group), [REACH - k for k in whole]
+        shapes = [(rows_of[REACH - e], points) for e in group] + [(rows_of[REACH - e], 128) for e in group]
+        sizes = [
+            ((in_level(group, v)[1] - in_level(group, v)[0]) * SLOT, level_sizes[v - 1])
+            for v in range(1, REACH + 1)
+            if in_level(group, v)[1]
+        ]
+        if ready:
+            cut, *held = lax.optimization_barrier((cut, *[ready[k] for k in ready]))
+            ready = dict(zip(ready, held))
+        mixed = pl.pallas_call(
+            functools.partial(mix_kernel, (fun_dev, reading, group, whole)),
+            out_shape=tuple(jax.ShapeDtypeStruct(shape, bf16) for shape in shapes),
+            in_specs=[smem, smem] + [vmem] * (4 + len(group)),
+            out_specs=(vmem,) * len(shapes),
+            scratch_shapes=[pltpu.VMEM((STEP, len(group) * SLOT, points), bf16)]
+            + [pltpu.VMEM(size, bf16) for size in sizes],
+            compiler_params=limit,
+            cost_estimate=pl.CostEstimate(
+                flops=8 * wide * len(group) * SLOT * boxes * points, bytes_accessed=40 * 2**20, transcendentals=0
+            ),
+            name="mix",
+        )(cut, active, places, pieces, region, kinetic, *[mixing_of[REACH - e] for e in group])
+        for at, e in enumerate(group):
+            ready[REACH - e], at_boxes[REACH - e] = mixed[at], mixed[len(group) + at]
+            if e not in whole:
+                near_by = jnp.dot(at_boxes[REACH - e], region, preferred_element_type=f32)
+                applied = jnp.dot(mixed[at], kinetic, preferred_element_type=f32)
+                ready[REACH - e] = (applied + near_by * mixed[at].astype(f32)).astype(bf16)
+    returned = all_sent(ready, [2, -2, 1, -1, REACH], -REACH, -1)
     returned[0] = ready[0]
 
     bases = {k: sum(back[: k + REACH]) for k in offsets}
-    early, late = [0] + now[:2], now[2:] + [last]
+    early, late = [0, 2, REACH, -2], [-1, 1, -REACH]
+    assert bases[REACH] == bases[2] + rows_of[2]
+    early_groups = [(bases[0], [0]), (bases[2], [1, 2]), (bases[-2], [3])]
+    late_groups = [(bases[k], [at]) for at, k in enumerate(late)]
     begun = pl.pallas_call(
-        functools.partial(early_kernel, [bases[k] for k in early]),
+        functools.partial(early_kernel, early_groups),
         out_shape=jax.ShapeDtypeStruct(flat.shape, bf16),
         in_specs=[vmem] * (1 + len(early)),
         out_specs=vmem,
@@ -599,7 +621,7 @@
         name="early",
     )(home_row, *[returned[k] for k in early])
     filtered = pl.pallas_call(
-        functools.partial(home_kernel, [bases[k] for k in late]),
+        functools.partial(home_kernel, late_groups),
         out_shape=jax.ShapeDtypeStruct(flat.shape, bf16),
         in_specs=[vmem] * (2 + len(late)),
         out_specs=pl.BlockSpec(memory_space=pl.ANY),

time: 121 us -> 114 us (0.942)
  the two profiles are of different devices: /device:TPU:1 before, /device:TPU:0 now
where the time goes in v6:
time: 114 us
  starting transfers between devices  56.2 us (49%)
  Pallas kernels  29.7 us (26%)
  waiting for transfers between devices  23.5 us (21%)
  matrix products  1.71 us (2%)
  local copies, waits for them, and re-layouts  1.65 us (1%)
    ppermute x24, starting transfers between devices, passed_along(): return lax.ppermute(value, AXES, pairs)  56.2 us
    ppermute x24, waiting for transfers between devices, passed_along(): return lax.ppermute(value, AXES, pairs)  23.5 us
    pallas_call x2, Pallas kernels, on_device(): pl.pallas_call(functools.partial(mix_kernel, (fun_dev, reading, group, wh...  11.7 us
    pallas_call x1, Pallas kernels, on_device(): pl.pallas_call(functools.partial(unpack_kernel, (fun_dev, box_dev, readin...  6.19 us
    pallas_call x1, Pallas kernels, on_device(): pl.pallas_call(functools.partial(pack_kernel, (fun_dev, support, devices,...  4.1 us
    pallas_call x1, Pallas kernels, on_device(): pl.pallas_call(functools.partial(table_kernel, (fun_dev, support, halo, b...  2.78 us
    pallas_call x1, Pallas kernels, on_device(): pl.pallas_call(functools.partial(home_kernel, late_groups), out_shape=jax...  2.38 us
  transfers between devices with their start and end apart: 24, of which 8 were waited for; matrix products, arithmetic and copies ran while one was open for 2% of the time, Pallas kernels for 14%

profile of v6, /device:TPU:0, one launch (start us, length us, event | category | flops | bytes accessed | tf_op | source)
XLA Modules:
  0.0 113.8 jit_solution(7034649714782790962)
XLA Ops:
  2.3 4.1 %pack.1 = (bf16[272,1024]{1,0:T(8,128)(2,1)}, bf16[240,1024]{1,0:T(8,128)(2,1)S(1)}, bf16[192,1024]{1,0:T(8,128)(2,1)S(1)}, bf16[160,1024]{1,0:T(8,128)(2,1)S(1)...) custom-call(s32[1]{0:T(128)} %bitcast.me_ref, ...), custom_call_target="tpu_custom_call" | custom-call | tf_op jit(solution)/shard_map/pack/pallas_call | solution.py:505
  6.4 6.4 %collective-permute-start.3 = (bf16[272,1024]{1,0:T(8,128)(2,1)}, bf16[272,1024]{1,0:T(8,128)(2,1)S(1)}, u32[]{:S(2)}, u32[]{:S(2)}) collective-permute-start(bf16[272,1024]{1,0:T(8,128)(2,1)} %get-tuple-element.56), channel_id=1, source_target_pairs={{0,31},{1,0},{2,1},{3,2},{4,3},{5,4},{6,5},{7,6},{8,7},{9,8},{10,9... | collective-permute-start | bytes 1671176 | tf_op jit(solution)/shard_map/ppermute | solution.py:21
  14.9 6.7 %collective-permute-done.3.refs_3_ = bf16[272,1024]{1,0:T(8,128)(2,1)S(1)} collective-permute-done((bf16[272,1024]{1,0:T(8,128)(2,1)}, bf16[272,1024]{1,0:T(8,128)(2,1)S(1)}, u32[]{:S(2)}, u32[]{:S(2)}) %collective-permute-start.3) | collective-permute-done | bytes 557088 | tf_op jit(solution)/shard_map/ppermute | solution.py:21
  21.5 15.6 %collective-permute-start.5 = (bf16[64,1024]{1,0:T(8,128)(2,1)S(1)}, bf16[64,1024]{1,0:T(8,128)(2,1)S(1)}, u32[]{:S(2)}, u32[]{:S(2)}) collective-permute-start(bf16[64,1024]{1,0:T(8,128)(2,1)S(1)} %get-tuple-element.59), channel_id=1, source_target_pairs={{0,29},{1,30},{2,31},{3,0},{4,1},{5,2},{6,3},{7,4},{8,5},{9,6},{10... | collective-permute-start | bytes 393224 | tf_op jit(solution)/shard_map/ppermute | solution.py:21
  37.1 2.8 %tables.1 = (f32[224,128]{1,0:T(8,128)S(1)}, f32[3,8,256]{2,1,0:T(8,128)S(1)}, s32[24]{0:T(128)S(1)}, bf16[24,32,1024]{2,1,0:T(8,128)(2,1)S(1)}) custom-call(s32[8]{0:T(128)S(1)} %get-tuple-element.74.cut_ref, f32[512,128]{1,0:T(8,128)S(1)} %get-tuple-element.46.near_ref, bf16[768,1024]{1,0:T(8,128)(2,1)S(1)} %bitcast.8), custom_call_target="tpu_custom_call" | custom-call | tf_op jit(solution)/shard_map/tables/pallas_call | solution.py:527
  39.9 4.4 %collective-permute-done.refs_0_ = bf16[48,1024]{1,0:T(8,128)(2,1)S(1)} collective-permute-done((bf16[48,1024]{1,0:T(8,128)(2,1)S(1)}, bf16[48,1024]{1,0:T(8,128)(2,1)S(1)}, u32[]{:S(2)}, u32[]{:S(2)}) %collective-permute-start) | collective-permute-done | bytes 98336 | tf_op jit(solution)/shard_map/ppermute | solution.py:21
  44.4 6.2 %unpack.1 = (bf16[24,224,1024]{2,1,0:T(8,128)(2,1)S(1)}, bf16[128,1024]{1,0:T(8,128)(2,1)S(1)}, f32[24,256]{1,0:T(8,128)S(1)}, f32[24,256]{1,0:T(8,128)S(1)}, f3...) custom-call(s32[8]{0:T(128)S(1)} %get-tuple-element.74.cut_ref, ...), custom_call_target="tpu_custom_call" | custom-call | tf_op jit(solution)/shard_map/unpack/pallas_call | solution.py:549
  51.2 5.4 %collective-permute-start.9 = (f32[24,256]{1,0:T(8,128)S(1)}, f32[24,256]{1,0:T(8,128)S(1)}, u32[]{:S(2)}, u32[]{:S(2)}) collective-permute-start(f32[24,256]{1,0:T(8,128)S(1)} %get-tuple-element.66), channel_id=1, source_target_pairs={{0,29},{1,30},{2,31},{3,0},{4,1},{5,2},{6,3},{7,4},{8,5},{9,6},{10... | collective-permute-start | bytes 73736 | tf_op jit(solution)/shard_map/ppermute | solution.py:21
  56.6 2.9 %collective-permute-start.10 = (f32[24,256]{1,0:T(8,128)S(1)}, f32[24,256]{1,0:T(8,128)S(1)}, u32[]{:S(2)}, u32[]{:S(2)}) collective-permute-start(f32[24,256]{1,0:T(8,128)S(1)} %get-tuple-element.67), channel_id=1, source_target_pairs={{0,30},{1,31},{2,0},{3,1},{4,2},{5,3},{6,4},{7,5},{8,6},{9,7},{10,... | collective-permute-start | bytes 73736 | tf_op jit(solution)/shard_map/ppermute | solution.py:21
  59.5 1.5 %collective-permute-done.10.refs_5_ = f32[24,256]{1,0:T(8,128)S(1)} collective-permute-done((f32[24,256]{1,0:T(8,128)S(1)}, f32[24,256]{1,0:T(8,128)S(1)}, u32[]{:S(2)}, u32[]{:S(2)}) %collective-permute-start.10) | collective-permute-done | bytes 24608 | tf_op jit(solution)/shard_map/ppermute | solution.py:21
  61.8 1.3 %collective-permute-start.15 = (bf16[32,256]{1,0:T(8,128)(2,1)S(1)}, bf16[32,256]{1,0:T(8,128)(2,1)S(1)}, u32[]{:S(2)}, u32[]{:S(2)}) collective-permute-start(bf16[32,256]{1,0:T(8,128)(2,1)S(1)} %get-tuple-element.69.refs_1_), channel_id=1, source_target_pairs={{0,29},{1,30},{2,31},{3,0},{4,1},{5,2},{6,3},{7,4},{8,5},{9,6},{10... | collective-permute-start | bytes 49160 | tf_op jit(solution)/shard_map/ppermute | solution.py:21
  63.2 4.4 %collective-permute-start.14 = (bf16[32,256]{1,0:T(8,128)(2,1)S(1)}, bf16[32,256]{1,0:T(8,128)(2,1)S(1)}, u32[]{:S(2)}, u32[]{:S(2)}) collective-permute-start(bf16[32,256]{1,0:T(8,128)(2,1)S(1)} %get-tuple-element.69.refs_1_), channel_id=1, source_target_pairs={{0,30},{1,31},{2,0},{3,1},{4,2},{5,3},{6,4},{7,5},{8,6},{9,7},{10,... | collective-permute-start | bytes 49160 | tf_op jit(solution)/shard_map/ppermute | solution.py:21
  69.0 5.6 %collective-permute-start.17 = (bf16[32,256]{1,0:T(8,128)(2,1)S(1)}, bf16[32,256]{1,0:T(8,128)(2,1)S(1)}, u32[]{:S(2)}, u32[]{:S(2)}) collective-permute-start(bf16[32,256]{1,0:T(8,128)(2,1)S(1)} %get-tuple-element.69.refs_1_), channel_id=1, source_target_pairs={{0,31},{1,0},{2,1},{3,2},{4,3},{5,4},{6,5},{7,6},{8,7},{9,8},{10,9... | collective-permute-start | bytes 49160 | tf_op jit(solution)/shard_map/ppermute | solution.py:21
  74.9 4.0 %mix.2 = (bf16[48,1024]{1,0:T(8,128)(2,1)S(1)}, bf16[160,1024]{1,0:T(8,128)(2,1)S(1)}, bf16[160,1024]{1,0:T(8,128)(2,1)S(1)}, bf16[48,1024]{1,0:T(8,128)(2,1)S(1...) custom-call(s32[8]{0:T(128)S(1)} %get-tuple-element.74.cut_ref, ...), custom_call_target="tpu_custom_call" | custom-call | flops 5637144576 | bytes 41943040 | tf_op jit(solution)/shard_map/mix/pallas_call | solution.py:588
  79.4 3.6 %collective-permute-start.18 = (bf16[160,1024]{1,0:T(8,128)(2,1)S(1)}, bf16[160,1024]{1,0:T(8,128)(2,1)S(1)}, u32[]{:S(2)}, u32[]{:S(2)}) collective-permute-start(bf16[160,1024]{1,0:T(8,128)(2,1)S(1)} %get-tuple-element.78), channel_id=1, source_target_pairs={{0,30},{1,31},{2,0},{3,1},{4,2},{5,3},{6,4},{7,5},{8,6},{9,7},{10,... | collective-permute-start | bytes 983048 | tf_op jit(solution)/shard_map/ppermute | solution.py:21
  82.9 1.6 %collective-permute-start.20 = (bf16[160,1024]{1,0:T(8,128)(2,1)S(1)}, bf16[160,1024]{1,0:T(8,128)(2,1)S(1)}, u32[]{:S(2)}, u32[]{:S(2)}) collective-permute-start(bf16[160,1024]{1,0:T(8,128)(2,1)S(1)} %get-tuple-element.81), channel_id=1, source_target_pairs={{0,2},{1,3},{2,4},{3,5},{4,6},{5,7},{6,8},{7,9},{8,10},{9,11},{10,... | collective-permute-start | bytes 983048 | tf_op jit(solution)/shard_map/ppermute | solution.py:21
  84.6 7.7 %mix.3 = (bf16[240,1024]{1,0:T(8,128)(2,1)S(1)}, bf16[512,1024]{1,0:T(8,128)(2,1)S(1)}, bf16[256,1024]{1,0:T(8,128)(2,1)S(1)}, bf16[240,128]{1,0:T(8,128)(2,1)},...) custom-call(s32[8]{0:T(128)S(1)} %get-tuple-element.74.cut_ref, s32[24]{0:T(128)S(1)} %get-tuple-element.47.active_ref, ...), custom_call_target="tpu_custom_call" | custom-call | flops 4227858432 | bytes 41943040 | tf_op jit(solution)/shard_map/mix/pallas_call | solution.py:588
  92.2 4.6 %collective-permute-start.22 = (bf16[240,1024]{1,0:T(8,128)(2,1)S(1)}, bf16[240,1024]{1,0:T(8,128)(2,1)S(1)}, u32[]{:S(2)}, u32[]{:S(2)}) collective-permute-start(bf16[240,1024]{1,0:T(8,128)(2,1)S(1)} %get-tuple-element.83), channel_id=1, source_target_pairs={{0,31},{1,0},{2,1},{3,2},{4,3},{5,4},{6,5},{7,6},{8,7},{9,8},{10,9... | collective-permute-start | bytes 1474568 | tf_op jit(solution)/shard_map/ppermute | solution.py:21
  97.5 1.3 %add_convert_fusion.refs_0_ = bf16[512,1024]{1,0:T(8,128)(2,1)S(1)} fusion(f32[512,1024]{1,0:T(8,128)S(1)} %fusion, bf16[512,1024]{1,0:T(8,128)(2,1)S(1)} %get-tuple-element.75, bf16[1024,1024]{1,0:T(8,128)(2,1)S(1)} %copy-done.3), kind=kOutput, calls=%fused_computation | convolution fusion | flops 1075838976 | bytes 6291456 | tf_op jit(solution)/shard_map/dot_general | solution.py:605
  98.8 2.6 %collective-permute-done.20.refs_3_ = bf16[160,1024]{1,0:T(8,128)(2,1)S(1)} collective-permute-done((bf16[160,1024]{1,0:T(8,128)(2,1)S(1)}, bf16[160,1024]{1,0:T(8,128)(2,1)S(1)}, u32[]{:S(2)}, u32[]{:S(2)}) %collective-permute-start.20) | collective-permute-done | bytes 327712 | tf_op jit(solution)/shard_map/ppermute | solution.py:21
  101.4 2.0 %early.1.early_ref = bf16[768,1024]{1,0:T(8,128)(2,1)S(1)} custom-call(f32[1,768]{1,0:T(1,128)S(1)} %get-tuple-element.44.home_ref, bf16[512,1024]{1,0:T(8,128)(2,1)S(1)} %add_convert_fusion.refs_0_, bf16[160,1024]{1,0:T(8,128)(2,1)S(1)} %collective-permute-done.18.refs_1_, bf16[48,1024]{1,0:T(8,128)(2,1)S(1)} %collective-permute-done.19.refs_2_, ...), custom_call_target="tpu_custom_call" | custom-call | tf_op jit(solution)/shard_map/early/pallas_call | solution.py:615
  103.4 6.2 %collective-permute-done.23.refs_2_ = bf16[48,1024]{1,0:T(8,128)(2,1)S(1)} collective-permute-done((bf16[48,1024]{1,0:T(8,128)(2,1)S(1)}, bf16[48,1024]{1,0:T(8,128)(2,1)S(1)}, u32[]{:S(2)}, u32[]{:S(2)}) %collective-permute-start.23) | collective-permute-done | bytes 98336 | tf_op jit(solution)/shard_map/ppermute | solution.py:21
  109.6 1.6 %collective-permute-done.21.refs_0_ = bf16[256,1024]{1,0:T(8,128)(2,1)S(1)} collective-permute-done((bf16[256,1024]{1,0:T(8,128)(2,1)S(1)}, bf16[256,1024]{1,0:T(8,128)(2,1)S(1)}, u32[]{:S(2)}, u32[]{:S(2)}) %collective-permute-start.21) | collective-permute-done | bytes 524320 | tf_op jit(solution)/shard_map/ppermute | solution.py:21
  111.2 2.4 %home.1 = bf16[768,1024]{1,0:T(8,128)(2,1)} custom-call(f32[1,768]{1,0:T(1,128)S(1)} %get-tuple-element.44.home_ref, bf16[768,1024]{1,0:T(8,128)(2,1)S(1)} %early.1.early_ref, bf16[256,1024]{1,0:T(8,128)(2,1)S(1)} %collective-permute-done.21.refs_0_, bf16[240,1024]{1,0:T(8,128)(2,1)S(1)} %collective-permute-done.22.refs_1_, ...), custom_call_target="tpu_custom_call" | custom-call | tf_op jit(solution)/shard_map/home/pallas_call | solution.py:623
  (42 shorter events, 8.0 us)
Async XLA Ops:
  6.4 15.1 %collective-permute-start.3 = (bf16[272,1024]{1,0:T(8,128)(2,1)}, bf16[272,1024]{1,0:T(8,128)(2,1)S(1)}, u32[]{:S(2)}, u32[]{:S(2)}) collective-permute-start(bf16[272,1024]{1,0:T(8,128)(2,1)} %get-tuple-element.56), channel_id=1, source_target_pairs={{0,31},{1,0},{2,1},{3,2},{4,3},{5,4},{6,5},{7,6},{8,7},{9,8},{10,9... | collective-permute-start | bytes 1671176 | tf_op jit(solution)/shard_map/ppermute | solution.py:21
  12.8 31.5 %collective-permute-start.2 = (bf16[240,1024]{1,0:T(8,128)(2,1)S(1)}, bf16[240,1024]{1,0:T(8,128)(2,1)S(1)}, u32[]{:S(2)}, u32[]{:S(2)}) collective-permute-start(bf16[240,1024]{1,0:T(8,128)(2,1)S(1)} %get-tuple-element.54), channel_id=1, source_target_pairs={{0,1},{1,2},{2,3},{3,4},{4,5},{5,6},{6,7},{7,8},{8,9},{9,10},{10,1... | collective-permute-start | bytes 1474568 | tf_op jit(solution)/shard_map/ppermute | solution.py:21
  12.8 31.5 %collective-permute-start.4 = (bf16[192,1024]{1,0:T(8,128)(2,1)S(1)}, bf16[192,1024]{1,0:T(8,128)(2,1)S(1)}, u32[]{:S(2)}, u32[]{:S(2)}) collective-permute-start(bf16[192,1024]{1,0:T(8,128)(2,1)S(1)} %get-tuple-element.58), channel_id=1, source_target_pairs={{0,30},{1,31},{2,0},{3,1},{4,2},{5,3},{6,4},{7,5},{8,6},{9,7},{10,... | collective-permute-start | bytes 1179656 | tf_op jit(solution)/shard_map/ppermute | solution.py:21
  13.9 30.5 %collective-permute-start.1 = (bf16[160,1024]{1,0:T(8,128)(2,1)S(1)}, bf16[160,1024]{1,0:T(8,128)(2,1)S(1)}, u32[]{:S(2)}, u32[]{:S(2)}) collective-permute-start(bf16[160,1024]{1,0:T(8,128)(2,1)S(1)} %get-tuple-element.53), channel_id=1, source_target_pairs={{0,2},{1,3},{2,4},{3,5},{4,6},{5,7},{6,8},{7,9},{8,10},{9,11},{10,... | collective-permute-start | bytes 983048 | tf_op jit(solution)/shard_map/ppermute | solution.py:21
  21.5 22.8 %collective-permute-start.5 = (bf16[64,1024]{1,0:T(8,128)(2,1)S(1)}, bf16[64,1024]{1,0:T(8,128)(2,1)S(1)}, u32[]{:S(2)}, u32[]{:S(2)}) collective-permute-start(bf16[64,1024]{1,0:T(8,128)(2,1)S(1)} %get-tuple-element.59), channel_id=1, source_target_pairs={{0,29},{1,30},{2,31},{3,0},{4,1},{5,2},{6,3},{7,4},{8,5},{9,6},{10... | collective-permute-start | bytes 393224 | tf_op jit(solution)/shard_map/ppermute | solution.py:21
  37.1 7.2 %collective-permute-start = (bf16[48,1024]{1,0:T(8,128)(2,1)S(1)}, bf16[48,1024]{1,0:T(8,128)(2,1)S(1)}, u32[]{:S(2)}, u32[]{:S(2)}) collective-permute-start(bf16[48,1024]{1,0:T(8,128)(2,1)S(1)} %get-tuple-element.52), channel_id=1, source_target_pairs={{0,3},{1,4},{2,5},{3,6},{4,7},{5,8},{6,9},{7,10},{8,11},{9,12},{10... | collective-permute-start | bytes 294920 | tf_op jit(solution)/shard_map/ppermute | solution.py:21
  50.6 8.9 %collective-permute-start.6 = (f32[24,256]{1,0:T(8,128)S(1)}, f32[24,256]{1,0:T(8,128)S(1)}, u32[]{:S(2)}, u32[]{:S(2)}) collective-permute-start(f32[24,256]{1,0:T(8,128)S(1)} %get-tuple-element.63), channel_id=1, source_target_pairs={{0,3},{1,4},{2,5},{3,6},{4,7},{5,8},{6,9},{7,10},{8,11},{9,12},{10... | collective-permute-start | bytes 73736 | tf_op jit(solution)/shard_map/ppermute | solution.py:21
  50.6 8.8 %collective-permute-start.7 = (f32[24,256]{1,0:T(8,128)S(1)}, f32[24,256]{1,0:T(8,128)S(1)}, u32[]{:S(2)}, u32[]{:S(2)}) collective-permute-start(f32[24,256]{1,0:T(8,128)S(1)} %get-tuple-element.64), channel_id=1, source_target_pairs={{0,2},{1,3},{2,4},{3,5},{4,6},{5,7},{6,8},{7,9},{8,10},{9,11},{10,... | collective-permute-start | bytes 73736 | tf_op jit(solution)/shard_map/ppermute | solution.py:21
  50.7 8.8 %collective-permute-start.8 = (f32[24,256]{1,0:T(8,128)S(1)}, f32[24,256]{1,0:T(8,128)S(1)}, u32[]{:S(2)}, u32[]{:S(2)}) collective-permute-start(f32[24,256]{1,0:T(8,128)S(1)} %get-tuple-element.65), channel_id=1, source_target_pairs={{0,1},{1,2},{2,3},{3,4},{4,5},{5,6},{6,7},{7,8},{8,9},{9,10},{10,1... | collective-permute-start | bytes 73736 | tf_op jit(solution)/shard_map/ppermute | solution.py:21
  51.2 8.3 %collective-permute-start.9 = (f32[24,256]{1,0:T(8,128)S(1)}, f32[24,256]{1,0:T(8,128)S(1)}, u32[]{:S(2)}, u32[]{:S(2)}) collective-permute-start(f32[24,256]{1,0:T(8,128)S(1)} %get-tuple-element.66), channel_id=1, source_target_pairs={{0,29},{1,30},{2,31},{3,0},{4,1},{5,2},{6,3},{7,4},{8,5},{9,6},{10... | collective-permute-start | bytes 73736 | tf_op jit(solution)/shard_map/ppermute | solution.py:21
  56.6 4.4 %collective-permute-start.10 = (f32[24,256]{1,0:T(8,128)S(1)}, f32[24,256]{1,0:T(8,128)S(1)}, u32[]{:S(2)}, u32[]{:S(2)}) collective-permute-start(f32[24,256]{1,0:T(8,128)S(1)} %get-tuple-element.67), channel_id=1, source_target_pairs={{0,30},{1,31},{2,0},{3,1},{4,2},{5,3},{6,4},{7,5},{8,6},{9,7},{10,... | collective-permute-start | bytes 73736 | tf_op jit(solution)/shard_map/ppermute | solution.py:21
  59.5 1.7 %collective-permute-start.11 = (f32[24,256]{1,0:T(8,128)S(1)}, f32[24,256]{1,0:T(8,128)S(1)}, u32[]{:S(2)}, u32[]{:S(2)}) collective-permute-start(f32[24,256]{1,0:T(8,128)S(1)} %get-tuple-element.68), channel_id=1, source_target_pairs={{0,31},{1,0},{2,1},{3,2},{4,3},{5,4},{6,5},{7,6},{8,7},{9,8},{10,9... | collective-permute-start | bytes 73736 | tf_op jit(solution)/shard_map/ppermute | solution.py:21
  61.8 12.8 %collective-permute-start.15 = (bf16[32,256]{1,0:T(8,128)(2,1)S(1)}, bf16[32,256]{1,0:T(8,128)(2,1)S(1)}, u32[]{:S(2)}, u32[]{:S(2)}) collective-permute-start(bf16[32,256]{1,0:T(8,128)(2,1)S(1)} %get-tuple-element.69.refs_1_), channel_id=1, source_target_pairs={{0,29},{1,30},{2,31},{3,0},{4,1},{5,2},{6,3},{7,4},{8,5},{9,6},{10... | collective-permute-start | bytes 49160 | tf_op jit(solution)/shard_map/ppermute | solution.py:21
  63.2 11.4 %collective-permute-start.14 = (bf16[32,256]{1,0:T(8,128)(2,1)S(1)}, bf16[32,256]{1,0:T(8,128)(2,1)S(1)}, u32[]{:S(2)}, u32[]{:S(2)}) collective-permute-start(bf16[32,256]{1,0:T(8,128)(2,1)S(1)} %get-tuple-element.69.refs_1_), channel_id=1, source_target_pairs={{0,30},{1,31},{2,0},{3,1},{4,2},{5,3},{6,4},{7,5},{8,6},{9,7},{10,... | collective-permute-start | bytes 49160 | tf_op jit(solution)/shard_map/ppermute | solution.py:21
  67.5 7.3 %collective-permute-start.13 = (bf16[32,256]{1,0:T(8,128)(2,1)S(1)}, bf16[32,256]{1,0:T(8,128)(2,1)S(1)}, u32[]{:S(2)}, u32[]{:S(2)}) collective-permute-start(bf16[32,256]{1,0:T(8,128)(2,1)S(1)} %get-tuple-element.69.refs_1_), channel_id=1, source_target_pairs={{0,2},{1,3},{2,4},{3,5},{4,6},{5,7},{6,8},{7,9},{8,10},{9,11},{10,... | collective-permute-start | bytes 49160 | tf_op jit(solution)/shard_map/ppermute | solution.py:21
  67.8 7.1 %collective-permute-start.12 = (bf16[32,256]{1,0:T(8,128)(2,1)S(1)}, bf16[32,256]{1,0:T(8,128)(2,1)S(1)}, u32[]{:S(2)}, u32[]{:S(2)}) collective-permute-start(bf16[32,256]{1,0:T(8,128)(2,1)S(1)} %get-tuple-element.69.refs_1_), channel_id=1, source_target_pairs={{0,3},{1,4},{2,5},{3,6},{4,7},{5,8},{6,9},{7,10},{8,11},{9,12},{10... | collective-permute-start | bytes 49160 | tf_op jit(solution)/shard_map/ppermute | solution.py:21
  69.0 15.5 %collective-permute-start.17 = (bf16[32,256]{1,0:T(8,128)(2,1)S(1)}, bf16[32,256]{1,0:T(8,128)(2,1)S(1)}, u32[]{:S(2)}, u32[]{:S(2)}) collective-permute-start(bf16[32,256]{1,0:T(8,128)(2,1)S(1)} %get-tuple-element.69.refs_1_), channel_id=1, source_target_pairs={{0,31},{1,0},{2,1},{3,2},{4,3},{5,4},{6,5},{7,6},{8,7},{9,8},{10,9... | collective-permute-start | bytes 49160 | tf_op jit(solution)/shard_map/ppermute | solution.py:21
  74.6 10.0 %collective-permute-start.16 = (bf16[32,256]{1,0:T(8,128)(2,1)S(1)}, bf16[32,256]{1,0:T(8,128)(2,1)S(1)}, u32[]{:S(2)}, u32[]{:S(2)}) collective-permute-start(bf16[32,256]{1,0:T(8,128)(2,1)S(1)} %get-tuple-element.69.refs_1_), channel_id=1, source_target_pairs={{0,1},{1,2},{2,3},{3,4},{4,5},{5,6},{6,7},{7,8},{8,9},{9,10},{10,1... | collective-permute-start | bytes 49160 | tf_op jit(solution)/shard_map/ppermute | solution.py:21
  78.9 19.9 %collective-permute-start.19 = (bf16[48,1024]{1,0:T(8,128)(2,1)S(1)}, bf16[48,1024]{1,0:T(8,128)(2,1)S(1)}, u32[]{:S(2)}, u32[]{:S(2)}) collective-permute-start(bf16[48,1024]{1,0:T(8,128)(2,1)S(1)} %get-tuple-element.80), channel_id=1, source_target_pairs={{0,29},{1,30},{2,31},{3,0},{4,1},{5,2},{6,3},{7,4},{8,5},{9,6},{10... | collective-permute-start | bytes 294920 | tf_op jit(solution)/shard_map/ppermute | solution.py:21
  79.4 17.9 %collective-permute-start.18 = (bf16[160,1024]{1,0:T(8,128)(2,1)S(1)}, bf16[160,1024]{1,0:T(8,128)(2,1)S(1)}, u32[]{:S(2)}, u32[]{:S(2)}) collective-permute-start(bf16[160,1024]{1,0:T(8,128)(2,1)S(1)} %get-tuple-element.78), channel_id=1, source_target_pairs={{0,30},{1,31},{2,0},{3,1},{4,2},{5,3},{6,4},{7,5},{8,6},{9,7},{10,... | collective-permute-start | bytes 983048 | tf_op jit(solution)/shard_map/ppermute | solution.py:21
  82.9 18.5 %collective-permute-start.20 = (bf16[160,1024]{1,0:T(8,128)(2,1)S(1)}, bf16[160,1024]{1,0:T(8,128)(2,1)S(1)}, u32[]{:S(2)}, u32[]{:S(2)}) collective-permute-start(bf16[160,1024]{1,0:T(8,128)(2,1)S(1)} %get-tuple-element.81), channel_id=1, source_target_pairs={{0,2},{1,3},{2,4},{3,5},{4,6},{5,7},{6,8},{7,9},{8,10},{9,11},{10,... | collective-permute-start | bytes 983048 | tf_op jit(solution)/shard_map/ppermute | solution.py:21
  92.2 17.4 %collective-permute-start.22 = (bf16[240,1024]{1,0:T(8,128)(2,1)S(1)}, bf16[240,1024]{1,0:T(8,128)(2,1)S(1)}, u32[]{:S(2)}, u32[]{:S(2)}) collective-permute-start(bf16[240,1024]{1,0:T(8,128)(2,1)S(1)} %get-tuple-element.83), channel_id=1, source_target_pairs={{0,31},{1,0},{2,1},{3,2},{4,3},{5,4},{6,5},{7,6},{8,7},{9,8},{10,9... | collective-permute-start | bytes 1474568 | tf_op jit(solution)/shard_map/ppermute | solution.py:21
  96.8 14.4 %collective-permute-start.21 = (bf16[256,1024]{1,0:T(8,128)(2,1)S(1)}, bf16[256,1024]{1,0:T(8,128)(2,1)S(1)}, u32[]{:S(2)}, u32[]{:S(2)}) collective-permute-start(bf16[256,1024]{1,0:T(8,128)(2,1)S(1)} %get-tuple-element.82), channel_id=1, source_target_pairs={{0,1},{1,2},{2,3},{3,4},{4,5},{5,6},{6,7},{7,8},{8,9},{9,10},{10,1... | collective-permute-start | bytes 1572872 | tf_op jit(solution)/shard_map/ppermute | solution.py:21
  97.2 12.4 %collective-permute-start.23 = (bf16[48,1024]{1,0:T(8,128)(2,1)S(1)}, bf16[48,1024]{1,0:T(8,128)(2,1)S(1)}, u32[]{:S(2)}, u32[]{:S(2)}) collective-permute-start(bf16[48,1024]{1,0:T(8,128)(2,1)S(1)} %get-tuple-element.84), channel_id=1, source_target_pairs={{0,3},{1,4},{2,5},{3,6},{4,7},{5,8},{6,9},{7,10},{8,11},{9,12},{10... | collective-permute-start | bytes 294920 | tf_op jit(solution)/shard_map/ppermute | solution.py:21
  (4 other events, 73.1 us)

commit v7 on v6

--- a/solution.py
+++ b/solution.py
@@ -18,6 +18,17 @@
 def passed_along(value, steps):
     count = lax.axis_size(AXES)
     pairs = [(source, (source + steps) % count) for source in range(count)]
+    return lax.ppermute(value, AXES, pairs)
+
+
+def half_of(device, k):
+    return (device // (k & -k)) % 2
+
+
+def swapped(value, k, part):
+    count = lax.axis_size(AXES)
+    assert count % (2 * (k & -k)) == 0
+    pairs = [(d, (d + (k if half_of(d, k) == part else -k)) % count) for d in range(count)]
     return lax.ppermute(value, AXES, pairs)
 
 
@@ -284,7 +295,7 @@
     return (REACH - level) * SLOT, (REACH + level + 1) * SLOT
 
 
-def unpack_kernel(plan, cut_ref, active_ref, column_ref, own_ref, local_ref, *refs):
+def unpack_kernel(plan, cut_ref, me_ref, active_ref, column_ref, own_ref, local_ref, *refs):
     fun_dev, box_dev, reading, volume, rows, back, blocks = plan
     slots = 2 * REACH + 1
     sources = refs[:REACH] + (None,) + refs[REACH : slots - 1]
@@ -357,9 +368,20 @@
     for part, total in enumerate(totals[:-1]):
         low, high = level_rows(part + 1)
         dense[low:high] += times(total[...], keep[low:high], precision=lax.Precision.HIGHEST)
+    bands = []
     for e in range(slots):
         rows_here = dense[e * SLOT : e * SLOT + fun_dev]
-        gram_refs[e][...] = skewed(moved(rows_here, reading - 1 - e * fun_dev), -1)[:, : 2 * reading]
+        bands.append(skewed(moved(rows_here, reading - 1 - e * fun_dev), -1)[:, : 2 * reading])
+    gram_refs[0][...] = bands[REACH]
+    for k in range(1, REACH + 1):
+        half = lax.rem(lax.div(me_ref[0], k & -k), 2)
+        for part in range(2):
+            ahead, behind = (REACH + k, REACH - k) if part == 0 else (REACH - k, REACH + k)
+
+            @pl.when(half == part)
+            def _():
+                gram_refs[2 * k - 1][...] = bands[ahead]
+                gram_refs[2 * k][...] = bands[behind]
 
 
 def sum_kernel(reading, *refs):
@@ -380,10 +402,10 @@
     return (at[0], at[-1] + 1) if at else (0, 0)
 
 
-def mix_kernel(plan, cut_ref, active_ref, place_ref, window_ref, region_ref, kinetic_ref, *refs):
-    fun_dev, reading, group, whole = plan
+def mix_kernel(plan, cut_ref, me_ref, active_ref, place_ref, window_ref, region_ref, kinetic_ref, *refs):
+    fun_dev, reading, group, whole, swaps = plan
     count = len(group)
-    bands = refs[:count]
+    bands = dict(zip(swaps, refs[:count]))
     outs = refs[count : 2 * count]
     at_boxes = refs[2 * count : 3 * count]
     mixed = refs[3 * count]
@@ -396,8 +418,13 @@
         at_box[...] = jnp.zeros_like(at_box)
     lanes = band_lanes(fun_dev, reading)
     parts = []
-    for e, band_ref in zip(group, bands):
-        band = band_ref[...].astype(jnp.float32)
+    for e in group:
+        k = abs(e - REACH)
+        band = bands[k, 0][...].astype(jnp.float32)
+        if k:
+            half = lax.rem(lax.div(me_ref[0], k & -k), 2).astype(jnp.float32)
+            other = half if e > REACH else 1.0 - half
+            band = band * (1.0 - other) + bands[k, 1][...].astype(jnp.float32) * other
         band = jnp.concatenate([band, jnp.zeros((SLOT, lanes - 2 * reading), jnp.float32)], axis=1)
         parts.append(moved(skewed(band, 1), e * fun_dev - (reading - 1)).astype(jnp.bfloat16))
     for level, mixing in mixings.items():
@@ -487,7 +514,6 @@
     offsets = list(range(-REACH, REACH + 1))
     last = -REACH
     now = [sign * k for k in range(1, REACH) for sign in (-1, 1)] + [REACH]
-    one_way = list(range(REACH, 0, -1)) + list(range(-REACH, 0))
     rows, low_cut, high_cut, boxes, blocks = bounds(fun_dev, support)
     assert blocks <= REACH + 1 and support & (support - 1) == 0
     back = tuple(rounded_up(r, 16) for r in rows)
@@ -553,15 +579,16 @@
             jax.ShapeDtypeStruct((128, points), bf16),
         )
         + tuple(jax.ShapeDtypeStruct(band, f32) for _ in range(slots)),
-        in_specs=[smem, smem] + [vmem] * (3 + len(sources)),
+        in_specs=[smem] * 3 + [vmem] * (3 + len(sources)),
         out_specs=(vmem,) * (2 + slots),
         scratch_shapes=[pltpu.VMEM((wide, band_lanes(fun_dev, reading)), f32)]
         + [pltpu.VMEM((size, size), f32) for size in level_sizes],
         compiler_params=limit,
         name="unpack",
-    )(cut, active, columns, own_region, local, *sources)
-
-    summed = sent({k: grams[REACH + k] for k in one_way}, one_way, 1)
+    )(cut, me, active, columns, own_region, local, *sources)
+
+    swaps = [(k, 0) for k in range(1, REACH + 1)] + [(k, 1) for k in range(REACH, 0, -1)]
+    summed = [swapped(grams[2 * k - 1 + part], k, part) for k, part in swaps]
     gram_band, mixing_rows = pl.pallas_call(
         functools.partial(sum_kernel, reading),
         out_shape=(jax.ShapeDtypeStruct(band, f32), jax.ShapeDtypeStruct((SLOT, 2 * reading), bf16)),
@@ -569,14 +596,16 @@
         out_specs=(vmem, vmem),
         compiler_params=limit,
         name="sum",
-    )(grams[REACH], *[summed[k] for k in one_way])
-    mixing_of = sent({k: mixing_rows for k in one_way}, one_way, 1)
-    mixing_of[0] = mixing_rows
-
+    )(grams[0], *summed)
+    mixing_of = {swap: swapped(mixing_rows, *swap) for swap in swaps}
+
+    mixing_of[0, 0] = mixing_rows
     ready, at_boxes = {}, {}
     for group, whole in [([2, -2, REACH, -REACH], [2, -2, REACH, -REACH]), ([0, 1, -1], [1, -1])]:
         group, whole = sorted(REACH - k for k in group), [REACH - k for k in whole]
         shapes = [(rows_of[REACH - e], points) for e in group] + [(rows_of[REACH - e], 128) for e in group]
+        far = {abs(e - REACH) for e in group}
+        group_swaps = [swap for swap in [(0, 0)] + swaps if swap[0] in far]
         sizes = [
             ((in_level(group, v)[1] - in_level(group, v)[0]) * SLOT, level_sizes[v - 1])
             for v in range(1, REACH + 1)
@@ -586,9 +615,9 @@
             cut, *held = lax.optimization_barrier((cut, *[ready[k] for k in ready]))
             ready = dict(zip(ready, held))
         mixed = pl.pallas_call(
-            functools.partial(mix_kernel, (fun_dev, reading, group, whole)),
+            functools.partial(mix_kernel, (fun_dev, reading, group, whole, group_swaps)),
             out_shape=tuple(jax.ShapeDtypeStruct(shape, bf16) for shape in shapes),
-            in_specs=[smem, smem] + [vmem] * (4 + len(group)),
+            in_specs=[smem] * 3 + [vmem] * (4 + len(group)),
             out_specs=(vmem,) * len(shapes),
             scratch_shapes=[pltpu.VMEM((STEP, len(group) * SLOT, points), bf16)]
             + [pltpu.VMEM(size, bf16) for size in sizes],
@@ -597,7 +626,7 @@
                 flops=8 * wide * len(group) * SLOT * boxes * points, bytes_accessed=40 * 2**20, transcendentals=0
             ),
             name="mix",
-        )(cut, active, places, pieces, region, kinetic, *[mixing_of[REACH - e] for e in group])
+        )(cut, me, active, places, pieces, region, kinetic, *[mixing_of[swap] for swap in group_swaps])
         for at, e in enumerate(group):
             ready[REACH - e], at_boxes[REACH - e] = mixed[at], mixed[len(group) + at]
             if e not in whole:

time: 114 us -> 111 us (0.974)
  the two profiles are of different devices: /device:TPU:0 before, /device:TPU:1 now
where the time goes in v7:
time: 111 us; the launch traced here: 110 us
  starting transfers between devices  56 us (50%)
  Pallas kernels  29.4 us (26%)
  waiting for transfers between devices  20.7 us (19%)
  matrix products  1.69 us (2%)
  local copies, waits for them, and re-layouts  1.65 us (1%)
    ppermute x12, starting transfers between devices, passed_along(): return lax.ppermute(value, AXES, pairs)  37.7 us
    ppermute x12, starting transfers between devices, swapped(): return lax.ppermute(value, AXES, pairs)  18.3 us
    ppermute x12, waiting for transfers between devices, passed_along(): return lax.ppermute(value, AXES, pairs)  16.4 us
    pallas_call x2, Pallas kernels, on_device(): pl.pallas_call(functools.partial(mix_kernel, (fun_dev, reading, group, wh...  11.3 us
    pallas_call x1, Pallas kernels, on_device(): pl.pallas_call(functools.partial(unpack_kernel, (fun_dev, box_dev, readin...  6.26 us
    ppermute x12, waiting for transfers between devices, swapped(): return lax.ppermute(value, AXES, pairs)  4.36 us
    pallas_call x1, Pallas kernels, on_device(): pl.pallas_call(functools.partial(pack_kernel, (fun_dev, support, devices,...  4.11 us
    pallas_call x1, Pallas kernels, on_device(): pl.pallas_call(functools.partial(table_kernel, (fun_dev, support, halo, b...  2.79 us
  transfers between devices with their start and end apart: 24, of which 8 were waited for; matrix products, arithmetic and copies ran while one was open for 2% of the time, Pallas kernels for 15%

profile of v7, /device:TPU:1, one launch (start us, length us, event | category | flops | bytes accessed | tf_op | source)
XLA Modules:
  0.0 110.4 jit_solution(13393805266289157311)
XLA Ops:
  2.3 4.1 %pack.1 = (bf16[272,1024]{1,0:T(8,128)(2,1)}, bf16[240,1024]{1,0:T(8,128)(2,1)S(1)}, bf16[192,1024]{1,0:T(8,128)(2,1)S(1)}, bf16[160,1024]{1,0:T(8,128)(2,1)S(1)...) custom-call(s32[1]{0:T(128)} %bitcast.me_ref, ...), custom_call_target="tpu_custom_call" | custom-call | tf_op jit(solution)/shard_map/pack/pallas_call | solution.py:531
  6.5 2.6 %collective-permute-start.2 = (bf16[240,1024]{1,0:T(8,128)(2,1)S(1)}, bf16[240,1024]{1,0:T(8,128)(2,1)S(1)}, u32[]{:S(2)}, u32[]{:S(2)}) collective-permute-start(bf16[240,1024]{1,0:T(8,128)(2,1)S(1)} %get-tuple-element.54), channel_id=1, source_target_pairs={{0,1},{1,2},{2,3},{3,4},{4,5},{5,6},{6,7},{7,8},{8,9},{9,10},{10,1... | collective-permute-start | bytes 1474568 | tf_op jit(solution)/shard_map/ppermute | solution.py:21
  9.1 8.7 %collective-permute-start.4 = (bf16[192,1024]{1,0:T(8,128)(2,1)S(1)}, bf16[192,1024]{1,0:T(8,128)(2,1)S(1)}, u32[]{:S(2)}, u32[]{:S(2)}) collective-permute-start(bf16[192,1024]{1,0:T(8,128)(2,1)S(1)} %get-tuple-element.58), channel_id=1, source_target_pairs={{0,30},{1,31},{2,0},{3,1},{4,2},{5,3},{6,4},{7,5},{8,6},{9,7},{10,... | collective-permute-start | bytes 1179656 | tf_op jit(solution)/shard_map/ppermute | solution.py:21
  17.8 3.3 %collective-permute-done.3.refs_3_ = bf16[272,1024]{1,0:T(8,128)(2,1)S(1)} collective-permute-done((bf16[272,1024]{1,0:T(8,128)(2,1)}, bf16[272,1024]{1,0:T(8,128)(2,1)S(1)}, u32[]{:S(2)}, u32[]{:S(2)}) %collective-permute-start.3) | collective-permute-done | bytes 557088 | tf_op jit(solution)/shard_map/ppermute | solution.py:21
  21.1 15.0 %collective-permute-start.5 = (bf16[64,1024]{1,0:T(8,128)(2,1)S(1)}, bf16[64,1024]{1,0:T(8,128)(2,1)S(1)}, u32[]{:S(2)}, u32[]{:S(2)}) collective-permute-start(bf16[64,1024]{1,0:T(8,128)(2,1)S(1)} %get-tuple-element.59), channel_id=1, source_target_pairs={{0,29},{1,30},{2,31},{3,0},{4,1},{5,2},{6,3},{7,4},{8,5},{9,6},{10... | collective-permute-start | bytes 393224 | tf_op jit(solution)/shard_map/ppermute | solution.py:21
  36.2 2.8 %tables.1 = (f32[224,128]{1,0:T(8,128)S(1)}, f32[3,8,256]{2,1,0:T(8,128)S(1)}, s32[24]{0:T(128)S(1)}, bf16[24,32,1024]{2,1,0:T(8,128)(2,1)S(1)}) custom-call(s32[8]{0:T(128)S(1)} %get-tuple-element.74.cut_ref, f32[512,128]{1,0:T(8,128)S(1)} %get-tuple-element.46.near_ref, bf16[768,1024]{1,0:T(8,128)(2,1)S(1)} %bitcast.8), custom_call_target="tpu_custom_call" | custom-call | tf_op jit(solution)/shard_map/tables/pallas_call | solution.py:553
  39.0 5.3 %collective-permute-done.refs_0_ = bf16[48,1024]{1,0:T(8,128)(2,1)S(1)} collective-permute-done((bf16[48,1024]{1,0:T(8,128)(2,1)S(1)}, bf16[48,1024]{1,0:T(8,128)(2,1)S(1)}, u32[]{:S(2)}, u32[]{:S(2)}) %collective-permute-start) | collective-permute-done | bytes 98336 | tf_op jit(solution)/shard_map/ppermute | solution.py:21
  44.3 6.3 %unpack.1 = (bf16[24,224,1024]{2,1,0:T(8,128)(2,1)S(1)}, bf16[128,1024]{1,0:T(8,128)(2,1)S(1)}, f32[24,256]{1,0:T(8,128)S(1)}, f32[24,256]{1,0:T(8,128)S(1)}, f3...) custom-call(s32[8]{0:T(128)S(1)} %get-tuple-element.74.cut_ref, ...), custom_call_target="tpu_custom_call" | custom-call | tf_op jit(solution)/shard_map/unpack/pallas_call | solution.py:575
  50.6 1.4 %collective-permute-start.6 = (f32[24,256]{1,0:T(8,128)S(1)}, f32[24,256]{1,0:T(8,128)S(1)}, u32[]{:S(2)}, u32[]{:S(2)}) collective-permute-start(f32[24,256]{1,0:T(8,128)S(1)} %get-tuple-element.63), channel_id=1, source_target_pairs={{0,1},{1,0},{2,3},{3,2},{4,5},{5,4},{6,7},{7,6},{8,9},{9,8},{10,11... | collective-permute-start | bytes 73736 | tf_op jit(solution)/shard_map/ppermute | solution.py:32
  51.9 2.6 %collective-permute-start.8 = (f32[24,256]{1,0:T(8,128)S(1)}, f32[24,256]{1,0:T(8,128)S(1)}, u32[]{:S(2)}, u32[]{:S(2)}) collective-permute-start(f32[24,256]{1,0:T(8,128)S(1)} %get-tuple-element.65), channel_id=1, source_target_pairs={{0,3},{1,30},{2,5},{3,0},{4,7},{5,2},{6,9},{7,4},{8,11},{9,6},{10,... | collective-permute-start | bytes 73736 | tf_op jit(solution)/shard_map/ppermute | solution.py:32
  54.6 2.9 %collective-permute-start.10 = (f32[24,256]{1,0:T(8,128)S(1)}, f32[24,256]{1,0:T(8,128)S(1)}, u32[]{:S(2)}, u32[]{:S(2)}) collective-permute-start(f32[24,256]{1,0:T(8,128)S(1)} %get-tuple-element.67), channel_id=1, source_target_pairs={{0,30},{1,31},{2,4},{3,5},{4,2},{5,3},{6,8},{7,9},{8,6},{9,7},{10,... | collective-permute-start | bytes 73736 | tf_op jit(solution)/shard_map/ppermute | solution.py:32
  59.1 1.7 %collective-permute-done.10.refs_5_ = f32[24,256]{1,0:T(8,128)S(1)} collective-permute-done((f32[24,256]{1,0:T(8,128)S(1)}, f32[24,256]{1,0:T(8,128)S(1)}, u32[]{:S(2)}, u32[]{:S(2)}) %collective-permute-start.10) | collective-permute-done | bytes 24608 | tf_op jit(solution)/shard_map/ppermute | solution.py:32
  61.5 5.6 %collective-permute-start.15 = (bf16[32,256]{1,0:T(8,128)(2,1)S(1)}, bf16[32,256]{1,0:T(8,128)(2,1)S(1)}, u32[]{:S(2)}, u32[]{:S(2)}) collective-permute-start(bf16[32,256]{1,0:T(8,128)(2,1)S(1)} %get-tuple-element.69.refs_0_), channel_id=1, source_target_pairs={{0,30},{1,31},{2,4},{3,5},{4,2},{5,3},{6,8},{7,9},{8,6},{9,7},{10,... | collective-permute-start | bytes 49160 | tf_op jit(solution)/shard_map/ppermute | solution.py:32
  67.1 3.3 %collective-permute-start.13 = (bf16[32,256]{1,0:T(8,128)(2,1)S(1)}, bf16[32,256]{1,0:T(8,128)(2,1)S(1)}, u32[]{:S(2)}, u32[]{:S(2)}) collective-permute-start(bf16[32,256]{1,0:T(8,128)(2,1)S(1)} %get-tuple-element.69.refs_0_), channel_id=1, source_target_pairs={{0,3},{1,30},{2,5},{3,0},{4,7},{5,2},{6,9},{7,4},{8,11},{9,6},{10,... | collective-permute-start | bytes 49160 | tf_op jit(solution)/shard_map/ppermute | solution.py:32
  70.4 2.2 %collective-permute-start.16 = (bf16[32,256]{1,0:T(8,128)(2,1)S(1)}, bf16[32,256]{1,0:T(8,128)(2,1)S(1)}, u32[]{:S(2)}, u32[]{:S(2)}) collective-permute-start(bf16[32,256]{1,0:T(8,128)(2,1)S(1)} %get-tuple-element.69.refs_0_), channel_id=1, source_target_pairs={{0,1},{1,0},{2,3},{3,2},{4,5},{5,4},{6,7},{7,6},{8,9},{9,8},{10,11... | collective-permute-start | bytes 49160 | tf_op jit(solution)/shard_map/ppermute | solution.py:32
  73.9 4.7 %mix.2 = (bf16[48,1024]{1,0:T(8,128)(2,1)S(1)}, bf16[160,1024]{1,0:T(8,128)(2,1)S(1)}, bf16[160,1024]{1,0:T(8,128)(2,1)S(1)}, bf16[48,1024]{1,0:T(8,128)(2,1)S(1...) custom-call(s32[8]{0:T(128)S(1)} %get-tuple-element.74.cut_ref, ...), custom_call_target="tpu_custom_call" | custom-call | flops 5637144576 | bytes 41943040 | tf_op jit(solution)/shard_map/mix/pallas_call | solution.py:617
  78.6 3.3 %collective-permute-start.19 = (bf16[48,1024]{1,0:T(8,128)(2,1)S(1)}, bf16[48,1024]{1,0:T(8,128)(2,1)S(1)}, u32[]{:S(2)}, u32[]{:S(2)}) collective-permute-start(bf16[48,1024]{1,0:T(8,128)(2,1)S(1)} %get-tuple-element.80), channel_id=1, source_target_pairs={{0,29},{1,30},{2,31},{3,0},{4,1},{5,2},{6,3},{7,4},{8,5},{9,6},{10... | collective-permute-start | bytes 294920 | tf_op jit(solution)/shard_map/ppermute | solution.py:21
  81.9 1.5 %collective-permute-start.20 = (bf16[160,1024]{1,0:T(8,128)(2,1)S(1)}, bf16[160,1024]{1,0:T(8,128)(2,1)S(1)}, u32[]{:S(2)}, u32[]{:S(2)}) collective-permute-start(bf16[160,1024]{1,0:T(8,128)(2,1)S(1)} %get-tuple-element.81), channel_id=1, source_target_pairs={{0,2},{1,3},{2,4},{3,5},{4,6},{5,7},{6,8},{7,9},{8,10},{9,11},{10,... | collective-permute-start | bytes 983048 | tf_op jit(solution)/shard_map/ppermute | solution.py:21
  83.3 6.5 %mix.3 = (bf16[240,1024]{1,0:T(8,128)(2,1)S(1)}, bf16[512,1024]{1,0:T(8,128)(2,1)S(1)}, bf16[256,1024]{1,0:T(8,128)(2,1)S(1)}, bf16[240,128]{1,0:T(8,128)(2,1)},...) custom-call(s32[8]{0:T(128)S(1)} %get-tuple-element.74.cut_ref, s32[1]{0:T(128)} %bitcast.me_ref, ...), custom_call_target="tpu_custom_call" | custom-call | flops 4227858432 | bytes 41943040 | tf_op jit(solution)/shard_map/mix/pallas_call | solution.py:617
  92.1 4.7 %collective-permute-start.23 = (bf16[48,1024]{1,0:T(8,128)(2,1)S(1)}, bf16[48,1024]{1,0:T(8,128)(2,1)S(1)}, u32[]{:S(2)}, u32[]{:S(2)}) collective-permute-start(bf16[48,1024]{1,0:T(8,128)(2,1)S(1)} %get-tuple-element.84), channel_id=1, source_target_pairs={{0,3},{1,4},{2,5},{3,6},{4,7},{5,8},{6,9},{7,10},{8,11},{9,12},{10... | collective-permute-start | bytes 294920 | tf_op jit(solution)/shard_map/ppermute | solution.py:21
  98.1 3.1 %collective-permute-done.20.refs_3_ = bf16[160,1024]{1,0:T(8,128)(2,1)S(1)} collective-permute-done((bf16[160,1024]{1,0:T(8,128)(2,1)S(1)}, bf16[160,1024]{1,0:T(8,128)(2,1)S(1)}, u32[]{:S(2)}, u32[]{:S(2)}) %collective-permute-start.20) | collective-permute-done | bytes 327712 | tf_op jit(solution)/shard_map/ppermute | solution.py:21
  101.2 2.0 %early.1.early_ref = bf16[768,1024]{1,0:T(8,128)(2,1)S(1)} custom-call(f32[1,768]{1,0:T(1,128)S(1)} %get-tuple-element.44.home_ref, bf16[512,1024]{1,0:T(8,128)(2,1)S(1)} %add_convert_fusion.refs_0_, bf16[160,1024]{1,0:T(8,128)(2,1)S(1)} %collective-permute-done.18.refs_1_, bf16[48,1024]{1,0:T(8,128)(2,1)S(1)} %collective-permute-done.19.refs_2_, ...), custom_call_target="tpu_custom_call" | custom-call | tf_op jit(solution)/shard_map/early/pallas_call | solution.py:644
  103.2 4.2 %collective-permute-done.23.refs_2_ = bf16[48,1024]{1,0:T(8,128)(2,1)S(1)} collective-permute-done((bf16[48,1024]{1,0:T(8,128)(2,1)S(1)}, bf16[48,1024]{1,0:T(8,128)(2,1)S(1)}, u32[]{:S(2)}, u32[]{:S(2)}) %collective-permute-start.23) | collective-permute-done | bytes 98336 | tf_op jit(solution)/shard_map/ppermute | solution.py:21
  107.8 2.4 %home.1 = bf16[768,1024]{1,0:T(8,128)(2,1)} custom-call(f32[1,768]{1,0:T(1,128)S(1)} %get-tuple-element.44.home_ref, bf16[768,1024]{1,0:T(8,128)(2,1)S(1)} %early.1.early_ref, bf16[256,1024]{1,0:T(8,128)(2,1)S(1)} %collective-permute-done.21.refs_0_, bf16[240,1024]{1,0:T(8,128)(2,1)S(1)} %collective-permute-done.22.refs_1_, ...), custom_call_target="tpu_custom_call" | custom-call | tf_op jit(solution)/shard_map/home/pallas_call | solution.py:652
  (42 shorter events, 9.2 us)
Async XLA Ops:
  6.4 14.7 %collective-permute-start.3 = (bf16[272,1024]{1,0:T(8,128)(2,1)}, bf16[272,1024]{1,0:T(8,128)(2,1)S(1)}, u32[]{:S(2)}, u32[]{:S(2)}) collective-permute-start(bf16[272,1024]{1,0:T(8,128)(2,1)} %get-tuple-element.56), channel_id=1, source_target_pairs={{0,31},{1,0},{2,1},{3,2},{4,3},{5,4},{6,5},{7,6},{8,7},{9,8},{10,9... | collective-permute-start | bytes 1671176 | tf_op jit(solution)/shard_map/ppermute | solution.py:21
  6.5 37.8 %collective-permute-start.2 = (bf16[240,1024]{1,0:T(8,128)(2,1)S(1)}, bf16[240,1024]{1,0:T(8,128)(2,1)S(1)}, u32[]{:S(2)}, u32[]{:S(2)}) collective-permute-start(bf16[240,1024]{1,0:T(8,128)(2,1)S(1)} %get-tuple-element.54), channel_id=1, source_target_pairs={{0,1},{1,2},{2,3},{3,4},{4,5},{5,6},{6,7},{7,8},{8,9},{9,10},{10,1... | collective-permute-start | bytes 1474568 | tf_op jit(solution)/shard_map/ppermute | solution.py:21
  9.1 35.2 %collective-permute-start.4 = (bf16[192,1024]{1,0:T(8,128)(2,1)S(1)}, bf16[192,1024]{1,0:T(8,128)(2,1)S(1)}, u32[]{:S(2)}, u32[]{:S(2)}) collective-permute-start(bf16[192,1024]{1,0:T(8,128)(2,1)S(1)} %get-tuple-element.58), channel_id=1, source_target_pairs={{0,30},{1,31},{2,0},{3,1},{4,2},{5,3},{6,4},{7,5},{8,6},{9,7},{10,... | collective-permute-start | bytes 1179656 | tf_op jit(solution)/shard_map/ppermute | solution.py:21
  17.8 26.5 %collective-permute-start.1 = (bf16[160,1024]{1,0:T(8,128)(2,1)S(1)}, bf16[160,1024]{1,0:T(8,128)(2,1)S(1)}, u32[]{:S(2)}, u32[]{:S(2)}) collective-permute-start(bf16[160,1024]{1,0:T(8,128)(2,1)S(1)} %get-tuple-element.53), channel_id=1, source_target_pairs={{0,2},{1,3},{2,4},{3,5},{4,6},{5,7},{6,8},{7,9},{8,10},{9,11},{10,... | collective-permute-start | bytes 983048 | tf_op jit(solution)/shard_map/ppermute | solution.py:21
  21.1 23.2 %collective-permute-start.5 = (bf16[64,1024]{1,0:T(8,128)(2,1)S(1)}, bf16[64,1024]{1,0:T(8,128)(2,1)S(1)}, u32[]{:S(2)}, u32[]{:S(2)}) collective-permute-start(bf16[64,1024]{1,0:T(8,128)(2,1)S(1)} %get-tuple-element.59), channel_id=1, source_target_pairs={{0,29},{1,30},{2,31},{3,0},{4,1},{5,2},{6,3},{7,4},{8,5},{9,6},{10... | collective-permute-start | bytes 393224 | tf_op jit(solution)/shard_map/ppermute | solution.py:21
  36.2 8.1 %collective-permute-start = (bf16[48,1024]{1,0:T(8,128)(2,1)S(1)}, bf16[48,1024]{1,0:T(8,128)(2,1)S(1)}, u32[]{:S(2)}, u32[]{:S(2)}) collective-permute-start(bf16[48,1024]{1,0:T(8,128)(2,1)S(1)} %get-tuple-element.52), channel_id=1, source_target_pairs={{0,3},{1,4},{2,5},{3,6},{4,7},{5,8},{6,9},{7,10},{8,11},{9,12},{10... | collective-permute-start | bytes 294920 | tf_op jit(solution)/shard_map/ppermute | solution.py:21
  50.6 6.9 %collective-permute-start.6 = (f32[24,256]{1,0:T(8,128)S(1)}, f32[24,256]{1,0:T(8,128)S(1)}, u32[]{:S(2)}, u32[]{:S(2)}) collective-permute-start(f32[24,256]{1,0:T(8,128)S(1)} %get-tuple-element.63), channel_id=1, source_target_pairs={{0,1},{1,0},{2,3},{3,2},{4,5},{5,4},{6,7},{7,6},{8,9},{9,8},{10,11... | collective-permute-start | bytes 73736 | tf_op jit(solution)/shard_map/ppermute | solution.py:32
  51.9 5.9 %collective-permute-start.7 = (f32[24,256]{1,0:T(8,128)S(1)}, f32[24,256]{1,0:T(8,128)S(1)}, u32[]{:S(2)}, u32[]{:S(2)}) collective-permute-start(f32[24,256]{1,0:T(8,128)S(1)} %get-tuple-element.64), channel_id=1, source_target_pairs={{0,2},{1,3},{2,0},{3,1},{4,6},{5,7},{6,4},{7,5},{8,10},{9,11},{10,... | collective-permute-start | bytes 73736 | tf_op jit(solution)/shard_map/ppermute | solution.py:32
  51.9 7.2 %collective-permute-start.8 = (f32[24,256]{1,0:T(8,128)S(1)}, f32[24,256]{1,0:T(8,128)S(1)}, u32[]{:S(2)}, u32[]{:S(2)}) collective-permute-start(f32[24,256]{1,0:T(8,128)S(1)} %get-tuple-element.65), channel_id=1, source_target_pairs={{0,3},{1,30},{2,5},{3,0},{4,7},{5,2},{6,9},{7,4},{8,11},{9,6},{10,... | collective-permute-start | bytes 73736 | tf_op jit(solution)/shard_map/ppermute | solution.py:32
  54.6 4.5 %collective-permute-start.9 = (f32[24,256]{1,0:T(8,128)S(1)}, f32[24,256]{1,0:T(8,128)S(1)}, u32[]{:S(2)}, u32[]{:S(2)}) collective-permute-start(f32[24,256]{1,0:T(8,128)S(1)} %get-tuple-element.66), channel_id=1, source_target_pairs={{0,29},{1,4},{2,31},{3,6},{4,1},{5,8},{6,3},{7,10},{8,5},{9,12},{1... | collective-permute-start | bytes 73736 | tf_op jit(solution)/shard_map/ppermute | solution.py:32
  54.6 6.3 %collective-permute-start.10 = (f32[24,256]{1,0:T(8,128)S(1)}, f32[24,256]{1,0:T(8,128)S(1)}, u32[]{:S(2)}, u32[]{:S(2)}) collective-permute-start(f32[24,256]{1,0:T(8,128)S(1)} %get-tuple-element.67), channel_id=1, source_target_pairs={{0,30},{1,31},{2,4},{3,5},{4,2},{5,3},{6,8},{7,9},{8,6},{9,7},{10,... | collective-permute-start | bytes 73736 | tf_op jit(solution)/shard_map/ppermute | solution.py:32
  57.5 3.3 %collective-permute-start.11 = (f32[24,256]{1,0:T(8,128)S(1)}, f32[24,256]{1,0:T(8,128)S(1)}, u32[]{:S(2)}, u32[]{:S(2)}) collective-permute-start(f32[24,256]{1,0:T(8,128)S(1)} %get-tuple-element.68), channel_id=1, source_target_pairs={{0,31},{1,2},{2,1},{3,4},{4,3},{5,6},{6,5},{7,8},{8,7},{9,10},{10,... | collective-permute-start | bytes 73736 | tf_op jit(solution)/shard_map/ppermute | solution.py:32
  61.5 8.9 %collective-permute-start.15 = (bf16[32,256]{1,0:T(8,128)(2,1)S(1)}, bf16[32,256]{1,0:T(8,128)(2,1)S(1)}, u32[]{:S(2)}, u32[]{:S(2)}) collective-permute-start(bf16[32,256]{1,0:T(8,128)(2,1)S(1)} %get-tuple-element.69.refs_0_), channel_id=1, source_target_pairs={{0,30},{1,31},{2,4},{3,5},{4,2},{5,3},{6,8},{7,9},{8,6},{9,7},{10,... | collective-permute-start | bytes 49160 | tf_op jit(solution)/shard_map/ppermute | solution.py:32
  67.1 5.5 %collective-permute-start.14 = (bf16[32,256]{1,0:T(8,128)(2,1)S(1)}, bf16[32,256]{1,0:T(8,128)(2,1)S(1)}, u32[]{:S(2)}, u32[]{:S(2)}) collective-permute-start(bf16[32,256]{1,0:T(8,128)(2,1)S(1)} %get-tuple-element.69.refs_0_), channel_id=1, source_target_pairs={{0,29},{1,4},{2,31},{3,6},{4,1},{5,8},{6,3},{7,10},{8,5},{9,12},{1... | collective-permute-start | bytes 49160 | tf_op jit(solution)/shard_map/ppermute | solution.py:32
  67.1 6.8 %collective-permute-start.13 = (bf16[32,256]{1,0:T(8,128)(2,1)S(1)}, bf16[32,256]{1,0:T(8,128)(2,1)S(1)}, u32[]{:S(2)}, u32[]{:S(2)}) collective-permute-start(bf16[32,256]{1,0:T(8,128)(2,1)S(1)} %get-tuple-element.69.refs_0_), channel_id=1, source_target_pairs={{0,3},{1,30},{2,5},{3,0},{4,7},{5,2},{6,9},{7,4},{8,11},{9,6},{10,... | collective-permute-start | bytes 49160 | tf_op jit(solution)/shard_map/ppermute | solution.py:32
  70.4 3.5 %collective-permute-start.12 = (bf16[32,256]{1,0:T(8,128)(2,1)S(1)}, bf16[32,256]{1,0:T(8,128)(2,1)S(1)}, u32[]{:S(2)}, u32[]{:S(2)}) collective-permute-start(bf16[32,256]{1,0:T(8,128)(2,1)S(1)} %get-tuple-element.69.refs_0_), channel_id=1, source_target_pairs={{0,2},{1,3},{2,0},{3,1},{4,6},{5,7},{6,4},{7,5},{8,10},{9,11},{10,... | collective-permute-start | bytes 49160 | tf_op jit(solution)/shard_map/ppermute | solution.py:32
  70.4 13.0 %collective-permute-start.17 = (bf16[32,256]{1,0:T(8,128)(2,1)S(1)}, bf16[32,256]{1,0:T(8,128)(2,1)S(1)}, u32[]{:S(2)}, u32[]{:S(2)}) collective-permute-start(bf16[32,256]{1,0:T(8,128)(2,1)S(1)} %get-tuple-element.69.refs_0_), channel_id=1, source_target_pairs={{0,31},{1,2},{2,1},{3,4},{4,3},{5,6},{6,5},{7,8},{8,7},{9,10},{10,... | collective-permute-start | bytes 49160 | tf_op jit(solution)/shard_map/ppermute | solution.py:32
  70.4 13.0 %collective-permute-start.16 = (bf16[32,256]{1,0:T(8,128)(2,1)S(1)}, bf16[32,256]{1,0:T(8,128)(2,1)S(1)}, u32[]{:S(2)}, u32[]{:S(2)}) collective-permute-start(bf16[32,256]{1,0:T(8,128)(2,1)S(1)} %get-tuple-element.69.refs_0_), channel_id=1, source_target_pairs={{0,1},{1,0},{2,3},{3,2},{4,5},{5,4},{6,7},{7,6},{8,9},{9,8},{10,11... | collective-permute-start | bytes 49160 | tf_op jit(solution)/shard_map/ppermute | solution.py:32
  78.6 19.5 %collective-permute-start.19 = (bf16[48,1024]{1,0:T(8,128)(2,1)S(1)}, bf16[48,1024]{1,0:T(8,128)(2,1)S(1)}, u32[]{:S(2)}, u32[]{:S(2)}) collective-permute-start(bf16[48,1024]{1,0:T(8,128)(2,1)S(1)} %get-tuple-element.80), channel_id=1, source_target_pairs={{0,29},{1,30},{2,31},{3,0},{4,1},{5,2},{6,3},{7,4},{8,5},{9,6},{10... | collective-permute-start | bytes 294920 | tf_op jit(solution)/shard_map/ppermute | solution.py:21
  81.9 10.2 %collective-permute-start.18 = (bf16[160,1024]{1,0:T(8,128)(2,1)S(1)}, bf16[160,1024]{1,0:T(8,128)(2,1)S(1)}, u32[]{:S(2)}, u32[]{:S(2)}) collective-permute-start(bf16[160,1024]{1,0:T(8,128)(2,1)S(1)} %get-tuple-element.78), channel_id=1, source_target_pairs={{0,30},{1,31},{2,0},{3,1},{4,2},{5,3},{6,4},{7,5},{8,6},{9,7},{10,... | collective-permute-start | bytes 983048 | tf_op jit(solution)/shard_map/ppermute | solution.py:21
  81.9 19.3 %collective-permute-start.20 = (bf16[160,1024]{1,0:T(8,128)(2,1)S(1)}, bf16[160,1024]{1,0:T(8,128)(2,1)S(1)}, u32[]{:S(2)}, u32[]{:S(2)}) collective-permute-start(bf16[160,1024]{1,0:T(8,128)(2,1)S(1)} %get-tuple-element.81), channel_id=1, source_target_pairs={{0,2},{1,3},{2,4},{3,5},{4,6},{5,7},{6,8},{7,9},{8,10},{9,11},{10,... | collective-permute-start | bytes 983048 | tf_op jit(solution)/shard_map/ppermute | solution.py:21
  89.9 17.5 %collective-permute-start.22 = (bf16[240,1024]{1,0:T(8,128)(2,1)S(1)}, bf16[240,1024]{1,0:T(8,128)(2,1)S(1)}, u32[]{:S(2)}, u32[]{:S(2)}) collective-permute-start(bf16[240,1024]{1,0:T(8,128)(2,1)S(1)} %get-tuple-element.83), channel_id=1, source_target_pairs={{0,31},{1,0},{2,1},{3,2},{4,3},{5,4},{6,5},{7,6},{8,7},{9,8},{10,9... | collective-permute-start | bytes 1474568 | tf_op jit(solution)/shard_map/ppermute | solution.py:21
  90.4 17.4 %collective-permute-start.21 = (bf16[256,1024]{1,0:T(8,128)(2,1)S(1)}, bf16[256,1024]{1,0:T(8,128)(2,1)S(1)}, u32[]{:S(2)}, u32[]{:S(2)}) collective-permute-start(bf16[256,1024]{1,0:T(8,128)(2,1)S(1)} %get-tuple-element.82), channel_id=1, source_target_pairs={{0,1},{1,2},{2,3},{3,4},{4,5},{5,6},{6,7},{7,8},{8,9},{9,10},{10,1... | collective-permute-start | bytes 1572872 | tf_op jit(solution)/shard_map/ppermute | solution.py:21
  92.1 15.3 %collective-permute-start.23 = (bf16[48,1024]{1,0:T(8,128)(2,1)S(1)}, bf16[48,1024]{1,0:T(8,128)(2,1)S(1)}, u32[]{:S(2)}, u32[]{:S(2)}) collective-permute-start(bf16[48,1024]{1,0:T(8,128)(2,1)S(1)} %get-tuple-element.84), channel_id=1, source_target_pairs={{0,3},{1,4},{2,5},{3,6},{4,7},{5,8},{6,9},{7,10},{8,11},{9,12},{10... | collective-permute-start | bytes 294920 | tf_op jit(solution)/shard_map/ppermute | solution.py:21
  (4 other events, 72.1 us)

commit v8 on v7

--- a/solution.py
+++ b/solution.py
@@ -406,10 +406,13 @@
     fun_dev, reading, group, whole, swaps = plan
     count = len(group)
     bands = dict(zip(swaps, refs[:count]))
-    outs = refs[count : 2 * count]
+    swap_outs = refs[count : 2 * count]
     at_boxes = refs[2 * count : 3 * count]
     mixed = refs[3 * count]
-    mixings = dict(zip([v for v in range(1, REACH + 1) if in_level(group, v)[1]], refs[3 * count + 1 :]))
+    levels = [v for v in range(1, REACH + 1) if in_level(group, v)[1]]
+    mixings = dict(zip(levels, refs[3 * count + 1 :]))
+    held = iter(refs[3 * count + 1 + len(levels) :])
+    outs = [swap_outs[at] if e == REACH else next(held) for at, e in enumerate(group)]
     slots = 2 * REACH + 1
     steps = window_ref.shape[0] // STEP
     width = cut_ref[REACH + 1] - cut_ref[REACH]
@@ -465,36 +468,46 @@
             applied = times(here, kinetic_ref[...])
             near_by = times(at_boxes[at][...], region_ref[...])
             outs[at][...] = (applied + near_by * here.astype(jnp.float32)).astype(jnp.bfloat16)
-
-
-def home_rows(bases, home_ref, sources, at, count):
+    for k in sorted({abs(e - REACH) for e in group} - {0}):
+        behind, ahead = group.index(REACH - k), group.index(REACH + k)
+        half = lax.rem(lax.div(me_ref[0], k & -k), 2)
+        for part, first, second in ((0, ahead, behind), (1, behind, ahead)):
+            @pl.when(half == part)
+            def _():
+                swap_outs[behind][...] = outs[first][...]
+                swap_outs[ahead][...] = outs[second][...]
+
+
+def home_rows(bases, me_ref, home_ref, sources, at, count):
     shape = (count, home_ref.shape[1])
     here = iota(shape, 1) == iota(shape, 0) + float(at)
     row = jnp.sum(jnp.where(here, home_ref[...], 0.0), axis=1, keepdims=True)
     value = None
-    for base, group in bases:
-        parts = [sources[at][...] for at in group]
-        held = parts[0] if len(parts) == 1 else jnp.concatenate(parts, axis=0)
-        pick = one_hot(iota((count, held.shape[0]), 1) == row - float(base))
-        term = times(pick, held)
+    for (ahead, behind, k, part), source in zip(bases, sources):
+        base = float(ahead)
+        if k:
+            half = lax.rem(lax.div(me_ref[0], k & -k), 2)
+            base = jnp.where(half == part, ahead, behind).astype(jnp.float32)
+        pick = one_hot(iota((count, source.shape[0]), 1) == row - base)
+        term = times(pick, source[...])
         value = term if value is None else value + term
     return value
 
 
-def early_kernel(bases, home_ref, *refs):
+def early_kernel(bases, me_ref, home_ref, *refs):
     sources, out_ref = refs[:-1], refs[-1]
     count = 256
     for at in range(0, out_ref.shape[0], count):
-        out_ref[at : at + count] = home_rows(bases, home_ref, sources, at, count).astype(jnp.bfloat16)
-
-
-def home_kernel(bases, home_ref, early_ref, *refs):
+        out_ref[at : at + count] = home_rows(bases, me_ref, home_ref, sources, at, count).astype(jnp.bfloat16)
+
+
+def home_kernel(bases, me_ref, home_ref, early_ref, *refs):
     sources, out_ref, held, sems = refs[:-3], refs[-3], refs[-2], refs[-1]
     copies = []
     count = held.shape[1]
     for part in range(held.shape[0]):
         at = part * count
-        value = home_rows(bases, home_ref, sources, at, count) + early_ref[at : at + count].astype(jnp.float32)
+        value = home_rows(bases, me_ref, home_ref, sources, at, count) + early_ref[at : at + count].astype(jnp.float32)
         held[part] = value.astype(jnp.bfloat16)
         copy = pltpu.make_async_copy(held.at[part], out_ref.at[pl.ds(at, count)], sems.at[part])
         copy.start()
@@ -603,7 +616,8 @@
     ready, at_boxes = {}, {}
     for group, whole in [([2, -2, REACH, -REACH], [2, -2, REACH, -REACH]), ([0, 1, -1], [1, -1])]:
         group, whole = sorted(REACH - k for k in group), [REACH - k for k in whole]
-        shapes = [(rows_of[REACH - e], points) for e in group] + [(rows_of[REACH - e], 128) for e in group]
+        most = [max(rows_of[REACH - e], rows_of[e - REACH]) for e in group]
+        shapes = [(r, points) for r in most] + [(r, 128) for r in most]
         far = {abs(e - REACH) for e in group}
         group_swaps = [swap for swap in [(0, 0)] + swaps if swap[0] in far]
         sizes = [
@@ -620,7 +634,8 @@
             in_specs=[smem] * 3 + [vmem] * (4 + len(group)),
             out_specs=(vmem,) * len(shapes),
             scratch_shapes=[pltpu.VMEM((STEP, len(group) * SLOT, points), bf16)]
-            + [pltpu.VMEM(size, bf16) for size in sizes],
+            + [pltpu.VMEM(size, bf16) for size in sizes]
+            + [pltpu.VMEM((r, points), bf16) for r, e in zip(most, group) if e != REACH],
             compiler_params=limit,
             cost_estimate=pl.CostEstimate(
                 flops=8 * wide * len(group) * SLOT * boxes * points, bytes_accessed=40 * 2**20, transcendentals=0
@@ -628,31 +643,34 @@
             name="mix",
         )(cut, me, active, places, pieces, region, kinetic, *[mixing_of[swap] for swap in group_swaps])
         for at, e in enumerate(group):
-            ready[REACH - e], at_boxes[REACH - e] = mixed[at], mixed[len(group) + at]
+            key = (abs(e - REACH), int(e > REACH))
+            ready[key], at_boxes[key] = mixed[at], mixed[len(group) + at]
             if e not in whole:
-                near_by = jnp.dot(at_boxes[REACH - e], region, preferred_element_type=f32)
+                near_by = jnp.dot(at_boxes[key], region, preferred_element_type=f32)
                 applied = jnp.dot(mixed[at], kinetic, preferred_element_type=f32)
-                ready[REACH - e] = (applied + near_by * mixed[at].astype(f32)).astype(bf16)
-    returned = all_sent(ready, [2, -2, 1, -1, REACH], -REACH, -1)
-    returned[0] = ready[0]
+                ready[key] = (applied + near_by * mixed[at].astype(f32)).astype(bf16)
+    far = (REACH, 1)
+    returned = {swap: swapped(ready[swap], *swap) for swap in swaps if swap != far}
+    value, returned[2, 0] = lax.optimization_barrier((ready[far], returned[2, 0]))
+    returned[far] = swapped(value, *far)
+    returned[0, 0] = ready[0, 0]
 
     bases = {k: sum(back[: k + REACH]) for k in offsets}
-    early, late = [0, 2, REACH, -2], [-1, 1, -REACH]
-    assert bases[REACH] == bases[2] + rows_of[2]
-    early_groups = [(bases[0], [0]), (bases[2], [1, 2]), (bases[-2], [3])]
-    late_groups = [(bases[k], [at]) for at, k in enumerate(late)]
+    early, late = [(0, 0), (2, 0), (2, 1), (REACH, 0)], [(1, 0), (1, 1), far]
+    early_bases = [(bases[k], bases[-k], k, part) for k, part in early]
+    late_bases = [(bases[k], bases[-k], k, part) for k, part in late]
     begun = pl.pallas_call(
-        functools.partial(early_kernel, early_groups),
+        functools.partial(early_kernel, early_bases),
         out_shape=jax.ShapeDtypeStruct(flat.shape, bf16),
-        in_specs=[vmem] * (1 + len(early)),
+        in_specs=[smem] + [vmem] * (1 + len(early)),
         out_specs=vmem,
         compiler_params=limit,
         name="early",
-    )(home_row, *[returned[k] for k in early])
+    )(me, home_row, *[returned[swap] for swap in early])
     filtered = pl.pallas_call(
-        functools.partial(home_kernel, late_groups),
+        functools.partial(home_kernel, late_bases),
         out_shape=jax.ShapeDtypeStruct(flat.shape, bf16),
-        in_specs=[vmem] * (2 + len(late)),
+        in_specs=[smem] + [vmem] * (2 + len(late)),
         out_specs=pl.BlockSpec(memory_space=pl.ANY),
         scratch_shapes=[
             pltpu.VMEM((flat.shape[0] // 256, 256, points), bf16),
@@ -660,7 +678,7 @@
         ],
         compiler_params=limit,
         name="home",
-    )(home_row, begun, *[returned[k] for k in late])
+    )(me, home_row, begun, *[returned[swap] for swap in late])
     return (filtered.reshape(coeffs.shape), gram_band)
 
 

time: 111 us -> 111 us (level)
  starting transfers between devices: 56 us -> 50.1 us
  Pallas kernels: 29.4 us -> 33.9 us
  waiting for transfers between devices: 20.7 us -> 22.7 us
    ppermute x12 -> x6, starting transfers between devices: 37.7 us -> 26.5 us  [passed_along(): return lax.ppermute(value, AXES, pairs)]
    ppermute x12 -> x18, waiting for transfers between devices: 4.36 us -> 14.1 us  [swapped(): return lax.ppermute(value, AXES, pairs)]
    ppermute x12 -> x6, waiting for transfers between devices: 16.4 us -> 8.6 us  [passed_along(): return lax.ppermute(value, AXES, pairs)]
    ppermute x12 -> x18, starting transfers between devices: 18.3 us -> 23.6 us  [swapped(): return lax.ppermute(value, AXES, pairs)]
    pallas_call x2, Pallas kernels: 11.3 us -> 13.9 us  [on_device(): pl.pallas_call(functools.partial(mix_kernel, (fun_dev, reading, group, wh...]
    pallas_call x1, Pallas kernels: 6.26 us -> 7.79 us  [on_device(): pl.pallas_call(functools.partial(unpack_kernel, (fun_dev, box_dev, readin...]
  transfers between devices with their start and end apart: 24 -> 24, of which waited for: 8 -> 9; matrix products, arithmetic and copies ran while one was open for 2% -> 2% of each run, Pallas kernels for 15% -> 17%
where the time goes in v8:
time: 111 us
  starting transfers between devices  50.1 us (45%)
  Pallas kernels  33.9 us (31%)
  waiting for transfers between devices  22.7 us (20%)
  matrix products  1.72 us (2%)
  local copies, waits for them, and re-layouts  1.65 us (1%)
    ppermute x6, starting transfers between devices, passed_along(): return lax.ppermute(value, AXES, pairs)  26.5 us
    ppermute x18, starting transfers between devices, swapped(): return lax.ppermute(value, AXES, pairs)  23.6 us
    ppermute x18, waiting for transfers between devices, swapped(): return lax.ppermute(value, AXES, pairs)  14.1 us
    pallas_call x2, Pallas kernels, on_device(): pl.pallas_call(functools.partial(mix_kernel, (fun_dev, reading, group, wh...  13.9 us
    ppermute x6, waiting for transfers between devices, passed_along(): return lax.ppermute(value, AXES, pairs)  8.6 us
    pallas_call x1, Pallas kernels, on_device(): pl.pallas_call(functools.partial(unpack_kernel, (fun_dev, box_dev, readin...  7.79 us
    pallas_call x1, Pallas kernels, on_device(): pl.pallas_call(functools.partial(pack_kernel, (fun_dev, support, devices,...  4.11 us
    pallas_call x1, Pallas kernels, on_device(): pl.pallas_call(functools.partial(table_kernel, (fun_dev, support, halo, b...  2.79 us
  transfers between devices with their start and end apart: 24, of which 9 were waited for; matrix products, arithmetic and copies ran while one was open for 2% of the time, Pallas kernels for 17%

profile of v8, /device:TPU:1, one launch (start us, length us, event | category | flops | bytes accessed | tf_op | source)
XLA Modules:
  0.0 111.0 jit_solution(1792565274098777214)
XLA Ops:
  2.3 4.1 %pack.1 = (bf16[272,1024]{1,0:T(8,128)(2,1)}, bf16[240,1024]{1,0:T(8,128)(2,1)S(1)}, bf16[192,1024]{1,0:T(8,128)(2,1)S(1)}, bf16[160,1024]{1,0:T(8,128)(2,1)S(1)...) custom-call(s32[1]{0:T(128)} %bitcast.me_ref, ...), custom_call_target="tpu_custom_call" | custom-call | tf_op jit(solution)/shard_map/pack/pallas_call | solution.py:544
  6.5 2.6 %collective-permute-start.2 = (bf16[240,1024]{1,0:T(8,128)(2,1)S(1)}, bf16[240,1024]{1,0:T(8,128)(2,1)S(1)}, u32[]{:S(2)}, u32[]{:S(2)}) collective-permute-start(bf16[240,1024]{1,0:T(8,128)(2,1)S(1)} %get-tuple-element.54), channel_id=1, source_target_pairs={{0,1},{1,2},{2,3},{3,4},{4,5},{5,6},{6,7},{7,8},{8,9},{9,10},{10,1... | collective-permute-start | bytes 1474568 | tf_op jit(solution)/shard_map/ppermute | solution.py:21
  9.1 8.7 %collective-permute-start.4 = (bf16[192,1024]{1,0:T(8,128)(2,1)S(1)}, bf16[192,1024]{1,0:T(8,128)(2,1)S(1)}, u32[]{:S(2)}, u32[]{:S(2)}) collective-permute-start(bf16[192,1024]{1,0:T(8,128)(2,1)S(1)} %get-tuple-element.58), channel_id=1, source_target_pairs={{0,30},{1,31},{2,0},{3,1},{4,2},{5,3},{6,4},{7,5},{8,6},{9,7},{10,... | collective-permute-start | bytes 1179656 | tf_op jit(solution)/shard_map/ppermute | solution.py:21
  17.8 3.3 %collective-permute-done.3.refs_3_ = bf16[272,1024]{1,0:T(8,128)(2,1)S(1)} collective-permute-done((bf16[272,1024]{1,0:T(8,128)(2,1)}, bf16[272,1024]{1,0:T(8,128)(2,1)S(1)}, u32[]{:S(2)}, u32[]{:S(2)}) %collective-permute-start.3) | collective-permute-done | bytes 557088 | tf_op jit(solution)/shard_map/ppermute | solution.py:21
  21.1 15.0 %collective-permute-start.5 = (bf16[64,1024]{1,0:T(8,128)(2,1)S(1)}, bf16[64,1024]{1,0:T(8,128)(2,1)S(1)}, u32[]{:S(2)}, u32[]{:S(2)}) collective-permute-start(bf16[64,1024]{1,0:T(8,128)(2,1)S(1)} %get-tuple-element.59), channel_id=1, source_target_pairs={{0,29},{1,30},{2,31},{3,0},{4,1},{5,2},{6,3},{7,4},{8,5},{9,6},{10... | collective-permute-start | bytes 393224 | tf_op jit(solution)/shard_map/ppermute | solution.py:21
  36.2 2.8 %tables.1 = (f32[224,128]{1,0:T(8,128)S(1)}, f32[3,8,256]{2,1,0:T(8,128)S(1)}, s32[24]{0:T(128)S(1)}, bf16[24,32,1024]{2,1,0:T(8,128)(2,1)S(1)}) custom-call(s32[8]{0:T(128)S(1)} %get-tuple-element.74.cut_ref, f32[512,128]{1,0:T(8,128)S(1)} %get-tuple-element.46.near_ref, bf16[768,1024]{1,0:T(8,128)(2,1)S(1)} %bitcast.8), custom_call_target="tpu_custom_call" | custom-call | tf_op jit(solution)/shard_map/tables/pallas_call | solution.py:566
  39.0 5.3 %collective-permute-done.refs_0_ = bf16[48,1024]{1,0:T(8,128)(2,1)S(1)} collective-permute-done((bf16[48,1024]{1,0:T(8,128)(2,1)S(1)}, bf16[48,1024]{1,0:T(8,128)(2,1)S(1)}, u32[]{:S(2)}, u32[]{:S(2)}) %collective-permute-start) | collective-permute-done | bytes 98336 | tf_op jit(solution)/shard_map/ppermute | solution.py:21
  44.3 7.8 %unpack.1 = (bf16[24,224,1024]{2,1,0:T(8,128)(2,1)S(1)}, bf16[128,1024]{1,0:T(8,128)(2,1)S(1)}, f32[24,256]{1,0:T(8,128)S(1)}, f32[24,256]{1,0:T(8,128)S(1)}, f3...) custom-call(s32[8]{0:T(128)S(1)} %get-tuple-element.74.cut_ref, ...), custom_call_target="tpu_custom_call" | custom-call | tf_op jit(solution)/shard_map/unpack/pallas_call | solution.py:588
  52.3 1.3 %collective-permute-start.8 = (f32[24,256]{1,0:T(8,128)S(1)}, f32[24,256]{1,0:T(8,128)S(1)}, u32[]{:S(2)}, u32[]{:S(2)}) collective-permute-start(f32[24,256]{1,0:T(8,128)S(1)} %get-tuple-element.65), channel_id=1, source_target_pairs={{0,3},{1,30},{2,5},{3,0},{4,7},{5,2},{6,9},{7,4},{8,11},{9,6},{10,... | collective-permute-start | bytes 73736 | tf_op jit(solution)/shard_map/ppermute | solution.py:32
  53.6 4.6 %collective-permute-start.10 = (f32[24,256]{1,0:T(8,128)S(1)}, f32[24,256]{1,0:T(8,128)S(1)}, u32[]{:S(2)}, u32[]{:S(2)}) collective-permute-start(f32[24,256]{1,0:T(8,128)S(1)} %get-tuple-element.67), channel_id=1, source_target_pairs={{0,30},{1,31},{2,4},{3,5},{4,2},{5,3},{6,8},{7,9},{8,6},{9,7},{10,... | collective-permute-start | bytes 73736 | tf_op jit(solution)/shard_map/ppermute | solution.py:32
  59.9 1.6 %collective-permute-done.11.refs_6_ = f32[24,256]{1,0:T(8,128)S(1)} collective-permute-done((f32[24,256]{1,0:T(8,128)S(1)}, f32[24,256]{1,0:T(8,128)S(1)}, u32[]{:S(2)}, u32[]{:S(2)}) %collective-permute-start.11) | collective-permute-done | bytes 24608 | tf_op jit(solution)/shard_map/ppermute | solution.py:32
  62.1 4.0 %collective-permute-start.15 = (bf16[32,256]{1,0:T(8,128)(2,1)S(1)}, bf16[32,256]{1,0:T(8,128)(2,1)S(1)}, u32[]{:S(2)}, u32[]{:S(2)}) collective-permute-start(bf16[32,256]{1,0:T(8,128)(2,1)S(1)} %get-tuple-element.69.refs_0_), channel_id=1, source_target_pairs={{0,30},{1,31},{2,4},{3,5},{4,2},{5,3},{6,8},{7,9},{8,6},{9,7},{10,... | collective-permute-start | bytes 49160 | tf_op jit(solution)/shard_map/ppermute | solution.py:32
  66.1 4.6 %collective-permute-start.13 = (bf16[32,256]{1,0:T(8,128)(2,1)S(1)}, bf16[32,256]{1,0:T(8,128)(2,1)S(1)}, u32[]{:S(2)}, u32[]{:S(2)}) collective-permute-start(bf16[32,256]{1,0:T(8,128)(2,1)S(1)} %get-tuple-element.69.refs_0_), channel_id=1, source_target_pairs={{0,3},{1,30},{2,5},{3,0},{4,7},{5,2},{6,9},{7,4},{8,11},{9,6},{10,... | collective-permute-start | bytes 49160 | tf_op jit(solution)/shard_map/ppermute | solution.py:32
  70.8 2.1 %collective-permute-start.16 = (bf16[32,256]{1,0:T(8,128)(2,1)S(1)}, bf16[32,256]{1,0:T(8,128)(2,1)S(1)}, u32[]{:S(2)}, u32[]{:S(2)}) collective-permute-start(bf16[32,256]{1,0:T(8,128)(2,1)S(1)} %get-tuple-element.69.refs_0_), channel_id=1, source_target_pairs={{0,1},{1,0},{2,3},{3,2},{4,5},{5,4},{6,7},{7,6},{8,9},{9,8},{10,11... | collective-permute-start | bytes 49160 | tf_op jit(solution)/shard_map/ppermute | solution.py:32
  73.7 6.2 %mix.2 = (bf16[48,1024]{1,0:T(8,128)(2,1)S(1)}, bf16[160,1024]{1,0:T(8,128)(2,1)S(1)}, bf16[160,1024]{1,0:T(8,128)(2,1)S(1)}, bf16[48,1024]{1,0:T(8,128)(2,1)S(1...) custom-call(s32[8]{0:T(128)S(1)} %get-tuple-element.74.cut_ref, ...), custom_call_target="tpu_custom_call" | custom-call | flops 5637144576 | bytes 41943040 | tf_op jit(solution)/shard_map/mix/pallas_call | solution.py:631
  79.8 3.1 %collective-permute-start.20 = (bf16[48,1024]{1,0:T(8,128)(2,1)S(1)}, bf16[48,1024]{1,0:T(8,128)(2,1)S(1)}, u32[]{:S(2)}, u32[]{:S(2)}) collective-permute-start(bf16[48,1024]{1,0:T(8,128)(2,1)S(1)} %get-tuple-element.81), channel_id=1, source_target_pairs={{0,3},{1,30},{2,5},{3,0},{4,7},{5,2},{6,9},{7,4},{8,11},{9,6},{10,... | collective-permute-start | bytes 294920 | tf_op jit(solution)/shard_map/ppermute | solution.py:32
  83.5 7.7 %mix.3 = (bf16[256,1024]{1,0:T(8,128)(2,1)S(1)}, bf16[512,1024]{1,0:T(8,128)(2,1)S(1)}, bf16[256,1024]{1,0:T(8,128)(2,1)S(1)}, bf16[256,128]{1,0:T(8,128)(2,1)},...) custom-call(s32[8]{0:T(128)S(1)} %get-tuple-element.74.cut_ref, s32[1]{0:T(128)} %bitcast.me_ref, ...), custom_call_target="tpu_custom_call" | custom-call | flops 4227858432 | bytes 41943040 | tf_op jit(solution)/shard_map/mix/pallas_call | solution.py:631
  91.2 3.0 %collective-permute-start.21 = (bf16[256,1024]{1,0:T(8,128)(2,1)S(1)}, bf16[256,1024]{1,0:T(8,128)(2,1)S(1)}, u32[]{:S(2)}, u32[]{:S(2)}) collective-permute-start(bf16[256,1024]{1,0:T(8,128)(2,1)S(1)} %get-tuple-element.82), channel_id=1, source_target_pairs={{0,1},{1,0},{2,3},{3,2},{4,5},{5,4},{6,7},{7,6},{8,9},{9,8},{10,11... | collective-permute-start | bytes 1572872 | tf_op jit(solution)/shard_map/ppermute | solution.py:32
  94.7 7.0 %collective-permute-done.18.refs_1_ = bf16[160,1024]{1,0:T(8,128)(2,1)S(1)} collective-permute-done((bf16[160,1024]{1,0:T(8,128)(2,1)S(1)}, bf16[160,1024]{1,0:T(8,128)(2,1)S(1)}, u32[]{:S(2)}, u32[]{:S(2)}) %collective-permute-start.18) | collective-permute-done | bytes 327712 | tf_op jit(solution)/shard_map/ppermute | solution.py:32
  101.6 1.3 %add_convert_fusion.refs_0_ = bf16[512,1024]{1,0:T(8,128)(2,1)S(1)} fusion(f32[512,1024]{1,0:T(8,128)S(1)} %fusion, bf16[512,1024]{1,0:T(8,128)(2,1)S(1)} %get-tuple-element.75, bf16[1024,1024]{1,0:T(8,128)(2,1)S(1)} %copy-done.3), kind=kOutput, calls=%fused_computation | convolution fusion | flops 1075838976 | bytes 6291456 | tf_op jit(solution)/shard_map/dot_general | solution.py:650
  103.0 2.4 %early.1.early_ref = bf16[768,1024]{1,0:T(8,128)(2,1)S(1)} custom-call(s32[1]{0:T(128)} %bitcast.me_ref, f32[1,768]{1,0:T(1,128)S(1)} %get-tuple-element.44.home_ref, bf16[512,1024]{1,0:T(8,128)(2,1)S(1)} %add_convert_fusion.refs_0_, bf16[160,1024]{1,0:T(8,128)(2,1)S(1)} %collective-permute-done.18.refs_1_, ...), custom_call_target="tpu_custom_call" | custom-call | tf_op jit(solution)/shard_map/early/pallas_call | solution.py:662
  105.4 1.8 %collective-permute-done.23.refs_2_ = bf16[48,1024]{1,0:T(8,128)(2,1)S(1)} collective-permute-done((bf16[48,1024]{1,0:T(8,128)(2,1)S(1)}, bf16[48,1024]{1,0:T(8,128)(2,1)S(1)}, u32[]{:S(2)}, u32[]{:S(2)}) %collective-permute-start.23) | collective-permute-done | bytes 98336 | tf_op jit(solution)/shard_map/ppermute | solution.py:32
  107.2 1.2 %collective-permute-done.22.refs_1_ = bf16[256,1024]{1,0:T(8,128)(2,1)S(1)} collective-permute-done((bf16[256,1024]{1,0:T(8,128)(2,1)S(1)}, bf16[256,1024]{1,0:T(8,128)(2,1)S(1)}, u32[]{:S(2)}, u32[]{:S(2)}) %collective-permute-start.22) | collective-permute-done | bytes 524320 | tf_op jit(solution)/shard_map/ppermute | solution.py:32
  108.4 2.4 %home.1 = bf16[768,1024]{1,0:T(8,128)(2,1)} custom-call(s32[1]{0:T(128)} %bitcast.me_ref, f32[1,768]{1,0:T(1,128)S(1)} %get-tuple-element.44.home_ref, bf16[768,1024]{1,0:T(8,128)(2,1)S(1)} %early.1.early_ref, bf16[256,1024]{1,0:T(8,128)(2,1)S(1)} %collective-permute-done.21.refs_0_, bf16[256,1024]{1,0:T(8,128)(2,1)S(1)} %collective-permute-done.22.refs_1_, ...), custom_call_target="tpu_custom_call" | custom-call | tf_op jit(solution)/shard_map/home/pallas_call | solution.py:670
  (42 shorter events, 6.0 us)
Async XLA Ops:
  6.4 14.7 %collective-permute-start.3 = (bf16[272,1024]{1,0:T(8,128)(2,1)}, bf16[272,1024]{1,0:T(8,128)(2,1)S(1)}, u32[]{:S(2)}, u32[]{:S(2)}) collective-permute-start(bf16[272,1024]{1,0:T(8,128)(2,1)} %get-tuple-element.56), channel_id=1, source_target_pairs={{0,31},{1,0},{2,1},{3,2},{4,3},{5,4},{6,5},{7,6},{8,7},{9,8},{10,9... | collective-permute-start | bytes 1671176 | tf_op jit(solution)/shard_map/ppermute | solution.py:21
  6.5 37.8 %collective-permute-start.2 = (bf16[240,1024]{1,0:T(8,128)(2,1)S(1)}, bf16[240,1024]{1,0:T(8,128)(2,1)S(1)}, u32[]{:S(2)}, u32[]{:S(2)}) collective-permute-start(bf16[240,1024]{1,0:T(8,128)(2,1)S(1)} %get-tuple-element.54), channel_id=1, source_target_pairs={{0,1},{1,2},{2,3},{3,4},{4,5},{5,6},{6,7},{7,8},{8,9},{9,10},{10,1... | collective-permute-start | bytes 1474568 | tf_op jit(solution)/shard_map/ppermute | solution.py:21
  9.1 35.2 %collective-permute-start.4 = (bf16[192,1024]{1,0:T(8,128)(2,1)S(1)}, bf16[192,1024]{1,0:T(8,128)(2,1)S(1)}, u32[]{:S(2)}, u32[]{:S(2)}) collective-permute-start(bf16[192,1024]{1,0:T(8,128)(2,1)S(1)} %get-tuple-element.58), channel_id=1, source_target_pairs={{0,30},{1,31},{2,0},{3,1},{4,2},{5,3},{6,4},{7,5},{8,6},{9,7},{10,... | collective-permute-start | bytes 1179656 | tf_op jit(solution)/shard_map/ppermute | solution.py:21
  17.8 26.5 %collective-permute-start.1 = (bf16[160,1024]{1,0:T(8,128)(2,1)S(1)}, bf16[160,1024]{1,0:T(8,128)(2,1)S(1)}, u32[]{:S(2)}, u32[]{:S(2)}) collective-permute-start(bf16[160,1024]{1,0:T(8,128)(2,1)S(1)} %get-tuple-element.53), channel_id=1, source_target_pairs={{0,2},{1,3},{2,4},{3,5},{4,6},{5,7},{6,8},{7,9},{8,10},{9,11},{10,... | collective-permute-start | bytes 983048 | tf_op jit(solution)/shard_map/ppermute | solution.py:21
  21.1 23.2 %collective-permute-start.5 = (bf16[64,1024]{1,0:T(8,128)(2,1)S(1)}, bf16[64,1024]{1,0:T(8,128)(2,1)S(1)}, u32[]{:S(2)}, u32[]{:S(2)}) collective-permute-start(bf16[64,1024]{1,0:T(8,128)(2,1)S(1)} %get-tuple-element.59), channel_id=1, source_target_pairs={{0,29},{1,30},{2,31},{3,0},{4,1},{5,2},{6,3},{7,4},{8,5},{9,6},{10... | collective-permute-start | bytes 393224 | tf_op jit(solution)/shard_map/ppermute | solution.py:21
  36.2 8.1 %collective-permute-start = (bf16[48,1024]{1,0:T(8,128)(2,1)S(1)}, bf16[48,1024]{1,0:T(8,128)(2,1)S(1)}, u32[]{:S(2)}, u32[]{:S(2)}) collective-permute-start(bf16[48,1024]{1,0:T(8,128)(2,1)S(1)} %get-tuple-element.52), channel_id=1, source_target_pairs={{0,3},{1,4},{2,5},{3,6},{4,7},{5,8},{6,9},{7,10},{8,11},{9,12},{10... | collective-permute-start | bytes 294920 | tf_op jit(solution)/shard_map/ppermute | solution.py:21
  52.1 6.1 %collective-permute-start.6 = (f32[24,256]{1,0:T(8,128)S(1)}, f32[24,256]{1,0:T(8,128)S(1)}, u32[]{:S(2)}, u32[]{:S(2)}) collective-permute-start(f32[24,256]{1,0:T(8,128)S(1)} %get-tuple-element.63), channel_id=1, source_target_pairs={{0,1},{1,0},{2,3},{3,2},{4,5},{5,4},{6,7},{7,6},{8,9},{9,8},{10,11... | collective-permute-start | bytes 73736 | tf_op jit(solution)/shard_map/ppermute | solution.py:32
  52.2 6.0 %collective-permute-start.7 = (f32[24,256]{1,0:T(8,128)S(1)}, f32[24,256]{1,0:T(8,128)S(1)}, u32[]{:S(2)}, u32[]{:S(2)}) collective-permute-start(f32[24,256]{1,0:T(8,128)S(1)} %get-tuple-element.64), channel_id=1, source_target_pairs={{0,2},{1,3},{2,0},{3,1},{4,6},{5,7},{6,4},{7,5},{8,10},{9,11},{10,... | collective-permute-start | bytes 73736 | tf_op jit(solution)/shard_map/ppermute | solution.py:32
  52.3 7.0 %collective-permute-start.8 = (f32[24,256]{1,0:T(8,128)S(1)}, f32[24,256]{1,0:T(8,128)S(1)}, u32[]{:S(2)}, u32[]{:S(2)}) collective-permute-start(f32[24,256]{1,0:T(8,128)S(1)} %get-tuple-element.65), channel_id=1, source_target_pairs={{0,3},{1,30},{2,5},{3,0},{4,7},{5,2},{6,9},{7,4},{8,11},{9,6},{10,... | collective-permute-start | bytes 73736 | tf_op jit(solution)/shard_map/ppermute | solution.py:32
  53.6 5.7 %collective-permute-start.9 = (f32[24,256]{1,0:T(8,128)S(1)}, f32[24,256]{1,0:T(8,128)S(1)}, u32[]{:S(2)}, u32[]{:S(2)}) collective-permute-start(f32[24,256]{1,0:T(8,128)S(1)} %get-tuple-element.66), channel_id=1, source_target_pairs={{0,29},{1,4},{2,31},{3,6},{4,1},{5,8},{6,3},{7,10},{8,5},{9,12},{1... | collective-permute-start | bytes 73736 | tf_op jit(solution)/shard_map/ppermute | solution.py:32
  53.6 6.3 %collective-permute-start.10 = (f32[24,256]{1,0:T(8,128)S(1)}, f32[24,256]{1,0:T(8,128)S(1)}, u32[]{:S(2)}, u32[]{:S(2)}) collective-permute-start(f32[24,256]{1,0:T(8,128)S(1)} %get-tuple-element.67), channel_id=1, source_target_pairs={{0,30},{1,31},{2,4},{3,5},{4,2},{5,3},{6,8},{7,9},{8,6},{9,7},{10,... | collective-permute-start | bytes 73736 | tf_op jit(solution)/shard_map/ppermute | solution.py:32
  58.2 3.3 %collective-permute-start.11 = (f32[24,256]{1,0:T(8,128)S(1)}, f32[24,256]{1,0:T(8,128)S(1)}, u32[]{:S(2)}, u32[]{:S(2)}) collective-permute-start(f32[24,256]{1,0:T(8,128)S(1)} %get-tuple-element.68), channel_id=1, source_target_pairs={{0,31},{1,2},{2,1},{3,4},{4,3},{5,6},{6,5},{7,8},{8,7},{9,10},{10,... | collective-permute-start | bytes 73736 | tf_op jit(solution)/shard_map/ppermute | solution.py:32
  62.1 8.7 %collective-permute-start.15 = (bf16[32,256]{1,0:T(8,128)(2,1)S(1)}, bf16[32,256]{1,0:T(8,128)(2,1)S(1)}, u32[]{:S(2)}, u32[]{:S(2)}) collective-permute-start(bf16[32,256]{1,0:T(8,128)(2,1)S(1)} %get-tuple-element.69.refs_0_), channel_id=1, source_target_pairs={{0,30},{1,31},{2,4},{3,5},{4,2},{5,3},{6,8},{7,9},{8,6},{9,7},{10,... | collective-permute-start | bytes 49160 | tf_op jit(solution)/shard_map/ppermute | solution.py:32
  66.1 6.8 %collective-permute-start.14 = (bf16[32,256]{1,0:T(8,128)(2,1)S(1)}, bf16[32,256]{1,0:T(8,128)(2,1)S(1)}, u32[]{:S(2)}, u32[]{:S(2)}) collective-permute-start(bf16[32,256]{1,0:T(8,128)(2,1)S(1)} %get-tuple-element.69.refs_0_), channel_id=1, source_target_pairs={{0,29},{1,4},{2,31},{3,6},{4,1},{5,8},{6,3},{7,10},{8,5},{9,12},{1... | collective-permute-start | bytes 49160 | tf_op jit(solution)/shard_map/ppermute | solution.py:32
  66.1 6.8 %collective-permute-start.13 = (bf16[32,256]{1,0:T(8,128)(2,1)S(1)}, bf16[32,256]{1,0:T(8,128)(2,1)S(1)}, u32[]{:S(2)}, u32[]{:S(2)}) collective-permute-start(bf16[32,256]{1,0:T(8,128)(2,1)S(1)} %get-tuple-element.69.refs_0_), channel_id=1, source_target_pairs={{0,3},{1,30},{2,5},{3,0},{4,7},{5,2},{6,9},{7,4},{8,11},{9,6},{10,... | collective-permute-start | bytes 49160 | tf_op jit(solution)/shard_map/ppermute | solution.py:32
  70.8 2.9 %collective-permute-start.12 = (bf16[32,256]{1,0:T(8,128)(2,1)S(1)}, bf16[32,256]{1,0:T(8,128)(2,1)S(1)}, u32[]{:S(2)}, u32[]{:S(2)}) collective-permute-start(bf16[32,256]{1,0:T(8,128)(2,1)S(1)} %get-tuple-element.69.refs_0_), channel_id=1, source_target_pairs={{0,2},{1,3},{2,0},{3,1},{4,6},{5,7},{6,4},{7,5},{8,10},{9,11},{10,... | collective-permute-start | bytes 49160 | tf_op jit(solution)/shard_map/ppermute | solution.py:32
  70.8 12.7 %collective-permute-start.17 = (bf16[32,256]{1,0:T(8,128)(2,1)S(1)}, bf16[32,256]{1,0:T(8,128)(2,1)S(1)}, u32[]{:S(2)}, u32[]{:S(2)}) collective-permute-start(bf16[32,256]{1,0:T(8,128)(2,1)S(1)} %get-tuple-element.69.refs_0_), channel_id=1, source_target_pairs={{0,31},{1,2},{2,1},{3,4},{4,3},{5,6},{6,5},{7,8},{8,7},{9,10},{10,... | collective-permute-start | bytes 49160 | tf_op jit(solution)/shard_map/ppermute | solution.py:32
  70.8 12.7 %collective-permute-start.16 = (bf16[32,256]{1,0:T(8,128)(2,1)S(1)}, bf16[32,256]{1,0:T(8,128)(2,1)S(1)}, u32[]{:S(2)}, u32[]{:S(2)}) collective-permute-start(bf16[32,256]{1,0:T(8,128)(2,1)S(1)} %get-tuple-element.69.refs_0_), channel_id=1, source_target_pairs={{0,1},{1,0},{2,3},{3,2},{4,5},{5,4},{6,7},{7,6},{8,9},{9,8},{10,11... | collective-permute-start | bytes 49160 | tf_op jit(solution)/shard_map/ppermute | solution.py:32
  79.8 23.1 %collective-permute-start.20 = (bf16[48,1024]{1,0:T(8,128)(2,1)S(1)}, bf16[48,1024]{1,0:T(8,128)(2,1)S(1)}, u32[]{:S(2)}, u32[]{:S(2)}) collective-permute-start(bf16[48,1024]{1,0:T(8,128)(2,1)S(1)} %get-tuple-element.81), channel_id=1, source_target_pairs={{0,3},{1,30},{2,5},{3,0},{4,7},{5,2},{6,9},{7,4},{8,11},{9,6},{10,... | collective-permute-start | bytes 294920 | tf_op jit(solution)/shard_map/ppermute | solution.py:32
  82.9 18.8 %collective-permute-start.18 = (bf16[160,1024]{1,0:T(8,128)(2,1)S(1)}, bf16[160,1024]{1,0:T(8,128)(2,1)S(1)}, u32[]{:S(2)}, u32[]{:S(2)}) collective-permute-start(bf16[160,1024]{1,0:T(8,128)(2,1)S(1)} %get-tuple-element.78), channel_id=1, source_target_pairs={{0,2},{1,3},{2,0},{3,1},{4,6},{5,7},{6,4},{7,5},{8,10},{9,11},{10,... | collective-permute-start | bytes 983048 | tf_op jit(solution)/shard_map/ppermute | solution.py:32
  82.9 20.1 %collective-permute-start.19 = (bf16[160,1024]{1,0:T(8,128)(2,1)S(1)}, bf16[160,1024]{1,0:T(8,128)(2,1)S(1)}, u32[]{:S(2)}, u32[]{:S(2)}) collective-permute-start(bf16[160,1024]{1,0:T(8,128)(2,1)S(1)} %get-tuple-element.80), channel_id=1, source_target_pairs={{0,30},{1,31},{2,4},{3,5},{4,2},{5,3},{6,8},{7,9},{8,6},{9,7},{10,... | collective-permute-start | bytes 983048 | tf_op jit(solution)/shard_map/ppermute | solution.py:32
  91.2 16.0 %collective-permute-start.21 = (bf16[256,1024]{1,0:T(8,128)(2,1)S(1)}, bf16[256,1024]{1,0:T(8,128)(2,1)S(1)}, u32[]{:S(2)}, u32[]{:S(2)}) collective-permute-start(bf16[256,1024]{1,0:T(8,128)(2,1)S(1)} %get-tuple-element.82), channel_id=1, source_target_pairs={{0,1},{1,0},{2,3},{3,2},{4,5},{5,4},{6,7},{7,6},{8,9},{9,8},{10,11... | collective-permute-start | bytes 1572872 | tf_op jit(solution)/shard_map/ppermute | solution.py:32
  94.2 14.2 %collective-permute-start.22 = (bf16[256,1024]{1,0:T(8,128)(2,1)S(1)}, bf16[256,1024]{1,0:T(8,128)(2,1)S(1)}, u32[]{:S(2)}, u32[]{:S(2)}) collective-permute-start(bf16[256,1024]{1,0:T(8,128)(2,1)S(1)} %get-tuple-element.83), channel_id=1, source_target_pairs={{0,31},{1,2},{2,1},{3,4},{4,3},{5,6},{6,5},{7,8},{8,7},{9,10},{10,... | collective-permute-start | bytes 1572872 | tf_op jit(solution)/shard_map/ppermute | solution.py:32
  101.6 5.6 %collective-permute-start.23 = (bf16[48,1024]{1,0:T(8,128)(2,1)S(1)}, bf16[48,1024]{1,0:T(8,128)(2,1)S(1)}, u32[]{:S(2)}, u32[]{:S(2)}) collective-permute-start(bf16[48,1024]{1,0:T(8,128)(2,1)S(1)} %get-tuple-element.84), channel_id=1, source_target_pairs={{0,29},{1,4},{2,31},{3,6},{4,1},{5,8},{6,3},{7,10},{8,5},{9,12},{1... | collective-permute-start | bytes 294920 | tf_op jit(solution)/shard_map/ppermute | solution.py:32
  (4 other events, 71.9 us)

commit v9 on v8

--- a/solution.py
+++ b/solution.py
@@ -212,7 +212,7 @@
     return jnp.concatenate(picks, axis=0)
 
 
-def table_kernel(plan, cut_ref, near_ref, flat_ref, column_ref, place_ref, active_ref, local_ref):
+def table_kernel(plan, cut_ref, near_ref, flat_ref, own_ref, column_ref, place_ref, active_ref, local_ref, *passed):
     fun_dev, support, halo, boxes = plan
     slots = 2 * REACH + 1
     first = cut_ref[REACH].astype(jnp.float32)
@@ -262,6 +262,9 @@
             levels[g] = jnp.maximum(levels[g], level)
     for g in range(boxes // STEP):
         active_ref[slots * (boxes // STEP) + g] = levels[g]
+    for side in range(slots + 1):
+        passed[0][side] = cut_ref[side]
+    passed[1][...] = own_ref[...]
     spare = place_ref.shape[1] - slots
     place_ref[:, slots:, :] = jnp.full((boxes // STEP, spare, STEP * SLOT), -1.0, jnp.float32)
 
@@ -558,24 +561,26 @@
             pltpu.VMEM(potential.shape, f32),
             pltpu.SemaphoreType.DMA((2,)),
         ],
-        compiler_params=pltpu.CompilerParams(vmem_limit_bytes=52 * 2**20),
+        compiler_params=pltpu.CompilerParams(vmem_limit_bytes=57 * 2**20),
         name="pack",
     )(me, centers, flat, potential)
     arrived = all_sent(dict(zip(now + [last], packed)), now, last, 1)
 
-    columns, places, active, local = pl.pallas_call(
+    columns, places, active, local, cut, own_region = pl.pallas_call(
         functools.partial(table_kernel, (fun_dev, support, halo, boxes)),
         out_shape=(
             jax.ShapeDtypeStruct((slots * SLOT, 128), f32),
             jax.ShapeDtypeStruct((boxes // STEP, 8, STEP * SLOT), f32),
             jax.ShapeDtypeStruct(((slots + 1) * (boxes // STEP),), jnp.int32),
             jax.ShapeDtypeStruct((boxes, SLOT, points), bf16),
+            jax.ShapeDtypeStruct(cut.shape, jnp.int32),
+            jax.ShapeDtypeStruct(own_region.shape, bf16),
         ),
-        in_specs=[smem, vmem, vmem],
-        out_specs=(vmem, vmem, smem, vmem),
+        in_specs=[smem, vmem, vmem, vmem],
+        out_specs=(vmem, vmem, smem, vmem, smem, vmem),
         compiler_params=limit,
         name="tables",
-    )(cut, near, flat)
+    )(cut, near, flat, own_region)
 
     wide = slots * SLOT
     sources = [arrived[REACH - e] for e in range(slots) if e != REACH]

time: 111 us -> 111 us (level); the launches traced: 111 us -> 110 us
  Pallas kernels: 33.9 us -> 32.4 us
    ppermute x6, waiting for transfers between devices: 8.6 us -> 6.15 us  [passed_along(): return lax.ppermute(value, AXES, pairs)]
    pallas_call x1, Pallas kernels: 7.79 us -> 6.25 us  [on_device(): pl.pallas_call(functools.partial(unpack_kernel, (fun_dev, box_dev, readin...]
    pallas_call x1, Pallas kernels: 4.11 us -> 5.55 us  [on_device(): pl.pallas_call(functools.partial(pack_kernel, (fun_dev, support, devices,...]
    pallas_call x2, Pallas kernels: 13.9 us -> 12.4 us  [on_device(): pl.pallas_call(functools.partial(mix_kernel, (fun_dev, reading, group, wh...]
    ppermute x18, waiting for transfers between devices: 14.1 us -> 15.4 us  [swapped(): return lax.ppermute(value, AXES, pairs)]
    unnamed x8 -> x12, local copies, waits for them, and re-layouts: 1.65 us -> 2.46 us
  transfers between devices with their start and end apart: 24 -> 24, of which waited for: 9 -> 8; matrix products, arithmetic and copies ran while one was open for 2% -> 2% of each run, Pallas kernels for 17% -> 16%
where the time goes in v9:
time: 111 us; the launch traced here: 110 us
  starting transfers between devices  50.4 us (45%)
  Pallas kernels  32.4 us (29%)
  waiting for transfers between devices  21.6 us (19%)
  local copies, waits for them, and re-layouts  2.46 us (2%)
  matrix products  1.74 us (2%)
    ppermute x6, starting transfers between devices, passed_along(): return lax.ppermute(value, AXES, pairs)  26.5 us
    ppermute x18, starting transfers between devices, swapped(): return lax.ppermute(value, AXES, pairs)  23.9 us
    ppermute x18, waiting for transfers between devices, swapped(): return lax.ppermute(value, AXES, pairs)  15.4 us
    pallas_call x2, Pallas kernels, on_device(): pl.pallas_call(functools.partial(mix_kernel, (fun_dev, reading, group, wh...  12.4 us
    pallas_call x1, Pallas kernels, on_device(): pl.pallas_call(functools.partial(unpack_kernel, (fun_dev, box_dev, readin...  6.25 us
    ppermute x6, waiting for transfers between devices, passed_along(): return lax.ppermute(value, AXES, pairs)  6.15 us
    pallas_call x1, Pallas kernels, on_device(): pl.pallas_call(functools.partial(pack_kernel, (fun_dev, support, devices,...  5.55 us
    pallas_call x1, Pallas kernels, on_device(): pl.pallas_call(functools.partial(table_kernel, (fun_dev, support, halo, b...  2.79 us
  transfers between devices with their start and end apart: 24, of which 8 were waited for; matrix products, arithmetic and copies ran while one was open for 2% of the time, Pallas kernels for 16%

profile of v9, /device:TPU:1, one launch (start us, length us, event | category | flops | bytes accessed | tf_op | source)
XLA Modules:
  0.0 109.5 jit_solution(12672207609060926629)
XLA Ops:
  0.6 5.5 %pack.1 = (bf16[272,1024]{1,0:T(8,128)(2,1)}, bf16[240,1024]{1,0:T(8,128)(2,1)}, bf16[192,1024]{1,0:T(8,128)(2,1)}, bf16[160,1024]{1,0:T(8,128)(2,1)}, bf16[48,1...) custom-call(s32[1]{0:T(128)} %bitcast.me_ref, ...), custom_call_target="tpu_custom_call" | custom-call | tf_op jit(solution)/shard_map/pack/pallas_call | solution.py:547
  6.3 2.6 %collective-permute-start.2 = (bf16[240,1024]{1,0:T(8,128)(2,1)}, bf16[240,1024]{1,0:T(8,128)(2,1)S(1)}, u32[]{:S(2)}, u32[]{:S(2)}) collective-permute-start(bf16[240,1024]{1,0:T(8,128)(2,1)} %get-tuple-element.58), channel_id=1, source_target_pairs={{0,1},{1,2},{2,3},{3,4},{4,5},{5,6},{6,7},{7,8},{8,9},{9,10},{10,1... | collective-permute-start | bytes 1474568 | tf_op jit(solution)/shard_map/ppermute | solution.py:21
  8.9 8.7 %collective-permute-start.4 = (bf16[192,1024]{1,0:T(8,128)(2,1)}, bf16[192,1024]{1,0:T(8,128)(2,1)S(1)}, u32[]{:S(2)}, u32[]{:S(2)}) collective-permute-start(bf16[192,1024]{1,0:T(8,128)(2,1)} %get-tuple-element.62), channel_id=1, source_target_pairs={{0,30},{1,31},{2,0},{3,1},{4,2},{5,3},{6,4},{7,5},{8,6},{9,7},{10,... | collective-permute-start | bytes 1179656 | tf_op jit(solution)/shard_map/ppermute | solution.py:21
  17.6 3.1 %collective-permute-done.3.refs_3_ = bf16[272,1024]{1,0:T(8,128)(2,1)S(1)} collective-permute-done((bf16[272,1024]{1,0:T(8,128)(2,1)}, bf16[272,1024]{1,0:T(8,128)(2,1)S(1)}, u32[]{:S(2)}, u32[]{:S(2)}) %collective-permute-start.3) | collective-permute-done | bytes 557088 | tf_op jit(solution)/shard_map/ppermute | solution.py:21
  20.7 15.0 %collective-permute-start.5 = (bf16[64,1024]{1,0:T(8,128)(2,1)}, bf16[64,1024]{1,0:T(8,128)(2,1)S(1)}, u32[]{:S(2)}, u32[]{:S(2)}) collective-permute-start(bf16[64,1024]{1,0:T(8,128)(2,1)} %get-tuple-element.63), channel_id=1, source_target_pairs={{0,29},{1,30},{2,31},{3,0},{4,1},{5,2},{6,3},{7,4},{8,5},{9,6},{10... | collective-permute-start | bytes 393224 | tf_op jit(solution)/shard_map/ppermute | solution.py:21
  38.2 2.8 %tables.1 = (f32[224,128]{1,0:T(8,128)S(1)}, f32[3,8,256]{2,1,0:T(8,128)S(1)}, s32[24]{0:T(128)S(1)}, bf16[24,32,1024]{2,1,0:T(8,128)(2,1)S(1)}, s32[8]{0:T(128)S(1)}, /*index=5*/bf16[32,1024]{1,0:T(8,128)(2,1)S(1)}) custom-call(s32[8]{0:T(128)S(1)} %copy-done.4, f32[512,128]{1,0:T(8,128)S(1)} %copy-done.1, bf16[768,1024]{1,0:T(8,128)(2,1)S(1)} %bitcast.8, ...), custom_call_target="tpu_custom_call" | custom-call | tf_op jit(solution)/shard_map/tables/pallas_call | solution.py:569
  41.0 3.1 %collective-permute-done.refs_0_ = bf16[48,1024]{1,0:T(8,128)(2,1)S(1)} collective-permute-done((bf16[48,1024]{1,0:T(8,128)(2,1)}, bf16[48,1024]{1,0:T(8,128)(2,1)S(1)}, u32[]{:S(2)}, u32[]{:S(2)}) %collective-permute-start) | collective-permute-done | bytes 98336 | tf_op jit(solution)/shard_map/ppermute | solution.py:21
  44.1 6.2 %unpack.1 = (bf16[24,224,1024]{2,1,0:T(8,128)(2,1)S(1)}, bf16[128,1024]{1,0:T(8,128)(2,1)S(1)}, f32[24,256]{1,0:T(8,128)S(1)}, f32[24,256]{1,0:T(8,128)S(1)}, f3...) custom-call(s32[8]{0:T(128)S(1)} %get-tuple-element.78.cut_ref, ...), custom_call_target="tpu_custom_call" | custom-call | tf_op jit(solution)/shard_map/unpack/pallas_call | solution.py:593
  50.5 3.4 %collective-permute-start.8 = (f32[24,256]{1,0:T(8,128)S(1)}, f32[24,256]{1,0:T(8,128)S(1)}, u32[]{:S(2)}, u32[]{:S(2)}) collective-permute-start(f32[24,256]{1,0:T(8,128)S(1)} %get-tuple-element.69), channel_id=1, source_target_pairs={{0,3},{1,30},{2,5},{3,0},{4,7},{5,2},{6,9},{7,4},{8,11},{9,6},{10,... | collective-permute-start | bytes 73736 | tf_op jit(solution)/shard_map/ppermute | solution.py:32
  53.9 2.5 %collective-permute-start.10 = (f32[24,256]{1,0:T(8,128)S(1)}, f32[24,256]{1,0:T(8,128)S(1)}, u32[]{:S(2)}, u32[]{:S(2)}) collective-permute-start(f32[24,256]{1,0:T(8,128)S(1)} %get-tuple-element.71), channel_id=1, source_target_pairs={{0,30},{1,31},{2,4},{3,5},{4,2},{5,3},{6,8},{7,9},{8,6},{9,7},{10,... | collective-permute-start | bytes 73736 | tf_op jit(solution)/shard_map/ppermute | solution.py:32
  57.5 2.7 %collective-permute-done.10.refs_5_ = f32[24,256]{1,0:T(8,128)S(1)} collective-permute-done((f32[24,256]{1,0:T(8,128)S(1)}, f32[24,256]{1,0:T(8,128)S(1)}, u32[]{:S(2)}, u32[]{:S(2)}) %collective-permute-start.10) | collective-permute-done | bytes 24608 | tf_op jit(solution)/shard_map/ppermute | solution.py:32
  60.9 5.6 %collective-permute-start.15 = (bf16[32,256]{1,0:T(8,128)(2,1)S(1)}, bf16[32,256]{1,0:T(8,128)(2,1)S(1)}, u32[]{:S(2)}, u32[]{:S(2)}) collective-permute-start(bf16[32,256]{1,0:T(8,128)(2,1)S(1)} %get-tuple-element.73.refs_0_), channel_id=1, source_target_pairs={{0,30},{1,31},{2,4},{3,5},{4,2},{5,3},{6,8},{7,9},{8,6},{9,7},{10,... | collective-permute-start | bytes 49160 | tf_op jit(solution)/shard_map/ppermute | solution.py:32
  66.5 2.6 %collective-permute-start.13 = (bf16[32,256]{1,0:T(8,128)(2,1)S(1)}, bf16[32,256]{1,0:T(8,128)(2,1)S(1)}, u32[]{:S(2)}, u32[]{:S(2)}) collective-permute-start(bf16[32,256]{1,0:T(8,128)(2,1)S(1)} %get-tuple-element.73.refs_0_), channel_id=1, source_target_pairs={{0,3},{1,30},{2,5},{3,0},{4,7},{5,2},{6,9},{7,4},{8,11},{9,6},{10,... | collective-permute-start | bytes 49160 | tf_op jit(solution)/shard_map/ppermute | solution.py:32
  69.0 2.1 %collective-permute-start.16 = (bf16[32,256]{1,0:T(8,128)(2,1)S(1)}, bf16[32,256]{1,0:T(8,128)(2,1)S(1)}, u32[]{:S(2)}, u32[]{:S(2)}) collective-permute-start(bf16[32,256]{1,0:T(8,128)(2,1)S(1)} %get-tuple-element.73.refs_0_), channel_id=1, source_target_pairs={{0,1},{1,0},{2,3},{3,2},{4,5},{5,4},{6,7},{7,6},{8,9},{9,8},{10,11... | collective-permute-start | bytes 49160 | tf_op jit(solution)/shard_map/ppermute | solution.py:32
  71.1 2.1 %collective-permute-done.13.refs_1_ = bf16[32,256]{1,0:T(8,128)(2,1)S(1)} collective-permute-done((bf16[32,256]{1,0:T(8,128)(2,1)S(1)}, bf16[32,256]{1,0:T(8,128)(2,1)S(1)}, u32[]{:S(2)}, u32[]{:S(2)}) %collective-permute-start.13) | collective-permute-done | bytes 16416 | tf_op jit(solution)/shard_map/ppermute | solution.py:32
  73.2 4.9 %mix.2 = (bf16[48,1024]{1,0:T(8,128)(2,1)S(1)}, bf16[160,1024]{1,0:T(8,128)(2,1)S(1)}, bf16[160,1024]{1,0:T(8,128)(2,1)S(1)}, bf16[48,1024]{1,0:T(8,128)(2,1)S(1...) custom-call(s32[8]{0:T(128)S(1)} %get-tuple-element.78.cut_ref, ...), custom_call_target="tpu_custom_call" | custom-call | flops 5637144576 | bytes 41943040 | tf_op jit(solution)/shard_map/mix/pallas_call | solution.py:636
  78.2 3.0 %collective-permute-start.20 = (bf16[48,1024]{1,0:T(8,128)(2,1)S(1)}, bf16[48,1024]{1,0:T(8,128)(2,1)S(1)}, u32[]{:S(2)}, u32[]{:S(2)}) collective-permute-start(bf16[48,1024]{1,0:T(8,128)(2,1)S(1)} %get-tuple-element.85), channel_id=1, source_target_pairs={{0,3},{1,30},{2,5},{3,0},{4,7},{5,2},{6,9},{7,4},{8,11},{9,6},{10,... | collective-permute-start | bytes 294920 | tf_op jit(solution)/shard_map/ppermute | solution.py:32
  81.9 7.5 %mix.3 = (bf16[256,1024]{1,0:T(8,128)(2,1)S(1)}, bf16[512,1024]{1,0:T(8,128)(2,1)S(1)}, bf16[256,1024]{1,0:T(8,128)(2,1)S(1)}, bf16[256,128]{1,0:T(8,128)(2,1)},...) custom-call(s32[8]{0:T(128)S(1)} %get-tuple-element.78.cut_ref, s32[1]{0:T(128)} %bitcast.me_ref, ...), custom_call_target="tpu_custom_call" | custom-call | flops 4227858432 | bytes 41943040 | tf_op jit(solution)/shard_map/mix/pallas_call | solution.py:636
  89.4 3.1 %collective-permute-start.21 = (bf16[256,1024]{1,0:T(8,128)(2,1)S(1)}, bf16[256,1024]{1,0:T(8,128)(2,1)S(1)}, u32[]{:S(2)}, u32[]{:S(2)}) collective-permute-start(bf16[256,1024]{1,0:T(8,128)(2,1)S(1)} %get-tuple-element.86), channel_id=1, source_target_pairs={{0,1},{1,0},{2,3},{3,2},{4,5},{5,4},{6,7},{7,6},{8,9},{9,8},{10,11... | collective-permute-start | bytes 1572872 | tf_op jit(solution)/shard_map/ppermute | solution.py:32
  93.0 7.0 %collective-permute-done.18.refs_1_ = bf16[160,1024]{1,0:T(8,128)(2,1)S(1)} collective-permute-done((bf16[160,1024]{1,0:T(8,128)(2,1)S(1)}, bf16[160,1024]{1,0:T(8,128)(2,1)S(1)}, u32[]{:S(2)}, u32[]{:S(2)}) %collective-permute-start.18) | collective-permute-done | bytes 327712 | tf_op jit(solution)/shard_map/ppermute | solution.py:32
  101.4 2.4 %early.1.early_ref = bf16[768,1024]{1,0:T(8,128)(2,1)S(1)} custom-call(s32[1]{0:T(128)} %bitcast.me_ref, f32[1,768]{1,0:T(1,128)S(1)} %copy-done.3, bf16[512,1024]{1,0:T(8,128)(2,1)S(1)} %add_convert_fusion.refs_0_, bf16[160,1024]{1,0:T(8,128)(2,1)S(1)} %collective-permute-done.18.refs_1_, bf16[160,1024]{1,0:T(8,128)(2,1)S(1)} %collective-permute-done.19.refs_2_, ...), custom_call_target="tpu_custom_call" | custom-call | tf_op jit(solution)/shard_map/early/pallas_call | solution.py:667
  103.8 1.5 %collective-permute-done.23.refs_2_ = bf16[48,1024]{1,0:T(8,128)(2,1)S(1)} collective-permute-done((bf16[48,1024]{1,0:T(8,128)(2,1)S(1)}, bf16[48,1024]{1,0:T(8,128)(2,1)S(1)}, u32[]{:S(2)}, u32[]{:S(2)}) %collective-permute-start.23) | collective-permute-done | bytes 98336 | tf_op jit(solution)/shard_map/ppermute | solution.py:32
  105.2 1.7 %collective-permute-done.22.refs_1_ = bf16[256,1024]{1,0:T(8,128)(2,1)S(1)} collective-permute-done((bf16[256,1024]{1,0:T(8,128)(2,1)S(1)}, bf16[256,1024]{1,0:T(8,128)(2,1)S(1)}, u32[]{:S(2)}, u32[]{:S(2)}) %collective-permute-start.22) | collective-permute-done | bytes 524320 | tf_op jit(solution)/shard_map/ppermute | solution.py:32
  107.0 2.4 %home.1 = bf16[768,1024]{1,0:T(8,128)(2,1)} custom-call(s32[1]{0:T(128)} %bitcast.me_ref, f32[1,768]{1,0:T(1,128)S(1)} %copy-done.3, bf16[768,1024]{1,0:T(8,128)(2,1)S(1)} %early.1.early_ref, bf16[256,1024]{1,0:T(8,128)(2,1)S(1)} %collective-permute-done.21.refs_0_, bf16[256,1024]{1,0:T(8,128)(2,1)S(1)} %collective-permute-done.22.refs_1_, ...), custom_call_target="tpu_custom_call" | custom-call | tf_op jit(solution)/shard_map/home/pallas_call | solution.py:675
  (46 shorter events, 7.0 us)
Async XLA Ops:
  6.2 14.5 %collective-permute-start.3 = (bf16[272,1024]{1,0:T(8,128)(2,1)}, bf16[272,1024]{1,0:T(8,128)(2,1)S(1)}, u32[]{:S(2)}, u32[]{:S(2)}) collective-permute-start(bf16[272,1024]{1,0:T(8,128)(2,1)} %get-tuple-element.60), channel_id=1, source_target_pairs={{0,31},{1,0},{2,1},{3,2},{4,3},{5,4},{6,5},{7,6},{8,7},{9,8},{10,9... | collective-permute-start | bytes 1671176 | tf_op jit(solution)/shard_map/ppermute | solution.py:21
  6.3 37.8 %collective-permute-start.2 = (bf16[240,1024]{1,0:T(8,128)(2,1)}, bf16[240,1024]{1,0:T(8,128)(2,1)S(1)}, u32[]{:S(2)}, u32[]{:S(2)}) collective-permute-start(bf16[240,1024]{1,0:T(8,128)(2,1)} %get-tuple-element.58), channel_id=1, source_target_pairs={{0,1},{1,2},{2,3},{3,4},{4,5},{5,6},{6,7},{7,8},{8,9},{9,10},{10,1... | collective-permute-start | bytes 1474568 | tf_op jit(solution)/shard_map/ppermute | solution.py:21
  8.9 35.2 %collective-permute-start.4 = (bf16[192,1024]{1,0:T(8,128)(2,1)}, bf16[192,1024]{1,0:T(8,128)(2,1)S(1)}, u32[]{:S(2)}, u32[]{:S(2)}) collective-permute-start(bf16[192,1024]{1,0:T(8,128)(2,1)} %get-tuple-element.62), channel_id=1, source_target_pairs={{0,30},{1,31},{2,0},{3,1},{4,2},{5,3},{6,4},{7,5},{8,6},{9,7},{10,... | collective-permute-start | bytes 1179656 | tf_op jit(solution)/shard_map/ppermute | solution.py:21
  17.6 26.5 %collective-permute-start.1 = (bf16[160,1024]{1,0:T(8,128)(2,1)}, bf16[160,1024]{1,0:T(8,128)(2,1)S(1)}, u32[]{:S(2)}, u32[]{:S(2)}) collective-permute-start(bf16[160,1024]{1,0:T(8,128)(2,1)} %get-tuple-element.57), channel_id=1, source_target_pairs={{0,2},{1,3},{2,4},{3,5},{4,6},{5,7},{6,8},{7,9},{8,10},{9,11},{10,... | collective-permute-start | bytes 983048 | tf_op jit(solution)/shard_map/ppermute | solution.py:21
  20.7 23.4 %collective-permute-start.5 = (bf16[64,1024]{1,0:T(8,128)(2,1)}, bf16[64,1024]{1,0:T(8,128)(2,1)S(1)}, u32[]{:S(2)}, u32[]{:S(2)}) collective-permute-start(bf16[64,1024]{1,0:T(8,128)(2,1)} %get-tuple-element.63), channel_id=1, source_target_pairs={{0,29},{1,30},{2,31},{3,0},{4,1},{5,2},{6,3},{7,4},{8,5},{9,6},{10... | collective-permute-start | bytes 393224 | tf_op jit(solution)/shard_map/ppermute | solution.py:21
  35.7 8.3 %collective-permute-start = (bf16[48,1024]{1,0:T(8,128)(2,1)}, bf16[48,1024]{1,0:T(8,128)(2,1)S(1)}, u32[]{:S(2)}, u32[]{:S(2)}) collective-permute-start(bf16[48,1024]{1,0:T(8,128)(2,1)} %get-tuple-element.56), channel_id=1, source_target_pairs={{0,3},{1,4},{2,5},{3,6},{4,7},{5,8},{6,9},{7,10},{8,11},{9,12},{10... | collective-permute-start | bytes 294920 | tf_op jit(solution)/shard_map/ppermute | solution.py:21
  50.4 6.1 %collective-permute-start.6 = (f32[24,256]{1,0:T(8,128)S(1)}, f32[24,256]{1,0:T(8,128)S(1)}, u32[]{:S(2)}, u32[]{:S(2)}) collective-permute-start(f32[24,256]{1,0:T(8,128)S(1)} %get-tuple-element.67), channel_id=1, source_target_pairs={{0,1},{1,0},{2,3},{3,2},{4,5},{5,4},{6,7},{7,6},{8,9},{9,8},{10,11... | collective-permute-start | bytes 73736 | tf_op jit(solution)/shard_map/ppermute | solution.py:32
  50.5 6.6 %collective-permute-start.7 = (f32[24,256]{1,0:T(8,128)S(1)}, f32[24,256]{1,0:T(8,128)S(1)}, u32[]{:S(2)}, u32[]{:S(2)}) collective-permute-start(f32[24,256]{1,0:T(8,128)S(1)} %get-tuple-element.68), channel_id=1, source_target_pairs={{0,2},{1,3},{2,0},{3,1},{4,6},{5,7},{6,4},{7,5},{8,10},{9,11},{10,... | collective-permute-start | bytes 73736 | tf_op jit(solution)/shard_map/ppermute | solution.py:32
  50.5 7.0 %collective-permute-start.8 = (f32[24,256]{1,0:T(8,128)S(1)}, f32[24,256]{1,0:T(8,128)S(1)}, u32[]{:S(2)}, u32[]{:S(2)}) collective-permute-start(f32[24,256]{1,0:T(8,128)S(1)} %get-tuple-element.69), channel_id=1, source_target_pairs={{0,3},{1,30},{2,5},{3,0},{4,7},{5,2},{6,9},{7,4},{8,11},{9,6},{10,... | collective-permute-start | bytes 73736 | tf_op jit(solution)/shard_map/ppermute | solution.py:32
  53.9 3.6 %collective-permute-start.9 = (f32[24,256]{1,0:T(8,128)S(1)}, f32[24,256]{1,0:T(8,128)S(1)}, u32[]{:S(2)}, u32[]{:S(2)}) collective-permute-start(f32[24,256]{1,0:T(8,128)S(1)} %get-tuple-element.70), channel_id=1, source_target_pairs={{0,29},{1,4},{2,31},{3,6},{4,1},{5,8},{6,3},{7,10},{8,5},{9,12},{1... | collective-permute-start | bytes 73736 | tf_op jit(solution)/shard_map/ppermute | solution.py:32
  53.9 6.3 %collective-permute-start.10 = (f32[24,256]{1,0:T(8,128)S(1)}, f32[24,256]{1,0:T(8,128)S(1)}, u32[]{:S(2)}, u32[]{:S(2)}) collective-permute-start(f32[24,256]{1,0:T(8,128)S(1)} %get-tuple-element.71), channel_id=1, source_target_pairs={{0,30},{1,31},{2,4},{3,5},{4,2},{5,3},{6,8},{7,9},{8,6},{9,7},{10,... | collective-permute-start | bytes 73736 | tf_op jit(solution)/shard_map/ppermute | solution.py:32
  56.5 3.8 %collective-permute-start.11 = (f32[24,256]{1,0:T(8,128)S(1)}, f32[24,256]{1,0:T(8,128)S(1)}, u32[]{:S(2)}, u32[]{:S(2)}) collective-permute-start(f32[24,256]{1,0:T(8,128)S(1)} %get-tuple-element.72), channel_id=1, source_target_pairs={{0,31},{1,2},{2,1},{3,4},{4,3},{5,6},{6,5},{7,8},{8,7},{9,10},{10,... | collective-permute-start | bytes 73736 | tf_op jit(solution)/shard_map/ppermute | solution.py:32
  60.9 8.2 %collective-permute-start.15 = (bf16[32,256]{1,0:T(8,128)(2,1)S(1)}, bf16[32,256]{1,0:T(8,128)(2,1)S(1)}, u32[]{:S(2)}, u32[]{:S(2)}) collective-permute-start(bf16[32,256]{1,0:T(8,128)(2,1)S(1)} %get-tuple-element.73.refs_0_), channel_id=1, source_target_pairs={{0,30},{1,31},{2,4},{3,5},{4,2},{5,3},{6,8},{7,9},{8,6},{9,7},{10,... | collective-permute-start | bytes 49160 | tf_op jit(solution)/shard_map/ppermute | solution.py:32
  66.5 4.7 %collective-permute-start.14 = (bf16[32,256]{1,0:T(8,128)(2,1)S(1)}, bf16[32,256]{1,0:T(8,128)(2,1)S(1)}, u32[]{:S(2)}, u32[]{:S(2)}) collective-permute-start(bf16[32,256]{1,0:T(8,128)(2,1)S(1)} %get-tuple-element.73.refs_0_), channel_id=1, source_target_pairs={{0,29},{1,4},{2,31},{3,6},{4,1},{5,8},{6,3},{7,10},{8,5},{9,12},{1... | collective-permute-start | bytes 49160 | tf_op jit(solution)/shard_map/ppermute | solution.py:32
  66.5 6.8 %collective-permute-start.13 = (bf16[32,256]{1,0:T(8,128)(2,1)S(1)}, bf16[32,256]{1,0:T(8,128)(2,1)S(1)}, u32[]{:S(2)}, u32[]{:S(2)}) collective-permute-start(bf16[32,256]{1,0:T(8,128)(2,1)S(1)} %get-tuple-element.73.refs_0_), channel_id=1, source_target_pairs={{0,3},{1,30},{2,5},{3,0},{4,7},{5,2},{6,9},{7,4},{8,11},{9,6},{10,... | collective-permute-start | bytes 49160 | tf_op jit(solution)/shard_map/ppermute | solution.py:32
  69.0 4.2 %collective-permute-start.12 = (bf16[32,256]{1,0:T(8,128)(2,1)S(1)}, bf16[32,256]{1,0:T(8,128)(2,1)S(1)}, u32[]{:S(2)}, u32[]{:S(2)}) collective-permute-start(bf16[32,256]{1,0:T(8,128)(2,1)S(1)} %get-tuple-element.73.refs_0_), channel_id=1, source_target_pairs={{0,2},{1,3},{2,0},{3,1},{4,6},{5,7},{6,4},{7,5},{8,10},{9,11},{10,... | collective-permute-start | bytes 49160 | tf_op jit(solution)/shard_map/ppermute | solution.py:32
  69.0 12.8 %collective-permute-start.17 = (bf16[32,256]{1,0:T(8,128)(2,1)S(1)}, bf16[32,256]{1,0:T(8,128)(2,1)S(1)}, u32[]{:S(2)}, u32[]{:S(2)}) collective-permute-start(bf16[32,256]{1,0:T(8,128)(2,1)S(1)} %get-tuple-element.73.refs_0_), channel_id=1, source_target_pairs={{0,31},{1,2},{2,1},{3,4},{4,3},{5,6},{6,5},{7,8},{8,7},{9,10},{10,... | collective-permute-start | bytes 49160 | tf_op jit(solution)/shard_map/ppermute | solution.py:32
  69.0 12.8 %collective-permute-start.16 = (bf16[32,256]{1,0:T(8,128)(2,1)S(1)}, bf16[32,256]{1,0:T(8,128)(2,1)S(1)}, u32[]{:S(2)}, u32[]{:S(2)}) collective-permute-start(bf16[32,256]{1,0:T(8,128)(2,1)S(1)} %get-tuple-element.73.refs_0_), channel_id=1, source_target_pairs={{0,1},{1,0},{2,3},{3,2},{4,5},{5,4},{6,7},{7,6},{8,9},{9,8},{10,11... | collective-permute-start | bytes 49160 | tf_op jit(solution)/shard_map/ppermute | solution.py:32
  78.2 23.2 %collective-permute-start.20 = (bf16[48,1024]{1,0:T(8,128)(2,1)S(1)}, bf16[48,1024]{1,0:T(8,128)(2,1)S(1)}, u32[]{:S(2)}, u32[]{:S(2)}) collective-permute-start(bf16[48,1024]{1,0:T(8,128)(2,1)S(1)} %get-tuple-element.85), channel_id=1, source_target_pairs={{0,3},{1,30},{2,5},{3,0},{4,7},{5,2},{6,9},{7,4},{8,11},{9,6},{10,... | collective-permute-start | bytes 294920 | tf_op jit(solution)/shard_map/ppermute | solution.py:32
  81.1 18.9 %collective-permute-start.18 = (bf16[160,1024]{1,0:T(8,128)(2,1)S(1)}, bf16[160,1024]{1,0:T(8,128)(2,1)S(1)}, u32[]{:S(2)}, u32[]{:S(2)}) collective-permute-start(bf16[160,1024]{1,0:T(8,128)(2,1)S(1)} %get-tuple-element.82), channel_id=1, source_target_pairs={{0,2},{1,3},{2,0},{3,1},{4,6},{5,7},{6,4},{7,5},{8,10},{9,11},{10,... | collective-permute-start | bytes 983048 | tf_op jit(solution)/shard_map/ppermute | solution.py:32
  81.1 20.2 %collective-permute-start.19 = (bf16[160,1024]{1,0:T(8,128)(2,1)S(1)}, bf16[160,1024]{1,0:T(8,128)(2,1)S(1)}, u32[]{:S(2)}, u32[]{:S(2)}) collective-permute-start(bf16[160,1024]{1,0:T(8,128)(2,1)S(1)} %get-tuple-element.84), channel_id=1, source_target_pairs={{0,30},{1,31},{2,4},{3,5},{4,2},{5,3},{6,8},{7,9},{8,6},{9,7},{10,... | collective-permute-start | bytes 983048 | tf_op jit(solution)/shard_map/ppermute | solution.py:32
  89.4 15.8 %collective-permute-start.21 = (bf16[256,1024]{1,0:T(8,128)(2,1)S(1)}, bf16[256,1024]{1,0:T(8,128)(2,1)S(1)}, u32[]{:S(2)}, u32[]{:S(2)}) collective-permute-start(bf16[256,1024]{1,0:T(8,128)(2,1)S(1)} %get-tuple-element.86), channel_id=1, source_target_pairs={{0,1},{1,0},{2,3},{3,2},{4,5},{5,4},{6,7},{7,6},{8,9},{9,8},{10,11... | collective-permute-start | bytes 1572872 | tf_op jit(solution)/shard_map/ppermute | solution.py:32
  92.5 14.4 %collective-permute-start.22 = (bf16[256,1024]{1,0:T(8,128)(2,1)S(1)}, bf16[256,1024]{1,0:T(8,128)(2,1)S(1)}, u32[]{:S(2)}, u32[]{:S(2)}) collective-permute-start(bf16[256,1024]{1,0:T(8,128)(2,1)S(1)} %get-tuple-element.87), channel_id=1, source_target_pairs={{0,31},{1,2},{2,1},{3,4},{4,3},{5,6},{6,5},{7,8},{8,7},{9,10},{10,... | collective-permute-start | bytes 1572872 | tf_op jit(solution)/shard_map/ppermute | solution.py:32
  100.0 5.2 %collective-permute-start.23 = (bf16[48,1024]{1,0:T(8,128)(2,1)S(1)}, bf16[48,1024]{1,0:T(8,128)(2,1)S(1)}, u32[]{:S(2)}, u32[]{:S(2)}) collective-permute-start(bf16[48,1024]{1,0:T(8,128)(2,1)S(1)} %get-tuple-element.88), channel_id=1, source_target_pairs={{0,29},{1,4},{2,31},{3,6},{4,1},{5,8},{6,3},{7,10},{8,5},{9,12},{1... | collective-permute-start | bytes 294920 | tf_op jit(solution)/shard_map/ppermute | solution.py:32
  (6 other events, 71.2 us)

commit v10 on v8

--- a/solution.py
+++ b/solution.py
@@ -12,7 +12,7 @@
 AXES = ("func", "box")
 REACH = 3
 SLOT = 32
-STEP = 8
+STEP = 12
 
 
 def passed_along(value, steps):

time: 111 us -> 111 us (level)
  Pallas kernels: 33.9 us -> 31 us
  starting transfers between devices: 50.1 us -> 52.1 us
    ppermute x18, starting transfers between devices: 23.6 us -> 25.6 us  [swapped(): return lax.ppermute(value, AXES, pairs)]
    pallas_call x2, Pallas kernels: 13.9 us -> 12.2 us  [on_device(): pl.pallas_call(functools.partial(mix_kernel, (fun_dev, reading, group, wh...]
    pallas_call x1, Pallas kernels: 7.79 us -> 6.59 us  [on_device(): pl.pallas_call(functools.partial(unpack_kernel, (fun_dev, box_dev, readin...]
  transfers between devices with their start and end apart: 24 -> 24, of which waited for: 9 -> 9; matrix products, arithmetic and copies ran while one was open for 2% -> 2% of each run, Pallas kernels for 17% -> 16%
where the time goes in v10:
time: 111 us
  starting transfers between devices  52.1 us (47%)
  Pallas kernels  31 us (28%)
  waiting for transfers between devices  23.3 us (21%)
  matrix products  1.72 us (2%)
  local copies, waits for them, and re-layouts  1.65 us (1%)
    ppermute x6, starting transfers between devices, passed_along(): return lax.ppermute(value, AXES, pairs)  26.5 us
    ppermute x18, starting transfers between devices, swapped(): return lax.ppermute(value, AXES, pairs)  25.6 us
    ppermute x18, waiting for transfers between devices, swapped(): return lax.ppermute(value, AXES, pairs)  14.6 us
    pallas_call x2, Pallas kernels, on_device(): pl.pallas_call(functools.partial(mix_kernel, (fun_dev, reading, group, wh...  12.2 us
    ppermute x6, waiting for transfers between devices, passed_along(): return lax.ppermute(value, AXES, pairs)  8.68 us
    pallas_call x1, Pallas kernels, on_device(): pl.pallas_call(functools.partial(unpack_kernel, (fun_dev, box_dev, readin...  6.59 us
    pallas_call x1, Pallas kernels, on_device(): pl.pallas_call(functools.partial(pack_kernel, (fun_dev, support, devices,...  4.11 us
    pallas_call x1, Pallas kernels, on_device(): pl.pallas_call(functools.partial(table_kernel, (fun_dev, support, halo, b...  2.71 us
  transfers between devices with their start and end apart: 24, of which 9 were waited for; matrix products, arithmetic and copies ran while one was open for 2% of the time, Pallas kernels for 16%

profile of v10, /device:TPU:1, one launch (start us, length us, event | category | flops | bytes accessed | tf_op | source)
XLA Modules:
  0.0 110.7 jit_solution(4408558454870564555)
XLA Ops:
  2.3 4.1 %pack.1 = (bf16[272,1024]{1,0:T(8,128)(2,1)}, bf16[240,1024]{1,0:T(8,128)(2,1)S(1)}, bf16[192,1024]{1,0:T(8,128)(2,1)S(1)}, bf16[160,1024]{1,0:T(8,128)(2,1)S(1)...) custom-call(s32[1]{0:T(128)} %bitcast.me_ref, ...), custom_call_target="tpu_custom_call" | custom-call | tf_op jit(solution)/shard_map/pack/pallas_call | solution.py:544
  6.5 2.6 %collective-permute-start.2 = (bf16[240,1024]{1,0:T(8,128)(2,1)S(1)}, bf16[240,1024]{1,0:T(8,128)(2,1)S(1)}, u32[]{:S(2)}, u32[]{:S(2)}) collective-permute-start(bf16[240,1024]{1,0:T(8,128)(2,1)S(1)} %get-tuple-element.54), channel_id=1, source_target_pairs={{0,1},{1,2},{2,3},{3,4},{4,5},{5,6},{6,7},{7,8},{8,9},{9,10},{10,1... | collective-permute-start | bytes 1474568 | tf_op jit(solution)/shard_map/ppermute | solution.py:21
  9.1 8.7 %collective-permute-start.4 = (bf16[192,1024]{1,0:T(8,128)(2,1)S(1)}, bf16[192,1024]{1,0:T(8,128)(2,1)S(1)}, u32[]{:S(2)}, u32[]{:S(2)}) collective-permute-start(bf16[192,1024]{1,0:T(8,128)(2,1)S(1)} %get-tuple-element.58), channel_id=1, source_target_pairs={{0,30},{1,31},{2,0},{3,1},{4,2},{5,3},{6,4},{7,5},{8,6},{9,7},{10,... | collective-permute-start | bytes 1179656 | tf_op jit(solution)/shard_map/ppermute | solution.py:21
  17.8 3.3 %collective-permute-done.3.refs_3_ = bf16[272,1024]{1,0:T(8,128)(2,1)S(1)} collective-permute-done((bf16[272,1024]{1,0:T(8,128)(2,1)}, bf16[272,1024]{1,0:T(8,128)(2,1)S(1)}, u32[]{:S(2)}, u32[]{:S(2)}) %collective-permute-start.3) | collective-permute-done | bytes 557088 | tf_op jit(solution)/shard_map/ppermute | solution.py:21
  21.1 15.0 %collective-permute-start.5 = (bf16[64,1024]{1,0:T(8,128)(2,1)S(1)}, bf16[64,1024]{1,0:T(8,128)(2,1)S(1)}, u32[]{:S(2)}, u32[]{:S(2)}) collective-permute-start(bf16[64,1024]{1,0:T(8,128)(2,1)S(1)} %get-tuple-element.59), channel_id=1, source_target_pairs={{0,29},{1,30},{2,31},{3,0},{4,1},{5,2},{6,3},{7,4},{8,5},{9,6},{10... | collective-permute-start | bytes 393224 | tf_op jit(solution)/shard_map/ppermute | solution.py:21
  36.2 2.7 %tables.1 = (f32[224,128]{1,0:T(8,128)S(1)}, f32[2,8,384]{2,1,0:T(8,128)S(1)}, s32[16]{0:T(128)S(1)}, bf16[24,32,1024]{2,1,0:T(8,128)(2,1)S(1)}) custom-call(s32[8]{0:T(128)S(1)} %get-tuple-element.74.cut_ref, f32[512,128]{1,0:T(8,128)S(1)} %get-tuple-element.46.near_ref, bf16[768,1024]{1,0:T(8,128)(2,1)S(1)} %bitcast.8), custom_call_target="tpu_custom_call" | custom-call | tf_op jit(solution)/shard_map/tables/pallas_call | solution.py:566
  38.9 5.4 %collective-permute-done.refs_0_ = bf16[48,1024]{1,0:T(8,128)(2,1)S(1)} collective-permute-done((bf16[48,1024]{1,0:T(8,128)(2,1)S(1)}, bf16[48,1024]{1,0:T(8,128)(2,1)S(1)}, u32[]{:S(2)}, u32[]{:S(2)}) %collective-permute-start) | collective-permute-done | bytes 98336 | tf_op jit(solution)/shard_map/ppermute | solution.py:21
  44.3 6.6 %unpack.1 = (bf16[24,224,1024]{2,1,0:T(8,128)(2,1)S(1)}, bf16[128,1024]{1,0:T(8,128)(2,1)S(1)}, f32[24,256]{1,0:T(8,128)S(1)}, f32[24,256]{1,0:T(8,128)S(1)}, f3...) custom-call(s32[8]{0:T(128)S(1)} %get-tuple-element.74.cut_ref, ...), custom_call_target="tpu_custom_call" | custom-call | tf_op jit(solution)/shard_map/unpack/pallas_call | solution.py:588
  52.1 2.2 %collective-permute-start.8 = (f32[24,256]{1,0:T(8,128)S(1)}, f32[24,256]{1,0:T(8,128)S(1)}, u32[]{:S(2)}, u32[]{:S(2)}) collective-permute-start(f32[24,256]{1,0:T(8,128)S(1)} %get-tuple-element.65), channel_id=1, source_target_pairs={{0,3},{1,30},{2,5},{3,0},{4,7},{5,2},{6,9},{7,4},{8,11},{9,6},{10,... | collective-permute-start | bytes 73736 | tf_op jit(solution)/shard_map/ppermute | solution.py:32
  54.2 3.4 %collective-permute-start.10 = (f32[24,256]{1,0:T(8,128)S(1)}, f32[24,256]{1,0:T(8,128)S(1)}, u32[]{:S(2)}, u32[]{:S(2)}) collective-permute-start(f32[24,256]{1,0:T(8,128)S(1)} %get-tuple-element.67), channel_id=1, source_target_pairs={{0,30},{1,31},{2,4},{3,5},{4,2},{5,3},{6,8},{7,9},{8,6},{9,7},{10,... | collective-permute-start | bytes 73736 | tf_op jit(solution)/shard_map/ppermute | solution.py:32
  57.7 1.6 %collective-permute-done.8.refs_3_ = f32[24,256]{1,0:T(8,128)S(1)} collective-permute-done((f32[24,256]{1,0:T(8,128)S(1)}, f32[24,256]{1,0:T(8,128)S(1)}, u32[]{:S(2)}, u32[]{:S(2)}) %collective-permute-start.8) | collective-permute-done | bytes 24608 | tf_op jit(solution)/shard_map/ppermute | solution.py:32
  59.3 1.3 %collective-permute-done.10.refs_5_ = f32[24,256]{1,0:T(8,128)S(1)} collective-permute-done((f32[24,256]{1,0:T(8,128)S(1)}, f32[24,256]{1,0:T(8,128)S(1)}, u32[]{:S(2)}, u32[]{:S(2)}) %collective-permute-start.10) | collective-permute-done | bytes 24608 | tf_op jit(solution)/shard_map/ppermute | solution.py:32
  61.8 4.9 %collective-permute-start.15 = (bf16[32,256]{1,0:T(8,128)(2,1)S(1)}, bf16[32,256]{1,0:T(8,128)(2,1)S(1)}, u32[]{:S(2)}, u32[]{:S(2)}) collective-permute-start(bf16[32,256]{1,0:T(8,128)(2,1)S(1)} %get-tuple-element.69.refs_0_), channel_id=1, source_target_pairs={{0,30},{1,31},{2,4},{3,5},{4,2},{5,3},{6,8},{7,9},{8,6},{9,7},{10,... | collective-permute-start | bytes 49160 | tf_op jit(solution)/shard_map/ppermute | solution.py:32
  66.8 3.7 %collective-permute-start.13 = (bf16[32,256]{1,0:T(8,128)(2,1)S(1)}, bf16[32,256]{1,0:T(8,128)(2,1)S(1)}, u32[]{:S(2)}, u32[]{:S(2)}) collective-permute-start(bf16[32,256]{1,0:T(8,128)(2,1)S(1)} %get-tuple-element.69.refs_0_), channel_id=1, source_target_pairs={{0,3},{1,30},{2,5},{3,0},{4,7},{5,2},{6,9},{7,4},{8,11},{9,6},{10,... | collective-permute-start | bytes 49160 | tf_op jit(solution)/shard_map/ppermute | solution.py:32
  70.5 2.1 %collective-permute-start.16 = (bf16[32,256]{1,0:T(8,128)(2,1)S(1)}, bf16[32,256]{1,0:T(8,128)(2,1)S(1)}, u32[]{:S(2)}, u32[]{:S(2)}) collective-permute-start(bf16[32,256]{1,0:T(8,128)(2,1)S(1)} %get-tuple-element.69.refs_0_), channel_id=1, source_target_pairs={{0,1},{1,0},{2,3},{3,2},{4,5},{5,4},{6,7},{7,6},{8,9},{9,8},{10,11... | collective-permute-start | bytes 49160 | tf_op jit(solution)/shard_map/ppermute | solution.py:32
  73.5 5.5 %mix.2 = (bf16[48,1024]{1,0:T(8,128)(2,1)S(1)}, bf16[160,1024]{1,0:T(8,128)(2,1)S(1)}, bf16[160,1024]{1,0:T(8,128)(2,1)S(1)}, bf16[48,1024]{1,0:T(8,128)(2,1)S(1...) custom-call(s32[8]{0:T(128)S(1)} %get-tuple-element.74.cut_ref, ...), custom_call_target="tpu_custom_call" | custom-call | flops 5637144576 | bytes 41943040 | tf_op jit(solution)/shard_map/mix/pallas_call | solution.py:631
  79.1 3.8 %collective-permute-start.20 = (bf16[48,1024]{1,0:T(8,128)(2,1)S(1)}, bf16[48,1024]{1,0:T(8,128)(2,1)S(1)}, u32[]{:S(2)}, u32[]{:S(2)}) collective-permute-start(bf16[48,1024]{1,0:T(8,128)(2,1)S(1)} %get-tuple-element.81), channel_id=1, source_target_pairs={{0,3},{1,30},{2,5},{3,0},{4,7},{5,2},{6,9},{7,4},{8,11},{9,6},{10,... | collective-permute-start | bytes 294920 | tf_op jit(solution)/shard_map/ppermute | solution.py:32
  83.4 6.7 %mix.3 = (bf16[256,1024]{1,0:T(8,128)(2,1)S(1)}, bf16[512,1024]{1,0:T(8,128)(2,1)S(1)}, bf16[256,1024]{1,0:T(8,128)(2,1)S(1)}, bf16[256,128]{1,0:T(8,128)(2,1)},...) custom-call(s32[8]{0:T(128)S(1)} %get-tuple-element.74.cut_ref, s32[1]{0:T(128)} %bitcast.me_ref, ...), custom_call_target="tpu_custom_call" | custom-call | flops 4227858432 | bytes 41943040 | tf_op jit(solution)/shard_map/mix/pallas_call | solution.py:631
  90.1 3.8 %collective-permute-start.21 = (bf16[256,1024]{1,0:T(8,128)(2,1)S(1)}, bf16[256,1024]{1,0:T(8,128)(2,1)S(1)}, u32[]{:S(2)}, u32[]{:S(2)}) collective-permute-start(bf16[256,1024]{1,0:T(8,128)(2,1)S(1)} %get-tuple-element.82), channel_id=1, source_target_pairs={{0,1},{1,0},{2,3},{3,2},{4,5},{5,4},{6,7},{7,6},{8,9},{9,8},{10,11... | collective-permute-start | bytes 1572872 | tf_op jit(solution)/shard_map/ppermute | solution.py:32
  94.3 7.4 %collective-permute-done.18.refs_1_ = bf16[160,1024]{1,0:T(8,128)(2,1)S(1)} collective-permute-done((bf16[160,1024]{1,0:T(8,128)(2,1)S(1)}, bf16[160,1024]{1,0:T(8,128)(2,1)S(1)}, u32[]{:S(2)}, u32[]{:S(2)}) %collective-permute-start.18) | collective-permute-done | bytes 327712 | tf_op jit(solution)/shard_map/ppermute | solution.py:32
  103.0 2.4 %early.1.early_ref = bf16[768,1024]{1,0:T(8,128)(2,1)S(1)} custom-call(s32[1]{0:T(128)} %bitcast.me_ref, f32[1,768]{1,0:T(1,128)S(1)} %get-tuple-element.44.home_ref, bf16[512,1024]{1,0:T(8,128)(2,1)S(1)} %add_convert_fusion.refs_0_, bf16[160,1024]{1,0:T(8,128)(2,1)S(1)} %collective-permute-done.18.refs_1_, ...), custom_call_target="tpu_custom_call" | custom-call | tf_op jit(solution)/shard_map/early/pallas_call | solution.py:662
  105.4 1.4 %collective-permute-done.23.refs_2_ = bf16[48,1024]{1,0:T(8,128)(2,1)S(1)} collective-permute-done((bf16[48,1024]{1,0:T(8,128)(2,1)S(1)}, bf16[48,1024]{1,0:T(8,128)(2,1)S(1)}, u32[]{:S(2)}, u32[]{:S(2)}) %collective-permute-start.23) | collective-permute-done | bytes 98336 | tf_op jit(solution)/shard_map/ppermute | solution.py:32
  106.8 1.3 %collective-permute-done.22.refs_1_ = bf16[256,1024]{1,0:T(8,128)(2,1)S(1)} collective-permute-done((bf16[256,1024]{1,0:T(8,128)(2,1)S(1)}, bf16[256,1024]{1,0:T(8,128)(2,1)S(1)}, u32[]{:S(2)}, u32[]{:S(2)}) %collective-permute-start.22) | collective-permute-done | bytes 524320 | tf_op jit(solution)/shard_map/ppermute | solution.py:32
  108.2 2.4 %home.1 = bf16[768,1024]{1,0:T(8,128)(2,1)} custom-call(s32[1]{0:T(128)} %bitcast.me_ref, f32[1,768]{1,0:T(1,128)S(1)} %get-tuple-element.44.home_ref, bf16[768,1024]{1,0:T(8,128)(2,1)S(1)} %early.1.early_ref, bf16[256,1024]{1,0:T(8,128)(2,1)S(1)} %collective-permute-done.21.refs_0_, bf16[256,1024]{1,0:T(8,128)(2,1)S(1)} %collective-permute-done.22.refs_1_, ...), custom_call_target="tpu_custom_call" | custom-call | tf_op jit(solution)/shard_map/home/pallas_call | solution.py:670
  (42 shorter events, 7.4 us)
Async XLA Ops:
  6.4 14.7 %collective-permute-start.3 = (bf16[272,1024]{1,0:T(8,128)(2,1)}, bf16[272,1024]{1,0:T(8,128)(2,1)S(1)}, u32[]{:S(2)}, u32[]{:S(2)}) collective-permute-start(bf16[272,1024]{1,0:T(8,128)(2,1)} %get-tuple-element.56), channel_id=1, source_target_pairs={{0,31},{1,0},{2,1},{3,2},{4,3},{5,4},{6,5},{7,6},{8,7},{9,8},{10,9... | collective-permute-start | bytes 1671176 | tf_op jit(solution)/shard_map/ppermute | solution.py:21
  6.5 37.8 %collective-permute-start.2 = (bf16[240,1024]{1,0:T(8,128)(2,1)S(1)}, bf16[240,1024]{1,0:T(8,128)(2,1)S(1)}, u32[]{:S(2)}, u32[]{:S(2)}) collective-permute-start(bf16[240,1024]{1,0:T(8,128)(2,1)S(1)} %get-tuple-element.54), channel_id=1, source_target_pairs={{0,1},{1,2},{2,3},{3,4},{4,5},{5,6},{6,7},{7,8},{8,9},{9,10},{10,1... | collective-permute-start | bytes 1474568 | tf_op jit(solution)/shard_map/ppermute | solution.py:21
  9.1 35.2 %collective-permute-start.4 = (bf16[192,1024]{1,0:T(8,128)(2,1)S(1)}, bf16[192,1024]{1,0:T(8,128)(2,1)S(1)}, u32[]{:S(2)}, u32[]{:S(2)}) collective-permute-start(bf16[192,1024]{1,0:T(8,128)(2,1)S(1)} %get-tuple-element.58), channel_id=1, source_target_pairs={{0,30},{1,31},{2,0},{3,1},{4,2},{5,3},{6,4},{7,5},{8,6},{9,7},{10,... | collective-permute-start | bytes 1179656 | tf_op jit(solution)/shard_map/ppermute | solution.py:21
  17.8 26.5 %collective-permute-start.1 = (bf16[160,1024]{1,0:T(8,128)(2,1)S(1)}, bf16[160,1024]{1,0:T(8,128)(2,1)S(1)}, u32[]{:S(2)}, u32[]{:S(2)}) collective-permute-start(bf16[160,1024]{1,0:T(8,128)(2,1)S(1)} %get-tuple-element.53), channel_id=1, source_target_pairs={{0,2},{1,3},{2,4},{3,5},{4,6},{5,7},{6,8},{7,9},{8,10},{9,11},{10,... | collective-permute-start | bytes 983048 | tf_op jit(solution)/shard_map/ppermute | solution.py:21
  21.1 23.2 %collective-permute-start.5 = (bf16[64,1024]{1,0:T(8,128)(2,1)S(1)}, bf16[64,1024]{1,0:T(8,128)(2,1)S(1)}, u32[]{:S(2)}, u32[]{:S(2)}) collective-permute-start(bf16[64,1024]{1,0:T(8,128)(2,1)S(1)} %get-tuple-element.59), channel_id=1, source_target_pairs={{0,29},{1,30},{2,31},{3,0},{4,1},{5,2},{6,3},{7,4},{8,5},{9,6},{10... | collective-permute-start | bytes 393224 | tf_op jit(solution)/shard_map/ppermute | solution.py:21
  36.2 8.1 %collective-permute-start = (bf16[48,1024]{1,0:T(8,128)(2,1)S(1)}, bf16[48,1024]{1,0:T(8,128)(2,1)S(1)}, u32[]{:S(2)}, u32[]{:S(2)}) collective-permute-start(bf16[48,1024]{1,0:T(8,128)(2,1)S(1)} %get-tuple-element.52), channel_id=1, source_target_pairs={{0,3},{1,4},{2,5},{3,6},{4,7},{5,8},{6,9},{7,10},{8,11},{9,12},{10... | collective-permute-start | bytes 294920 | tf_op jit(solution)/shard_map/ppermute | solution.py:21
  50.9 6.8 %collective-permute-start.6 = (f32[24,256]{1,0:T(8,128)S(1)}, f32[24,256]{1,0:T(8,128)S(1)}, u32[]{:S(2)}, u32[]{:S(2)}) collective-permute-start(f32[24,256]{1,0:T(8,128)S(1)} %get-tuple-element.63), channel_id=1, source_target_pairs={{0,1},{1,0},{2,3},{3,2},{4,5},{5,4},{6,7},{7,6},{8,9},{9,8},{10,11... | collective-permute-start | bytes 73736 | tf_op jit(solution)/shard_map/ppermute | solution.py:32
  52.1 5.6 %collective-permute-start.7 = (f32[24,256]{1,0:T(8,128)S(1)}, f32[24,256]{1,0:T(8,128)S(1)}, u32[]{:S(2)}, u32[]{:S(2)}) collective-permute-start(f32[24,256]{1,0:T(8,128)S(1)} %get-tuple-element.64), channel_id=1, source_target_pairs={{0,2},{1,3},{2,0},{3,1},{4,6},{5,7},{6,4},{7,5},{8,10},{9,11},{10,... | collective-permute-start | bytes 73736 | tf_op jit(solution)/shard_map/ppermute | solution.py:32
  52.1 7.2 %collective-permute-start.8 = (f32[24,256]{1,0:T(8,128)S(1)}, f32[24,256]{1,0:T(8,128)S(1)}, u32[]{:S(2)}, u32[]{:S(2)}) collective-permute-start(f32[24,256]{1,0:T(8,128)S(1)} %get-tuple-element.65), channel_id=1, source_target_pairs={{0,3},{1,30},{2,5},{3,0},{4,7},{5,2},{6,9},{7,4},{8,11},{9,6},{10,... | collective-permute-start | bytes 73736 | tf_op jit(solution)/shard_map/ppermute | solution.py:32
  54.2 5.0 %collective-permute-start.9 = (f32[24,256]{1,0:T(8,128)S(1)}, f32[24,256]{1,0:T(8,128)S(1)}, u32[]{:S(2)}, u32[]{:S(2)}) collective-permute-start(f32[24,256]{1,0:T(8,128)S(1)} %get-tuple-element.66), channel_id=1, source_target_pairs={{0,29},{1,4},{2,31},{3,6},{4,1},{5,8},{6,3},{7,10},{8,5},{9,12},{1... | collective-permute-start | bytes 73736 | tf_op jit(solution)/shard_map/ppermute | solution.py:32
  54.2 6.3 %collective-permute-start.10 = (f32[24,256]{1,0:T(8,128)S(1)}, f32[24,256]{1,0:T(8,128)S(1)}, u32[]{:S(2)}, u32[]{:S(2)}) collective-permute-start(f32[24,256]{1,0:T(8,128)S(1)} %get-tuple-element.67), channel_id=1, source_target_pairs={{0,30},{1,31},{2,4},{3,5},{4,2},{5,3},{6,8},{7,9},{8,6},{9,7},{10,... | collective-permute-start | bytes 73736 | tf_op jit(solution)/shard_map/ppermute | solution.py:32
  57.7 3.5 %collective-permute-start.11 = (f32[24,256]{1,0:T(8,128)S(1)}, f32[24,256]{1,0:T(8,128)S(1)}, u32[]{:S(2)}, u32[]{:S(2)}) collective-permute-start(f32[24,256]{1,0:T(8,128)S(1)} %get-tuple-element.68), channel_id=1, source_target_pairs={{0,31},{1,2},{2,1},{3,4},{4,3},{5,6},{6,5},{7,8},{8,7},{9,10},{10,... | collective-permute-start | bytes 73736 | tf_op jit(solution)/shard_map/ppermute | solution.py:32
  61.8 8.7 %collective-permute-start.15 = (bf16[32,256]{1,0:T(8,128)(2,1)S(1)}, bf16[32,256]{1,0:T(8,128)(2,1)S(1)}, u32[]{:S(2)}, u32[]{:S(2)}) collective-permute-start(bf16[32,256]{1,0:T(8,128)(2,1)S(1)} %get-tuple-element.69.refs_0_), channel_id=1, source_target_pairs={{0,30},{1,31},{2,4},{3,5},{4,2},{5,3},{6,8},{7,9},{8,6},{9,7},{10,... | collective-permute-start | bytes 49160 | tf_op jit(solution)/shard_map/ppermute | solution.py:32
  66.8 5.9 %collective-permute-start.14 = (bf16[32,256]{1,0:T(8,128)(2,1)S(1)}, bf16[32,256]{1,0:T(8,128)(2,1)S(1)}, u32[]{:S(2)}, u32[]{:S(2)}) collective-permute-start(bf16[32,256]{1,0:T(8,128)(2,1)S(1)} %get-tuple-element.69.refs_0_), channel_id=1, source_target_pairs={{0,29},{1,4},{2,31},{3,6},{4,1},{5,8},{6,3},{7,10},{8,5},{9,12},{1... | collective-permute-start | bytes 49160 | tf_op jit(solution)/shard_map/ppermute | solution.py:32
  66.8 6.8 %collective-permute-start.13 = (bf16[32,256]{1,0:T(8,128)(2,1)S(1)}, bf16[32,256]{1,0:T(8,128)(2,1)S(1)}, u32[]{:S(2)}, u32[]{:S(2)}) collective-permute-start(bf16[32,256]{1,0:T(8,128)(2,1)S(1)} %get-tuple-element.69.refs_0_), channel_id=1, source_target_pairs={{0,3},{1,30},{2,5},{3,0},{4,7},{5,2},{6,9},{7,4},{8,11},{9,6},{10,... | collective-permute-start | bytes 49160 | tf_op jit(solution)/shard_map/ppermute | solution.py:32
  70.5 3.0 %collective-permute-start.12 = (bf16[32,256]{1,0:T(8,128)(2,1)S(1)}, bf16[32,256]{1,0:T(8,128)(2,1)S(1)}, u32[]{:S(2)}, u32[]{:S(2)}) collective-permute-start(bf16[32,256]{1,0:T(8,128)(2,1)S(1)} %get-tuple-element.69.refs_0_), channel_id=1, source_target_pairs={{0,2},{1,3},{2,0},{3,1},{4,6},{5,7},{6,4},{7,5},{8,10},{9,11},{10,... | collective-permute-start | bytes 49160 | tf_op jit(solution)/shard_map/ppermute | solution.py:32
  70.5 12.8 %collective-permute-start.17 = (bf16[32,256]{1,0:T(8,128)(2,1)S(1)}, bf16[32,256]{1,0:T(8,128)(2,1)S(1)}, u32[]{:S(2)}, u32[]{:S(2)}) collective-permute-start(bf16[32,256]{1,0:T(8,128)(2,1)S(1)} %get-tuple-element.69.refs_0_), channel_id=1, source_target_pairs={{0,31},{1,2},{2,1},{3,4},{4,3},{5,6},{6,5},{7,8},{8,7},{9,10},{10,... | collective-permute-start | bytes 49160 | tf_op jit(solution)/shard_map/ppermute | solution.py:32
  70.5 12.8 %collective-permute-start.16 = (bf16[32,256]{1,0:T(8,128)(2,1)S(1)}, bf16[32,256]{1,0:T(8,128)(2,1)S(1)}, u32[]{:S(2)}, u32[]{:S(2)}) collective-permute-start(bf16[32,256]{1,0:T(8,128)(2,1)S(1)} %get-tuple-element.69.refs_0_), channel_id=1, source_target_pairs={{0,1},{1,0},{2,3},{3,2},{4,5},{5,4},{6,7},{7,6},{8,9},{9,8},{10,11... | collective-permute-start | bytes 49160 | tf_op jit(solution)/shard_map/ppermute | solution.py:32
  79.1 24.0 %collective-permute-start.20 = (bf16[48,1024]{1,0:T(8,128)(2,1)S(1)}, bf16[48,1024]{1,0:T(8,128)(2,1)S(1)}, u32[]{:S(2)}, u32[]{:S(2)}) collective-permute-start(bf16[48,1024]{1,0:T(8,128)(2,1)S(1)} %get-tuple-element.81), channel_id=1, source_target_pairs={{0,3},{1,30},{2,5},{3,0},{4,7},{5,2},{6,9},{7,4},{8,11},{9,6},{10,... | collective-permute-start | bytes 294920 | tf_op jit(solution)/shard_map/ppermute | solution.py:32
  82.8 18.9 %collective-permute-start.18 = (bf16[160,1024]{1,0:T(8,128)(2,1)S(1)}, bf16[160,1024]{1,0:T(8,128)(2,1)S(1)}, u32[]{:S(2)}, u32[]{:S(2)}) collective-permute-start(bf16[160,1024]{1,0:T(8,128)(2,1)S(1)} %get-tuple-element.78), channel_id=1, source_target_pairs={{0,2},{1,3},{2,0},{3,1},{4,6},{5,7},{6,4},{7,5},{8,10},{9,11},{10,... | collective-permute-start | bytes 983048 | tf_op jit(solution)/shard_map/ppermute | solution.py:32
  82.8 20.2 %collective-permute-start.19 = (bf16[160,1024]{1,0:T(8,128)(2,1)S(1)}, bf16[160,1024]{1,0:T(8,128)(2,1)S(1)}, u32[]{:S(2)}, u32[]{:S(2)}) collective-permute-start(bf16[160,1024]{1,0:T(8,128)(2,1)S(1)} %get-tuple-element.80), channel_id=1, source_target_pairs={{0,30},{1,31},{2,4},{3,5},{4,2},{5,3},{6,8},{7,9},{8,6},{9,7},{10,... | collective-permute-start | bytes 983048 | tf_op jit(solution)/shard_map/ppermute | solution.py:32
  90.1 16.7 %collective-permute-start.21 = (bf16[256,1024]{1,0:T(8,128)(2,1)S(1)}, bf16[256,1024]{1,0:T(8,128)(2,1)S(1)}, u32[]{:S(2)}, u32[]{:S(2)}) collective-permute-start(bf16[256,1024]{1,0:T(8,128)(2,1)S(1)} %get-tuple-element.82), channel_id=1, source_target_pairs={{0,1},{1,0},{2,3},{3,2},{4,5},{5,4},{6,7},{7,6},{8,9},{9,8},{10,11... | collective-permute-start | bytes 1572872 | tf_op jit(solution)/shard_map/ppermute | solution.py:32
  93.9 14.3 %collective-permute-start.22 = (bf16[256,1024]{1,0:T(8,128)(2,1)S(1)}, bf16[256,1024]{1,0:T(8,128)(2,1)S(1)}, u32[]{:S(2)}, u32[]{:S(2)}) collective-permute-start(bf16[256,1024]{1,0:T(8,128)(2,1)S(1)} %get-tuple-element.83), channel_id=1, source_target_pairs={{0,31},{1,2},{2,1},{3,4},{4,3},{5,6},{6,5},{7,8},{8,7},{9,10},{10,... | collective-permute-start | bytes 1572872 | tf_op jit(solution)/shard_map/ppermute | solution.py:32
  101.7 5.1 %collective-permute-start.23 = (bf16[48,1024]{1,0:T(8,128)(2,1)S(1)}, bf16[48,1024]{1,0:T(8,128)(2,1)S(1)}, u32[]{:S(2)}, u32[]{:S(2)}) collective-permute-start(bf16[48,1024]{1,0:T(8,128)(2,1)S(1)} %get-tuple-element.84), channel_id=1, source_target_pairs={{0,29},{1,4},{2,31},{3,6},{4,1},{5,8},{6,3},{7,10},{8,5},{9,12},{1... | collective-permute-start | bytes 294920 | tf_op jit(solution)/shard_map/ppermute | solution.py:32
  (4 other events, 71.8 us)
